TPU v7x, 32 devices: a whole 2x2x4 slice. The times are simulated.
32 devices in a mesh: seq: 16 (over z, y, x), res: 2 (over core).
Axes of the slice: x: 2, y: 2, z: 4, core: 2. Of those that a mesh axis runs over, the one named last changes fastest.
Arguments:
- alignment: bfloat16 [32, 128, 64], P('seq', 'res'), may hold values from -16 to 16
- cotangent: bfloat16 [32, 128, 64], P('seq', 'res'), may hold values from -6 to 6
- pair_bias: bfloat16 [8, 128, 128], P(None, 'res'), may hold values from -8 to 360
- norm_gains: float32 [2, 64], replicated, may hold values from 0.5 to 1.5
- row_project: float32 [64, 256], replicated, may hold values from -0.75 to 0.75
- row_output: float32 [64, 64], replicated, may hold values from -0.75 to 0.75
- column_project: float32 [64, 144], replicated, may hold values from -16 to 16
- column_output: float32 [64, 64], replicated, may hold values from -0.75 to 0.75
- residue_mask: int32 [128], P('res'), may hold values 0 or 1
- sequence_mask: int32 [32], P('seq'), may hold values from 0 to 1, as said below
Outputs:
- grad_alignment: bfloat16 [32, 128, 64], P('seq', 'res')
- grad_pair_bias: float32 [8, 128, 128], P(None, 'res', 'seq')
- grad_gains: float32 [2, 64], replicated
- grad_row_project: float32 [64, 256], replicated
- grad_row_output: float32 [64, 64], replicated
- grad_column_project: float32 [64, 144], replicated
- grad_column_output: float32 [64, 64], replicated
Inputs may be any that keep to these rules, and one draw needn't show every extreme that they name: `sequence_mask`: at least one extra sequence is present.
All inputs are finite; a program needn't handle non-finite values. No bound on the sum of `residue_mask` on one device may be relied on, other than what follows from the above.
Results may differ from a plain program's by a relative error of at most 0.0027.
Values sent between devices are 32-bit elements; how exact they have to be, the bound alone decides.
No kernel may reach another device: no remote copies, remote signals or barrier semaphores. Data moves between devices by JAX's collectives and lax.ppermute only.
A program may use at most 128 MiB of HBM per device.

v0:
```python
import jax
import jax.numpy as jnp
from jax import lax
from jax.sharding import PartitionSpec as P

C = 64
H = 8
DH = 8


PRECISE = lax.Precision.HIGHEST
EPSILON = 1e-05
MASKED = 1000000000.0


def layer_norm(values, gain_vector):
    centre = jnp.mean(values, axis=-1, keepdims=True)
    centred = values - centre
    spread = jnp.mean(centred * centred, axis=-1, keepdims=True)
    return centred * lax.rsqrt(spread + EPSILON) * gain_vector


def split_heads(memory):
    key_rows = memory[:, :C].reshape(memory.shape[0], H, DH)
    value_rows = memory[:, C:].reshape(memory.shape[0], H, DH)
    return (key_rows, value_rows)


def row_softmax(queries, key_rows, bias_block, key_bias):
    scores = (
        jnp.einsum("qhd,khd->hqk", queries, key_rows, precision=PRECISE)
        + bias_block
        + key_bias[None, None, :]
    )
    peak_value = jnp.max(scores, axis=-1, keepdims=True)
    exponent = jnp.exp(scores - peak_value)
    return exponent / jnp.sum(exponent, axis=-1, keepdims=True)


def column_moments(exponent, value_col):
    total_exp = jnp.sum(exponent, axis=0)
    weighted = jnp.einsum("srh,srd->rhd", exponent, value_col, precision=PRECISE)
    return (total_exp, weighted)


def local(
    alignment,
    cotangent,
    pair_bias,
    norm_gains,
    row_project,
    row_output,
    column_project,
    column_output,
    residue_mask,
    sequence_mask,
):
    sequence_count = alignment.shape[0]
    residue_count = alignment.shape[1]
    scaling = DH ** (-0.5)
    initial = alignment.astype(jnp.float32)
    key_bias = MASKED * (residue_mask.astype(jnp.float32) - 1.0)
    normed_row, row_backward = jax.vjp(layer_norm, initial, norm_gains[0])
    query_weights = jnp.concatenate([row_project[:, :C], row_project[:, 3 * C :]], axis=1)
    query_gate = jnp.einsum("src,cd->srd", normed_row, query_weights, precision=PRECISE)
    memory_weights = row_project[:, C : 3 * C]
    memory_local = jnp.einsum("src,cd->srd", normed_row, memory_weights, precision=PRECISE)
    memory_all, bias_all = (
        lax.all_gather(memory_local, "res", axis=1, tiled=True),
        lax.all_gather(key_bias, "res", axis=0, tiled=True),
    )
    queries_row = (query_gate[..., :C] * scaling).reshape(sequence_count, residue_count, H, DH)
    gate_row = jax.nn.sigmoid(query_gate[..., C:])

    def mix_single(members):
        queries, memory = members
        key_rows, value_rows = split_heads(memory)
        weights = row_softmax(queries, key_rows, pair_bias, bias_all)
        return jnp.einsum("hqk,khd->qhd", weights, value_rows, precision=PRECISE).reshape(-1, C)

    mixture_row = lax.map(mix_single, (queries_row, memory_all))
    middle = initial + jnp.einsum(
        "src,cd->srd", gate_row * mixture_row, row_output, precision=PRECISE
    )
    present = sequence_mask.astype(jnp.float32)
    normed_col, col_backward = jax.vjp(layer_norm, middle, norm_gains[1])
    gate_col = jax.nn.sigmoid(
        jnp.einsum("src,cd->srd", normed_col, column_project[:, C + 2 * DH :], precision=PRECISE)
    )
    grad_top = cotangent.astype(jnp.float32)
    grad_gate_col = jnp.einsum("srd,cd->src", grad_top, column_output, precision=PRECISE)
    local_sum = jnp.einsum("s,src->rc", present, normed_col, precision=PRECISE)
    gated_local = jnp.sum(gate_col * grad_gate_col, axis=0)
    total_sum, counted, grad_mixture_col = lax.psum(
        (local_sum, jnp.sum(present), gated_local), "seq"
    )
    mean_normed = total_sum / counted
    queries_col = (
        jnp.dot(mean_normed, column_project[:, :C], precision=PRECISE) * scaling
    ).reshape(residue_count, H, DH)
    key_value_col = jnp.einsum(
        "src,cd->srd", normed_col, column_project[:, C : C + 2 * DH], precision=PRECISE
    )
    key_col = key_value_col[..., :DH]
    value_col = key_value_col[..., DH:]
    scores_col = (
        jnp.einsum("rhd,srd->srh", queries_col, key_col, precision=PRECISE)
        + MASKED * (present - 1.0)[:, None, None]
    )
    peak_col = lax.pmax(jnp.max(scores_col, axis=0), "seq")
    exponent_col = jnp.exp(scores_col - peak_col[None])
    local_exp, local_packed = column_moments(exponent_col, value_col)
    totals_exp, totals_packed = lax.psum((local_exp, local_packed), "seq")
    mixture_col = totals_packed / totals_exp[..., None]
    weights_col = exponent_col / totals_exp[None]
    mixture_flat = mixture_col.reshape(residue_count, C)
    grad_col_output = jnp.einsum(
        "src,srd->cd", gate_col * mixture_flat[None], grad_top, precision=PRECISE
    )
    grad_gate_pre = grad_gate_col * mixture_flat[None] * gate_col * (1.0 - gate_col)
    grad_heads_col = grad_mixture_col.reshape(residue_count, H, DH)
    grad_weights_col = jnp.einsum("rhd,srd->srh", grad_heads_col, value_col, precision=PRECISE)
    inner_dot = jnp.sum(grad_heads_col * mixture_col, axis=-1)
    grad_scores_col = weights_col * (grad_weights_col - inner_dot[None])
    grad_key_col = jnp.einsum("srh,rhd->srd", grad_scores_col, queries_col, precision=PRECISE)
    grad_value_col = jnp.einsum("srh,rhd->srd", weights_col, grad_heads_col, precision=PRECISE)
    grad_key_value = jnp.concatenate([grad_key_col, grad_value_col], axis=-1)
    grad_queries = lax.psum(
        jnp.einsum("srh,srd->rhd", grad_scores_col, key_col, precision=PRECISE), "seq"
    )
    grad_query_flat = grad_queries.reshape(residue_count, C) * scaling
    grad_mean = jnp.dot(grad_query_flat, column_project[:, :C].T, precision=PRECISE)
    grad_col_project = jnp.concatenate(
        [
            jnp.dot((local_sum / counted).T, grad_query_flat, precision=PRECISE),
            jnp.einsum("src,srd->cd", normed_col, grad_key_value, precision=PRECISE),
            jnp.einsum("src,srd->cd", normed_col, grad_gate_pre, precision=PRECISE),
        ],
        axis=1,
    )
    grad_normed_col = present[:, None, None] / counted * grad_mean[None]
    grad_normed_col = grad_normed_col + jnp.einsum(
        "srd,cd->src", grad_key_value, column_project[:, C : C + 2 * DH], precision=PRECISE
    )
    grad_normed_col = grad_normed_col + jnp.einsum(
        "srd,cd->src", grad_gate_pre, column_project[:, C + 2 * DH :], precision=PRECISE
    )
    grad_middle_norm, grad_gain_col = col_backward(grad_normed_col)
    grad_middle = grad_top + grad_middle_norm
    grad_gate_row = jnp.einsum("srd,cd->src", grad_middle, row_output, precision=PRECISE)
    grad_row_output = jnp.einsum(
        "src,srd->cd", gate_row * mixture_row, grad_middle, precision=PRECISE
    )
    grad_row_pre = grad_gate_row * mixture_row * gate_row * (1.0 - gate_row)
    grad_mixture_row = grad_gate_row * gate_row

    def back_single(accumulated, members):
        queries, memory, grad_mixed = members
        key_rows, value_rows = split_heads(memory)
        weights = row_softmax(queries, key_rows, pair_bias, bias_all)
        grad_heads = grad_mixed.reshape(-1, H, DH)
        grad_weights = jnp.einsum("qhd,khd->hqk", grad_heads, value_rows, precision=PRECISE)
        inner_row = jnp.sum(weights * grad_weights, axis=-1, keepdims=True)
        grad_scores = weights * (grad_weights - inner_row)
        grad_query = jnp.einsum("hqk,khd->qhd", grad_scores, key_rows, precision=PRECISE).reshape(
            -1, C
        )
        grad_key = jnp.einsum("hqk,qhd->khd", grad_scores, queries, precision=PRECISE).reshape(
            -1, C
        )
        grad_value = jnp.einsum("hqk,qhd->khd", weights, grad_heads, precision=PRECISE).reshape(
            -1, C
        )
        return (
            accumulated + grad_scores,
            (grad_query, jnp.concatenate([grad_key, grad_value], axis=1)),
        )

    start_bias = jnp.zeros(pair_bias.shape, jnp.float32)
    bias_part, (grad_query_rows, grad_memory_all) = lax.scan(
        back_single, start_bias, (queries_row, memory_all, grad_mixture_row)
    )
    grad_memory = lax.psum_scatter(grad_memory_all, "res", scatter_dimension=1, tiled=True)
    grad_memory_weights = jnp.einsum("src,srd->cd", normed_row, grad_memory, precision=PRECISE)
    grad_from_keys = jnp.einsum("srd,cd->src", grad_memory, memory_weights, precision=PRECISE)
    grad_query_scaled = grad_query_rows * scaling
    grad_row_project = jnp.concatenate(
        [
            jnp.einsum("src,srd->cd", normed_row, grad_query_scaled, precision=PRECISE),
            grad_memory_weights,
            jnp.einsum("src,srd->cd", normed_row, grad_row_pre, precision=PRECISE),
        ],
        axis=1,
    )
    grad_normed_row = grad_from_keys + jnp.einsum(
        "srd,cd->src", grad_query_scaled, row_project[:, :C], precision=PRECISE
    )
    grad_normed_row = grad_normed_row + jnp.einsum(
        "srd,cd->src", grad_row_pre, row_project[:, 3 * C :], precision=PRECISE
    )
    grad_initial, grad_gain_row = row_backward(grad_normed_row)
    grad_alignment = (grad_middle + grad_initial).astype(jnp.bfloat16)
    grad_pair_bias = lax.psum_scatter(bias_part, "seq", scatter_dimension=2, tiled=True)
    grad_gains, summed_row_project, summed_row_output, summed_col_project, summed_col_output = (
        lax.psum(
            (
                jnp.stack([grad_gain_row, grad_gain_col]),
                grad_row_project,
                grad_row_output,
                grad_col_project,
                grad_col_output,
            ),
            ("seq", "res"),
        )
    )
    return (
        grad_alignment,
        grad_pair_bias,
        grad_gains,
        summed_row_project,
        summed_row_output,
        summed_col_project,
        summed_col_output,
    )


def solution(mesh):
    placed = (
        P("seq", "res", None),
        P("seq", "res", None),
        P(None, "res", None),
        P(),
        P(),
        P(),
        P(),
        P(),
        P("res"),
        P("seq"),
    )
    return jax.shard_map(
        local,
        mesh=mesh,
        in_specs=placed,
        out_specs=(P("seq", "res", None), P(None, "res", "seq"), P(), P(), P(), P(), P()),
        check_vma=False,
    )
```

profile of v0, /device:TPU:0, one launch (start us, length us, event | category | flops | bytes accessed | tf_op | source)
XLA Modules:
  0.0 631.9 jit_solution(9021324585754479570)
XLA Ops:
  8.1 1.3 convert_reduce_fusion.1
  12.0 2.7 all-reduce
  17.6 1.9 all_gather.6
  20.1 0.8 copy-done.1
  20.9 3.5 while.25
  25.1 0.7 copy-done.4
  27.3 79.6 %all-reduce.4 = (f32[64,64]{1,0:T(8,128)S(1)}, f32[]{:T(128)}) all-reduce(f32[64,64]{1,0:T(8,128)S(1)} %bitcast.212, f32[]{:T(128)} %convert_reduce_fusion.1), channel_id=1, replica_groups=mesh['seq'=16,'res'=2] {'seq'}, use_global_device_ids=true, to_apply=%region_10.11 | all-reduce | flops 4097 | bytes 32776 | tf_op jit(solution)/shard_map/psum | solution.py:94
  107.5 0.8 convolution_multiply_fusion
  109.6 71.9 %pmax.7 = f32[64,8]{1,0:T(8,128)S(1)} all-reduce(f32[64,8]{1,0:T(8,128)S(1)} %get-tuple-element.279), channel_id=1, replica_groups=mesh['seq'=16,'res'=2] {'seq'}, use_global_device_ids=true, to_apply=%region_12.13 | all-reduce | flops 512 | bytes 4096 | tf_op jit(solution)/shard_map/pmax | solution.py:110
  182.4 77.8 %all-reduce.3 = (f32[64,8,8]{2,1,0:T(8,128)S(1)}, f32[64,8,8]{2,1,0:T(8,128)S(1)}, f32[64,8]{1,0:T(8,128)S(1)}) all-reduce(f32[64,8,8]{2,1,0:T(8,128)S(1)} %copy.145, f32[64,8,8]{2,1,0:T(8,128)S(1)} %fusion.121, f32[64,8]{1,0:T(8,128)S(1)} %fusion.122), channel_id=1, replica_groups=mesh['seq'=16,'res'=2] {'seq'}, use_global_device_ids=true, to_apply=%region_16.17 | all-reduce | flops 8704 | bytes 69632 | tf_op jit(solution)/shard_map/psum | solution.py:94
  263.4 74.2 %psum.82 = f32[64,8,8]{0,2,1:T(8,128)S(1)} all-reduce(f32[64,8,8]{0,2,1:T(8,128)S(1)} %copy.149), channel_id=1, replica_groups=mesh['seq'=16,'res'=2] {'seq'}, use_global_device_ids=true, to_apply=%region_19.20 | all-reduce | flops 4096 | bytes 32768 | tf_op jit(solution)/shard_map/psum | solution.py:128
  338.9 10.4 %while.26 = (s32[]{:T(128)}, f32[8,64,128]{2,1,0:T(8,128)S(1)}, f32[2,64,64]{2,1,0:T(8,128)S(1)}, f32[2,128,128]{2,0,1:T(2,128)S(1)}, f32[2,64,8,8]{1,3,2,0:T(8,...) while((s32[]{:T(128)}, f32[8,64,128]{2,1,0:T(8,128)S(1)}, ...), condition=%wide.region_26.27_spmd.clone, body=%wide.region_22.0_spmd.clone.sunk | while | flops 32651780 | bytes 4287127 | solution.py:180
  342.7 1.5 dynamic_update_slice.20
  347.9 1.5 dynamic_update_slice.20
  350.5 0.9 convolution_bitcast_fusion.6
  351.3 0.9 fusion.59
  352.2 1.0 convolution_bitcast_fusion.9
  353.5 0.7 pad_maximum_fusion.1
  355.2 8.7 %all-reduce.11.cloned.1.call-done = f32[2,128,128]{2,0,1:T(2,128)} async-done(((f32[2,128,128]{2,0,1:T(2,128)}), f32[2,128,128]{2,0,1:T(2,128)}) %all-reduce.11.cloned.1.call-update) | async-done | bytes 131088
  364.0 0.8 constant_dynamic-slice_fusion.1
  367.8 1.0 copy.163
  369.7 120.1 %all-reduce.9.cloned.1.call-done = f32[64,256]{1,0:T(8,128)} async-done(((f32[64,256]{1,0:T(8,128)}), f32[64,256]{1,0:T(8,128)}) %all-reduce.9.cloned.1.call-update) | async-done | bytes 65552 | tf_op jit(solution)/shard_map/psum | solution.py:205
  489.8 130.1 %all-reduce.13.cloned.1.call-done = (f32[2,64]{1,0:T(2,128)}, f32[64,64]{1,0:T(8,128)}, f32[64,144]{1,0:T(8,128)}, f32[64,64]{1,0:T(8,128)}) async-done(((f32[2,64]{1,0:T(2,128)}, f32[64,64]{1,0:T(8,128)}, f32[64,144]{1,0:T(8,128)}, f32[64,64]{1,0:T(8,128)}), (f32[2,64]{1,0:T(2,128)}, f32[64,64]{1,0:T(8,128)}, f32[64,144]{1,0:T(8,128)}, f32[64,64]{1,0:T(8,128)})) %all-reduce.13.cloned.1.call-update) | async-done | bytes 70160 | tf_op jit(solution)/shard_map/psum | solution.py:205
  621.1 1.5 copy.250
  (156 shorter events, 34.4 us)
Async XLA Ops:
  8.0 16.5 %copy-start = (f32[64,64]{1,0:T(8,128)S(1)}, f32[64,64]{1,0:T(8,128)}, u32[]{:S(2)}) copy-start(f32[64,64]{1,0:T(8,128)} %param.19) | copy-start | bytes 49156
  8.0 6.7 %copy-start.7 = (bf16[2,64,64]{2,1,0:T(8,128)(2,1)S(1)}, bf16[2,64,64]{2,1,0:T(8,128)(2,1)}, u32[]{:S(2)}) copy-start(bf16[2,64,64]{2,1,0:T(8,128)(2,1)} %param.14) | copy-start | bytes 49156
  8.0 355.9 %all-reduce.11.cloned.1.call-start = ((), (), s32[]{:S(2)}) async-start(), calls=%async_computation.3 | async-start | bytes 262144
  9.4 0.7 copy-start.11
  11.3 0.7 copy-start.15
  12.0 2.7 copy-start.12
  14.8 0.8 copy-start.3
  15.6 0.8 copy-start.10
  16.3 0.8 copy-start.2
  20.0 0.9 copy-start.1
  25.0 0.8 copy-start.4
  26.3 0.7 copy-start.14
  349.3 0.7 copy-start.5
  350.0 139.8 %all-reduce.9.cloned.1.call-start = ((), (), s32[]{:S(2)}) async-start(), calls=%async_computation.2 | async-start | bytes 131072 | tf_op jit(solution)/shard_map/psum | solution.py:205
  367.0 252.9 %all-reduce.13.cloned.1.call-start = ((), (), s32[]{:S(2)}) async-start(), calls=%async_computation.4 | async-start | bytes 264192 | tf_op jit(solution)/shard_map/psum | solution.py:205
  367.8 252.1 %reduce-scatter.2.cloned.1.call-start = ((), (), s32[]{:S(2)}) async-start(), calls=%async_computation.1 | async-start | bytes 557056 | tf_op jit(solution)/shard_map/reduce_scatter | solution.py:203
  619.9 0.6 copy-start.13
  621.1 1.5 copy-start.9
  622.6 0.9 copy-start.6
  623.4 0.8 copy-start.8
Sparse Core Ops, SparseCore 0:
  350.1 13.7 all-reduce.10
  371.0 118.7 all-reduce.8
  497.6 122.2 all-reduce.12
Sparse Core Ops, SparseCore 1:
  371.1 77.8 reduce-scatter.1
where the time goes:
time: 634 us; the launch traced here: 632 us
  blocking collectives  308 us (49%)
  waiting for transfers between devices  259 us (41%)
  matrix products  21.3 us (3%)
  local copies, waits for them, and re-layouts  19.5 us (3%)
  between operations  17 us (3%)
  other arithmetic  6.69 us (1%)
    psum x2, waiting for transfers between devices, local(): lax.psum((jnp.stack([grad_gain_row, grad_gain_col]), grad_row_project, gr...  250 us
    psum x2, blocking collectives, local(): lax.psum((local_sum, jnp.sum(present), gated_local), 'seq')  157 us
    psum x1, blocking collectives, local(): lax.psum(jnp.einsum('srh,srd->rhd', grad_scores_col, key_col, precision=P...  74.2 us
    pmax x1, blocking collectives, local(): peak_col = lax.pmax(jnp.max(scores_col, axis=0), 'seq')  71.9 us
    unnamed x43, local copies, waits for them, and re-layouts  13.3 us
  transfers between devices with their start and end apart: 4, of which 3 were waited for; matrix products, arithmetic and copies ran while one was open for 1% of the time, Pallas kernels for 0%

commit v1 on v0

v1 whole, which is shorter than its diff:
```python
import functools

import jax
import jax.numpy as jnp
from jax import lax
from jax.experimental import pallas as pl
from jax.experimental.pallas import tpu as pltpu
from jax.sharding import PartitionSpec as P

C = 64
H = 8
DH = 8
LANES = 128
TILE = 8
SLABS = 5

PRECISE = lax.Precision.HIGHEST
EPSILON = 1e-05
MASKED = 1000000000.0
SCALE = DH ** (-0.5)
F32 = jnp.float32


def dot(a, b, over=((1,), (0,))):
    return lax.dot_general(a, b, (over, ((), ())), precision=PRECISE, preferred_element_type=F32)


def dot_rows(a, b):
    return dot(a, b, ((0,), (0,)))


def dot_t(a, b):
    return dot(a, b, ((1,), (1,)))


def normalise(values):
    centred = values - jnp.mean(values, axis=-1, keepdims=True)
    inverse = lax.rsqrt(jnp.mean(centred * centred, axis=-1, keepdims=True) + EPSILON)
    return centred * inverse, inverse


def normalise_back(grad_normed, gain, unit, inverse):
    grad_unit = grad_normed * gain
    along = jnp.mean(grad_unit * unit, axis=-1, keepdims=True)
    return inverse * (grad_unit - jnp.mean(grad_unit, axis=-1, keepdims=True) - unit * along)


def head_mask(rows):
    row = lax.broadcasted_iota(jnp.int32, (H, rows, C), 0)
    channel = lax.broadcasted_iota(jnp.int32, (H, rows, C), 2)
    return (row == channel // DH).astype(F32).reshape(H * rows, C)


def spread_heads(values, mask):
    return jnp.concatenate([values] * H, axis=0) * mask


def join_heads(values, mask):
    masked = values * mask
    return jnp.sum(masked.reshape(H, -1, C), axis=0)


def row_forward(n_res, me, seq_mask, *refs):
    sent = refs[:n_res]
    own, cotangent, bias, gains, w_row, w_out = refs[n_res : n_res + 6]
    payload, weights_out, unit_out, memory_out, query_gate_out, mixture_out, gathered = refs[n_res + 6 :]
    n_seq, n_rows, _ = own.shape
    for away in range(n_res):
        gathered[lax.rem(me[0] + away, n_res)] = sent[away][...]
    n_keys = n_res * n_rows
    n_blocks = payload.shape[0]
    block = n_rows // n_blocks
    data_rows = n_seq * block
    gain = gains[0:1, :]
    w_all = w_row[...]
    residue = gathered[:, n_seq].reshape(n_keys, C)
    key_bias = MASKED * (jnp.transpose(residue)[0:1, :] - 1.0)
    bias_rows = bias[...].reshape(H * n_rows, n_keys).astype(F32)
    mask = head_mask(n_rows)
    for s in range(n_seq):
        unit, _ = normalise(gathered[:, s].reshape(n_keys, C))
        unit_out[s] = unit
        memory = dot(unit * gain, w_all[:, C : 3 * C])
        memory_out[s] = memory
        initial = own[s].astype(F32)
        own_unit, _ = normalise(initial)
        projected = dot(own_unit * gain, w_all)
        query = projected[:, :C] * SCALE
        gate = jax.nn.sigmoid(projected[:, 3 * C :])
        query_gate_out[s] = jnp.concatenate([query, gate], axis=1)
        scores = dot_t(spread_heads(query, mask), memory[:, :C]) + bias_rows + key_bias
        exponent = jnp.exp(scores - jnp.max(scores, axis=-1, keepdims=True))
        weights = exponent / jnp.sum(exponent, axis=-1, keepdims=True)
        weights_out[s] = weights
        mixture = join_heads(dot(weights, memory[:, C:]), mask)
        mixture_out[s] = mixture
        middle = initial + dot(gate * mixture, w_out[...])
        both = jnp.concatenate([middle, cotangent[s].astype(F32)], axis=1)
        for b in range(n_blocks):
            payload[b, s * block : (s + 1) * block, :] = both[b * block : (b + 1) * block, :]
        for b in range(n_blocks):
            payload[b, data_rows + s * block : data_rows + (s + 1) * block, :] = jnp.full(
                (block, 2 * C), seq_mask[s].astype(F32)
            )


def column_step(arrived, gains, w_col, w_out, returned, col_slab, rest_slab, out_grad, n_seq):
    n_src, both_rows, _ = arrived.shape
    group = both_rows // 2
    block = group // n_seq
    rows = n_src * group
    arrived_rows = arrived[...]
    data = arrived_rows[:, :group, :].reshape(rows, 2 * C)
    present = arrived_rows[:, group:, :C]
    middle = data[:, :C]
    cot = data[:, C:]
    gain = gains[1:2, :]

    def over_sequences(values, combine, reduce):
        total = reduce(values.reshape(n_src, group, C), axis=0)
        result = total
        for shift in range(1, n_seq):
            result = combine(result, pltpu.roll(total, shift * block, 0))
        return result

    def total_of(values):
        return over_sequences(values, jnp.add, jnp.sum)

    def spread(values):
        return jnp.broadcast_to(values[None], (n_src, group, C)).reshape(rows, C)

    lane = lax.broadcasted_iota(jnp.int32, (C, C), 1)
    row = lax.broadcasted_iota(jnp.int32, (C, C), 0)
    same_head = (row // DH == lane // DH).astype(F32)
    repeat = (lax.broadcasted_iota(jnp.int32, (DH, C), 0) == lax.broadcasted_iota(jnp.int32, (DH, C), 1) % DH).astype(F32)
    w_all = w_col[...]
    w_query = w_all[:, :C]
    w_key = dot(w_all[:, C : C + DH], repeat)
    w_value = dot(w_all[:, C + DH : C + 2 * DH], repeat)
    w_gate = w_all[:, C + 2 * DH :]
    w_rest = jnp.concatenate([w_key, w_value, w_gate], axis=1)

    unit, inverse = normalise(middle)
    normed = unit * gain
    present_rows = present.reshape(rows, C)
    counted = total_of(present_rows)
    mean_normed = total_of(present_rows * normed) / counted
    query = dot(mean_normed, w_query) * SCALE
    query_rows = spread(query)
    rest = dot(normed, w_rest)
    key, value = rest[:, :C], rest[:, C : 2 * C]
    gate = jax.nn.sigmoid(rest[:, 2 * C :])
    scores = dot(query_rows * key, same_head) + MASKED * (present_rows - 1.0)
    peak = over_sequences(scores, jnp.maximum, jnp.max)
    exponent = jnp.exp(scores - spread(peak))
    weights = exponent / spread(total_of(exponent))
    mixture = total_of(weights * value)
    mixture_rows = spread(mixture)

    grad_gated = dot_t(cot, w_out[...])
    out_grad[...] = dot_rows(gate * mixture_rows, cot)
    grad_mixture = total_of(gate * grad_gated)
    grad_mixture_rows = spread(grad_mixture)
    grad_gate = grad_gated * mixture_rows * gate * (1.0 - gate)
    grad_weights = dot(grad_mixture_rows * value, same_head)
    inner = spread(dot(grad_mixture * mixture, same_head))
    grad_scores = weights * (grad_weights - inner)
    grad_rest = jnp.concatenate([grad_scores * query_rows, weights * grad_mixture_rows, grad_gate], axis=1)
    grad_query = total_of(grad_scores * key) * SCALE
    grad_mean = dot_t(grad_query, w_query)
    grad_normed = present_rows * spread(grad_mean / counted) + dot_t(grad_rest, w_rest)
    grad_query_weights = dot_rows(mean_normed, grad_query) * (1.0 / n_seq)
    grad_rest_weights = dot_rows(normed, grad_rest)
    fold_row = lax.broadcasted_iota(jnp.int32, (2 * C, 2 * DH), 0)
    fold_lane = lax.broadcasted_iota(jnp.int32, (2 * C, 2 * DH), 1)
    fold = ((fold_row // C == fold_lane // DH) & (fold_row % DH == fold_lane % DH)).astype(F32)
    grad_key_value = dot(grad_rest_weights[:, : 2 * C], fold)
    col_slab[...] = jnp.concatenate([grad_query_weights, grad_rest_weights[:, 2 * C :]], axis=1)
    rest_slab[...] = jnp.zeros(rest_slab.shape, F32)
    rest_slab[:, : 2 * DH] = grad_key_value
    rest_slab[1:2, C:] = jnp.sum(grad_normed * unit, axis=0, keepdims=True)
    grad_middle = cot + normalise_back(grad_normed, gain, unit, inverse)
    returned[:, :, :C] = grad_middle.reshape(n_src, group, C)
    returned[:, :, C:] = jnp.zeros((n_src, group, C), F32)


def row_backward(n_res, me, returned, own, weights_in, unit_in, memory_in, query_gate_in, mixture_in, gains, w_row,
                 w_out, col_slab, rest_slab, col_out_grad, payload, middle_grad, *refs):
    grads_out, normed_grad, slab = refs[:n_res], refs[n_res], refs[n_res + 1]
    n_seq, n_rows, _ = own.shape
    n_keys = memory_in.shape[1]
    n_blocks, group, _ = returned.shape
    block = group // n_seq
    gain = gains[0:1, :]
    w_all = w_row[...]
    w_memory = w_all[:, C : 3 * C]
    w_query_gate = jnp.concatenate([w_all[:, :C], w_all[:, 3 * C :]], axis=1)
    mask = head_mask(n_rows)
    for b in range(n_blocks):
        for s in range(n_seq):
            middle_grad[s, b * block : (b + 1) * block, :] = returned[b, s * block : (s + 1) * block, :C]
    slab[...] = jnp.zeros(slab.shape, F32)
    grad_out = jnp.zeros((C, C), F32)
    grad_query_gate_weights = jnp.zeros((C, 2 * C), F32)
    grad_memory_weights = jnp.zeros((C, 2 * C), F32)
    grad_gain = jnp.zeros((1, C), F32)
    bias_grad = jnp.zeros((H * n_rows, n_keys), F32)
    for s in range(n_seq):
        grad_middle = middle_grad[s]
        query = query_gate_in[s, :, :C]
        gate = query_gate_in[s, :, C:]
        mixture = mixture_in[s]
        memory = memory_in[s]
        weights = weights_in[s]
        grad_gated = dot_t(grad_middle, w_out[...])
        grad_out = grad_out + dot_rows(gate * mixture, grad_middle)
        grad_gate = grad_gated * mixture * gate * (1.0 - gate)
        grad_heads = spread_heads(grad_gated * gate, mask)
        query_heads = spread_heads(query, mask)
        inner = grad_heads * jnp.concatenate([mixture] * H, axis=0)
        left = jnp.concatenate([grad_heads, inner], axis=1)
        right = jnp.concatenate([memory[:, C:], jnp.full((n_keys, C), -1.0, F32)], axis=1)
        grad_scores = weights * dot_t(left, right)
        bias_grad = bias_grad + grad_scores
        grad_query = join_heads(dot(grad_scores, memory[:, :C]), mask) * SCALE
        grad_key = dot_rows(grad_scores, query_heads)
        grad_value = dot_rows(weights, grad_heads)
        grad_memory = jnp.concatenate([grad_key, grad_value], axis=1)
        grad_query_gate = jnp.concatenate([grad_query, grad_gate], axis=1)
        own_unit, _ = normalise(own[s].astype(F32))
        unit = unit_in[s]
        grad_query_gate_weights = grad_query_gate_weights + dot_rows(own_unit * gain, grad_query_gate)
        grad_memory_weights = grad_memory_weights + dot_rows(unit * gain, grad_memory)
        from_memory = dot_t(grad_memory, w_memory)
        from_own = dot_t(grad_query_gate, w_query_gate)
        grad_gain = grad_gain + jnp.sum(from_memory * unit, axis=0, keepdims=True)
        grad_gain = grad_gain + jnp.sum(from_own * own_unit, axis=0, keepdims=True)
        normed_grad[:, s] = from_memory.reshape(-1, n_rows, C)
        grads_out[0][s] = from_own
    grads_out[0][...] += normed_grad[me[0]]
    for away in range(1, n_res):
        grads_out[away][...] = normed_grad[lax.rem(me[0] + away, n_res)]
    slab[0:C, :] = grad_query_gate_weights
    slab[C : 2 * C, :] = grad_memory_weights
    slab[2 * C : 3 * C, :] = col_slab[...]
    slab[3 * C : 4 * C, :] = jnp.concatenate([grad_out, col_out_grad[...]], axis=1)
    slab[4 * C : 5 * C, :] = rest_slab[...]
    slab[4 * C : 4 * C + 1, C:] = grad_gain
    bias_t = jnp.transpose(bias_grad)
    keys_each = n_keys // n_blocks
    tiles = H * n_rows // LANES
    piece = slab.shape[0] // n_blocks
    for b in range(n_blocks):
        for t in range(tiles):
            payload[b, t * keys_each : (t + 1) * keys_each, :] = bias_t[
                b * keys_each : (b + 1) * keys_each, t * LANES : (t + 1) * LANES
            ]
        payload[b, tiles * keys_each :, :] = slab[b * piece : (b + 1) * piece, :]


def finish_alignment(own, middle_grad, gains, *refs):
    parts, out = refs[:-1], refs[-1]
    n_seq = own.shape[0]
    for s in range(n_seq):
        unit, inverse = normalise(own[s].astype(F32))
        grad_normed = parts[0][s]
        for part in parts[1:]:
            grad_normed = grad_normed + part[s]
        out[s] = (middle_grad[s] + normalise_back(grad_normed, gains[0:1, :], unit, inverse)).astype(out.dtype)


def add_arrivals(arrived, bias_out, piece_out):
    total = jnp.sum(arrived[...], axis=0)
    _, keys_each, n_rows = bias_out.shape
    each = LANES // n_rows
    tiles = H // each
    for t in range(tiles):
        for u in range(each):
            bias_out[t * each + u] = total[t * keys_each : (t + 1) * keys_each, u * n_rows : (u + 1) * n_rows]
    piece_out[...] = total[tiles * keys_each :, :]


def unpack(slab, gains_out, row_project_out, row_out_out, col_project_out, col_out_out):
    values = slab[...].reshape(-1, LANES)
    query_gate = values[0:C]
    row_project_out[:, :C] = query_gate[:, :C]
    row_project_out[:, C : 3 * C] = values[C : 2 * C]
    row_project_out[:, 3 * C :] = query_gate[:, C:]
    col_query_gate = values[2 * C : 3 * C]
    rest = values[4 * C : 5 * C]
    col_project_out[:, :C] = col_query_gate[:, :C]
    col_project_out[:, C : C + 2 * DH] = rest[:, : 2 * DH]
    col_project_out[:, C + 2 * DH :] = col_query_gate[:, C:]
    outs = values[3 * C : 4 * C]
    row_out_out[...] = outs[:, :C]
    col_out_out[...] = outs[:, C:]
    gains_out[...] = rest[0:2, C:]


def call(body, outs, *operands, smem=0, scratch=(), name):
    vmem = pl.BlockSpec(memory_space=pltpu.VMEM)
    scalar = pl.BlockSpec(memory_space=pltpu.SMEM)
    return pl.pallas_call(
        body,
        out_shape=[jax.ShapeDtypeStruct(shape, kind) for shape, kind in outs],
        in_specs=[scalar] * smem + [vmem] * (len(operands) - smem),
        out_specs=[vmem] * len(outs),
        scratch_shapes=list(scratch),
        compiler_params=pltpu.CompilerParams(vmem_limit_bytes=48 * 1024 * 1024),
        name=name,
    )(*operands)


def shift_residues(values, away, count):
    return lax.ppermute(values, "res", [((i + away) % count, i) for i in range(count)])


def swap_blocks(values):
    return lax.all_to_all(values, "seq", 0, 0, tiled=True)


def local(
    alignment,
    cotangent,
    pair_bias,
    norm_gains,
    row_project,
    row_output,
    column_project,
    column_output,
    residue_mask,
    sequence_mask,
    seq_count,
    res_count,
):
    n_seq, n_rows, _ = alignment.shape
    n_keys = pair_bias.shape[2]
    block = n_rows // seq_count
    group = n_seq * block
    present_keys = jnp.broadcast_to(residue_mask.astype(F32)[None, :, None], (1, n_rows, C))
    sent = jnp.concatenate([alignment.astype(F32), present_keys], axis=0)
    sent = [sent] + [shift_residues(sent, away, res_count) for away in range(1, res_count)]
    me = jnp.reshape(lax.axis_index("res"), (1,))
    payload, weights, unit, memory, query_gate, mixture = call(
        functools.partial(row_forward, res_count),
        [
            ((seq_count, 2 * group, 2 * C), F32),
            ((n_seq, H * n_rows, n_keys), F32),
            ((n_seq, n_keys, C), F32),
            ((n_seq, n_keys, 2 * C), F32),
            ((n_seq, n_rows, 2 * C), F32),
            ((n_seq, n_rows, C), F32),
        ],
        me, sequence_mask, *sent, alignment, cotangent, pair_bias, norm_gains, row_project, row_output,
        smem=2,
        scratch=[pltpu.VMEM((res_count, n_seq + 1, n_rows, C), F32)],
        name="row_forward",
    )
    arrived = swap_blocks(payload)
    returned, col_slab, rest_slab, col_out_grad = call(
        functools.partial(column_step, n_seq=n_seq),
        [((seq_count, group, 2 * C), F32), ((C, 2 * C), F32), ((C, 2 * C), F32), ((C, C), F32)],
        arrived, norm_gains, column_project, column_output,
        name="column_step",
    )
    returned = swap_blocks(returned)
    bias_rows = H * n_rows // LANES * (n_keys // seq_count)
    piece = -(-SLABS * C // (TILE * seq_count)) * TILE
    payload, middle_grad, *parts = call(
        functools.partial(row_backward, res_count),
        [((seq_count, bias_rows + piece, LANES), F32)] + [((n_seq, n_rows, C), F32)] * (res_count + 1),
        me, returned, alignment, weights, unit, memory, query_gate, mixture, norm_gains,
        row_project, row_output, col_slab, rest_slab, col_out_grad,
        smem=1,
        scratch=[pltpu.VMEM((res_count, n_seq, n_rows, C), F32), pltpu.VMEM((piece * seq_count, LANES), F32)],
        name="row_backward",
    )
    parts = parts[:1] + [shift_residues(parts[away], -away, res_count) for away in range(1, res_count)]
    arrived = swap_blocks(payload)
    (grad_alignment,) = call(
        finish_alignment,
        [(alignment.shape, alignment.dtype)],
        alignment, middle_grad, norm_gains, *parts,
        name="finish_alignment",
    )
    bias_grad, summed = call(
        add_arrivals,
        [((H, n_keys // seq_count, n_rows), F32), ((piece, LANES), F32)],
        arrived,
        name="add_arrivals",
    )
    others = [shift_residues(summed, away, res_count) for away in range(1, res_count)]
    summed = functools.reduce(jnp.add, others, summed)
    slab = swap_blocks(jnp.broadcast_to(summed[None], (seq_count, piece, LANES)))
    grads = call(
        unpack,
        [((2, C), F32), ((C, 4 * C), F32), ((C, C), F32), ((C, 2 * C + 2 * DH), F32), ((C, C), F32)],
        slab,
        name="unpack",
    )
    return (grad_alignment, jnp.transpose(bias_grad, (0, 2, 1)), *grads)


def solution(mesh):
    placed = (
        P("seq", "res", None),
        P("seq", "res", None),
        P(None, "res", None),
        P(),
        P(),
        P(),
        P(),
        P(),
        P("res"),
        P("seq"),
    )
    return jax.shard_map(
        functools.partial(local, seq_count=mesh.shape["seq"], res_count=mesh.shape["res"]),
        mesh=mesh,
        in_specs=placed,
        out_specs=(P("seq", "res", None), P(None, "res", "seq"), P(), P(), P(), P(), P()),
        check_vma=False,
    )
```

time: 634 us -> 71.5 us (0.11)
  blocking collectives: 308 us -> 41.4 us
  waiting for transfers between devices: 259 us -> 9.9 us
  matrix products: 21.3 us -> 0 us
  local copies, waits for them, and re-layouts: 19.5 us -> 0.81 us
  between operations: 17 us -> 0.72 us
  Pallas kernels: 0 us -> 12.5 us
    psum x2 -> x0, waiting for transfers between devices: 250 us -> none  [local(): lax.psum((jnp.stack([grad_gain_row, grad_gain_col]), grad_row_project, gr...]
    psum x3 -> x0, blocking collectives: 232 us -> none  [the longest x2 157 us: local(): lax.psum((local_sum, jnp.sum(present), gated_local), 'seq')]
    pmax x1 -> x0, blocking collectives: 71.9 us -> none  [local(): peak_col = lax.pmax(jnp.max(scores_col, axis=0), 'seq')]
    all_to_all x0 -> x3, blocking collectives: none -> 41.4 us  [swap_blocks(): return lax.all_to_all(values, 'seq', 0, 0, tiled=True)]
    dot_general x43 -> x0, matrix products: 21.3 us -> none  [the longest x4 2.85 us: row_softmax(): jnp.einsum('qhd,khd->hqk', queries, key_rows, precision=PRECISE)]
    unnamed x43 -> x18, local copies, waits for them, and re-layouts: 13.3 us -> 0.04 us
    pallas_call x0 -> x6, Pallas kernels: none -> 12.5 us  [call(): pl.pallas_call(body, out_shape=[jax.ShapeDtypeStruct(shape, kind) for sha...]
    unnamed x5 -> x0, waiting for transfers between devices: 8.78 us -> none
  transfers between devices with their start and end apart: 4 -> 4, of which waited for: 3 -> 4; matrix products, arithmetic and copies ran while one was open for 1% -> 0% of each run, Pallas kernels for 0% -> 1%
where the time goes in v1:
time: 71.5 us; the launch traced here: 71.1 us
  blocking collectives  41.4 us (58%)
  Pallas kernels  12.5 us (17%)
  waiting for transfers between devices  9.9 us (14%)
  starting transfers between devices  4.27 us (6%)
  other arithmetic  1.44 us (2%)
  local copies, waits for them, and re-layouts  0.81 us (1%)
  between operations  0.72 us (1%)
    all_to_all x3, blocking collectives, swap_blocks(): return lax.all_to_all(values, 'seq', 0, 0, tiled=True)  41.4 us
    pallas_call x6, Pallas kernels, call(): pl.pallas_call(body, out_shape=[jax.ShapeDtypeStruct(shape, kind) for sha...  12.5 us
    all_to_all x1, waiting for transfers between devices, swap_blocks(): return lax.all_to_all(values, 'seq', 0, 0, tiled=True)  6.55 us
    all_to_all x1, starting transfers between devices, swap_blocks(): return lax.all_to_all(values, 'seq', 0, 0, tiled=True)  3.67 us
    ppermute x3, waiting for transfers between devices, shift_residues(): lax.ppermute(values, 'res', [((i + away) % count, i) for i in range(count)])  3.36 us
  transfers between devices with their start and end apart: 4, of which 4 were waited for; matrix products, arithmetic and copies ran while one was open for 0% of the time, Pallas kernels for 1%

profile of v1, /device:TPU:0, one launch (start us, length us, event | category | flops | bytes accessed | tf_op | source)
XLA Modules:
  0.0 71.1 jit_solution(16887744088872635857)
XLA Ops:
  0.6 0.7 convert_element_type.7
  1.3 0.8 %convert_element_type.6 = f32[2,64,64]{2,1,0:T(8,128)S(1)} convert(bf16[2,64,64]{2,1,0:T(8,128)(2,1)} %own.3) | non-fusion elementwise | flops 8192 | bytes 49152 | tf_op jit(solution)/shard_map/convert_element_type | solution.py:341
  2.1 0.1 broadcast_in_dim.4
  2.2 0.5 collective-permute-start
  2.7 0.9 %collective-permute-done.refs_1_ = f32[3,64,64]{2,1,0:T(8,128)S(1)} collective-permute-done((f32[3,64,64]{2,1,0:T(8,128)S(1)}, f32[3,64,64]{2,1,0:T(8,128)S(1)}, u32[]{:S(2)}, u32[]{:S(2)}) %collective-permute-start) | collective-permute-done | bytes 49184 | tf_op jit(solution)/shard_map/ppermute | solution.py:315
  3.6 0.0 copy-done.3
  3.7 4.1 %row_forward.1 = (f32[16,16,128]{2,1,0:T(8,128)S(1)}, f32[2,512,128]{2,1,0:T(8,128)S(1)}, f32[2,128,64]{2,1,0:T(8,128)S(1)}, f32[2,128,128]{2,1,0:T(8,128)S(1)},...) custom-call(s32[1]{0:T(128)} %bitcast.me, s32[2]{0:T(128)S(1)} %copy-done.8, ...), custom_call_target="tpu_custom_call" | custom-call | tf_op jit(solution)/shard_map/row_forward/pallas_call | solution.py:303
  7.8 0.0 copy-start.4
  7.8 0.0 copy-start.5
  7.8 16.0 %all_to_all.20.arrived = f32[16,16,128]{2,1,0:T(8,128)S(1)} all-to-all(f32[16,16,128]{2,1,0:T(8,128)S(1)} %get-tuple-element.28), channel_id=1, replica_groups=mesh['seq'=16,'res'=2] {'seq'}, dimensions={0} | all-to-all | bytes 262144 | tf_op jit(solution)/shard_map/all_to_all | solution.py:319
  23.8 1.9 %column_step.1 = (f32[16,8,128]{2,1,0:T(8,128)S(1)}, f32[64,128]{1,0:T(8,128)S(1)}, f32[64,128]{1,0:T(8,128)S(1)}, f32[64,64]{1,0:T(8,128)S(1)}) custom-call(f32[16,16,128]{2,1,0:T(8,128)S(1)} %all_to_all.20.arrived, f32[2,64]{1,0:T(2,128)S(1)} %copy-done.7, f32[64,144]{1,0:T(8,128)S(1)} %copy-done.4, f32[64,64]{1,0:T(8,128)S(1)} %copy-done.5), custom_call_target="tpu_custom_call" | custom-call | tf_op jit(solution)/shard_map/column_step/pallas_call | solution.py:303
  25.7 10.4 %all_to_all.21.returned = f32[16,8,128]{2,1,0:T(8,128)S(1)} all-to-all(f32[16,8,128]{2,1,0:T(8,128)S(1)} %get-tuple-element.29), channel_id=1, replica_groups=mesh['seq'=16,'res'=2] {'seq'}, dimensions={0} | all-to-all | bytes 131072 | tf_op jit(solution)/shard_map/all_to_all | solution.py:319
  36.1 4.2 %row_backward.1 = (f32[16,56,128]{2,1,0:T(8,128)S(1)}, f32[2,64,64]{2,1,0:T(8,128)S(1)}, f32[2,64,64]{2,1,0:T(8,128)S(1)}, f32[2,64,64]{2,1,0:T(8,128)S(1)}) custom-call(s32[1]{0:T(128)} %bitcast.me, f32[16,8,128]{2,1,0:T(8,128)S(1)} %all_to_all.21.returned, bf16[2,64,64]{2,1,0:T(8,128)(2,1)S(1)} %copy-done, ...), custom_call_target="tpu_custom_call" | custom-call | tf_op jit(solution)/shard_map/row_backward/pallas_call | solution.py:303
  40.3 15.0 %all_to_all.22.arrived = f32[16,56,128]{2,1,0:T(8,128)S(1)} all-to-all(f32[16,56,128]{2,1,0:T(8,128)S(1)} %get-tuple-element.41), channel_id=1, replica_groups=mesh['seq'=16,'res'=2] {'seq'}, dimensions={0} | all-to-all | bytes 917504 | tf_op jit(solution)/shard_map/all_to_all | solution.py:319
  55.3 0.7 add_arrivals.1
  56.0 0.0 collective-permute-start.2
  56.0 1.2 %collective-permute-done.2 = f32[24,128]{1,0:T(8,128)S(1)} collective-permute-done((f32[24,128]{1,0:T(8,128)S(1)}, f32[24,128]{1,0:T(8,128)S(1)}, u32[]{:S(2)}, u32[]{:S(2)}) %collective-permute-start.2) | collective-permute-done | bytes 12320 | tf_op jit(solution)/shard_map/ppermute | solution.py:315
  57.2 0.7 broadcast_in_dim.5
  57.9 3.7 %all-to-all-start.3 = ((f32[16,24,128]{2,1,0:T(8,128)}), f32[16,24,128]{2,1,0:T(8,128)S(1)}, u32[]{:S(2)}, u32[]{:S(2)}) async-start(f32[16,24,128]{2,1,0:T(8,128)} %broadcast_in_dim.5), calls=%async_computation.3 | async-start | bytes 393216 | tf_op jit(solution)/shard_map/all_to_all | solution.py:319
  61.6 0.1 collective-permute-start.1
  61.7 1.2 %collective-permute-done.1.refs_1_ = f32[2,64,64]{2,1,0:T(8,128)S(1)} collective-permute-done((f32[2,64,64]{2,1,0:T(8,128)S(1)}, f32[2,64,64]{2,1,0:T(8,128)S(1)}, u32[]{:S(2)}, u32[]{:S(2)}) %collective-permute-start.1) | collective-permute-done | bytes 32800 | tf_op jit(solution)/shard_map/ppermute | solution.py:315
  62.9 0.9 %finish_alignment.1 = bf16[2,64,64]{2,1,0:T(8,128)(2,1)} custom-call(bf16[2,64,64]{2,1,0:T(8,128)(2,1)S(1)} %copy-done, f32[2,64,64]{2,1,0:T(8,128)S(1)} %get-tuple-element.38.middle_grad, f32[2,64]{1,0:T(2,128)S(1)} %copy-done.7, f32[2,64,64]{2,1,0:T(8,128)S(1)} %get-tuple-element.39.refs_0_, f32[2,64,64]{2,1,0:T(8,128)S(1)} %collective-permute-done.1.refs_1_), custom_call_target="tpu_custom_call" | custom-call | tf_op jit(solution)/shard_map/finish_alignment/pallas_call | solution.py:303
  63.8 6.5 %all-to-all-done.3.slab = f32[16,24,128]{2,1,0:T(8,128)S(1)} async-done(((f32[16,24,128]{2,1,0:T(8,128)}), f32[16,24,128]{2,1,0:T(8,128)S(1)}, u32[]{:S(2)}, u32[]{:S(2)}) %all-to-all-start.3) | async-done | bytes 196640 | tf_op jit(solution)/shard_map/all_to_all | solution.py:319
  70.3 0.7 %unpack.1 = (f32[2,64]{1,0:T(2,128)}, f32[64,256]{1,0:T(8,128)}, f32[64,64]{1,0:T(8,128)}, f32[64,144]{1,0:T(8,128)}, f32[64,64]{1,0:T(8,128)}) custom-call(f32[16,24,128]{2,1,0:T(8,128)S(1)} %all-to-all-done.3.slab), custom_call_target="tpu_custom_call" | custom-call | tf_op jit(solution)/shard_map/unpack/pallas_call | solution.py:303
  (17 shorter events, 0.0 us)
Async XLA Ops:
  1.3 2.3 %copy-start.3 = (f32[64,64]{1,0:T(8,128)S(1)}, f32[64,64]{1,0:T(8,128)}, u32[]{:S(2)}) copy-start(f32[64,64]{1,0:T(8,128)} %w_out.3) | copy-start | bytes 49156
  1.3 2.3 %copy-start.6 = (bf16[2,64,64]{2,1,0:T(8,128)(2,1)S(1)}, bf16[2,64,64]{2,1,0:T(8,128)(2,1)}, u32[]{:S(2)}) copy-start(bf16[2,64,64]{2,1,0:T(8,128)(2,1)} %refs_3_.1) | copy-start | bytes 49156
  2.1 1.6 %copy-start.2 = (bf16[8,64,128]{2,1,0:T(8,128)(2,1)S(1)}, bf16[8,64,128]{2,1,0:T(8,128)(2,1)}, u32[]{:S(2)}) copy-start(bf16[8,64,128]{2,1,0:T(8,128)(2,1)} %refs_4_.1) | copy-start | bytes 393220
  2.1 1.5 %copy-start = (bf16[2,64,64]{2,1,0:T(8,128)(2,1)S(1)}, bf16[2,64,64]{2,1,0:T(8,128)(2,1)}, u32[]{:S(2)}) copy-start(bf16[2,64,64]{2,1,0:T(8,128)(2,1)} %own.3) | copy-start | bytes 49156
  2.1 1.5 %copy-start.1 = (f32[64,256]{1,0:T(8,128)S(1)}, f32[64,256]{1,0:T(8,128)}, u32[]{:S(2)}) copy-start(f32[64,256]{1,0:T(8,128)} %w_row.1) | copy-start | bytes 196612
  2.2 1.5 %collective-permute-start = (f32[3,64,64]{2,1,0:T(8,128)S(1)}, f32[3,64,64]{2,1,0:T(8,128)S(1)}, u32[]{:S(2)}, u32[]{:S(2)}) collective-permute-start(f32[3,64,64]{2,1,0:T(8,128)S(1)} %pad_maximum_fusion.refs_0_), channel_id=1, source_target_pairs={{1,0},{0,1},{3,2},{2,3},{5,4},{4,5},{7,6},{6,7},{9,8},{8,9},{11,10... | collective-permute-start | bytes 147464 | tf_op jit(solution)/shard_map/ppermute | solution.py:315
  2.7 1.0 %copy-start.7 = (f32[2,64]{1,0:T(2,128)S(1)}, f32[2,64]{1,0:T(2,128)}, u32[]{:S(2)}) copy-start(f32[2,64]{1,0:T(2,128)} %gains.5) | copy-start | bytes 1540
  2.7 1.0 %copy-start.8 = (s32[2]{0:T(128)S(1)}, s32[2]{0:T(128)}, u32[]{:S(2)}) copy-start(s32[2]{0:T(128)} %seq_mask.1) | copy-start | bytes 28
  7.8 16.0 %copy-start.4 = (f32[64,144]{1,0:T(8,128)S(1)}, f32[64,144]{1,0:T(8,128)}, u32[]{:S(2)}) copy-start(f32[64,144]{1,0:T(8,128)} %w_col.1) | copy-start | bytes 110596
  7.8 16.0 %copy-start.5 = (f32[64,64]{1,0:T(8,128)S(1)}, f32[64,64]{1,0:T(8,128)}, u32[]{:S(2)}) copy-start(f32[64,64]{1,0:T(8,128)} %w_out.2) | copy-start | bytes 49156
  56.0 1.2 %collective-permute-start.2 = (f32[24,128]{1,0:T(8,128)S(1)}, f32[24,128]{1,0:T(8,128)S(1)}, u32[]{:S(2)}, u32[]{:S(2)}) collective-permute-start(f32[24,128]{1,0:T(8,128)S(1)} %get-tuple-element.43), channel_id=1, source_target_pairs={{1,0},{0,1},{3,2},{2,3},{5,4},{4,5},{7,6},{6,7},{9,8},{8,9},{11,10... | collective-permute-start | bytes 36872 | tf_op jit(solution)/shard_map/ppermute | solution.py:315
  57.9 12.4 %all-to-all-start.3 = ((f32[16,24,128]{2,1,0:T(8,128)}), f32[16,24,128]{2,1,0:T(8,128)S(1)}, u32[]{:S(2)}, u32[]{:S(2)}) async-start(f32[16,24,128]{2,1,0:T(8,128)} %broadcast_in_dim.5), calls=%async_computation.3 | async-start | bytes 393216 | tf_op jit(solution)/shard_map/all_to_all | solution.py:319
  61.6 1.3 %collective-permute-start.1 = (f32[2,64,64]{2,1,0:T(8,128)S(1)}, f32[2,64,64]{2,1,0:T(8,128)S(1)}, u32[]{:S(2)}, u32[]{:S(2)}) collective-permute-start(f32[2,64,64]{2,1,0:T(8,128)S(1)} %get-tuple-element.40), channel_id=1, source_target_pairs={{1,0},{0,1},{3,2},{2,3},{5,4},{4,5},{7,6},{6,7},{9,8},{8,9},{11,10... | collective-permute-start | bytes 98312 | tf_op jit(solution)/shard_map/ppermute | solution.py:315

commit v2 on v1

v2 whole, which is shorter than its diff:
```python
import functools

import jax
import jax.numpy as jnp
from jax import lax
from jax.experimental import pallas as pl
from jax.experimental.pallas import tpu as pltpu
from jax.sharding import PartitionSpec as P

C = 64
H = 8
DH = 8
LANES = 128
ROWS = 8
FOUR = 4
WIDE = FOUR * LANES
SLABS = 5

EXACT = lax.Precision.HIGHEST
THREE = lax.Precision.HIGH
EPSILON = 1e-05
MASKED = 1000000000.0
SCALE = DH ** (-0.5)
F32 = jnp.float32


def dot(a, b, over=((1,), (0,)), precision=THREE):
    return lax.dot_general(a, b, (over, ((), ())), precision=precision, preferred_element_type=F32)


def dot_rows(a, b):
    return dot(a, b, ((0,), (0,)))


def dot_t(a, b, precision=THREE):
    return dot(a, b, ((1,), (1,)), precision)


def tile(blocks, at):
    return blocks[at // FOUR, :, at % FOUR * LANES : (at % FOUR + 1) * LANES]


def put_tiles(blocks, first, values):
    for i in range(values.shape[0] // ROWS):
        at = first + i
        blocks[at // FOUR, :, at % FOUR * LANES : (at % FOUR + 1) * LANES] = values[i * ROWS : (i + 1) * ROWS, :]


def take_tiles(blocks, first, count):
    return jnp.concatenate([tile(blocks, first + i) for i in range(count)], axis=0)


def to_column(row):
    eye = lax.broadcasted_iota(jnp.int32, (C, C), 0) == lax.broadcasted_iota(jnp.int32, (C, C), 1)
    return jnp.sum(jnp.where(eye, row, 0.0), axis=1, keepdims=True)


def to_row(column):
    eye = lax.broadcasted_iota(jnp.int32, (C, C), 0) == lax.broadcasted_iota(jnp.int32, (C, C), 1)
    return jnp.sum(jnp.where(eye, column, 0.0), axis=0, keepdims=True)


def normalise(values):
    centred = values - jnp.mean(values, axis=-1, keepdims=True)
    inverse = lax.rsqrt(jnp.mean(centred * centred, axis=-1, keepdims=True) + EPSILON)
    return centred * inverse, inverse


def normalise_back(grad_normed, gain, unit, inverse):
    grad_unit = grad_normed * gain
    along = jnp.mean(grad_unit * unit, axis=-1, keepdims=True)
    return inverse * (grad_unit - jnp.mean(grad_unit, axis=-1, keepdims=True) - unit * along)


def head_mask(rows):
    row = lax.broadcasted_iota(jnp.int32, (H, rows, C), 0)
    channel = lax.broadcasted_iota(jnp.int32, (H, rows, C), 2)
    return (row == channel // DH).astype(F32).reshape(H * rows, C)


def spread_heads(values, mask):
    return jnp.concatenate([values] * H, axis=0) * mask


def join_heads(values, mask):
    masked = values * mask
    return jnp.sum(masked.reshape(H, -1, C), axis=0)


def near_size(count):
    return 1 << (count.bit_length() // 2)


def row_forward(n_res, seq_mask, *refs):
    sent = refs[:n_res]
    own, cotangent, bias, gains, w_row, w_out = refs[n_res : n_res + 6]
    payload, weights_out, unit_out, own_unit_out, memory_out, query_gate_out, mixture_out, gathered = refs[n_res + 6 :]
    n_seq, n_rows, _ = own.shape
    me = lax.axis_index("res")
    for away in range(n_res):
        gathered[lax.rem(me + away, n_res)] = sent[away][...]
    n_keys = n_res * n_rows
    n_blocks = payload.shape[0]
    block = n_rows // n_blocks
    near = near_size(n_blocks)
    gain = gains[0:1, :]
    w_all = w_row[...]
    w_query_gate = jnp.concatenate([w_all[:, :C], w_all[:, 3 * C :]], axis=1)
    residue = gathered[:, n_seq].reshape(n_keys, C)
    key_bias = MASKED * (jnp.transpose(residue)[0:1, :] - 1.0)
    bias_rows = bias[...].reshape(H * n_rows, n_keys).astype(F32)
    mask = head_mask(n_rows)
    for s in range(n_seq):
        unit, _ = normalise(gathered[:, s].reshape(n_keys, C))
        unit_out[s] = unit
        memory = dot(unit * gain, w_all[:, C : 3 * C], precision=EXACT)
        memory_out[s] = memory
        initial = own[s].astype(F32)
        own_unit, _ = normalise(initial)
        own_unit_out[s] = own_unit
        projected = dot(own_unit * gain, w_query_gate, precision=EXACT)
        query = projected[:, :C] * SCALE
        gate = jax.nn.sigmoid(projected[:, C:])
        query_gate_out[s] = jnp.concatenate([query, gate], axis=1)
        scores = dot_t(spread_heads(query, mask), memory[:, :C], EXACT) + bias_rows + key_bias
        exponent = jnp.exp(scores - jnp.max(scores, axis=-1, keepdims=True))
        weights = exponent / jnp.sum(exponent, axis=-1, keepdims=True)
        weights_out[s] = weights
        mixture = join_heads(dot(weights, memory[:, C:]), mask)
        mixture_out[s] = mixture
        middle = initial + dot(gate * mixture, w_out[...])
        both = jnp.concatenate([middle, cotangent[s].astype(F32)], axis=1)
        for b in range(n_blocks):
            payload[b % near * (n_blocks // near) + b // near, s] = both[b * block : (b + 1) * block, :]
    lane = lax.broadcasted_iota(jnp.int32, (block, 2 * C), 1) // (2 * C // n_seq)
    present = jnp.zeros((block, 2 * C), F32)
    for s in range(n_seq):
        present = jnp.where(lane == s, seq_mask[s].astype(F32), present)
    for b in range(n_blocks):
        payload[b, n_seq] = present


def column_step(arrived, gains, w_col, w_out, returned, col_slab, rest_slab, out_grad, gathered, mask_rows, n_seq):
    n_src, _, block, _ = arrived.shape
    group = n_seq * block
    rows = n_src * group
    wide = 2 * C // n_seq
    for src in range(n_src):
        for s in range(n_seq):
            gathered[src, s * block : (s + 1) * block, :] = arrived[src, s]
            mask_rows[src, s * block : (s + 1) * block, :] = jnp.broadcast_to(
                arrived[src, n_seq, :, s * wide : s * wide + 1], (block, C)
            )
    data = gathered[...].reshape(rows, 2 * C)
    present = mask_rows[...]
    middle = data[:, :C]
    cot = data[:, C:]
    gain = gains[1:2, :]

    def over_sequences(values, combine, reduce):
        total = reduce(values.reshape(n_src, group, C), axis=0)
        result = total
        for shift in range(1, n_seq):
            result = combine(result, pltpu.roll(total, shift * block, 0))
        return result

    def total_of(values):
        return over_sequences(values, jnp.add, jnp.sum)

    def spread(values):
        return jnp.broadcast_to(values[None], (n_src, group, C)).reshape(rows, C)

    lane = lax.broadcasted_iota(jnp.int32, (C, C), 1)
    row = lax.broadcasted_iota(jnp.int32, (C, C), 0)
    same_head = (row // DH == lane // DH).astype(F32)
    repeat = (lax.broadcasted_iota(jnp.int32, (DH, C), 0) == lax.broadcasted_iota(jnp.int32, (DH, C), 1) % DH).astype(F32)
    w_all = w_col[...]
    w_query = w_all[:, :C]
    w_key = dot(w_all[:, C : C + DH], repeat, precision=EXACT)
    w_value = dot(w_all[:, C + DH : C + 2 * DH], repeat)
    w_gate = w_all[:, C + 2 * DH :]
    w_rest = jnp.concatenate([w_key, w_value, w_gate], axis=1)

    unit, inverse = normalise(middle)
    normed = unit * gain
    present_rows = present.reshape(rows, C)
    counted = total_of(present_rows)
    mean_unit = total_of(present_rows * unit) / counted
    mean_normed = mean_unit * gain
    query = dot(mean_normed, w_query, precision=EXACT) * SCALE
    query_rows = spread(query)
    rest = dot(normed, w_rest, precision=EXACT)
    key, value = rest[:, :C], rest[:, C : 2 * C]
    gate = jax.nn.sigmoid(rest[:, 2 * C :])
    scores = dot(query_rows * key, same_head, precision=EXACT) + MASKED * (present_rows - 1.0)
    peak = over_sequences(scores, jnp.maximum, jnp.max)
    exponent = jnp.exp(scores - spread(peak))
    weights = exponent / spread(total_of(exponent))
    mixture = total_of(weights * value)
    mixture_rows = spread(mixture)

    grad_gated = dot_t(cot, w_out[...])
    out_grad[...] = dot_rows(gate * mixture_rows, cot)
    grad_mixture = total_of(gate * grad_gated)
    grad_mixture_rows = spread(grad_mixture)
    grad_gate = grad_gated * mixture_rows * gate * (1.0 - gate)
    grad_weights = dot(grad_mixture_rows * value, same_head)
    inner = spread(dot(grad_mixture * mixture, same_head))
    grad_scores = weights * (grad_weights - inner)
    grad_rest = jnp.concatenate([grad_scores * query_rows, weights * grad_mixture_rows, grad_gate], axis=1)
    grad_query = total_of(grad_scores * key) * SCALE
    grad_mean = dot_t(grad_query, w_query)
    grad_normed = present_rows * spread(grad_mean / counted) + dot_t(grad_rest, w_rest)
    grad_query_weights = dot_rows(mean_unit, grad_query) * (1.0 / n_seq)
    grad_rest_weights = dot_rows(unit, grad_rest)
    fold_row = lax.broadcasted_iota(jnp.int32, (2 * C, 2 * DH), 0)
    fold_lane = lax.broadcasted_iota(jnp.int32, (2 * C, 2 * DH), 1)
    fold = ((fold_row // C == fold_lane // DH) & (fold_row % DH == fold_lane % DH)).astype(F32)
    grad_key_value = dot(grad_rest_weights[:, : 2 * C], fold)
    col_slab[...] = jnp.concatenate([grad_query_weights, grad_rest_weights[:, 2 * C :]], axis=1)
    rest_slab[...] = jnp.zeros(rest_slab.shape, F32)
    rest_slab[:, : 2 * DH] = grad_key_value
    grad_middle = (cot + normalise_back(grad_normed, gain, unit, inverse)).reshape(n_src, group, C)
    for src in range(n_src):
        for s in range(n_seq):
            returned[src, :, s * C : (s + 1) * C] = grad_middle[src, s * block : (s + 1) * block, :]


def row_backward(n_res, returned, weights_in, unit_in, memory_in, query_gate_in, mixture_in, own_unit_in, gains,
                 w_row, w_out, col_slab, rest_slab, col_out_grad, bias_out, middle_grad, *refs):
    sums_out, shares = refs[:n_res], refs[n_res]
    me = lax.axis_index("res")
    n_seq, n_rows, _ = middle_grad.shape
    n_keys = memory_in.shape[1]
    n_blocks, block, _ = returned.shape
    near = near_size(n_blocks)
    gain = gains[0:1, :]
    w_all = w_row[...]
    w_memory = w_all[:, C : 3 * C]
    w_query_gate = jnp.concatenate([w_all[:, :C], w_all[:, 3 * C :]], axis=1)
    mask = head_mask(n_rows)
    for b in range(n_blocks):
        for s in range(n_seq):
            at = b % near * (n_blocks // near) + b // near
            middle_grad[s, b * block : (b + 1) * block, :] = returned[at, :, s * C : (s + 1) * C]
    grad_out = jnp.zeros((C, C), F32)
    grad_query_gate_weights = jnp.zeros((C, 2 * C), F32)
    grad_memory_weights = jnp.zeros((C, 2 * C), F32)
    bias_grad = jnp.zeros((H * n_rows, n_keys), F32)
    from_own = []
    from_memory = []
    for s in range(n_seq):
        grad_middle = middle_grad[s]
        query = query_gate_in[s, :, :C]
        gate = query_gate_in[s, :, C:]
        mixture = mixture_in[s]
        memory = memory_in[s]
        weights = weights_in[s]
        grad_gated = dot_t(grad_middle, w_out[...])
        grad_out = grad_out + dot_rows(gate * mixture, grad_middle)
        grad_gate = grad_gated * mixture * gate * (1.0 - gate)
        grad_heads = spread_heads(grad_gated * gate, mask)
        query_heads = spread_heads(query, mask)
        inner = grad_heads * jnp.concatenate([mixture] * H, axis=0)
        left = jnp.concatenate([grad_heads, inner], axis=1)
        right = jnp.concatenate([memory[:, C:], jnp.full((n_keys, C), -1.0, F32)], axis=1)
        grad_scores = weights * dot_t(left, right)
        bias_grad = bias_grad + grad_scores
        grad_query = join_heads(dot(grad_scores, memory[:, :C]), mask) * SCALE
        grad_key = dot_rows(grad_scores, query_heads)
        grad_value = dot_rows(weights, grad_heads)
        grad_memory = jnp.concatenate([grad_key, grad_value], axis=1)
        grad_query_gate = jnp.concatenate([grad_query, grad_gate], axis=1)
        grad_query_gate_weights = grad_query_gate_weights + dot_rows(own_unit_in[s], grad_query_gate)
        grad_memory_weights = grad_memory_weights + dot_rows(unit_in[s], grad_memory)
        from_memory.append(dot_t(grad_memory, w_memory))
        from_own.append(dot_t(grad_query_gate, w_query_gate))
    bias_out[...] = jnp.transpose(bias_grad)
    slabs = (
        grad_query_gate_weights,
        grad_memory_weights,
        col_slab[...],
        jnp.concatenate([grad_out, col_out_grad[...]], axis=1),
        rest_slab[...],
    )
    normed_tiles = n_rows // ROWS
    part = shares.shape[1] * FOUR - normed_tiles
    shares[...] = jnp.zeros(shares.shape, F32)
    for i, values in enumerate(slabs):
        for k in range(C // ROWS):
            at = i * (C // ROWS) + k
            put_tiles(shares.at[at // part], at % part, values[k * ROWS : (k + 1) * ROWS, :])
    normed = jnp.concatenate(from_memory, axis=1)
    for i in range(n_res):
        put_tiles(shares.at[i], part, normed[i * n_rows : (i + 1) * n_rows, :])
    for away in range(n_res):
        sums_out[away][...] = shares[lax.rem(me + away, n_res)]
    own_normed = take_tiles(sums_out[0], part, normed_tiles) + jnp.concatenate(from_own, axis=1)
    put_tiles(sums_out[0], part, own_normed)


def step_bits(n_seq_devices, odd):
    bits = list(range(n_seq_devices.bit_length() - 1))
    if odd:
        for i in range(0, len(bits) - 1, 2):
            bits[i], bits[i + 1] = bits[i + 1], bits[i]
    return bits


def slot_mask(slot, bits):
    last = len(bits) - 1
    return sum(1 << bit for step, bit in enumerate(bits) if slot >> (last - step) & 1)


def combine(n_blocks, own, middle_grad, bias_grad, gains, *refs):
    sums, state, send, out = refs[:-3], refs[-3], refs[-2], refs[-1]
    n_seq, n_rows, _ = own.shape
    total = sums[0][...]
    for more in sums[1:]:
        total = total + more[...]
    shared = state.shape[0] - n_blocks
    part = shared * FOUR
    normed = take_tiles(total, part, n_rows // ROWS)
    for s in range(n_seq):
        unit, inverse = normalise(own[s].astype(F32))
        grad_normed = normed[:, s * C : (s + 1) * C]
        out[s] = (middle_grad[s] + normalise_back(grad_normed, gains[0:1, :], unit, inverse)).astype(out.dtype)
    place = lax.axis_index("seq")
    odd = lax.rem(lax.axis_index("res"), 2)
    even_bits, odd_bits = step_bits(n_blocks, False), step_bits(n_blocks, True)
    half = n_blocks // 2
    for slot in range(n_blocks):
        even_mask, odd_mask = slot_mask(slot, even_bits), slot_mask(slot, odd_bits)
        block = place ^ (even_mask + odd * (odd_mask - even_mask))
        values = bias_grad[pl.ds(pl.multiple_of(block * ROWS, ROWS), ROWS), :]
        if slot < half:
            state[slot] = values
        else:
            send[slot - half] = values
    state[n_blocks:] = total[:shared]
    send[half:] = total[:shared]


def step(left, state, arrived, state_out, send_out):
    half = left // 2
    blocks = state[:left] + arrived[:left]
    shared = state[state.shape[0] - (arrived.shape[0] - left) :] + arrived[left:]
    state_out[:left] = blocks
    state_out[left:] = shared
    send_out[:half] = blocks[half:]
    send_out[half:] = shared


def last_step(state, arrived, bias_out, shared_out):
    total = state[0] + arrived[0]
    shared_out[...] = state[state.shape[0] - shared_out.shape[0] :] + arrived[1:]
    heads, _, n_rows = bias_out.shape
    for h in range(heads):
        bias_out[h] = total[:, h * n_rows : (h + 1) * n_rows]


def unpack(n_res, *refs):
    parts = refs[:n_res]
    gains, w_row, w_col, gains_out, row_project_out, row_out_out, col_project_out, col_out_out, shares = refs[n_res:]
    me = lax.axis_index("res")
    for away in range(n_res):
        shares[lax.rem(me + away, n_res)] = parts[away][...]
    part = shares.shape[1] * FOUR
    each = C // ROWS
    slabs = [
        jnp.concatenate([tile(shares.at[at // part], at % part) for at in range(i * each, (i + 1) * each)], axis=0)
        for i in range(SLABS)
    ]
    gain_row = to_column(gains[0:1, :])
    gain_col = to_column(gains[1:2, :])
    w_all = w_row[...]
    w_column = w_col[...]
    query_gate, memory, col_query_gate, outs, rest = slabs
    rest = rest[:, : 2 * DH]
    row_gain_grad = (
        jnp.sum(query_gate[:, :C] * w_all[:, :C], axis=1, keepdims=True)
        + jnp.sum(memory * w_all[:, C : 3 * C], axis=1, keepdims=True)
        + jnp.sum(query_gate[:, C:] * w_all[:, 3 * C :], axis=1, keepdims=True)
    )
    col_gain_grad = (
        jnp.sum(col_query_gate[:, :C] * w_column[:, :C], axis=1, keepdims=True)
        + jnp.sum(rest * w_column[:, C : C + 2 * DH], axis=1, keepdims=True)
        + jnp.sum(col_query_gate[:, C:] * w_column[:, C + 2 * DH :], axis=1, keepdims=True)
    )
    gains_out[0:1, :] = to_row(row_gain_grad)
    gains_out[1:2, :] = to_row(col_gain_grad)
    row_project_out[:, :C] = query_gate[:, :C] * gain_row
    row_project_out[:, C : 3 * C] = memory * gain_row
    row_project_out[:, 3 * C :] = query_gate[:, C:] * gain_row
    col_project_out[:, :C] = col_query_gate[:, :C] * gain_col
    col_project_out[:, C : C + 2 * DH] = rest * gain_col
    col_project_out[:, C + 2 * DH :] = col_query_gate[:, C:] * gain_col
    row_out_out[...] = outs[:, :C]
    col_out_out[...] = outs[:, C:]


def call(body, outs, *operands, smem=0, scratch=(), name):
    vmem = pl.BlockSpec(memory_space=pltpu.VMEM)
    scalar = pl.BlockSpec(memory_space=pltpu.SMEM)
    return pl.pallas_call(
        body,
        out_shape=[jax.ShapeDtypeStruct(shape, kind) for shape, kind in outs],
        in_specs=[scalar] * smem + [vmem] * (len(operands) - smem),
        out_specs=[vmem] * len(outs),
        scratch_shapes=list(scratch),
        compiler_params=pltpu.CompilerParams(vmem_limit_bytes=32 * 1024 * 1024),
        name=name,
    )(*operands)


def shift_residues(values, away, count):
    return lax.ppermute(values, "res", [((i + away) % count, i) for i in range(count)])


def cross(values, at, seq_count, res_count):
    pairs = []
    for r in range(res_count):
        bit = 1 << step_bits(seq_count, r % 2)[at]
        pairs += [(i * res_count + r, (i ^ bit) * res_count + r) for i in range(seq_count)]
    return lax.ppermute(values, ("seq", "res"), pairs)


def regroup(source, out):
    for i in range(source.shape[0]):
        for j in range(source.shape[1]):
            out[j, i] = source[i, j]


def swap_groups(values, groups):
    return lax.all_to_all(values, "seq", 0, 0, axis_index_groups=groups, tiled=True)


def swap_blocks(values, near_first):
    count = values.shape[0]
    near = near_size(count)
    far = count // near
    near_groups = [[f * near + n for n in range(near)] for f in range(far)]
    far_groups = [[f * near + n for f in range(far)] for n in range(near)]
    shape = values.shape[1:]
    if near_first:
        first, second, sizes = near_groups, far_groups, (near, far)
    else:
        first, second, sizes = far_groups, near_groups, (far, near)
    values = swap_groups(values.reshape(sizes + shape), first)
    (values,) = call(regroup, [(sizes[::-1] + shape, values.dtype)], values, name="regroup")
    return swap_groups(values, second)


def local(
    alignment,
    cotangent,
    pair_bias,
    norm_gains,
    row_project,
    row_output,
    column_project,
    column_output,
    residue_mask,
    sequence_mask,
    seq_count,
    res_count,
):
    n_seq, n_rows, _ = alignment.shape
    n_keys = pair_bias.shape[2]
    block = n_rows // seq_count
    group = n_seq * block
    away_range = range(1, res_count)
    present_keys = jnp.broadcast_to(residue_mask.astype(F32)[None, :, None], (1, n_rows, C))
    sent = jnp.concatenate([alignment.astype(F32), present_keys], axis=0)
    payload, weights, unit, own_unit, memory, query_gate, mixture = call(
        functools.partial(row_forward, res_count),
        [
            ((seq_count, n_seq + 1, block, 2 * C), F32),
            ((n_seq, H * n_rows, n_keys), F32),
            ((n_seq, n_keys, C), F32),
            ((n_seq, n_rows, C), F32),
            ((n_seq, n_keys, 2 * C), F32),
            ((n_seq, n_rows, 2 * C), F32),
            ((n_seq, n_rows, C), F32),
        ],
        sequence_mask, sent, *[shift_residues(sent, away, res_count) for away in away_range],
        alignment, cotangent, pair_bias, norm_gains, row_project, row_output,
        smem=1,
        scratch=[pltpu.VMEM((res_count, n_seq + 1, n_rows, C), F32)],
        name="row_forward",
    )
    arrived = swap_blocks(payload, True).reshape(payload.shape)
    returned, col_slab, rest_slab, col_out_grad = call(
        functools.partial(column_step, n_seq=n_seq),
        [((seq_count, block, n_seq * C), F32), ((C, 2 * C), F32), ((C, 2 * C), F32), ((C, C), F32)],
        arrived, norm_gains, column_project, column_output,
        scratch=[pltpu.VMEM((seq_count, group, 2 * C), F32), pltpu.VMEM((seq_count, group, C), F32)],
        name="column_step",
    )
    returned = swap_blocks(returned, False).reshape(returned.shape)
    shared = -(-SLABS * C // (ROWS * FOUR * res_count))
    normed = n_rows // ROWS // FOUR
    bias_grad, middle_grad, *sums = call(
        functools.partial(row_backward, res_count),
        [((n_keys, H * n_rows), F32), ((n_seq, n_rows, C), F32)]
        + [((shared + normed, ROWS, WIDE), F32)] * res_count,
        returned, weights, unit, memory, query_gate, mixture, own_unit, norm_gains, row_project, row_output,
        col_slab, rest_slab, col_out_grad,
        scratch=[pltpu.VMEM((res_count, shared + normed, ROWS, WIDE), F32)],
        name="row_backward",
    )
    sums = sums[:1] + [shift_residues(sums[away], -away, res_count) for away in away_range]
    left = seq_count // 2
    state, send, grad_alignment = call(
        functools.partial(combine, seq_count),
        [
            ((seq_count + shared, ROWS, WIDE), F32),
            ((left + shared, ROWS, WIDE), F32),
            (alignment.shape, alignment.dtype),
        ],
        alignment, middle_grad, bias_grad, norm_gains, *sums,
        name="combine",
    )
    at = 0
    while left > 1:
        arrived = cross(send, at, seq_count, res_count)
        state, send = call(
            functools.partial(step, left),
            [((left + shared, ROWS, WIDE), F32), ((left // 2 + shared, ROWS, WIDE), F32)],
            state, arrived,
            name="step",
        )
        left, at = left // 2, at + 1
    arrived = cross(send, at, seq_count, res_count)
    bias_grad, summed = call(
        last_step,
        [((H, n_keys // seq_count, n_rows), F32), ((shared, ROWS, WIDE), F32)],
        state, arrived,
        name="last_step",
    )
    grads = call(
        functools.partial(unpack, res_count),
        [((2, C), F32), ((C, 4 * C), F32), ((C, C), F32), ((C, 2 * C + 2 * DH), F32), ((C, C), F32)],
        summed, *[shift_residues(summed, away, res_count) for away in away_range],
        norm_gains, row_project, column_project,
        scratch=[pltpu.VMEM((res_count, shared, ROWS, WIDE), F32)],
        name="unpack",
    )
    return (grad_alignment, jnp.transpose(bias_grad, (0, 2, 1)), *grads)


def solution(mesh):
    placed = (
        P("seq", "res", None),
        P("seq", "res", None),
        P(None, "res", None),
        P(),
        P(),
        P(),
        P(),
        P(),
        P("res"),
        P("seq"),
    )
    return jax.shard_map(
        functools.partial(local, seq_count=mesh.shape["seq"], res_count=mesh.shape["res"]),
        mesh=mesh,
        in_specs=placed,
        out_specs=(P("seq", "res", None), P(None, "res", "seq"), P(), P(), P(), P(), P()),
        check_vma=False,
    )
```

time: 71.5 us -> 76 us (1.063)
  waiting for transfers between devices: 9.9 us -> 23.9 us
  blocking collectives: 41.4 us -> 35.6 us
  Pallas kernels: 12.5 us -> 11 us
  starting transfers between devices: 4.27 us -> 2.94 us
    ppermute x0 -> x4, waiting for transfers between devices: none -> 20.4 us  [cross(): return lax.ppermute(values, ('seq', 'res'), pairs)]
    all_to_all x1 -> x0, waiting for transfers between devices: 6.55 us -> none  [swap_blocks(): return lax.all_to_all(values, 'seq', 0, 0, tiled=True)]
    all_to_all x3 -> x4, blocking collectives: 41.4 us -> 35.6 us  [swap_groups(): lax.all_to_all(values, 'seq', 0, 0, axis_index_groups=groups, tiled=True)]
    all_to_all x1 -> x0, starting transfers between devices: 3.67 us -> none  [swap_blocks(): return lax.all_to_all(values, 'seq', 0, 0, tiled=True)]
    ppermute x0 -> x4, starting transfers between devices: none -> 2.35 us  [cross(): return lax.ppermute(values, ('seq', 'res'), pairs)]
    pallas_call x6 -> x11, Pallas kernels: 12.5 us -> 11 us  [call(): pl.pallas_call(body, out_shape=[jax.ShapeDtypeStruct(shape, kind) for sha...]
  transfers between devices with their start and end apart: 4 -> 7, of which waited for: 4 -> 7; matrix products, arithmetic and copies ran while one was open for 0% -> 0% of each run, Pallas kernels for 1% -> 0%
where the time goes in v2:
time: 76 us; the launch traced here: 75.6 us
  blocking collectives  35.6 us (47%)
  waiting for transfers between devices  23.9 us (31%)
  Pallas kernels  11 us (14%)
  starting transfers between devices  2.94 us (4%)
  other arithmetic  1.44 us (2%)
    all_to_all x4, blocking collectives, swap_groups(): lax.all_to_all(values, 'seq', 0, 0, axis_index_groups=groups, tiled=True)  35.6 us
    ppermute x4, waiting for transfers between devices, cross(): return lax.ppermute(values, ('seq', 'res'), pairs)  20.4 us
    pallas_call x11, Pallas kernels, call(): pl.pallas_call(body, out_shape=[jax.ShapeDtypeStruct(shape, kind) for sha...  11 us
    ppermute x3, waiting for transfers between devices, shift_residues(): lax.ppermute(values, 'res', [((i + away) % count, i) for i in range(count)])  3.53 us
    ppermute x4, starting transfers between devices, cross(): return lax.ppermute(values, ('seq', 'res'), pairs)  2.35 us
  transfers between devices with their start and end apart: 7, of which 7 were waited for; matrix products, arithmetic and copies ran while one was open for 0% of the time, Pallas kernels for 0%

profile of v2, /device:TPU:0, one launch (start us, length us, event | category | flops | bytes accessed | tf_op | source)
XLA Modules:
  0.0 75.6 jit_solution(15292828133075767293)
XLA Ops:
  0.6 0.7 convert_element_type.7
  1.3 0.8 %convert_element_type.6 = f32[2,64,64]{2,1,0:T(8,128)S(1)} convert(bf16[2,64,64]{2,1,0:T(8,128)(2,1)} %own.1) | non-fusion elementwise | flops 8192 | bytes 49152 | tf_op jit(solution)/shard_map/convert_element_type | solution.py:474
  2.2 0.5 collective-permute-start
  2.7 0.9 %collective-permute-done.refs_1_ = f32[3,64,64]{2,1,0:T(8,128)S(1)} collective-permute-done((f32[3,64,64]{2,1,0:T(8,128)S(1)}, f32[3,64,64]{2,1,0:T(8,128)S(1)}, u32[]{:S(2)}, u32[]{:S(2)}) %collective-permute-start) | collective-permute-done | bytes 49184 | tf_op jit(solution)/shard_map/ppermute | solution.py:417
  3.7 3.7 %row_forward.1 = (f32[16,3,4,128]{3,2,1,0:T(4,128)S(1)}, f32[2,512,128]{2,1,0:T(8,128)S(1)}, f32[2,128,64]{2,1,0:T(8,128)S(1)}, f32[2,64,64]{2,1,0:T(8,128)S(1)}...) custom-call(s32[2]{0:T(128)S(1)} %copy-done.8, ...), custom_call_target="tpu_custom_call" | custom-call | tf_op jit(solution)/shard_map/row_forward/pallas_call | solution.py:405
  7.4 9.8 %all_to_all.20.source = f32[4,4,3,4,128]{4,3,2,1,0:T(4,128)S(1)} all-to-all(f32[4,4,3,4,128]{4,3,2,1,0:T(4,128)S(1)} %bitcast.7), channel_id=1, replica_groups={{0,2,4,6},{8,10,12,14},{16,18,20,22},{24,26,28,30},{1,3,5,7},{9,11,13,1..., dimensions={0} | all-to-all | bytes 196608 | tf_op jit(solution)/shard_map/all_to_all | solution.py:435
  17.2 10.6 %all_to_all.21 = f32[4,4,3,4,128]{4,3,2,1,0:T(4,128)S(1)} all-to-all(f32[4,4,3,4,128]{4,3,2,1,0:T(4,128)S(1)} %regroup.2), channel_id=1, replica_groups={{0,8,16,24},{2,10,18,26},{4,12,20,28},{6,14,22,30},{1,9,17,25},{3,11,19..., dimensions={0} | all-to-all | bytes 196608 | tf_op jit(solution)/shard_map/all_to_all | solution.py:435
  27.9 1.6 %column_step.1 = (f32[16,4,128]{2,1,0:T(4,128)S(1)}, f32[64,128]{1,0:T(8,128)S(1)}, f32[64,128]{1,0:T(8,128)S(1)}, f32[64,64]{1,0:T(8,128)S(1)}) custom-call(f32[16,3,4,128]{3,2,1,0:T(4,128)S(1)} %bitcast.5, f32[2,64]{1,0:T(2,128)S(1)} %copy-done.7, f32[64,144]{1,0:T(8,128)S(1)} %copy-done.2, f32[64,64]{1,0:T(8,128)S(1)} %copy-done.6), custom_call_target="tpu_custom_call" | custom-call | tf_op jit(solution)/shard_map/column_step/pallas_call | solution.py:405
  29.5 8.0 %all_to_all.22.source = f32[4,4,4,128]{3,2,1,0:T(4,128)S(1)} all-to-all(f32[4,4,4,128]{3,2,1,0:T(4,128)S(1)} %bitcast.8), channel_id=1, replica_groups={{0,8,16,24},{2,10,18,26},{4,12,20,28},{6,14,22,30},{1,9,17,25},{3,11,19..., dimensions={0} | all-to-all | bytes 65536 | tf_op jit(solution)/shard_map/all_to_all | solution.py:435
  37.5 7.1 %all_to_all.23 = f32[4,4,4,128]{3,2,1,0:T(4,128)S(1)} all-to-all(f32[4,4,4,128]{3,2,1,0:T(4,128)S(1)} %regroup.3), channel_id=1, replica_groups={{0,2,4,6},{8,10,12,14},{16,18,20,22},{24,26,28,30},{1,3,5,7},{9,11,13,1..., dimensions={0} | all-to-all | bytes 65536 | tf_op jit(solution)/shard_map/all_to_all | solution.py:435
  44.6 2.6 %row_backward.1 = (f32[128,512]{1,0:T(8,128)S(1)}, f32[2,64,64]{2,1,0:T(8,128)S(1)}, f32[7,8,512]{2,1,0:T(8,128)S(1)}, f32[7,8,512]{2,1,0:T(8,128)S(1)}) custom-call(f32[16,4,128]{2,1,0:T(4,128)S(1)} %bitcast.6, f32[2,512,128]{2,1,0:T(8,128)S(1)} %get-tuple-element.40.weights_in, f32[2,128,64]{2,1,0:T(8,128)S(1)} %get-tuple-element.41.unit_in, ...), custom_call_target="tpu_custom_call" | custom-call | tf_op jit(solution)/shard_map/row_backward/pallas_call | solution.py:405
  47.3 1.3 %collective-permute-done.1.refs_1_ = f32[7,8,512]{2,1,0:T(8,128)S(1)} collective-permute-done((f32[7,8,512]{2,1,0:T(8,128)S(1)}, f32[7,8,512]{2,1,0:T(8,128)S(1)}, u32[]{:S(2)}, u32[]{:S(2)}) %collective-permute-start.1) | collective-permute-done | bytes 114720 | tf_op jit(solution)/shard_map/ppermute | solution.py:417
  48.6 1.1 %combine.1 = (f32[21,8,512]{2,1,0:T(8,128)S(1)}, f32[13,8,512]{2,1,0:T(8,128)S(1)}, bf16[2,64,64]{2,1,0:T(8,128)(2,1)}) custom-call(bf16[2,64,64]{2,1,0:T(8,128)(2,1)S(1)} %copy-done.1, f32[2,64,64]{2,1,0:T(8,128)S(1)} %get-tuple-element.49.middle_grad, f32[128,512]{1,0:T(8,128)S(1)} %get-tuple-element.50.bias_grad, f32[2,64]{1,0:T(2,128)S(1)} %copy-done.7, ...), custom_call_target="tpu_custom_call" | custom-call | tf_op jit(solution)/shard_map/combine/pallas_call | solution.py:405
  49.7 0.7 collective-permute-start.2
  50.4 5.2 %collective-permute-done.2.arrived = f32[13,8,512]{2,1,0:T(8,128)S(1)} collective-permute-done((f32[13,8,512]{2,1,0:T(8,128)S(1)}, f32[13,8,512]{2,1,0:T(8,128)S(1)}, u32[]{:S(2)}, u32[]{:S(2)}) %collective-permute-start.2) | collective-permute-done | bytes 213024 | tf_op jit(solution)/shard_map/ppermute | solution.py:425
  55.6 0.7 collective-permute-start.3
  56.3 4.5 %collective-permute-done.3.arrived = f32[9,8,512]{2,1,0:T(8,128)S(1)} collective-permute-done((f32[9,8,512]{2,1,0:T(8,128)S(1)}, f32[9,8,512]{2,1,0:T(8,128)S(1)}, u32[]{:S(2)}, u32[]{:S(2)}) %collective-permute-start.3) | collective-permute-done | bytes 147488 | tf_op jit(solution)/shard_map/ppermute | solution.py:425
  60.9 0.8 %collective-permute-start.4 = (f32[7,8,512]{2,1,0:T(8,128)S(1)}, f32[7,8,512]{2,1,0:T(8,128)S(1)}, u32[]{:S(2)}, u32[]{:S(2)}) collective-permute-start(f32[7,8,512]{2,1,0:T(8,128)S(1)} %get-tuple-element.59), channel_id=1, source_target_pairs={{0,8},{2,10},{4,12},{6,14},{8,0},{10,2},{12,4},{14,6},{16,24},{18,... | collective-permute-start | bytes 344072 | tf_op jit(solution)/shard_map/ppermute | solution.py:425
  61.7 4.6 %collective-permute-done.4.arrived = f32[7,8,512]{2,1,0:T(8,128)S(1)} collective-permute-done((f32[7,8,512]{2,1,0:T(8,128)S(1)}, f32[7,8,512]{2,1,0:T(8,128)S(1)}, u32[]{:S(2)}, u32[]{:S(2)}) %collective-permute-start.4) | collective-permute-done | bytes 114720 | tf_op jit(solution)/shard_map/ppermute | solution.py:425
  66.3 0.2 collective-permute-start.5
  66.4 6.1 %collective-permute-done.5.arrived = f32[6,8,512]{2,1,0:T(8,128)S(1)} collective-permute-done((f32[6,8,512]{2,1,0:T(8,128)S(1)}, f32[6,8,512]{2,1,0:T(8,128)S(1)}, u32[]{:S(2)}, u32[]{:S(2)}) %collective-permute-start.5) | collective-permute-done | bytes 98336 | tf_op jit(solution)/shard_map/ppermute | solution.py:425
  72.5 0.7 last_step.1
  73.2 1.3 %collective-permute-done.6.refs_1_ = f32[5,8,512]{2,1,0:T(8,128)S(1)} collective-permute-done((f32[5,8,512]{2,1,0:T(8,128)S(1)}, f32[5,8,512]{2,1,0:T(8,128)S(1)}, u32[]{:S(2)}, u32[]{:S(2)}) %collective-permute-start.6) | collective-permute-done | bytes 81952 | tf_op jit(solution)/shard_map/ppermute | solution.py:417
  74.5 1.1 %unpack.1 = (f32[2,64]{1,0:T(2,128)}, f32[64,256]{1,0:T(8,128)}, f32[64,64]{1,0:T(8,128)}, f32[64,144]{1,0:T(8,128)}, f32[64,64]{1,0:T(8,128)}) custom-call(f32[5,8,512]{2,1,0:T(8,128)S(1)} %get-tuple-element.63.refs_0_, f32[5,8,512]{2,1,0:T(8,128)S(1)} %collective-permute-done.6.refs_1_, f32[2,64]{1,0:T(2,128)S(1)} %copy-done.7, f32[64,256]{1,0:T(8,128)S(1)} %copy-done, ...), custom_call_target="tpu_custom_call" | custom-call | tf_op jit(solution)/shard_map/unpack/pallas_call | solution.py:405
  (27 shorter events, 0.3 us)
Async XLA Ops:
  1.3 2.3 %copy-start.4 = (f32[64,64]{1,0:T(8,128)S(1)}, f32[64,64]{1,0:T(8,128)}, u32[]{:S(2)}) copy-start(f32[64,64]{1,0:T(8,128)} %w_out.3) | copy-start | bytes 49156
  1.3 2.3 %copy-start.5 = (bf16[2,64,64]{2,1,0:T(8,128)(2,1)S(1)}, bf16[2,64,64]{2,1,0:T(8,128)(2,1)}, u32[]{:S(2)}) copy-start(bf16[2,64,64]{2,1,0:T(8,128)(2,1)} %refs_3_.2) | copy-start | bytes 49156
  1.3 2.3 %copy-start.7 = (f32[2,64]{1,0:T(2,128)S(1)}, f32[2,64]{1,0:T(2,128)}, u32[]{:S(2)}) copy-start(f32[2,64]{1,0:T(2,128)} %refs_2_.3) | copy-start | bytes 1540
  2.1 1.6 %copy-start.3 = (bf16[8,64,128]{2,1,0:T(8,128)(2,1)S(1)}, bf16[8,64,128]{2,1,0:T(8,128)(2,1)}, u32[]{:S(2)}) copy-start(bf16[8,64,128]{2,1,0:T(8,128)(2,1)} %refs_4_.2) | copy-start | bytes 393220
  2.1 1.5 %copy-start = (f32[64,256]{1,0:T(8,128)S(1)}, f32[64,256]{1,0:T(8,128)}, u32[]{:S(2)}) copy-start(f32[64,256]{1,0:T(8,128)} %refs_3_.3) | copy-start | bytes 196612
  2.1 1.5 %copy-start.1 = (bf16[2,64,64]{2,1,0:T(8,128)(2,1)S(1)}, bf16[2,64,64]{2,1,0:T(8,128)(2,1)}, u32[]{:S(2)}) copy-start(bf16[2,64,64]{2,1,0:T(8,128)(2,1)} %own.1) | copy-start | bytes 49156
  2.1 1.5 %copy-start.8 = (s32[2]{0:T(128)S(1)}, s32[2]{0:T(128)}, u32[]{:S(2)}) copy-start(s32[2]{0:T(128)} %seq_mask.1) | copy-start | bytes 28
  2.2 1.5 %collective-permute-start = (f32[3,64,64]{2,1,0:T(8,128)S(1)}, f32[3,64,64]{2,1,0:T(8,128)S(1)}, u32[]{:S(2)}, u32[]{:S(2)}) collective-permute-start(f32[3,64,64]{2,1,0:T(8,128)S(1)} %pad_maximum_fusion.refs_0_), channel_id=1, source_target_pairs={{1,0},{0,1},{3,2},{2,3},{5,4},{4,5},{7,6},{6,7},{9,8},{8,9},{11,10... | collective-permute-start | bytes 147464 | tf_op jit(solution)/shard_map/ppermute | solution.py:417
  17.2 10.7 %copy-start.2 = (f32[64,144]{1,0:T(8,128)S(1)}, f32[64,144]{1,0:T(8,128)}, u32[]{:S(2)}) copy-start(f32[64,144]{1,0:T(8,128)} %refs_4_.3) | copy-start | bytes 110596
  17.2 10.7 %copy-start.6 = (f32[64,64]{1,0:T(8,128)S(1)}, f32[64,64]{1,0:T(8,128)}, u32[]{:S(2)}) copy-start(f32[64,64]{1,0:T(8,128)} %w_out.2) | copy-start | bytes 49156
  47.2 1.4 %collective-permute-start.1 = (f32[7,8,512]{2,1,0:T(8,128)S(1)}, f32[7,8,512]{2,1,0:T(8,128)S(1)}, u32[]{:S(2)}, u32[]{:S(2)}) collective-permute-start(f32[7,8,512]{2,1,0:T(8,128)S(1)} %get-tuple-element.52), channel_id=1, source_target_pairs={{1,0},{0,1},{3,2},{2,3},{5,4},{4,5},{7,6},{6,7},{9,8},{8,9},{11,10... | collective-permute-start | bytes 344072 | tf_op jit(solution)/shard_map/ppermute | solution.py:417
  49.7 5.8 %collective-permute-start.2 = (f32[13,8,512]{2,1,0:T(8,128)S(1)}, f32[13,8,512]{2,1,0:T(8,128)S(1)}, u32[]{:S(2)}, u32[]{:S(2)}) collective-permute-start(f32[13,8,512]{2,1,0:T(8,128)S(1)} %get-tuple-element.55), channel_id=1, source_target_pairs={{0,2},{2,0},{4,6},{6,4},{8,10},{10,8},{12,14},{14,12},{16,18},{18,... | collective-permute-start | bytes 638984 | tf_op jit(solution)/shard_map/ppermute | solution.py:425
  55.6 5.2 %collective-permute-start.3 = (f32[9,8,512]{2,1,0:T(8,128)S(1)}, f32[9,8,512]{2,1,0:T(8,128)S(1)}, u32[]{:S(2)}, u32[]{:S(2)}) collective-permute-start(f32[9,8,512]{2,1,0:T(8,128)S(1)} %get-tuple-element.57), channel_id=1, source_target_pairs={{0,4},{2,6},{4,0},{6,2},{8,12},{10,14},{12,8},{14,10},{16,20},{18,... | collective-permute-start | bytes 442376 | tf_op jit(solution)/shard_map/ppermute | solution.py:425
  60.9 5.4 %collective-permute-start.4 = (f32[7,8,512]{2,1,0:T(8,128)S(1)}, f32[7,8,512]{2,1,0:T(8,128)S(1)}, u32[]{:S(2)}, u32[]{:S(2)}) collective-permute-start(f32[7,8,512]{2,1,0:T(8,128)S(1)} %get-tuple-element.59), channel_id=1, source_target_pairs={{0,8},{2,10},{4,12},{6,14},{8,0},{10,2},{12,4},{14,6},{16,24},{18,... | collective-permute-start | bytes 344072 | tf_op jit(solution)/shard_map/ppermute | solution.py:425
  66.3 6.3 %collective-permute-start.5 = (f32[6,8,512]{2,1,0:T(8,128)S(1)}, f32[6,8,512]{2,1,0:T(8,128)S(1)}, u32[]{:S(2)}, u32[]{:S(2)}) collective-permute-start(f32[6,8,512]{2,1,0:T(8,128)S(1)} %get-tuple-element.61), channel_id=1, source_target_pairs={{0,16},{2,18},{4,20},{6,22},{8,24},{10,26},{12,28},{14,30},{16,0},... | collective-permute-start | bytes 294920 | tf_op jit(solution)/shard_map/ppermute | solution.py:425
  73.2 1.3 %collective-permute-start.6 = (f32[5,8,512]{2,1,0:T(8,128)S(1)}, f32[5,8,512]{2,1,0:T(8,128)S(1)}, u32[]{:S(2)}, u32[]{:S(2)}) collective-permute-start(f32[5,8,512]{2,1,0:T(8,128)S(1)} %get-tuple-element.63.refs_0_), channel_id=1, source_target_pairs={{1,0},{0,1},{3,2},{2,3},{5,4},{4,5},{7,6},{6,7},{9,8},{8,9},{11,10... | collective-permute-start | bytes 245768 | tf_op jit(solution)/shard_map/ppermute | solution.py:417

commit v3 on v2

--- a/solution.py
+++ b/solution.py
@@ -12,9 +12,6 @@
 DH = 8
 LANES = 128
 ROWS = 8
-FOUR = 4
-WIDE = FOUR * LANES
-SLABS = 5
 
 EXACT = lax.Precision.HIGHEST
 THREE = lax.Precision.HIGH
@@ -36,20 +33,6 @@
     return dot(a, b, ((1,), (1,)), precision)
 
 
-def tile(blocks, at):
-    return blocks[at // FOUR, :, at % FOUR * LANES : (at % FOUR + 1) * LANES]
-
-
-def put_tiles(blocks, first, values):
-    for i in range(values.shape[0] // ROWS):
-        at = first + i
-        blocks[at // FOUR, :, at % FOUR * LANES : (at % FOUR + 1) * LANES] = values[i * ROWS : (i + 1) * ROWS, :]
-
-
-def take_tiles(blocks, first, count):
-    return jnp.concatenate([tile(blocks, first + i) for i in range(count)], axis=0)
-
-
 def to_column(row):
     eye = lax.broadcasted_iota(jnp.int32, (C, C), 0) == lax.broadcasted_iota(jnp.int32, (C, C), 1)
     return jnp.sum(jnp.where(eye, row, 0.0), axis=1, keepdims=True)
@@ -85,10 +68,6 @@
 def join_heads(values, mask):
     masked = values * mask
     return jnp.sum(masked.reshape(H, -1, C), axis=0)
-
-
-def near_size(count):
-    return 1 << (count.bit_length() // 2)
 
 
 def row_forward(n_res, seq_mask, *refs):
@@ -102,7 +81,6 @@
     n_keys = n_res * n_rows
     n_blocks = payload.shape[0]
     block = n_rows // n_blocks
-    near = near_size(n_blocks)
     gain = gains[0:1, :]
     w_all = w_row[...]
     w_query_gate = jnp.concatenate([w_all[:, :C], w_all[:, 3 * C :]], axis=1)
@@ -131,7 +109,7 @@
         middle = initial + dot(gate * mixture, w_out[...])
         both = jnp.concatenate([middle, cotangent[s].astype(F32)], axis=1)
         for b in range(n_blocks):
-            payload[b % near * (n_blocks // near) + b // near, s] = both[b * block : (b + 1) * block, :]
+            payload[b, s] = both[b * block : (b + 1) * block, :]
     lane = lax.broadcasted_iota(jnp.int32, (block, 2 * C), 1) // (2 * C // n_seq)
     present = jnp.zeros((block, 2 * C), F32)
     for s in range(n_seq):
@@ -140,11 +118,12 @@
         payload[b, n_seq] = present
 
 
-def column_step(arrived, gains, w_col, w_out, returned, col_slab, rest_slab, out_grad, gathered, mask_rows, n_seq):
+def column_step(arrived, gains, w_col, w_out, returned, gathered, mask_rows, n_seq):
     n_src, _, block, _ = arrived.shape
     group = n_seq * block
     rows = n_src * group
     wide = 2 * C // n_seq
+    share = C // n_src
     for src in range(n_src):
         for s in range(n_seq):
             gathered[src, s * block : (s + 1) * block, :] = arrived[src, s]
@@ -200,7 +179,7 @@
     mixture_rows = spread(mixture)
 
     grad_gated = dot_t(cot, w_out[...])
-    out_grad[...] = dot_rows(gate * mixture_rows, cot)
+    out_grad = dot_rows(gate * mixture_rows, cot)
     grad_mixture = total_of(gate * grad_gated)
     grad_mixture_rows = spread(grad_mixture)
     grad_gate = grad_gated * mixture_rows * gate * (1.0 - gate)
@@ -217,32 +196,30 @@
     fold_lane = lax.broadcasted_iota(jnp.int32, (2 * C, 2 * DH), 1)
     fold = ((fold_row // C == fold_lane // DH) & (fold_row % DH == fold_lane % DH)).astype(F32)
     grad_key_value = dot(grad_rest_weights[:, : 2 * C], fold)
-    col_slab[...] = jnp.concatenate([grad_query_weights, grad_rest_weights[:, 2 * C :]], axis=1)
-    rest_slab[...] = jnp.zeros(rest_slab.shape, F32)
-    rest_slab[:, : 2 * DH] = grad_key_value
+    first = jnp.concatenate([grad_query_weights, grad_rest_weights[:, 2 * C :]], axis=1)
+    second = jnp.concatenate([out_grad, grad_key_value, jnp.zeros((C, C - 2 * DH), F32)], axis=1)
     grad_middle = (cot + normalise_back(grad_normed, gain, unit, inverse)).reshape(n_src, group, C)
     for src in range(n_src):
         for s in range(n_seq):
-            returned[src, :, s * C : (s + 1) * C] = grad_middle[src, s * block : (s + 1) * block, :]
-
-
-def row_backward(n_res, returned, weights_in, unit_in, memory_in, query_gate_in, mixture_in, own_unit_in, gains,
-                 w_row, w_out, col_slab, rest_slab, col_out_grad, bias_out, middle_grad, *refs):
-    sums_out, shares = refs[:n_res], refs[n_res]
+            returned[src, 0, :, s * C : (s + 1) * C] = grad_middle[src, s * block : (s + 1) * block, :]
+        returned[src, 1] = first[src * share : (src + 1) * share, :]
+        returned[src, 2] = second[src * share : (src + 1) * share, :]
+
+
+def row_backward(n_res, returned, weights_in, unit_in, memory_in, query_gate_in, mixture_in, own_unit_in,
+                 w_row, w_out, state, send, middle_grad, *refs):
+    sums_out, shares, bias_t = refs[:n_res], refs[n_res], refs[n_res + 1]
     me = lax.axis_index("res")
     n_seq, n_rows, _ = middle_grad.shape
     n_keys = memory_in.shape[1]
-    n_blocks, block, _ = returned.shape
-    near = near_size(n_blocks)
-    gain = gains[0:1, :]
+    n_blocks, _, block, _ = returned.shape
     w_all = w_row[...]
     w_memory = w_all[:, C : 3 * C]
     w_query_gate = jnp.concatenate([w_all[:, :C], w_all[:, 3 * C :]], axis=1)
     mask = head_mask(n_rows)
     for b in range(n_blocks):
         for s in range(n_seq):
-            at = b % near * (n_blocks // near) + b // near
-            middle_grad[s, b * block : (b + 1) * block, :] = returned[at, :, s * C : (s + 1) * C]
+            middle_grad[s, b * block : (b + 1) * block, :] = returned[b, 0, :, s * C : (s + 1) * C]
     grad_out = jnp.zeros((C, C), F32)
     grad_query_gate_weights = jnp.zeros((C, 2 * C), F32)
     grad_memory_weights = jnp.zeros((C, 2 * C), F32)
@@ -275,108 +252,138 @@
         grad_memory_weights = grad_memory_weights + dot_rows(unit_in[s], grad_memory)
         from_memory.append(dot_t(grad_memory, w_memory))
         from_own.append(dot_t(grad_query_gate, w_query_gate))
-    bias_out[...] = jnp.transpose(bias_grad)
-    slabs = (
-        grad_query_gate_weights,
-        grad_memory_weights,
-        col_slab[...],
-        jnp.concatenate([grad_out, col_out_grad[...]], axis=1),
-        rest_slab[...],
-    )
-    normed_tiles = n_rows // ROWS
-    part = shares.shape[1] * FOUR - normed_tiles
+    bias_t[...] = jnp.transpose(bias_grad)
+    split_blocks(bias_t, state, send)
+
+    half = C // 2
+    weight_grads = jnp.concatenate(
+        [grad_query_gate_weights, grad_memory_weights, jnp.concatenate([grad_out[:half], grad_out[half:]], axis=1)],
+        axis=0,
+    )
+    part = shares.shape[1] - ROWS - n_rows
     shares[...] = jnp.zeros(shares.shape, F32)
-    for i, values in enumerate(slabs):
-        for k in range(C // ROWS):
-            at = i * (C // ROWS) + k
-            put_tiles(shares.at[at // part], at % part, values[k * ROWS : (k + 1) * ROWS, :])
+    share = C // n_blocks
+    column = jnp.sum(returned[:, 1:, :, :], axis=0)
     normed = jnp.concatenate(from_memory, axis=1)
     for i in range(n_res):
-        put_tiles(shares.at[i], part, normed[i * n_rows : (i + 1) * n_rows, :])
+        rows = min(part, max(0, weight_grads.shape[0] - i * part))
+        if rows:
+            shares[i, :rows, :] = weight_grads[i * part : i * part + rows, :]
+        shares[i, part : part + share, :] = column[0]
+        shares[i, part + share : part + 2 * share, :] = column[1]
+        shares[i, part + ROWS :, :] = normed[i * n_rows : (i + 1) * n_rows, :]
     for away in range(n_res):
         sums_out[away][...] = shares[lax.rem(me + away, n_res)]
-    own_normed = take_tiles(sums_out[0], part, normed_tiles) + jnp.concatenate(from_own, axis=1)
-    put_tiles(sums_out[0], part, own_normed)
-
-
-def step_bits(n_seq_devices, odd):
+    sums_out[0][part + ROWS :, :] += jnp.concatenate(from_own, axis=1)
+
+
+def step_bits(n_seq_devices, odd, late_first=False):
     bits = list(range(n_seq_devices.bit_length() - 1))
     if odd:
         for i in range(0, len(bits) - 1, 2):
             bits[i], bits[i + 1] = bits[i + 1], bits[i]
+    if late_first:
+        middle = len(bits) // 2
+        bits = bits[middle:] + bits[:middle]
     return bits
 
 
-def slot_mask(slot, bits):
-    last = len(bits) - 1
-    return sum(1 << bit for step, bit in enumerate(bits) if slot >> (last - step) & 1)
-
-
-def combine(n_blocks, own, middle_grad, bias_grad, gains, *refs):
-    sums, state, send, out = refs[:-3], refs[-3], refs[-2], refs[-1]
-    n_seq, n_rows, _ = own.shape
+def relative_block(mask_of_bits, n_blocks, late_first=False):
+    odd = lax.rem(lax.axis_index("res"), 2)
+    even_mask = mask_of_bits(step_bits(n_blocks, False, late_first))
+    odd_mask = mask_of_bits(step_bits(n_blocks, True, late_first))
+    return lax.axis_index("seq") ^ (even_mask + odd * (odd_mask - even_mask))
+
+
+def split_blocks(bias_t, state, send):
+    n_blocks = state.shape[0] + send.shape[0]
+    keys_each = bias_t.shape[0] // n_blocks
+    half = n_blocks // 2
+
+    for slot in range(n_blocks):
+
+        def mask_of_bits(bits):
+            last = len(bits) - 1
+            return sum(1 << bit for at, bit in enumerate(bits) if slot >> (last - at) & 1)
+
+        block = relative_block(mask_of_bits, n_blocks)
+        values = bias_t[pl.ds(pl.multiple_of(block * keys_each, keys_each), keys_each), :]
+        if slot < half:
+            state[slot] = values
+        else:
+            send[slot - half] = values
+
+
+def bias_step(state, arrived, state_out, send_out):
+    total = state[...] + arrived[...]
+    half = state_out.shape[0]
+    state_out[...] = total[:half]
+    send_out[...] = total[half:]
+
+
+def bias_last(state, arrived, bias_out):
+    total = state[0] + arrived[0]
+    heads, _, n_rows = bias_out.shape
+    for h in range(heads):
+        bias_out[h] = total[:, h * n_rows : (h + 1) * n_rows]
+
+
+def add_shares(*refs):
+    sums, shared, normed = refs[:-2], refs[-2], refs[-1]
     total = sums[0][...]
     for more in sums[1:]:
         total = total + more[...]
-    shared = state.shape[0] - n_blocks
-    part = shared * FOUR
-    normed = take_tiles(total, part, n_rows // ROWS)
+    rows = shared.shape[0]
+    shared[...] = total[:rows]
+    normed[...] = total[rows:]
+
+
+def shared_step(part, shared, arrived, *outs):
+    total = shared[:part] + arrived[:part]
+    pieces = shared.shape[0] - part
+    if len(outs) == 2:
+        outs[0][...] = total
+        joined, at = outs[1], 0
+    else:
+        outs[0][:part] = total
+        joined, at = outs[0], part
+    joined[at : at + pieces] = shared[part:]
+    joined[at + pieces :] = arrived[part:]
+
+
+def finish_alignment(own, middle_grad, gains, normed, out):
+    n_seq = own.shape[0]
     for s in range(n_seq):
         unit, inverse = normalise(own[s].astype(F32))
         grad_normed = normed[:, s * C : (s + 1) * C]
         out[s] = (middle_grad[s] + normalise_back(grad_normed, gains[0:1, :], unit, inverse)).astype(out.dtype)
-    place = lax.axis_index("seq")
-    odd = lax.rem(lax.axis_index("res"), 2)
-    even_bits, odd_bits = step_bits(n_blocks, False), step_bits(n_blocks, True)
-    half = n_blocks // 2
-    for slot in range(n_blocks):
-        even_mask, odd_mask = slot_mask(slot, even_bits), slot_mask(slot, odd_bits)
-        block = place ^ (even_mask + odd * (odd_mask - even_mask))
-        values = bias_grad[pl.ds(pl.multiple_of(block * ROWS, ROWS), ROWS), :]
-        if slot < half:
-            state[slot] = values
-        else:
-            send[slot - half] = values
-    state[n_blocks:] = total[:shared]
-    send[half:] = total[:shared]
-
-
-def step(left, state, arrived, state_out, send_out):
-    half = left // 2
-    blocks = state[:left] + arrived[:left]
-    shared = state[state.shape[0] - (arrived.shape[0] - left) :] + arrived[left:]
-    state_out[:left] = blocks
-    state_out[left:] = shared
-    send_out[:half] = blocks[half:]
-    send_out[half:] = shared
-
-
-def last_step(state, arrived, bias_out, shared_out):
-    total = state[0] + arrived[0]
-    shared_out[...] = state[state.shape[0] - shared_out.shape[0] :] + arrived[1:]
-    heads, _, n_rows = bias_out.shape
-    for h in range(heads):
-        bias_out[h] = total[:, h * n_rows : (h + 1) * n_rows]
-
-
-def unpack(n_res, *refs):
+
+
+def unpack(n_res, joined, *refs):
     parts = refs[:n_res]
-    gains, w_row, w_col, gains_out, row_project_out, row_out_out, col_project_out, col_out_out, shares = refs[n_res:]
+    gains, w_row, w_col, gains_out, row_project_out, row_out_out, col_project_out, col_out_out = refs[n_res : n_res + 8]
+    shares, column = refs[n_res + 8 :]
     me = lax.axis_index("res")
+    part = shares.shape[1]
     for away in range(n_res):
         shares[lax.rem(me + away, n_res)] = parts[away][...]
-    part = shares.shape[1] * FOUR
-    each = C // ROWS
-    slabs = [
-        jnp.concatenate([tile(shares.at[at // part], at % part) for at in range(i * each, (i + 1) * each)], axis=0)
-        for i in range(SLABS)
-    ]
+    n_blocks, _, share, _ = column.shape
+    for slot in range(n_blocks):
+        block = relative_block(
+            lambda bits: sum(1 << bit for at, bit in enumerate(bits) if slot >> at & 1), n_blocks, True
+        )
+        piece = joined[slot * ROWS : (slot + 1) * ROWS, :]
+        column[block, 0] = piece[:share]
+        column[block, 1] = piece[share : 2 * share]
+    flat = jnp.concatenate([shares[i] for i in range(n_res)], axis=0)
+    query_gate, memory, outs = flat[:C], flat[C : 2 * C], flat[2 * C : 2 * C + C // 2]
+    col_query_gate = jnp.concatenate([column[i, 0] for i in range(n_blocks)], axis=0)
+    col_rest = jnp.concatenate([column[i, 1] for i in range(n_blocks)], axis=0)
+    rest = col_rest[:, C : C + 2 * DH]
     gain_row = to_column(gains[0:1, :])
     gain_col = to_column(gains[1:2, :])
     w_all = w_row[...]
     w_column = w_col[...]
-    query_gate, memory, col_query_gate, outs, rest = slabs
-    rest = rest[:, : 2 * DH]
     row_gain_grad = (
         jnp.sum(query_gate[:, :C] * w_all[:, :C], axis=1, keepdims=True)
         + jnp.sum(memory * w_all[:, C : 3 * C], axis=1, keepdims=True)
@@ -395,8 +402,10 @@
     col_project_out[:, :C] = col_query_gate[:, :C] * gain_col
     col_project_out[:, C : C + 2 * DH] = rest * gain_col
     col_project_out[:, C + 2 * DH :] = col_query_gate[:, C:] * gain_col
-    row_out_out[...] = outs[:, :C]
-    col_out_out[...] = outs[:, C:]
+    half = C // 2
+    row_out_out[:half, :] = outs[:, :C]
+    row_out_out[half:, :] = outs[:, C:]
+    col_out_out[...] = col_rest[:, :C]
 
 
 def call(body, outs, *operands, smem=0, scratch=(), name):
@@ -417,38 +426,16 @@
     return lax.ppermute(values, "res", [((i + away) % count, i) for i in range(count)])
 
 
-def cross(values, at, seq_count, res_count):
+def cross(values, at, seq_count, res_count, late_first=False):
     pairs = []
     for r in range(res_count):
-        bit = 1 << step_bits(seq_count, r % 2)[at]
+        bit = 1 << step_bits(seq_count, r % 2, late_first)[at]
         pairs += [(i * res_count + r, (i ^ bit) * res_count + r) for i in range(seq_count)]
     return lax.ppermute(values, ("seq", "res"), pairs)
 
 
-def regroup(source, out):
-    for i in range(source.shape[0]):
-        for j in range(source.shape[1]):
-            out[j, i] = source[i, j]
-
-
-def swap_groups(values, groups):
-    return lax.all_to_all(values, "seq", 0, 0, axis_index_groups=groups, tiled=True)
-
-
-def swap_blocks(values, near_first):
-    count = values.shape[0]
-    near = near_size(count)
-    far = count // near
-    near_groups = [[f * near + n for n in range(near)] for f in range(far)]
-    far_groups = [[f * near + n for f in range(far)] for n in range(near)]
-    shape = values.shape[1:]
-    if near_first:
-        first, second, sizes = near_groups, far_groups, (near, far)
-    else:
-        first, second, sizes = far_groups, near_groups, (far, near)
-    values = swap_groups(values.reshape(sizes + shape), first)
-    (values,) = call(regroup, [(sizes[::-1] + shape, values.dtype)], values, name="regroup")
-    return swap_groups(values, second)
+def swap_blocks(values):
+    return lax.all_to_all(values, "seq", 0, 0, tiled=True)
 
 
 def local(
@@ -489,61 +476,73 @@
         scratch=[pltpu.VMEM((res_count, n_seq + 1, n_rows, C), F32)],
         name="row_forward",
     )
-    arrived = swap_blocks(payload, True).reshape(payload.shape)
-    returned, col_slab, rest_slab, col_out_grad = call(
+    arrived = swap_blocks(payload)
+    (returned,) = call(
         functools.partial(column_step, n_seq=n_seq),
-        [((seq_count, block, n_seq * C), F32), ((C, 2 * C), F32), ((C, 2 * C), F32), ((C, C), F32)],
+        [((seq_count, 3, block, 2 * C), F32)],
         arrived, norm_gains, column_project, column_output,
         scratch=[pltpu.VMEM((seq_count, group, 2 * C), F32), pltpu.VMEM((seq_count, group, C), F32)],
         name="column_step",
     )
-    returned = swap_blocks(returned, False).reshape(returned.shape)
-    shared = -(-SLABS * C // (ROWS * FOUR * res_count))
-    normed = n_rows // ROWS // FOUR
-    bias_grad, middle_grad, *sums = call(
+    returned = swap_blocks(returned)
+    part = -(-5 * C // (2 * ROWS * res_count)) * ROWS
+    wide = H * n_rows
+    keys_each = n_keys // seq_count
+    left = seq_count // 2
+    state, send, middle_grad, *sums = call(
         functools.partial(row_backward, res_count),
-        [((n_keys, H * n_rows), F32), ((n_seq, n_rows, C), F32)]
-        + [((shared + normed, ROWS, WIDE), F32)] * res_count,
-        returned, weights, unit, memory, query_gate, mixture, own_unit, norm_gains, row_project, row_output,
-        col_slab, rest_slab, col_out_grad,
-        scratch=[pltpu.VMEM((res_count, shared + normed, ROWS, WIDE), F32)],
+        [((left, keys_each, wide), F32)] * 2
+        + [((n_seq, n_rows, C), F32)]
+        + [((part + ROWS + n_rows, LANES), F32)] * res_count,
+        returned, weights, unit, memory, query_gate, mixture, own_unit, row_project, row_output,
+        scratch=[
+            pltpu.VMEM((res_count, part + ROWS + n_rows, LANES), F32),
+            pltpu.VMEM((n_keys, wide), F32),
+        ],
         name="row_backward",
     )
     sums = sums[:1] + [shift_residues(sums[away], -away, res_count) for away in away_range]
-    left = seq_count // 2
-    state, send, grad_alignment = call(
-        functools.partial(combine, seq_count),
-        [
-            ((seq_count + shared, ROWS, WIDE), F32),
-            ((left + shared, ROWS, WIDE), F32),
-            (alignment.shape, alignment.dtype),
-        ],
-        alignment, middle_grad, bias_grad, norm_gains, *sums,
-        name="combine",
-    )
-    at = 0
-    while left > 1:
-        arrived = cross(send, at, seq_count, res_count)
-        state, send = call(
-            functools.partial(step, left),
-            [((left + shared, ROWS, WIDE), F32), ((left // 2 + shared, ROWS, WIDE), F32)],
-            state, arrived,
-            name="step",
+    arrived = cross(send, 0, seq_count, res_count)
+    shared, normed = call(
+        add_shares,
+        [((part + ROWS, LANES), F32), ((n_rows, LANES), F32)],
+        *sums,
+        name="add_shares",
+    )
+    steps = seq_count.bit_length() - 1
+    for at in range(steps):
+        arrived_shared = cross(shared, at, seq_count, res_count, True)
+        if at < steps - 1:
+            left //= 2
+            state, send = call(
+                bias_step, [((left, keys_each, wide), F32)] * 2, state, arrived, name="bias_step"
+            )
+            arrived = cross(send, at + 1, seq_count, res_count)
+        else:
+            (bias_grad,) = call(bias_last, [((H, keys_each, n_rows), F32)], state, arrived, name="bias_last")
+        pieces = ROWS << (at + 1)
+        shapes = [(part + pieces, LANES)] if at < steps - 1 else [(part, LANES), (pieces, LANES)]
+        shared, *joined = call(
+            functools.partial(shared_step, part),
+            [(shape, F32) for shape in shapes],
+            shared, arrived_shared,
+            name="shared_step",
         )
-        left, at = left // 2, at + 1
-    arrived = cross(send, at, seq_count, res_count)
-    bias_grad, summed = call(
-        last_step,
-        [((H, n_keys // seq_count, n_rows), F32), ((shared, ROWS, WIDE), F32)],
-        state, arrived,
-        name="last_step",
+    (grad_alignment,) = call(
+        finish_alignment,
+        [(alignment.shape, alignment.dtype)],
+        alignment, middle_grad, norm_gains, normed,
+        name="finish_alignment",
     )
     grads = call(
         functools.partial(unpack, res_count),
         [((2, C), F32), ((C, 4 * C), F32), ((C, C), F32), ((C, 2 * C + 2 * DH), F32), ((C, C), F32)],
-        summed, *[shift_residues(summed, away, res_count) for away in away_range],
+        *joined, shared, *[shift_residues(shared, away, res_count) for away in away_range],
         norm_gains, row_project, column_project,
-        scratch=[pltpu.VMEM((res_count, shared, ROWS, WIDE), F32)],
+        scratch=[
+            pltpu.VMEM((res_count, part, LANES), F32),
+            pltpu.VMEM((seq_count, 2, C // seq_count, LANES), F32),
+        ],
         name="unpack",
     )
     return (grad_alignment, jnp.transpose(bias_grad, (0, 2, 1)), *grads)

time: 76 us -> 65.1 us (0.86)
  blocking collectives: 35.6 us -> 26.1 us
  waiting for transfers between devices: 23.9 us -> 20.1 us
  starting transfers between devices: 2.94 us -> 5.38 us
    all_to_all x4 -> x2, blocking collectives: 35.6 us -> 26.1 us  [swap_blocks(): return lax.all_to_all(values, 'seq', 0, 0, tiled=True)]
    ppermute x4 -> x8, waiting for transfers between devices: 20.4 us -> 17.9 us  [cross(): return lax.ppermute(values, ('seq', 'res'), pairs)]
    ppermute x4 -> x8, starting transfers between devices: 2.35 us -> 4.72 us  [cross(): return lax.ppermute(values, ('seq', 'res'), pairs)]
    ppermute x3, waiting for transfers between devices: 3.53 us -> 2.21 us  [shift_residues(): lax.ppermute(values, 'res', [((i + away) % count, i) for i in range(count)])]
    pallas_call x11 -> x14, Pallas kernels: 11 us -> 10.9 us  [call(): pl.pallas_call(body, out_shape=[jax.ShapeDtypeStruct(shape, kind) for sha...]
  transfers between devices with their start and end apart: 7 -> 11, of which waited for: 7 -> 8; matrix products, arithmetic and copies ran while one was open for 0% -> 0% of each run, Pallas kernels for 0% -> 3%
where the time goes in v3:
time: 65.1 us; the launch traced here: 64.8 us
  blocking collectives  26.1 us (40%)
  waiting for transfers between devices  20.1 us (31%)
  Pallas kernels  10.9 us (17%)
  starting transfers between devices  5.38 us (8%)
  other arithmetic  1.44 us (2%)
  between operations  0.76 us (1%)
    all_to_all x2, blocking collectives, swap_blocks(): return lax.all_to_all(values, 'seq', 0, 0, tiled=True)  26.1 us
    ppermute x8, waiting for transfers between devices, cross(): return lax.ppermute(values, ('seq', 'res'), pairs)  17.9 us
    pallas_call x14, Pallas kernels, call(): pl.pallas_call(body, out_shape=[jax.ShapeDtypeStruct(shape, kind) for sha...  10.9 us
    ppermute x8, starting transfers between devices, cross(): return lax.ppermute(values, ('seq', 'res'), pairs)  4.72 us
    ppermute x3, waiting for transfers between devices, shift_residues(): lax.ppermute(values, 'res', [((i + away) % count, i) for i in range(count)])  2.21 us
  transfers between devices with their start and end apart: 11, of which 8 were waited for; matrix products, arithmetic and copies ran while one was open for 0% of the time, Pallas kernels for 3%

profile of v3, /device:TPU:0, one launch (start us, length us, event | category | flops | bytes accessed | tf_op | source)
XLA Modules:
  0.0 64.8 jit_solution(2486099161018370119)
XLA Ops:
  0.6 0.7 %convert_element_type.7 = f32[64]{0:T(128)S(1)} convert(s32[64]{0:T(128)} %param.18) | non-fusion elementwise | flops 64 | bytes 512 | tf_op jit(solution)/shard_map/convert_element_type | solution.py:460
  1.3 0.8 %convert_element_type.6 = f32[2,64,64]{2,1,0:T(8,128)S(1)} convert(bf16[2,64,64]{2,1,0:T(8,128)(2,1)} %own.1) | non-fusion elementwise | flops 8192 | bytes 49152 | tf_op jit(solution)/shard_map/convert_element_type | solution.py:461
  2.2 0.5 collective-permute-start
  2.7 0.9 %collective-permute-done.refs_1_ = f32[3,64,64]{2,1,0:T(8,128)S(1)} collective-permute-done((f32[3,64,64]{2,1,0:T(8,128)S(1)}, f32[3,64,64]{2,1,0:T(8,128)S(1)}, u32[]{:S(2)}, u32[]{:S(2)}) %collective-permute-start) | collective-permute-done | bytes 49184 | tf_op jit(solution)/shard_map/ppermute | solution.py:426
  3.7 3.7 %row_forward.1 = (f32[16,3,4,128]{3,2,1,0:T(4,128)S(1)}, f32[2,512,128]{2,1,0:T(8,128)S(1)}, f32[2,128,64]{2,1,0:T(8,128)S(1)}, f32[2,64,64]{2,1,0:T(8,128)S(1)}...) custom-call(s32[2]{0:T(128)S(1)} %copy-done.8, ...), custom_call_target="tpu_custom_call" | custom-call | tf_op jit(solution)/shard_map/row_forward/pallas_call | solution.py:414
  7.4 15.8 %all_to_all.10.arrived = f32[16,3,4,128]{3,2,1,0:T(4,128)S(1)} all-to-all(f32[16,3,4,128]{3,2,1,0:T(4,128)S(1)} %get-tuple-element.34), channel_id=1, replica_groups=mesh['seq'=16,'res'=2] {'seq'}, dimensions={0} | all-to-all | bytes 196608 | tf_op jit(solution)/shard_map/all_to_all | solution.py:438
  23.2 1.7 %column_step.1 = f32[16,3,4,128]{3,2,1,0:T(4,128)S(1)} custom-call(f32[16,3,4,128]{3,2,1,0:T(4,128)S(1)} %all_to_all.10.arrived, f32[2,64]{1,0:T(2,128)S(1)} %copy-done.7, f32[64,144]{1,0:T(8,128)S(1)} %copy-done.2, f32[64,64]{1,0:T(8,128)S(1)} %copy-done.6), custom_call_target="tpu_custom_call" | custom-call | tf_op jit(solution)/shard_map/column_step/pallas_call | solution.py:414
  24.9 10.3 %all_to_all.11.returned = f32[16,3,4,128]{3,2,1,0:T(4,128)S(1)} all-to-all(f32[16,3,4,128]{3,2,1,0:T(4,128)S(1)} %column_step.1), channel_id=1, replica_groups=mesh['seq'=16,'res'=2] {'seq'}, dimensions={0} | all-to-all | bytes 196608 | tf_op jit(solution)/shard_map/all_to_all | solution.py:438
  35.2 2.6 %row_backward.1 = (f32[8,8,512]{2,1,0:T(8,128)S(1)}, f32[8,8,512]{2,1,0:T(8,128)S(1)}, f32[2,64,64]{2,1,0:T(8,128)S(1)}, f32[152,128]{1,0:T(8,128)S(1)}, f32[152,128]{1,0:T(8,128)S(1)}) custom-call(f32[16,3,4,128]{3,2,1,0:T(4,128)S(1)} %all_to_all.11.returned, f32[2,512,128]{2,1,0:T(8,128)S(1)} %get-tuple-element.35.weights_in, ...), custom_call_target="tpu_custom_call" | custom-call | tf_op jit(solution)/shard_map/row_backward/pallas_call | solution.py:414
  37.8 1.3 %collective-permute-done.1.refs_1_ = f32[152,128]{1,0:T(8,128)S(1)} collective-permute-done((f32[152,128]{1,0:T(8,128)S(1)}, f32[152,128]{1,0:T(8,128)S(1)}, u32[]{:S(2)}, u32[]{:S(2)}) %collective-permute-start.1) | collective-permute-done | bytes 77856 | tf_op jit(solution)/shard_map/ppermute | solution.py:426
  39.1 0.8 %collective-permute-start.6 = (f32[88,128]{1,0:T(8,128)S(1)}, f32[88,128]{1,0:T(8,128)S(1)}, u32[]{:S(2)}, u32[]{:S(2)}) collective-permute-start(f32[88,128]{1,0:T(8,128)S(1)} %get-tuple-element.53.shared), channel_id=1, source_target_pairs={{0,8},{2,10},{4,12},{6,14},{8,0},{10,2},{12,4},{14,6},{16,24},{18,... | collective-permute-start | bytes 135176 | tf_op jit(solution)/shard_map/ppermute | solution.py:434
  39.8 0.6 collective-permute-start.2
  40.4 3.3 %collective-permute-done.6.arrived = f32[88,128]{1,0:T(8,128)S(1)} collective-permute-done((f32[88,128]{1,0:T(8,128)S(1)}, f32[88,128]{1,0:T(8,128)S(1)}, u32[]{:S(2)}, u32[]{:S(2)}) %collective-permute-start.6) | collective-permute-done | bytes 45088 | tf_op jit(solution)/shard_map/ppermute | solution.py:434
  43.7 0.8 %collective-permute-start.7 = (f32[96,128]{1,0:T(8,128)S(1)}, f32[96,128]{1,0:T(8,128)S(1)}, u32[]{:S(2)}, u32[]{:S(2)}) collective-permute-start(f32[96,128]{1,0:T(8,128)S(1)} %shared_step.4.shared), channel_id=1, source_target_pairs={{0,16},{2,18},{4,20},{6,22},{8,24},{10,26},{12,28},{14,30},{16,0},... | collective-permute-start | bytes 147464 | tf_op jit(solution)/shard_map/ppermute | solution.py:434
  44.5 4.4 %collective-permute-done.7.arrived = f32[96,128]{1,0:T(8,128)S(1)} collective-permute-done((f32[96,128]{1,0:T(8,128)S(1)}, f32[96,128]{1,0:T(8,128)S(1)}, u32[]{:S(2)}, u32[]{:S(2)}) %collective-permute-start.7) | collective-permute-done | bytes 49184 | tf_op jit(solution)/shard_map/ppermute | solution.py:434
  48.8 0.7 %collective-permute-start.8 = (f32[112,128]{1,0:T(8,128)S(1)}, f32[112,128]{1,0:T(8,128)S(1)}, u32[]{:S(2)}, u32[]{:S(2)}) collective-permute-start(f32[112,128]{1,0:T(8,128)S(1)} %shared_step.5.shared), channel_id=1, source_target_pairs={{0,2},{2,0},{4,6},{6,4},{8,10},{10,8},{12,14},{14,12},{16,18},{18,... | collective-permute-start | bytes 172040 | tf_op jit(solution)/shard_map/ppermute | solution.py:434
  49.6 0.7 %collective-permute-start.3 = (f32[4,8,512]{2,1,0:T(8,128)S(1)}, f32[4,8,512]{2,1,0:T(8,128)S(1)}, u32[]{:S(2)}, u32[]{:S(2)}) collective-permute-start(f32[4,8,512]{2,1,0:T(8,128)S(1)} %get-tuple-element.48), channel_id=1, source_target_pairs={{0,4},{2,6},{4,0},{6,2},{8,12},{10,14},{12,8},{14,10},{16,20},{18,... | collective-permute-start | bytes 196616 | tf_op jit(solution)/shard_map/ppermute | solution.py:434
  50.2 3.4 %collective-permute-done.8.arrived = f32[112,128]{1,0:T(8,128)S(1)} collective-permute-done((f32[112,128]{1,0:T(8,128)S(1)}, f32[112,128]{1,0:T(8,128)S(1)}, u32[]{:S(2)}, u32[]{:S(2)}) %collective-permute-start.8) | collective-permute-done | bytes 57376 | tf_op jit(solution)/shard_map/ppermute | solution.py:434
  53.6 0.8 %collective-permute-start.9 = (f32[144,128]{1,0:T(8,128)S(1)}, f32[144,128]{1,0:T(8,128)S(1)}, u32[]{:S(2)}, u32[]{:S(2)}) collective-permute-start(f32[144,128]{1,0:T(8,128)S(1)} %shared_step.6.shared), channel_id=1, source_target_pairs={{0,4},{2,6},{4,0},{6,2},{8,12},{10,14},{12,8},{14,10},{16,20},{18,... | collective-permute-start | bytes 221192 | tf_op jit(solution)/shard_map/ppermute | solution.py:434
  54.5 3.6 %collective-permute-done.9.arrived = f32[144,128]{1,0:T(8,128)S(1)} collective-permute-done((f32[144,128]{1,0:T(8,128)S(1)}, f32[144,128]{1,0:T(8,128)S(1)}, u32[]{:S(2)}, u32[]{:S(2)}) %collective-permute-start.9) | collective-permute-done | bytes 73760 | tf_op jit(solution)/shard_map/ppermute | solution.py:434
  58.8 1.1 %finish_alignment.1 = bf16[2,64,64]{2,1,0:T(8,128)(2,1)} custom-call(bf16[2,64,64]{2,1,0:T(8,128)(2,1)S(1)} %copy-done.1, f32[2,64,64]{2,1,0:T(8,128)S(1)} %get-tuple-element.41.middle_grad, f32[2,64]{1,0:T(2,128)S(1)} %copy-done.7, f32[64,128]{1,0:T(8,128)S(1)} %get-tuple-element.44.normed), custom_call_target="tpu_custom_call" | custom-call | tf_op jit(solution)/shard_map/finish_alignment/pallas_call | solution.py:414
  59.9 3.1 %collective-permute-done.5.arrived = f32[1,8,512]{2,1,0:T(8,128)S(1)} collective-permute-done((f32[1,8,512]{2,1,0:T(8,128)S(1)}, f32[1,8,512]{2,1,0:T(8,128)S(1)}, u32[]{:S(2)}, u32[]{:S(2)}) %collective-permute-start.5) | collective-permute-done | bytes 16416 | tf_op jit(solution)/shard_map/ppermute | solution.py:434
  63.0 0.7 %bias_last.1 = f32[8,8,64]{2,1,0:T(8,128)} custom-call(f32[1,8,512]{2,1,0:T(8,128)S(1)} %get-tuple-element.51.state, f32[1,8,512]{2,1,0:T(8,128)S(1)} %collective-permute-done.5.arrived), custom_call_target="tpu_custom_call" | custom-call | tf_op jit(solution)/shard_map/bias_last/pallas_call | solution.py:414
  63.7 1.1 %unpack.1 = (f32[2,64]{1,0:T(2,128)}, f32[64,256]{1,0:T(8,128)}, f32[64,64]{1,0:T(8,128)}, f32[64,144]{1,0:T(8,128)}, f32[64,64]{1,0:T(8,128)}) custom-call(f32[128,128]{1,0:T(8,128)S(1)} %get-tuple-element.54.joined, f32[80,128]{1,0:T(8,128)S(1)} %get-tuple-element.55.refs_0_, f32[80,128]{1,0:T(8,128)S(1)} %collective-permute-done.10.refs_1_, ...), custom_call_target="tpu_custom_call" | custom-call | tf_op jit(solution)/shard_map/unpack/pallas_call | solution.py:414
  (36 shorter events, 1.1 us)
Async XLA Ops:
  1.3 2.3 %copy-start.4 = (f32[64,64]{1,0:T(8,128)S(1)}, f32[64,64]{1,0:T(8,128)}, u32[]{:S(2)}) copy-start(f32[64,64]{1,0:T(8,128)} %w_out.3) | copy-start | bytes 49156
  1.3 2.3 %copy-start.5 = (bf16[2,64,64]{2,1,0:T(8,128)(2,1)S(1)}, bf16[2,64,64]{2,1,0:T(8,128)(2,1)}, u32[]{:S(2)}) copy-start(bf16[2,64,64]{2,1,0:T(8,128)(2,1)} %refs_3_.2) | copy-start | bytes 49156
  1.3 2.3 %copy-start.7 = (f32[2,64]{1,0:T(2,128)S(1)}, f32[2,64]{1,0:T(2,128)}, u32[]{:S(2)}) copy-start(f32[2,64]{1,0:T(2,128)} %refs_2_.3) | copy-start | bytes 1540
  2.1 1.6 %copy-start.3 = (bf16[8,64,128]{2,1,0:T(8,128)(2,1)S(1)}, bf16[8,64,128]{2,1,0:T(8,128)(2,1)}, u32[]{:S(2)}) copy-start(bf16[8,64,128]{2,1,0:T(8,128)(2,1)} %refs_4_.2) | copy-start | bytes 393220
  2.1 1.5 %copy-start = (f32[64,256]{1,0:T(8,128)S(1)}, f32[64,256]{1,0:T(8,128)}, u32[]{:S(2)}) copy-start(f32[64,256]{1,0:T(8,128)} %refs_3_.3) | copy-start | bytes 196612
  2.1 1.5 %copy-start.1 = (bf16[2,64,64]{2,1,0:T(8,128)(2,1)S(1)}, bf16[2,64,64]{2,1,0:T(8,128)(2,1)}, u32[]{:S(2)}) copy-start(bf16[2,64,64]{2,1,0:T(8,128)(2,1)} %own.1) | copy-start | bytes 49156
  2.1 1.5 %copy-start.8 = (s32[2]{0:T(128)S(1)}, s32[2]{0:T(128)}, u32[]{:S(2)}) copy-start(s32[2]{0:T(128)} %seq_mask.1) | copy-start | bytes 28
  2.2 1.5 %collective-permute-start = (f32[3,64,64]{2,1,0:T(8,128)S(1)}, f32[3,64,64]{2,1,0:T(8,128)S(1)}, u32[]{:S(2)}, u32[]{:S(2)}) collective-permute-start(f32[3,64,64]{2,1,0:T(8,128)S(1)} %pad_maximum_fusion.refs_0_), channel_id=1, source_target_pairs={{1,0},{0,1},{3,2},{2,3},{5,4},{4,5},{7,6},{6,7},{9,8},{8,9},{11,10... | collective-permute-start | bytes 147464 | tf_op jit(solution)/shard_map/ppermute | solution.py:426
  7.4 15.8 %copy-start.2 = (f32[64,144]{1,0:T(8,128)S(1)}, f32[64,144]{1,0:T(8,128)}, u32[]{:S(2)}) copy-start(f32[64,144]{1,0:T(8,128)} %refs_4_.3) | copy-start | bytes 110596
  7.4 15.8 %copy-start.6 = (f32[64,64]{1,0:T(8,128)S(1)}, f32[64,64]{1,0:T(8,128)}, u32[]{:S(2)}) copy-start(f32[64,64]{1,0:T(8,128)} %w_out.2) | copy-start | bytes 49156
  37.7 1.3 %collective-permute-start.1 = (f32[152,128]{1,0:T(8,128)S(1)}, f32[152,128]{1,0:T(8,128)S(1)}, u32[]{:S(2)}, u32[]{:S(2)}) collective-permute-start(f32[152,128]{1,0:T(8,128)S(1)} %get-tuple-element.43), channel_id=1, source_target_pairs={{1,0},{0,1},{3,2},{2,3},{5,4},{4,5},{7,6},{6,7},{9,8},{8,9},{11,10... | collective-permute-start | bytes 233480 | tf_op jit(solution)/shard_map/ppermute | solution.py:426
  39.1 4.6 %collective-permute-start.6 = (f32[88,128]{1,0:T(8,128)S(1)}, f32[88,128]{1,0:T(8,128)S(1)}, u32[]{:S(2)}, u32[]{:S(2)}) collective-permute-start(f32[88,128]{1,0:T(8,128)S(1)} %get-tuple-element.53.shared), channel_id=1, source_target_pairs={{0,8},{2,10},{4,12},{6,14},{8,0},{10,2},{12,4},{14,6},{16,24},{18,... | collective-permute-start | bytes 135176 | tf_op jit(solution)/shard_map/ppermute | solution.py:434
  39.8 9.7 %collective-permute-start.2 = (f32[8,8,512]{2,1,0:T(8,128)S(1)}, f32[8,8,512]{2,1,0:T(8,128)S(1)}, u32[]{:S(2)}, u32[]{:S(2)}) collective-permute-start(f32[8,8,512]{2,1,0:T(8,128)S(1)} %get-tuple-element.46), channel_id=1, source_target_pairs={{0,2},{2,0},{4,6},{6,4},{8,10},{10,8},{12,14},{14,12},{16,18},{18,... | collective-permute-start | bytes 393224 | tf_op jit(solution)/shard_map/ppermute | solution.py:434
  43.7 5.2 %collective-permute-start.7 = (f32[96,128]{1,0:T(8,128)S(1)}, f32[96,128]{1,0:T(8,128)S(1)}, u32[]{:S(2)}, u32[]{:S(2)}) collective-permute-start(f32[96,128]{1,0:T(8,128)S(1)} %shared_step.4.shared), channel_id=1, source_target_pairs={{0,16},{2,18},{4,20},{6,22},{8,24},{10,26},{12,28},{14,30},{16,0},... | collective-permute-start | bytes 147464 | tf_op jit(solution)/shard_map/ppermute | solution.py:434
  48.8 4.8 %collective-permute-start.8 = (f32[112,128]{1,0:T(8,128)S(1)}, f32[112,128]{1,0:T(8,128)S(1)}, u32[]{:S(2)}, u32[]{:S(2)}) collective-permute-start(f32[112,128]{1,0:T(8,128)S(1)} %shared_step.5.shared), channel_id=1, source_target_pairs={{0,2},{2,0},{4,6},{6,4},{8,10},{10,8},{12,14},{14,12},{16,18},{18,... | collective-permute-start | bytes 172040 | tf_op jit(solution)/shard_map/ppermute | solution.py:434
  49.6 4.8 %collective-permute-start.3 = (f32[4,8,512]{2,1,0:T(8,128)S(1)}, f32[4,8,512]{2,1,0:T(8,128)S(1)}, u32[]{:S(2)}, u32[]{:S(2)}) collective-permute-start(f32[4,8,512]{2,1,0:T(8,128)S(1)} %get-tuple-element.48), channel_id=1, source_target_pairs={{0,4},{2,6},{4,0},{6,2},{8,12},{10,14},{12,8},{14,10},{16,20},{18,... | collective-permute-start | bytes 196616 | tf_op jit(solution)/shard_map/ppermute | solution.py:434
  53.6 4.4 %collective-permute-start.9 = (f32[144,128]{1,0:T(8,128)S(1)}, f32[144,128]{1,0:T(8,128)S(1)}, u32[]{:S(2)}, u32[]{:S(2)}) collective-permute-start(f32[144,128]{1,0:T(8,128)S(1)} %shared_step.6.shared), channel_id=1, source_target_pairs={{0,4},{2,6},{4,0},{6,2},{8,12},{10,14},{12,8},{14,10},{16,20},{18,... | collective-permute-start | bytes 221192 | tf_op jit(solution)/shard_map/ppermute | solution.py:434
  54.4 4.0 %collective-permute-start.4 = (f32[2,8,512]{2,1,0:T(8,128)S(1)}, f32[2,8,512]{2,1,0:T(8,128)S(1)}, u32[]{:S(2)}, u32[]{:S(2)}) collective-permute-start(f32[2,8,512]{2,1,0:T(8,128)S(1)} %get-tuple-element.50), channel_id=1, source_target_pairs={{0,8},{2,10},{4,12},{6,14},{8,0},{10,2},{12,4},{14,6},{16,24},{18,... | collective-permute-start | bytes 98312 | tf_op jit(solution)/shard_map/ppermute | solution.py:434
  58.0 5.7 %collective-permute-start.10 = (f32[80,128]{1,0:T(8,128)S(1)}, f32[80,128]{1,0:T(8,128)S(1)}, u32[]{:S(2)}, u32[]{:S(2)}) collective-permute-start(f32[80,128]{1,0:T(8,128)S(1)} %get-tuple-element.55.refs_0_), channel_id=1, source_target_pairs={{1,0},{0,1},{3,2},{2,3},{5,4},{4,5},{7,6},{6,7},{9,8},{8,9},{11,10... | collective-permute-start | bytes 122888 | tf_op jit(solution)/shard_map/ppermute | solution.py:426
  58.4 4.6 %collective-permute-start.5 = (f32[1,8,512]{2,1,0:T(8,128)S(1)}, f32[1,8,512]{2,1,0:T(8,128)S(1)}, u32[]{:S(2)}, u32[]{:S(2)}) collective-permute-start(f32[1,8,512]{2,1,0:T(8,128)S(1)} %get-tuple-element.52), channel_id=1, source_target_pairs={{0,16},{2,18},{4,20},{6,22},{8,24},{10,26},{12,28},{14,30},{16,0},... | collective-permute-start | bytes 49160 | tf_op jit(solution)/shard_map/ppermute | solution.py:434

commit v4 on v3

--- a/solution.py
+++ b/solution.py
@@ -67,13 +67,13 @@
 
 def join_heads(values, mask):
     masked = values * mask
-    return jnp.sum(masked.reshape(H, -1, C), axis=0)
+    return jnp.sum(masked.reshape(H, -1, masked.shape[1]), axis=0)
 
 
 def row_forward(n_res, seq_mask, *refs):
     sent = refs[:n_res]
     own, cotangent, bias, gains, w_row, w_out = refs[n_res : n_res + 6]
-    payload, weights_out, unit_out, own_unit_out, memory_out, query_gate_out, mixture_out, gathered = refs[n_res + 6 :]
+    payload, exponent_out, unit_out, own_unit_out, memory_out, query_gate_out, mixture_out, inverse_out, gathered = refs[n_res + 6 :]
     n_seq, n_rows, _ = own.shape
     me = lax.axis_index("res")
     for away in range(n_res):
@@ -84,10 +84,11 @@
     gain = gains[0:1, :]
     w_all = w_row[...]
     w_query_gate = jnp.concatenate([w_all[:, :C], w_all[:, 3 * C :]], axis=1)
-    residue = gathered[:, n_seq].reshape(n_keys, C)
-    key_bias = MASKED * (jnp.transpose(residue)[0:1, :] - 1.0)
+    present_keys = jnp.concatenate([gathered[i, n_seq, 0:1, :n_rows] for i in range(n_res)], axis=1)
+    key_bias = MASKED * (present_keys - 1.0)
     bias_rows = bias[...].reshape(H * n_rows, n_keys).astype(F32)
     mask = head_mask(n_rows)
+    wide_mask = jnp.concatenate([mask, mask], axis=1)
     for s in range(n_seq):
         unit, _ = normalise(gathered[:, s].reshape(n_keys, C))
         unit_out[s] = unit
@@ -102,9 +103,12 @@
         query_gate_out[s] = jnp.concatenate([query, gate], axis=1)
         scores = dot_t(spread_heads(query, mask), memory[:, :C], EXACT) + bias_rows + key_bias
         exponent = jnp.exp(scores - jnp.max(scores, axis=-1, keepdims=True))
-        weights = exponent / jnp.sum(exponent, axis=-1, keepdims=True)
-        weights_out[s] = weights
-        mixture = join_heads(dot(weights, memory[:, C:]), mask)
+        exponent_out[s] = exponent
+        summed = dot(exponent, jnp.concatenate([memory[:, C:], jnp.ones((n_keys, C), F32)], axis=1))
+        summed = join_heads(summed, wide_mask)
+        inverse = 1.0 / summed[:, C:]
+        inverse_out[s] = inverse
+        mixture = summed[:, :C] * inverse
         mixture_out[s] = mixture
         middle = initial + dot(gate * mixture, w_out[...])
         both = jnp.concatenate([middle, cotangent[s].astype(F32)], axis=1)
@@ -206,7 +210,7 @@
         returned[src, 2] = second[src * share : (src + 1) * share, :]
 
 
-def row_backward(n_res, returned, weights_in, unit_in, memory_in, query_gate_in, mixture_in, own_unit_in,
+def row_backward(n_res, returned, exponent_in, unit_in, memory_in, query_gate_in, mixture_in, inverse_in, own_unit_in,
                  w_row, w_out, state, send, middle_grad, *refs):
     sums_out, shares, bias_t = refs[:n_res], refs[n_res], refs[n_res + 1]
     me = lax.axis_index("res")
@@ -232,20 +236,20 @@
         gate = query_gate_in[s, :, C:]
         mixture = mixture_in[s]
         memory = memory_in[s]
-        weights = weights_in[s]
+        exponent = exponent_in[s]
         grad_gated = dot_t(grad_middle, w_out[...])
         grad_out = grad_out + dot_rows(gate * mixture, grad_middle)
         grad_gate = grad_gated * mixture * gate * (1.0 - gate)
-        grad_heads = spread_heads(grad_gated * gate, mask)
+        grad_heads = spread_heads(grad_gated * gate * inverse_in[s], mask)
         query_heads = spread_heads(query, mask)
         inner = grad_heads * jnp.concatenate([mixture] * H, axis=0)
         left = jnp.concatenate([grad_heads, inner], axis=1)
         right = jnp.concatenate([memory[:, C:], jnp.full((n_keys, C), -1.0, F32)], axis=1)
-        grad_scores = weights * dot_t(left, right)
+        grad_scores = exponent * dot_t(left, right)
         bias_grad = bias_grad + grad_scores
         grad_query = join_heads(dot(grad_scores, memory[:, :C]), mask) * SCALE
         grad_key = dot_rows(grad_scores, query_heads)
-        grad_value = dot_rows(weights, grad_heads)
+        grad_value = dot_rows(exponent, grad_heads)
         grad_memory = jnp.concatenate([grad_key, grad_value], axis=1)
         grad_query_gate = jnp.concatenate([grad_query, grad_gate], axis=1)
         grad_query_gate_weights = grad_query_gate_weights + dot_rows(own_unit_in[s], grad_query_gate)
@@ -338,7 +342,8 @@
     normed[...] = total[rows:]
 
 
-def shared_step(part, shared, arrived, *outs):
+def shared_step(part, n_before, shared, arrived, *refs):
+    outs = refs[n_before:]
     total = shared[:part] + arrived[:part]
     pieces = shared.shape[0] - part
     if len(outs) == 2:
@@ -408,13 +413,14 @@
     col_out_out[...] = col_rest[:, :C]
 
 
-def call(body, outs, *operands, smem=0, scratch=(), name):
+def call(body, outs, *operands, smem=0, unread=0, scratch=(), name):
     vmem = pl.BlockSpec(memory_space=pltpu.VMEM)
     scalar = pl.BlockSpec(memory_space=pltpu.SMEM)
     return pl.pallas_call(
         body,
         out_shape=[jax.ShapeDtypeStruct(shape, kind) for shape, kind in outs],
-        in_specs=[scalar] * smem + [vmem] * (len(operands) - smem),
+        in_specs=[scalar] * smem + [vmem] * (len(operands) - smem - unread)
+        + [pl.BlockSpec(memory_space=pl.ANY)] * unread,
         out_specs=[vmem] * len(outs),
         scratch_shapes=list(scratch),
         compiler_params=pltpu.CompilerParams(vmem_limit_bytes=32 * 1024 * 1024),
@@ -457,9 +463,10 @@
     block = n_rows // seq_count
     group = n_seq * block
     away_range = range(1, res_count)
-    present_keys = jnp.broadcast_to(residue_mask.astype(F32)[None, :, None], (1, n_rows, C))
+    present_keys = jnp.pad(residue_mask.astype(F32), (0, C - n_rows))
+    present_keys = jnp.broadcast_to(present_keys[None, None, :], (1, n_rows, C))
     sent = jnp.concatenate([alignment.astype(F32), present_keys], axis=0)
-    payload, weights, unit, own_unit, memory, query_gate, mixture = call(
+    payload, exponent, unit, own_unit, memory, query_gate, mixture, inverse = call(
         functools.partial(row_forward, res_count),
         [
             ((seq_count, n_seq + 1, block, 2 * C), F32),
@@ -468,6 +475,7 @@
             ((n_seq, n_rows, C), F32),
             ((n_seq, n_keys, 2 * C), F32),
             ((n_seq, n_rows, 2 * C), F32),
+            ((n_seq, n_rows, C), F32),
             ((n_seq, n_rows, C), F32),
         ],
         sequence_mask, sent, *[shift_residues(sent, away, res_count) for away in away_range],
@@ -494,7 +502,7 @@
         [((left, keys_each, wide), F32)] * 2
         + [((n_seq, n_rows, C), F32)]
         + [((part + ROWS + n_rows, LANES), F32)] * res_count,
-        returned, weights, unit, memory, query_gate, mixture, own_unit, row_project, row_output,
+        returned, exponent, unit, memory, query_gate, mixture, inverse, own_unit, row_project, row_output,
         scratch=[
             pltpu.VMEM((res_count, part + ROWS + n_rows, LANES), F32),
             pltpu.VMEM((n_keys, wide), F32),
@@ -518,14 +526,17 @@
                 bias_step, [((left, keys_each, wide), F32)] * 2, state, arrived, name="bias_step"
             )
             arrived = cross(send, at + 1, seq_count, res_count)
+            before = [send]
         else:
             (bias_grad,) = call(bias_last, [((H, keys_each, n_rows), F32)], state, arrived, name="bias_last")
+            before = [bias_grad]
         pieces = ROWS << (at + 1)
         shapes = [(part + pieces, LANES)] if at < steps - 1 else [(part, LANES), (pieces, LANES)]
         shared, *joined = call(
-            functools.partial(shared_step, part),
+            functools.partial(shared_step, part, len(before)),
             [(shape, F32) for shape in shapes],
-            shared, arrived_shared,
+            shared, arrived_shared, *before,
+            unread=len(before),
             name="shared_step",
         )
     (grad_alignment,) = call(

time: 65.1 us -> 64.3 us (0.988)
  waiting for transfers between devices: 20.1 us -> 17.9 us
  starting transfers between devices: 5.38 us -> 6.1 us
  local copies, waits for them, and re-layouts: 0.11 us -> 0.81 us
    ppermute x8, waiting for transfers between devices: 17.9 us -> 15.7 us  [cross(): return lax.ppermute(values, ('seq', 'res'), pairs)]
    ppermute x8, starting transfers between devices: 4.72 us -> 5.51 us  [cross(): return lax.ppermute(values, ('seq', 'res'), pairs)]
    unnamed x18 -> x20, local copies, waits for them, and re-layouts: 0.04 us -> 0.8 us
  transfers between devices with their start and end apart: 11 -> 11, of which waited for: 8 -> 9; matrix products, arithmetic and copies ran while one was open for 0% -> 0% of each run, Pallas kernels for 3% -> 3%
where the time goes in v4:
time: 64.3 us; the launch traced here: 64 us
  blocking collectives  26.1 us (41%)
  waiting for transfers between devices  17.9 us (28%)
  Pallas kernels  10.8 us (17%)
  starting transfers between devices  6.1 us (9%)
  other arithmetic  1.44 us (2%)
  local copies, waits for them, and re-layouts  0.81 us (1%)
  between operations  0.77 us (1%)
    all_to_all x2, blocking collectives, swap_blocks(): return lax.all_to_all(values, 'seq', 0, 0, tiled=True)  26.1 us
    ppermute x8, waiting for transfers between devices, cross(): return lax.ppermute(values, ('seq', 'res'), pairs)  15.7 us
    pallas_call x14, Pallas kernels, call(): pl.pallas_call(body, out_shape=[jax.ShapeDtypeStruct(shape, kind) for sha...  10.8 us
    ppermute x8, starting transfers between devices, cross(): return lax.ppermute(values, ('seq', 'res'), pairs)  5.51 us
    ppermute x3, waiting for transfers between devices, shift_residues(): lax.ppermute(values, 'res', [((i + away) % count, i) for i in range(count)])  2.27 us
  transfers between devices with their start and end apart: 11, of which 9 were waited for; matrix products, arithmetic and copies ran while one was open for 0% of the time, Pallas kernels for 3%

profile of v4, /device:TPU:0, one launch (start us, length us, event | category | flops | bytes accessed | tf_op | source)
XLA Modules:
  0.0 64.0 jit_solution(16060432291074062891)
XLA Ops:
  0.6 0.7 %convert_element_type.7 = f32[64]{0:T(128)S(1)} convert(s32[64]{0:T(128)} %param.18) | non-fusion elementwise | flops 64 | bytes 512 | tf_op jit(solution)/shard_map/convert_element_type | solution.py:466
  1.3 0.8 %convert_element_type.6 = f32[2,64,64]{2,1,0:T(8,128)S(1)} convert(bf16[2,64,64]{2,1,0:T(8,128)(2,1)} %own.1) | non-fusion elementwise | flops 8192 | bytes 49152 | tf_op jit(solution)/shard_map/convert_element_type | solution.py:468
  2.7 0.9 %collective-permute-done.refs_1_ = f32[3,64,64]{2,1,0:T(8,128)S(1)} collective-permute-done((f32[3,64,64]{2,1,0:T(8,128)S(1)}, f32[3,64,64]{2,1,0:T(8,128)S(1)}, u32[]{:S(2)}, u32[]{:S(2)}) %collective-permute-start) | collective-permute-done | bytes 49184 | tf_op jit(solution)/shard_map/ppermute | solution.py:432
  3.6 3.6 %row_forward.1 = (f32[16,3,4,128]{3,2,1,0:T(4,128)S(1)}, f32[2,512,128]{2,1,0:T(8,128)S(1)}, f32[2,128,64]{2,1,0:T(8,128)S(1)}, f32[2,64,64]{2,1,0:T(8,128)S(1)}...) custom-call(s32[2]{0:T(128)S(1)} %copy-done.9, ...), custom_call_target="tpu_custom_call" | custom-call | tf_op jit(solution)/shard_map/row_forward/pallas_call | solution.py:419
  7.3 15.8 %all_to_all.10.arrived = f32[16,3,4,128]{3,2,1,0:T(4,128)S(1)} all-to-all(f32[16,3,4,128]{3,2,1,0:T(4,128)S(1)} %get-tuple-element.35), channel_id=1, replica_groups=mesh['seq'=16,'res'=2] {'seq'}, dimensions={0} | all-to-all | bytes 196608 | tf_op jit(solution)/shard_map/all_to_all | solution.py:444
  23.1 1.7 %column_step.1 = f32[16,3,4,128]{3,2,1,0:T(4,128)S(1)} custom-call(f32[16,3,4,128]{3,2,1,0:T(4,128)S(1)} %all_to_all.10.arrived, f32[2,64]{1,0:T(2,128)S(1)} %copy-done.8, f32[64,144]{1,0:T(8,128)S(1)} %copy-done.2, f32[64,64]{1,0:T(8,128)S(1)} %copy-done.7), custom_call_target="tpu_custom_call" | custom-call | tf_op jit(solution)/shard_map/column_step/pallas_call | solution.py:419
  24.8 10.3 %all_to_all.11.returned = f32[16,3,4,128]{3,2,1,0:T(4,128)S(1)} all-to-all(f32[16,3,4,128]{3,2,1,0:T(4,128)S(1)} %column_step.1), channel_id=1, replica_groups=mesh['seq'=16,'res'=2] {'seq'}, dimensions={0} | all-to-all | bytes 196608 | tf_op jit(solution)/shard_map/all_to_all | solution.py:444
  35.0 2.6 %row_backward.1 = (f32[8,8,512]{2,1,0:T(8,128)S(1)}, f32[8,8,512]{2,1,0:T(8,128)S(1)}, f32[2,64,64]{2,1,0:T(8,128)S(1)}, f32[152,128]{1,0:T(8,128)S(1)}, f32[152,128]{1,0:T(8,128)S(1)}) custom-call(f32[16,3,4,128]{3,2,1,0:T(4,128)S(1)} %all_to_all.11.returned, f32[2,512,128]{2,1,0:T(8,128)S(1)} %get-tuple-element.36.exponent_in, ...), custom_call_target="tpu_custom_call" | custom-call | tf_op jit(solution)/shard_map/row_backward/pallas_call | solution.py:419
  37.6 1.0 %collective-permute-start.2 = (f32[8,8,512]{2,1,0:T(8,128)S(1)}, f32[8,8,512]{2,1,0:T(8,128)S(1)}, u32[]{:S(2)}, u32[]{:S(2)}) collective-permute-start(f32[8,8,512]{2,1,0:T(8,128)S(1)} %get-tuple-element.48), channel_id=1, source_target_pairs={{0,2},{2,0},{4,6},{6,4},{8,10},{10,8},{12,14},{14,12},{16,18},{18,... | collective-permute-start | bytes 393224 | tf_op jit(solution)/shard_map/ppermute | solution.py:440
  38.6 1.3 %collective-permute-done.1.refs_1_ = f32[152,128]{1,0:T(8,128)S(1)} collective-permute-done((f32[152,128]{1,0:T(8,128)S(1)}, f32[152,128]{1,0:T(8,128)S(1)}, u32[]{:S(2)}, u32[]{:S(2)}) %collective-permute-start.1) | collective-permute-done | bytes 77856 | tf_op jit(solution)/shard_map/ppermute | solution.py:432
  40.3 2.4 %collective-permute-done.2.arrived = f32[8,8,512]{2,1,0:T(8,128)S(1)} collective-permute-done((f32[8,8,512]{2,1,0:T(8,128)S(1)}, f32[8,8,512]{2,1,0:T(8,128)S(1)}, u32[]{:S(2)}, u32[]{:S(2)}) %collective-permute-start.2) | collective-permute-done | bytes 131104 | tf_op jit(solution)/shard_map/ppermute | solution.py:440
  42.7 0.7 %collective-permute-start.3 = (f32[4,8,512]{2,1,0:T(8,128)S(1)}, f32[4,8,512]{2,1,0:T(8,128)S(1)}, u32[]{:S(2)}, u32[]{:S(2)}) collective-permute-start(f32[4,8,512]{2,1,0:T(8,128)S(1)} %get-tuple-element.50.refs_0_), channel_id=1, source_target_pairs={{0,4},{2,6},{4,0},{6,2},{8,12},{10,14},{12,8},{14,10},{16,20},{18,... | collective-permute-start | bytes 196616 | tf_op jit(solution)/shard_map/ppermute | solution.py:440
  43.4 1.0 %collective-permute-done.6.arrived = f32[88,128]{1,0:T(8,128)S(1)} collective-permute-done((f32[88,128]{1,0:T(8,128)S(1)}, f32[88,128]{1,0:T(8,128)S(1)}, u32[]{:S(2)}, u32[]{:S(2)}) %collective-permute-start.6) | collective-permute-done | bytes 45088 | tf_op jit(solution)/shard_map/ppermute | solution.py:440
  44.9 2.1 %collective-permute-done.3.arrived = f32[4,8,512]{2,1,0:T(8,128)S(1)} collective-permute-done((f32[4,8,512]{2,1,0:T(8,128)S(1)}, f32[4,8,512]{2,1,0:T(8,128)S(1)}, u32[]{:S(2)}, u32[]{:S(2)}) %collective-permute-start.3) | collective-permute-done | bytes 65568 | tf_op jit(solution)/shard_map/ppermute | solution.py:440
  47.0 2.4 %collective-permute-done.7.arrived = f32[96,128]{1,0:T(8,128)S(1)} collective-permute-done((f32[96,128]{1,0:T(8,128)S(1)}, f32[96,128]{1,0:T(8,128)S(1)}, u32[]{:S(2)}, u32[]{:S(2)}) %collective-permute-start.7) | collective-permute-done | bytes 49184 | tf_op jit(solution)/shard_map/ppermute | solution.py:440
  49.4 1.5 %collective-permute-start.8 = (f32[112,128]{1,0:T(8,128)S(1)}, f32[112,128]{1,0:T(8,128)S(1)}, u32[]{:S(2)}, u32[]{:S(2)}) collective-permute-start(f32[112,128]{1,0:T(8,128)S(1)} %shared_step.5.shared), channel_id=1, source_target_pairs={{0,2},{2,0},{4,6},{6,4},{8,10},{10,8},{12,14},{14,12},{16,18},{18,... | collective-permute-start | bytes 172040 | tf_op jit(solution)/shard_map/ppermute | solution.py:440
  50.9 3.9 %collective-permute-done.4.arrived = f32[2,8,512]{2,1,0:T(8,128)S(1)} collective-permute-done((f32[2,8,512]{2,1,0:T(8,128)S(1)}, f32[2,8,512]{2,1,0:T(8,128)S(1)}, u32[]{:S(2)}, u32[]{:S(2)}) %collective-permute-start.4) | collective-permute-done | bytes 32800 | tf_op jit(solution)/shard_map/ppermute | solution.py:440
  54.8 0.7 %collective-permute-start.9 = (f32[144,128]{1,0:T(8,128)S(1)}, f32[144,128]{1,0:T(8,128)S(1)}, u32[]{:S(2)}, u32[]{:S(2)}) collective-permute-start(f32[144,128]{1,0:T(8,128)S(1)} %shared_step.6.shared), channel_id=1, source_target_pairs={{0,4},{2,6},{4,0},{6,2},{8,12},{10,14},{12,8},{14,10},{16,20},{18,... | collective-permute-start | bytes 221192 | tf_op jit(solution)/shard_map/ppermute | solution.py:440
  55.5 0.6 collective-permute-start.5
  56.1 4.0 %collective-permute-done.5.arrived = f32[1,8,512]{2,1,0:T(8,128)S(1)} collective-permute-done((f32[1,8,512]{2,1,0:T(8,128)S(1)}, f32[1,8,512]{2,1,0:T(8,128)S(1)}, u32[]{:S(2)}, u32[]{:S(2)}) %collective-permute-start.5) | collective-permute-done | bytes 16416 | tf_op jit(solution)/shard_map/ppermute | solution.py:440
  60.1 0.7 %bias_last.1.refs_0_ = f32[8,8,64]{2,1,0:T(8,128)} custom-call(f32[1,8,512]{2,1,0:T(8,128)S(1)} %get-tuple-element.53.state, f32[1,8,512]{2,1,0:T(8,128)S(1)} %collective-permute-done.5.arrived), custom_call_target="tpu_custom_call" | custom-call | tf_op jit(solution)/shard_map/bias_last/pallas_call | solution.py:419
  60.8 0.8 %copy-done.5 = f32[8,8,64]{2,1,0:T(8,128)S(1)} copy-done((f32[8,8,64]{2,1,0:T(8,128)S(1)}, f32[8,8,64]{2,1,0:T(8,128)}, u32[]{:S(2)}) %copy-start.5) | copy-done | bytes 16408
  61.7 1.1 %finish_alignment.1 = bf16[2,64,64]{2,1,0:T(8,128)(2,1)} custom-call(bf16[2,64,64]{2,1,0:T(8,128)(2,1)S(1)} %copy-done.1, f32[2,64,64]{2,1,0:T(8,128)S(1)} %get-tuple-element.43.middle_grad, f32[2,64]{1,0:T(2,128)S(1)} %copy-done.8, f32[64,128]{1,0:T(8,128)S(1)} %get-tuple-element.46.normed), custom_call_target="tpu_custom_call" | custom-call | tf_op jit(solution)/shard_map/finish_alignment/pallas_call | solution.py:419
  62.9 1.1 %unpack.1 = (f32[2,64]{1,0:T(2,128)}, f32[64,256]{1,0:T(8,128)}, f32[64,64]{1,0:T(8,128)}, f32[64,144]{1,0:T(8,128)}, f32[64,64]{1,0:T(8,128)}) custom-call(f32[128,128]{1,0:T(8,128)S(1)} %get-tuple-element.56.joined, f32[80,128]{1,0:T(8,128)S(1)} %get-tuple-element.57.refs_0_, f32[80,128]{1,0:T(8,128)S(1)} %collective-permute-done.10.refs_1_, ...), custom_call_target="tpu_custom_call" | custom-call | tf_op jit(solution)/shard_map/unpack/pallas_call | solution.py:419
  (38 shorter events, 1.7 us)
Async XLA Ops:
  1.3 2.3 %copy-start.4 = (f32[64,64]{1,0:T(8,128)S(1)}, f32[64,64]{1,0:T(8,128)}, u32[]{:S(2)}) copy-start(f32[64,64]{1,0:T(8,128)} %w_out.3) | copy-start | bytes 49156
  1.3 2.3 %copy-start.6 = (bf16[2,64,64]{2,1,0:T(8,128)(2,1)S(1)}, bf16[2,64,64]{2,1,0:T(8,128)(2,1)}, u32[]{:S(2)}) copy-start(bf16[2,64,64]{2,1,0:T(8,128)(2,1)} %refs_3_.2) | copy-start | bytes 49156
  1.3 2.3 %copy-start.8 = (f32[2,64]{1,0:T(2,128)S(1)}, f32[2,64]{1,0:T(2,128)}, u32[]{:S(2)}) copy-start(f32[2,64]{1,0:T(2,128)} %refs_2_.3) | copy-start | bytes 1540
  2.1 1.5 %copy-start.3 = (bf16[8,64,128]{2,1,0:T(8,128)(2,1)S(1)}, bf16[8,64,128]{2,1,0:T(8,128)(2,1)}, u32[]{:S(2)}) copy-start(bf16[8,64,128]{2,1,0:T(8,128)(2,1)} %refs_4_.2) | copy-start | bytes 393220
  2.1 1.5 %copy-start = (f32[64,256]{1,0:T(8,128)S(1)}, f32[64,256]{1,0:T(8,128)}, u32[]{:S(2)}) copy-start(f32[64,256]{1,0:T(8,128)} %refs_3_.3) | copy-start | bytes 196612
  2.1 1.5 %copy-start.1 = (bf16[2,64,64]{2,1,0:T(8,128)(2,1)S(1)}, bf16[2,64,64]{2,1,0:T(8,128)(2,1)}, u32[]{:S(2)}) copy-start(bf16[2,64,64]{2,1,0:T(8,128)(2,1)} %own.1) | copy-start | bytes 49156
  2.1 1.5 %copy-start.9 = (s32[2]{0:T(128)S(1)}, s32[2]{0:T(128)}, u32[]{:S(2)}) copy-start(s32[2]{0:T(128)} %seq_mask.1) | copy-start | bytes 28
  2.1 1.5 %collective-permute-start = (f32[3,64,64]{2,1,0:T(8,128)S(1)}, f32[3,64,64]{2,1,0:T(8,128)S(1)}, u32[]{:S(2)}, u32[]{:S(2)}) collective-permute-start(f32[3,64,64]{2,1,0:T(8,128)S(1)} %pad_maximum_fusion.refs_0_), channel_id=1, source_target_pairs={{1,0},{0,1},{3,2},{2,3},{5,4},{4,5},{7,6},{6,7},{9,8},{8,9},{11,10... | collective-permute-start | bytes 147464 | tf_op jit(solution)/shard_map/ppermute | solution.py:432
  7.3 15.8 %copy-start.2 = (f32[64,144]{1,0:T(8,128)S(1)}, f32[64,144]{1,0:T(8,128)}, u32[]{:S(2)}) copy-start(f32[64,144]{1,0:T(8,128)} %refs_4_.3) | copy-start | bytes 110596
  7.3 15.8 %copy-start.7 = (f32[64,64]{1,0:T(8,128)S(1)}, f32[64,64]{1,0:T(8,128)}, u32[]{:S(2)}) copy-start(f32[64,64]{1,0:T(8,128)} %w_out.2) | copy-start | bytes 49156
  37.6 5.0 %collective-permute-start.2 = (f32[8,8,512]{2,1,0:T(8,128)S(1)}, f32[8,8,512]{2,1,0:T(8,128)S(1)}, u32[]{:S(2)}, u32[]{:S(2)}) collective-permute-start(f32[8,8,512]{2,1,0:T(8,128)S(1)} %get-tuple-element.48), channel_id=1, source_target_pairs={{0,2},{2,0},{4,6},{6,4},{8,10},{10,8},{12,14},{14,12},{16,18},{18,... | collective-permute-start | bytes 393224 | tf_op jit(solution)/shard_map/ppermute | solution.py:440
  38.6 1.3 %collective-permute-start.1 = (f32[152,128]{1,0:T(8,128)S(1)}, f32[152,128]{1,0:T(8,128)S(1)}, u32[]{:S(2)}, u32[]{:S(2)}) collective-permute-start(f32[152,128]{1,0:T(8,128)S(1)} %get-tuple-element.45), channel_id=1, source_target_pairs={{1,0},{0,1},{3,2},{2,3},{5,4},{4,5},{7,6},{6,7},{9,8},{8,9},{11,10... | collective-permute-start | bytes 233480 | tf_op jit(solution)/shard_map/ppermute | solution.py:432
  39.9 4.4 %collective-permute-start.6 = (f32[88,128]{1,0:T(8,128)S(1)}, f32[88,128]{1,0:T(8,128)S(1)}, u32[]{:S(2)}, u32[]{:S(2)}) collective-permute-start(f32[88,128]{1,0:T(8,128)S(1)} %get-tuple-element.55.shared), channel_id=1, source_target_pairs={{0,8},{2,10},{4,12},{6,14},{8,0},{10,2},{12,4},{14,6},{16,24},{18,... | collective-permute-start | bytes 135176 | tf_op jit(solution)/shard_map/ppermute | solution.py:440
  42.7 4.3 %collective-permute-start.3 = (f32[4,8,512]{2,1,0:T(8,128)S(1)}, f32[4,8,512]{2,1,0:T(8,128)S(1)}, u32[]{:S(2)}, u32[]{:S(2)}) collective-permute-start(f32[4,8,512]{2,1,0:T(8,128)S(1)} %get-tuple-element.50.refs_0_), channel_id=1, source_target_pairs={{0,4},{2,6},{4,0},{6,2},{8,12},{10,14},{12,8},{14,10},{16,20},{18,... | collective-permute-start | bytes 196616 | tf_op jit(solution)/shard_map/ppermute | solution.py:440
  44.4 5.0 %collective-permute-start.7 = (f32[96,128]{1,0:T(8,128)S(1)}, f32[96,128]{1,0:T(8,128)S(1)}, u32[]{:S(2)}, u32[]{:S(2)}) collective-permute-start(f32[96,128]{1,0:T(8,128)S(1)} %shared_step.4.shared), channel_id=1, source_target_pairs={{0,16},{2,18},{4,20},{6,22},{8,24},{10,26},{12,28},{14,30},{16,0},... | collective-permute-start | bytes 147464 | tf_op jit(solution)/shard_map/ppermute | solution.py:440
  49.4 5.4 %collective-permute-start.8 = (f32[112,128]{1,0:T(8,128)S(1)}, f32[112,128]{1,0:T(8,128)S(1)}, u32[]{:S(2)}, u32[]{:S(2)}) collective-permute-start(f32[112,128]{1,0:T(8,128)S(1)} %shared_step.5.shared), channel_id=1, source_target_pairs={{0,2},{2,0},{4,6},{6,4},{8,10},{10,8},{12,14},{14,12},{16,18},{18,... | collective-permute-start | bytes 172040 | tf_op jit(solution)/shard_map/ppermute | solution.py:440
  50.8 3.9 %collective-permute-start.4 = (f32[2,8,512]{2,1,0:T(8,128)S(1)}, f32[2,8,512]{2,1,0:T(8,128)S(1)}, u32[]{:S(2)}, u32[]{:S(2)}) collective-permute-start(f32[2,8,512]{2,1,0:T(8,128)S(1)} %get-tuple-element.52.refs_0_), channel_id=1, source_target_pairs={{0,8},{2,10},{4,12},{6,14},{8,0},{10,2},{12,4},{14,6},{16,24},{18,... | collective-permute-start | bytes 98312 | tf_op jit(solution)/shard_map/ppermute | solution.py:440
  54.8 6.1 %collective-permute-start.9 = (f32[144,128]{1,0:T(8,128)S(1)}, f32[144,128]{1,0:T(8,128)S(1)}, u32[]{:S(2)}, u32[]{:S(2)}) collective-permute-start(f32[144,128]{1,0:T(8,128)S(1)} %shared_step.6.shared), channel_id=1, source_target_pairs={{0,4},{2,6},{4,0},{6,2},{8,12},{10,14},{12,8},{14,10},{16,20},{18,... | collective-permute-start | bytes 221192 | tf_op jit(solution)/shard_map/ppermute | solution.py:440
  55.5 4.6 %collective-permute-start.5 = (f32[1,8,512]{2,1,0:T(8,128)S(1)}, f32[1,8,512]{2,1,0:T(8,128)S(1)}, u32[]{:S(2)}, u32[]{:S(2)}) collective-permute-start(f32[1,8,512]{2,1,0:T(8,128)S(1)} %get-tuple-element.54.refs_0_), channel_id=1, source_target_pairs={{0,16},{2,18},{4,20},{6,22},{8,24},{10,26},{12,28},{14,30},{16,0},... | collective-permute-start | bytes 49160 | tf_op jit(solution)/shard_map/ppermute | solution.py:440
  60.8 0.8 %copy-start.5 = (f32[8,8,64]{2,1,0:T(8,128)S(1)}, f32[8,8,64]{2,1,0:T(8,128)}, u32[]{:S(2)}) copy-start(f32[8,8,64]{2,1,0:T(8,128)} %bias_last.1.refs_0_) | copy-start | bytes 49156
  61.6 1.3 %collective-permute-start.10 = (f32[80,128]{1,0:T(8,128)S(1)}, f32[80,128]{1,0:T(8,128)S(1)}, u32[]{:S(2)}, u32[]{:S(2)}) collective-permute-start(f32[80,128]{1,0:T(8,128)S(1)} %get-tuple-element.57.refs_0_), channel_id=1, source_target_pairs={{1,0},{0,1},{3,2},{2,3},{5,4},{4,5},{7,6},{6,7},{9,8},{8,9},{11,10... | collective-permute-start | bytes 122888 | tf_op jit(solution)/shard_map/ppermute | solution.py:432

commit v5 on v4

--- a/solution.py
+++ b/solution.py
@@ -89,31 +89,38 @@
     bias_rows = bias[...].reshape(H * n_rows, n_keys).astype(F32)
     mask = head_mask(n_rows)
     wide_mask = jnp.concatenate([mask, mask], axis=1)
+    units = jnp.concatenate([gathered[:, s].reshape(n_keys, C) for s in range(n_seq)], axis=0)
+    units, _ = normalise(units)
+    memories = dot(units * gain, w_all[:, C : 3 * C], precision=EXACT)
+    initial = own[...].reshape(n_seq * n_rows, C).astype(F32)
+    own_units, _ = normalise(initial)
+    projected = dot(own_units * gain, w_query_gate, precision=EXACT)
+    queries = projected[:, :C] * SCALE
+    gates = jax.nn.sigmoid(projected[:, C:])
+    unit_out[...] = units.reshape(n_seq, n_keys, C)
+    memory_out[...] = memories.reshape(n_seq, n_keys, 2 * C)
+    own_unit_out[...] = own_units.reshape(n_seq, n_rows, C)
+    query_gate_out[...] = jnp.concatenate([queries, gates], axis=1).reshape(n_seq, n_rows, 2 * C)
+    sums = []
     for s in range(n_seq):
-        unit, _ = normalise(gathered[:, s].reshape(n_keys, C))
-        unit_out[s] = unit
-        memory = dot(unit * gain, w_all[:, C : 3 * C], precision=EXACT)
-        memory_out[s] = memory
-        initial = own[s].astype(F32)
-        own_unit, _ = normalise(initial)
-        own_unit_out[s] = own_unit
-        projected = dot(own_unit * gain, w_query_gate, precision=EXACT)
-        query = projected[:, :C] * SCALE
-        gate = jax.nn.sigmoid(projected[:, C:])
-        query_gate_out[s] = jnp.concatenate([query, gate], axis=1)
+        memory = memories[s * n_keys : (s + 1) * n_keys]
+        query = queries[s * n_rows : (s + 1) * n_rows]
         scores = dot_t(spread_heads(query, mask), memory[:, :C], EXACT) + bias_rows + key_bias
         exponent = jnp.exp(scores - jnp.max(scores, axis=-1, keepdims=True))
         exponent_out[s] = exponent
         summed = dot(exponent, jnp.concatenate([memory[:, C:], jnp.ones((n_keys, C), F32)], axis=1))
-        summed = join_heads(summed, wide_mask)
-        inverse = 1.0 / summed[:, C:]
-        inverse_out[s] = inverse
-        mixture = summed[:, :C] * inverse
-        mixture_out[s] = mixture
-        middle = initial + dot(gate * mixture, w_out[...])
-        both = jnp.concatenate([middle, cotangent[s].astype(F32)], axis=1)
+        sums.append(join_heads(summed, wide_mask))
+    summed = jnp.concatenate(sums, axis=0)
+    inverse = 1.0 / summed[:, C:]
+    mixture = summed[:, :C] * inverse
+    inverse_out[...] = inverse.reshape(n_seq, n_rows, C)
+    mixture_out[...] = mixture.reshape(n_seq, n_rows, C)
+    middle = initial + dot(gates * mixture, w_out[...])
+    both = jnp.concatenate([middle, cotangent[...].reshape(n_seq * n_rows, C).astype(F32)], axis=1)
+    for s in range(n_seq):
         for b in range(n_blocks):
-            payload[b, s] = both[b * block : (b + 1) * block, :]
+            row = s * n_rows + b * block
+            payload[b, s] = both[row : row + block, :]
     lane = lax.broadcasted_iota(jnp.int32, (block, 2 * C), 1) // (2 * C // n_seq)
     present = jnp.zeros((block, 2 * C), F32)
     for s in range(n_seq):
@@ -224,38 +231,40 @@
     for b in range(n_blocks):
         for s in range(n_seq):
             middle_grad[s, b * block : (b + 1) * block, :] = returned[b, 0, :, s * C : (s + 1) * C]
-    grad_out = jnp.zeros((C, C), F32)
-    grad_query_gate_weights = jnp.zeros((C, 2 * C), F32)
-    grad_memory_weights = jnp.zeros((C, 2 * C), F32)
+    grad_middle = middle_grad[...].reshape(n_seq * n_rows, C)
+    queries_gates = query_gate_in[...].reshape(n_seq * n_rows, 2 * C)
+    gates = queries_gates[:, C:]
+    mixtures = mixture_in[...].reshape(n_seq * n_rows, C)
+    grad_gated = dot_t(grad_middle, w_out[...])
+    grad_out = dot_rows(gates * mixtures, grad_middle)
+    grad_gates = grad_gated * mixtures * gates * (1.0 - gates)
+    grad_mixtures = grad_gated * gates * inverse_in[...].reshape(n_seq * n_rows, C)
+    inners = grad_mixtures * mixtures
     bias_grad = jnp.zeros((H * n_rows, n_keys), F32)
-    from_own = []
-    from_memory = []
+    grad_queries = []
+    grad_memories = []
     for s in range(n_seq):
-        grad_middle = middle_grad[s]
-        query = query_gate_in[s, :, :C]
-        gate = query_gate_in[s, :, C:]
-        mixture = mixture_in[s]
+        rows = slice(s * n_rows, (s + 1) * n_rows)
         memory = memory_in[s]
         exponent = exponent_in[s]
-        grad_gated = dot_t(grad_middle, w_out[...])
-        grad_out = grad_out + dot_rows(gate * mixture, grad_middle)
-        grad_gate = grad_gated * mixture * gate * (1.0 - gate)
-        grad_heads = spread_heads(grad_gated * gate * inverse_in[s], mask)
-        query_heads = spread_heads(query, mask)
-        inner = grad_heads * jnp.concatenate([mixture] * H, axis=0)
-        left = jnp.concatenate([grad_heads, inner], axis=1)
+        grad_heads = spread_heads(grad_mixtures[rows], mask)
+        query_heads = spread_heads(queries_gates[rows, :C], mask)
+        left = jnp.concatenate([grad_heads, spread_heads(inners[rows], mask)], axis=1)
         right = jnp.concatenate([memory[:, C:], jnp.full((n_keys, C), -1.0, F32)], axis=1)
         grad_scores = exponent * dot_t(left, right)
         bias_grad = bias_grad + grad_scores
-        grad_query = join_heads(dot(grad_scores, memory[:, :C]), mask) * SCALE
+        grad_queries.append(join_heads(dot(grad_scores, memory[:, :C]), mask) * SCALE)
         grad_key = dot_rows(grad_scores, query_heads)
         grad_value = dot_rows(exponent, grad_heads)
-        grad_memory = jnp.concatenate([grad_key, grad_value], axis=1)
-        grad_query_gate = jnp.concatenate([grad_query, grad_gate], axis=1)
-        grad_query_gate_weights = grad_query_gate_weights + dot_rows(own_unit_in[s], grad_query_gate)
-        grad_memory_weights = grad_memory_weights + dot_rows(unit_in[s], grad_memory)
-        from_memory.append(dot_t(grad_memory, w_memory))
-        from_own.append(dot_t(grad_query_gate, w_query_gate))
+        grad_memories.append(jnp.concatenate([grad_key, grad_value], axis=1))
+    grad_query_gate = jnp.concatenate([jnp.concatenate(grad_queries, axis=0), grad_gates], axis=1)
+    grad_memory = jnp.concatenate(grad_memories, axis=0)
+    grad_query_gate_weights = dot_rows(own_unit_in[...].reshape(n_seq * n_rows, C), grad_query_gate)
+    grad_memory_weights = dot_rows(unit_in[...].reshape(n_seq * n_keys, C), grad_memory)
+    from_memory = dot_t(grad_memory, w_memory)
+    from_own = dot_t(grad_query_gate, w_query_gate)
+    from_memory = [from_memory[s * n_keys : (s + 1) * n_keys] for s in range(n_seq)]
+    from_own = [from_own[s * n_rows : (s + 1) * n_rows] for s in range(n_seq)]
     bias_t[...] = jnp.transpose(bias_grad)
     split_blocks(bias_t, state, send)
 
@@ -510,33 +519,34 @@
         name="row_backward",
     )
     sums = sums[:1] + [shift_residues(sums[away], -away, res_count) for away in away_range]
-    arrived = cross(send, 0, seq_count, res_count)
+    steps = seq_count.bit_length() - 1
+    arrivals = []
+    before = []
+    for at in range(steps):
+        arrivals.append(cross(send, at, seq_count, res_count))
+        if at < steps - 1:
+            left //= 2
+            state, send = call(
+                bias_step, [((left, keys_each, wide), F32)] * 2, state, arrivals[at], name="bias_step"
+            )
+            before.append([send] if at == 0 else [])
+    before = [before[0]] + [[arrived] for arrived in arrivals[2:]] + [[]]
+    (bias_grad,) = call(bias_last, [((H, keys_each, n_rows), F32)], state, arrivals[-1], name="bias_last")
     shared, normed = call(
         add_shares,
         [((part + ROWS, LANES), F32), ((n_rows, LANES), F32)],
         *sums,
         name="add_shares",
     )
-    steps = seq_count.bit_length() - 1
     for at in range(steps):
         arrived_shared = cross(shared, at, seq_count, res_count, True)
-        if at < steps - 1:
-            left //= 2
-            state, send = call(
-                bias_step, [((left, keys_each, wide), F32)] * 2, state, arrived, name="bias_step"
-            )
-            arrived = cross(send, at + 1, seq_count, res_count)
-            before = [send]
-        else:
-            (bias_grad,) = call(bias_last, [((H, keys_each, n_rows), F32)], state, arrived, name="bias_last")
-            before = [bias_grad]
         pieces = ROWS << (at + 1)
         shapes = [(part + pieces, LANES)] if at < steps - 1 else [(part, LANES), (pieces, LANES)]
         shared, *joined = call(
-            functools.partial(shared_step, part, len(before)),
+            functools.partial(shared_step, part, len(before[at])),
             [(shape, F32) for shape in shapes],
-            shared, arrived_shared, *before,
-            unread=len(before),
+            shared, arrived_shared, *before[at],
+            unread=len(before[at]),
             name="shared_step",
         )
     (grad_alignment,) = call(

time: 64.3 us -> 66 us (1.026)
  waiting for transfers between devices: 17.9 us -> 19.7 us
  starting transfers between devices: 6.1 us -> 7.66 us
  Pallas kernels: 10.8 us -> 9.95 us
  local copies, waits for them, and re-layouts: 0.81 us -> 0.05 us
    ppermute x8, waiting for transfers between devices: 15.7 us -> 18.7 us  [cross(): return lax.ppermute(values, ('seq', 'res'), pairs)]
    ppermute x8, starting transfers between devices: 5.51 us -> 7.07 us  [cross(): return lax.ppermute(values, ('seq', 'res'), pairs)]
    ppermute x3, waiting for transfers between devices: 2.27 us -> 0.95 us  [shift_residues(): lax.ppermute(values, 'res', [((i + away) % count, i) for i in range(count)])]
    pallas_call x14, Pallas kernels: 10.8 us -> 9.95 us  [call(): pl.pallas_call(body, out_shape=[jax.ShapeDtypeStruct(shape, kind) for sha...]
    unnamed x20 -> x18, local copies, waits for them, and re-layouts: 0.8 us -> 0.05 us
  transfers between devices with their start and end apart: 11 -> 11, of which waited for: 9 -> 6; matrix products, arithmetic and copies ran while one was open for 0% -> 0% of each run, Pallas kernels for 3% -> 3%
where the time goes in v5:
time: 66 us; the launch traced here: 65.6 us
  blocking collectives  26.1 us (40%)
  waiting for transfers between devices  19.7 us (30%)
  Pallas kernels  9.95 us (15%)
  starting transfers between devices  7.66 us (12%)
  other arithmetic  1.44 us (2%)
  between operations  0.76 us (1%)
    all_to_all x2, blocking collectives, swap_blocks(): return lax.all_to_all(values, 'seq', 0, 0, tiled=True)  26.1 us
    ppermute x8, waiting for transfers between devices, cross(): return lax.ppermute(values, ('seq', 'res'), pairs)  18.7 us
    pallas_call x14, Pallas kernels, call(): pl.pallas_call(body, out_shape=[jax.ShapeDtypeStruct(shape, kind) for sha...  9.95 us
    ppermute x8, starting transfers between devices, cross(): return lax.ppermute(values, ('seq', 'res'), pairs)  7.07 us
  transfers between devices with their start and end apart: 11, of which 6 were waited for; matrix products, arithmetic and copies ran while one was open for 0% of the time, Pallas kernels for 3%

profile of v5, /device:TPU:0, one launch (start us, length us, event | category | flops | bytes accessed | tf_op | source)
XLA Modules:
  0.0 65.6 jit_solution(15276859674932169872)
XLA Ops:
  0.6 0.7 %convert_element_type.7 = f32[64]{0:T(128)S(1)} convert(s32[64]{0:T(128)} %param.18) | non-fusion elementwise | flops 64 | bytes 512 | tf_op jit(solution)/shard_map/convert_element_type | solution.py:475
  1.3 0.8 %convert_element_type.6 = f32[2,64,64]{2,1,0:T(8,128)S(1)} convert(bf16[2,64,64]{2,1,0:T(8,128)(2,1)} %own.1) | non-fusion elementwise | flops 8192 | bytes 49152 | tf_op jit(solution)/shard_map/convert_element_type | solution.py:477
  2.1 0.5 collective-permute-start
  2.7 0.9 %collective-permute-done.refs_1_ = f32[3,64,64]{2,1,0:T(8,128)S(1)} collective-permute-done((f32[3,64,64]{2,1,0:T(8,128)S(1)}, f32[3,64,64]{2,1,0:T(8,128)S(1)}, u32[]{:S(2)}, u32[]{:S(2)}) %collective-permute-start) | collective-permute-done | bytes 49184 | tf_op jit(solution)/shard_map/ppermute | solution.py:441
  3.6 3.1 %row_forward.1 = (f32[16,3,4,128]{3,2,1,0:T(4,128)S(1)}, f32[2,512,128]{2,1,0:T(8,128)S(1)}, f32[2,128,64]{2,1,0:T(8,128)S(1)}, f32[2,64,64]{2,1,0:T(8,128)S(1)}...) custom-call(s32[2]{0:T(128)S(1)} %copy-done.8, ...), custom_call_target="tpu_custom_call" | custom-call | tf_op jit(solution)/shard_map/row_forward/pallas_call | solution.py:428
  6.8 15.8 %all_to_all.10.arrived = f32[16,3,4,128]{3,2,1,0:T(4,128)S(1)} all-to-all(f32[16,3,4,128]{3,2,1,0:T(4,128)S(1)} %get-tuple-element.35), channel_id=1, replica_groups=mesh['seq'=16,'res'=2] {'seq'}, dimensions={0} | all-to-all | bytes 196608 | tf_op jit(solution)/shard_map/all_to_all | solution.py:453
  22.6 1.7 %column_step.1 = f32[16,3,4,128]{3,2,1,0:T(4,128)S(1)} custom-call(f32[16,3,4,128]{3,2,1,0:T(4,128)S(1)} %all_to_all.10.arrived, f32[2,64]{1,0:T(2,128)S(1)} %copy-done.7, f32[64,144]{1,0:T(8,128)S(1)} %copy-done.2, f32[64,64]{1,0:T(8,128)S(1)} %copy-done.6), custom_call_target="tpu_custom_call" | custom-call | tf_op jit(solution)/shard_map/column_step/pallas_call | solution.py:428
  24.3 10.3 %all_to_all.11.returned = f32[16,3,4,128]{3,2,1,0:T(4,128)S(1)} all-to-all(f32[16,3,4,128]{3,2,1,0:T(4,128)S(1)} %column_step.1), channel_id=1, replica_groups=mesh['seq'=16,'res'=2] {'seq'}, dimensions={0} | all-to-all | bytes 196608 | tf_op jit(solution)/shard_map/all_to_all | solution.py:453
  34.5 2.2 %row_backward.1 = (f32[8,8,512]{2,1,0:T(8,128)S(1)}, f32[8,8,512]{2,1,0:T(8,128)S(1)}, f32[2,64,64]{2,1,0:T(8,128)S(1)}, f32[152,128]{1,0:T(8,128)S(1)}, f32[152,128]{1,0:T(8,128)S(1)}) custom-call(f32[16,3,4,128]{3,2,1,0:T(4,128)S(1)} %all_to_all.11.returned, f32[2,512,128]{2,1,0:T(8,128)S(1)} %get-tuple-element.36.exponent_in, ...), custom_call_target="tpu_custom_call" | custom-call | tf_op jit(solution)/shard_map/row_backward/pallas_call | solution.py:428
  36.7 1.0 %collective-permute-start.2 = (f32[8,8,512]{2,1,0:T(8,128)S(1)}, f32[8,8,512]{2,1,0:T(8,128)S(1)}, u32[]{:S(2)}, u32[]{:S(2)}) collective-permute-start(f32[8,8,512]{2,1,0:T(8,128)S(1)} %get-tuple-element.48), channel_id=1, source_target_pairs={{0,2},{2,0},{4,6},{6,4},{8,10},{10,8},{12,14},{14,12},{16,18},{18,... | collective-permute-start | bytes 393224 | tf_op jit(solution)/shard_map/ppermute | solution.py:449
  37.7 4.6 %collective-permute-done.2.arrived = f32[8,8,512]{2,1,0:T(8,128)S(1)} collective-permute-done((f32[8,8,512]{2,1,0:T(8,128)S(1)}, f32[8,8,512]{2,1,0:T(8,128)S(1)}, u32[]{:S(2)}, u32[]{:S(2)}) %collective-permute-start.2) | collective-permute-done | bytes 131104 | tf_op jit(solution)/shard_map/ppermute | solution.py:449
  42.4 0.8 %collective-permute-start.3 = (f32[4,8,512]{2,1,0:T(8,128)S(1)}, f32[4,8,512]{2,1,0:T(8,128)S(1)}, u32[]{:S(2)}, u32[]{:S(2)}) collective-permute-start(f32[4,8,512]{2,1,0:T(8,128)S(1)} %get-tuple-element.50.refs_0_), channel_id=1, source_target_pairs={{0,4},{2,6},{4,0},{6,2},{8,12},{10,14},{12,8},{14,10},{16,20},{18,... | collective-permute-start | bytes 196616 | tf_op jit(solution)/shard_map/ppermute | solution.py:449
  43.2 0.5 collective-permute-start.6
  43.7 4.0 %collective-permute-done.6.arrived = f32[88,128]{1,0:T(8,128)S(1)} collective-permute-done((f32[88,128]{1,0:T(8,128)S(1)}, f32[88,128]{1,0:T(8,128)S(1)}, u32[]{:S(2)}, u32[]{:S(2)}) %collective-permute-start.6) | collective-permute-done | bytes 45088 | tf_op jit(solution)/shard_map/ppermute | solution.py:449
  48.2 0.6 collective-permute-start.4
  48.7 4.1 %collective-permute-done.7.arrived = f32[96,128]{1,0:T(8,128)S(1)} collective-permute-done((f32[96,128]{1,0:T(8,128)S(1)}, f32[96,128]{1,0:T(8,128)S(1)}, u32[]{:S(2)}, u32[]{:S(2)}) %collective-permute-start.7) | collective-permute-done | bytes 49184 | tf_op jit(solution)/shard_map/ppermute | solution.py:449
  52.8 0.7 %collective-permute-start.8 = (f32[112,128]{1,0:T(8,128)S(1)}, f32[112,128]{1,0:T(8,128)S(1)}, u32[]{:S(2)}, u32[]{:S(2)}) collective-permute-start(f32[112,128]{1,0:T(8,128)S(1)} %shared_step.5.shared), channel_id=1, source_target_pairs={{0,2},{2,0},{4,6},{6,4},{8,10},{10,8},{12,14},{14,12},{16,18},{18,... | collective-permute-start | bytes 172040 | tf_op jit(solution)/shard_map/ppermute | solution.py:449
  53.5 1.4 %collective-permute-start.5 = (f32[1,8,512]{2,1,0:T(8,128)S(1)}, f32[1,8,512]{2,1,0:T(8,128)S(1)}, u32[]{:S(2)}, u32[]{:S(2)}) collective-permute-start(f32[1,8,512]{2,1,0:T(8,128)S(1)} %get-tuple-element.54), channel_id=1, source_target_pairs={{0,16},{2,18},{4,20},{6,22},{8,24},{10,26},{12,28},{14,30},{16,0},... | collective-permute-start | bytes 49160 | tf_op jit(solution)/shard_map/ppermute | solution.py:449
  54.9 3.2 %collective-permute-done.5.arrived.refs_0_ = f32[1,8,512]{2,1,0:T(8,128)S(1)} collective-permute-done((f32[1,8,512]{2,1,0:T(8,128)S(1)}, f32[1,8,512]{2,1,0:T(8,128)S(1)}, u32[]{:S(2)}, u32[]{:S(2)}) %collective-permute-start.5) | collective-permute-done | bytes 16416 | tf_op jit(solution)/shard_map/ppermute | solution.py:449
  58.2 1.6 %collective-permute-start.9 = (f32[144,128]{1,0:T(8,128)S(1)}, f32[144,128]{1,0:T(8,128)S(1)}, u32[]{:S(2)}, u32[]{:S(2)}) collective-permute-start(f32[144,128]{1,0:T(8,128)S(1)} %shared_step.6.shared), channel_id=1, source_target_pairs={{0,4},{2,6},{4,0},{6,2},{8,12},{10,14},{12,8},{14,10},{16,20},{18,... | collective-permute-start | bytes 221192 | tf_op jit(solution)/shard_map/ppermute | solution.py:449
  59.8 2.8 %collective-permute-done.9.arrived = f32[144,128]{1,0:T(8,128)S(1)} collective-permute-done((f32[144,128]{1,0:T(8,128)S(1)}, f32[144,128]{1,0:T(8,128)S(1)}, u32[]{:S(2)}, u32[]{:S(2)}) %collective-permute-start.9) | collective-permute-done | bytes 73760 | tf_op jit(solution)/shard_map/ppermute | solution.py:449
  62.7 1.1 %finish_alignment.1 = bf16[2,64,64]{2,1,0:T(8,128)(2,1)} custom-call(bf16[2,64,64]{2,1,0:T(8,128)(2,1)S(1)} %copy-done.1, f32[2,64,64]{2,1,0:T(8,128)S(1)} %get-tuple-element.43.middle_grad, f32[2,64]{1,0:T(2,128)S(1)} %copy-done.7, f32[64,128]{1,0:T(8,128)S(1)} %get-tuple-element.46.normed), custom_call_target="tpu_custom_call" | custom-call | tf_op jit(solution)/shard_map/finish_alignment/pallas_call | solution.py:428
  63.8 0.7 %bias_last.1 = f32[8,8,64]{2,1,0:T(8,128)} custom-call(f32[1,8,512]{2,1,0:T(8,128)S(1)} %get-tuple-element.53.state, f32[1,8,512]{2,1,0:T(8,128)S(1)} %collective-permute-done.5.arrived.refs_0_), custom_call_target="tpu_custom_call" | custom-call | tf_op jit(solution)/shard_map/bias_last/pallas_call | solution.py:428
  64.5 1.1 %unpack.1 = (f32[2,64]{1,0:T(2,128)}, f32[64,256]{1,0:T(8,128)}, f32[64,64]{1,0:T(8,128)}, f32[64,144]{1,0:T(8,128)}, f32[64,64]{1,0:T(8,128)}) custom-call(f32[128,128]{1,0:T(8,128)S(1)} %get-tuple-element.56.joined, f32[80,128]{1,0:T(8,128)S(1)} %get-tuple-element.57.refs_0_, f32[80,128]{1,0:T(8,128)S(1)} %collective-permute-done.10.refs_1_, ...), custom_call_target="tpu_custom_call" | custom-call | tf_op jit(solution)/shard_map/unpack/pallas_call | solution.py:428
  (36 shorter events, 0.7 us)
Async XLA Ops:
  1.3 2.3 %copy-start.4 = (f32[64,64]{1,0:T(8,128)S(1)}, f32[64,64]{1,0:T(8,128)}, u32[]{:S(2)}) copy-start(f32[64,64]{1,0:T(8,128)} %w_out.3) | copy-start | bytes 49156
  1.3 2.3 %copy-start.5 = (bf16[2,64,64]{2,1,0:T(8,128)(2,1)S(1)}, bf16[2,64,64]{2,1,0:T(8,128)(2,1)}, u32[]{:S(2)}) copy-start(bf16[2,64,64]{2,1,0:T(8,128)(2,1)} %refs_3_.2) | copy-start | bytes 49156
  1.3 2.3 %copy-start.7 = (f32[2,64]{1,0:T(2,128)S(1)}, f32[2,64]{1,0:T(2,128)}, u32[]{:S(2)}) copy-start(f32[2,64]{1,0:T(2,128)} %refs_2_.3) | copy-start | bytes 1540
  2.1 1.5 %copy-start.3 = (bf16[8,64,128]{2,1,0:T(8,128)(2,1)S(1)}, bf16[8,64,128]{2,1,0:T(8,128)(2,1)}, u32[]{:S(2)}) copy-start(bf16[8,64,128]{2,1,0:T(8,128)(2,1)} %refs_4_.2) | copy-start | bytes 393220
  2.1 1.5 %copy-start = (f32[64,256]{1,0:T(8,128)S(1)}, f32[64,256]{1,0:T(8,128)}, u32[]{:S(2)}) copy-start(f32[64,256]{1,0:T(8,128)} %refs_3_.3) | copy-start | bytes 196612
  2.1 1.5 %copy-start.1 = (bf16[2,64,64]{2,1,0:T(8,128)(2,1)S(1)}, bf16[2,64,64]{2,1,0:T(8,128)(2,1)}, u32[]{:S(2)}) copy-start(bf16[2,64,64]{2,1,0:T(8,128)(2,1)} %own.1) | copy-start | bytes 49156
  2.1 1.5 %copy-start.8 = (s32[2]{0:T(128)S(1)}, s32[2]{0:T(128)}, u32[]{:S(2)}) copy-start(s32[2]{0:T(128)} %seq_mask.1) | copy-start | bytes 28
  2.1 1.5 %collective-permute-start = (f32[3,64,64]{2,1,0:T(8,128)S(1)}, f32[3,64,64]{2,1,0:T(8,128)S(1)}, u32[]{:S(2)}, u32[]{:S(2)}) collective-permute-start(f32[3,64,64]{2,1,0:T(8,128)S(1)} %pad_maximum_fusion.refs_0_), channel_id=1, source_target_pairs={{1,0},{0,1},{3,2},{2,3},{5,4},{4,5},{7,6},{6,7},{9,8},{8,9},{11,10... | collective-permute-start | bytes 147464 | tf_op jit(solution)/shard_map/ppermute | solution.py:441
  6.8 15.8 %copy-start.2 = (f32[64,144]{1,0:T(8,128)S(1)}, f32[64,144]{1,0:T(8,128)}, u32[]{:S(2)}) copy-start(f32[64,144]{1,0:T(8,128)} %refs_4_.3) | copy-start | bytes 110596
  6.8 15.8 %copy-start.6 = (f32[64,64]{1,0:T(8,128)S(1)}, f32[64,64]{1,0:T(8,128)}, u32[]{:S(2)}) copy-start(f32[64,64]{1,0:T(8,128)} %w_out.2) | copy-start | bytes 49156
  36.7 5.6 %collective-permute-start.2 = (f32[8,8,512]{2,1,0:T(8,128)S(1)}, f32[8,8,512]{2,1,0:T(8,128)S(1)}, u32[]{:S(2)}, u32[]{:S(2)}) collective-permute-start(f32[8,8,512]{2,1,0:T(8,128)S(1)} %get-tuple-element.48), channel_id=1, source_target_pairs={{0,2},{2,0},{4,6},{6,4},{8,10},{10,8},{12,14},{14,12},{16,18},{18,... | collective-permute-start | bytes 393224 | tf_op jit(solution)/shard_map/ppermute | solution.py:449
  37.7 5.4 %collective-permute-start.1 = (f32[152,128]{1,0:T(8,128)S(1)}, f32[152,128]{1,0:T(8,128)S(1)}, u32[]{:S(2)}, u32[]{:S(2)}) collective-permute-start(f32[152,128]{1,0:T(8,128)S(1)} %get-tuple-element.45), channel_id=1, source_target_pairs={{1,0},{0,1},{3,2},{2,3},{5,4},{4,5},{7,6},{6,7},{9,8},{8,9},{11,10... | collective-permute-start | bytes 233480 | tf_op jit(solution)/shard_map/ppermute | solution.py:441
  42.4 5.8 %collective-permute-start.3 = (f32[4,8,512]{2,1,0:T(8,128)S(1)}, f32[4,8,512]{2,1,0:T(8,128)S(1)}, u32[]{:S(2)}, u32[]{:S(2)}) collective-permute-start(f32[4,8,512]{2,1,0:T(8,128)S(1)} %get-tuple-element.50.refs_0_), channel_id=1, source_target_pairs={{0,4},{2,6},{4,0},{6,2},{8,12},{10,14},{12,8},{14,10},{16,20},{18,... | collective-permute-start | bytes 196616 | tf_op jit(solution)/shard_map/ppermute | solution.py:449
  43.2 4.5 %collective-permute-start.6 = (f32[88,128]{1,0:T(8,128)S(1)}, f32[88,128]{1,0:T(8,128)S(1)}, u32[]{:S(2)}, u32[]{:S(2)}) collective-permute-start(f32[88,128]{1,0:T(8,128)S(1)} %get-tuple-element.55.shared), channel_id=1, source_target_pairs={{0,8},{2,10},{4,12},{6,14},{8,0},{10,2},{12,4},{14,6},{16,24},{18,... | collective-permute-start | bytes 135176 | tf_op jit(solution)/shard_map/ppermute | solution.py:449
  47.7 5.2 %collective-permute-start.7 = (f32[96,128]{1,0:T(8,128)S(1)}, f32[96,128]{1,0:T(8,128)S(1)}, u32[]{:S(2)}, u32[]{:S(2)}) collective-permute-start(f32[96,128]{1,0:T(8,128)S(1)} %shared_step.4.shared), channel_id=1, source_target_pairs={{0,16},{2,18},{4,20},{6,22},{8,24},{10,26},{12,28},{14,30},{16,0},... | collective-permute-start | bytes 147464 | tf_op jit(solution)/shard_map/ppermute | solution.py:449
  48.2 4.7 %collective-permute-start.4 = (f32[2,8,512]{2,1,0:T(8,128)S(1)}, f32[2,8,512]{2,1,0:T(8,128)S(1)}, u32[]{:S(2)}, u32[]{:S(2)}) collective-permute-start(f32[2,8,512]{2,1,0:T(8,128)S(1)} %get-tuple-element.52), channel_id=1, source_target_pairs={{0,8},{2,10},{4,12},{6,14},{8,0},{10,2},{12,4},{14,6},{16,24},{18,... | collective-permute-start | bytes 98312 | tf_op jit(solution)/shard_map/ppermute | solution.py:449
  52.8 5.4 %collective-permute-start.8 = (f32[112,128]{1,0:T(8,128)S(1)}, f32[112,128]{1,0:T(8,128)S(1)}, u32[]{:S(2)}, u32[]{:S(2)}) collective-permute-start(f32[112,128]{1,0:T(8,128)S(1)} %shared_step.5.shared), channel_id=1, source_target_pairs={{0,2},{2,0},{4,6},{6,4},{8,10},{10,8},{12,14},{14,12},{16,18},{18,... | collective-permute-start | bytes 172040 | tf_op jit(solution)/shard_map/ppermute | solution.py:449
  53.5 4.6 %collective-permute-start.5 = (f32[1,8,512]{2,1,0:T(8,128)S(1)}, f32[1,8,512]{2,1,0:T(8,128)S(1)}, u32[]{:S(2)}, u32[]{:S(2)}) collective-permute-start(f32[1,8,512]{2,1,0:T(8,128)S(1)} %get-tuple-element.54), channel_id=1, source_target_pairs={{0,16},{2,18},{4,20},{6,22},{8,24},{10,26},{12,28},{14,30},{16,0},... | collective-permute-start | bytes 49160 | tf_op jit(solution)/shard_map/ppermute | solution.py:449
  58.2 4.4 %collective-permute-start.9 = (f32[144,128]{1,0:T(8,128)S(1)}, f32[144,128]{1,0:T(8,128)S(1)}, u32[]{:S(2)}, u32[]{:S(2)}) collective-permute-start(f32[144,128]{1,0:T(8,128)S(1)} %shared_step.6.shared), channel_id=1, source_target_pairs={{0,4},{2,6},{4,0},{6,2},{8,12},{10,14},{12,8},{14,10},{16,20},{18,... | collective-permute-start | bytes 221192 | tf_op jit(solution)/shard_map/ppermute | solution.py:449
  62.6 1.9 %collective-permute-start.10 = (f32[80,128]{1,0:T(8,128)S(1)}, f32[80,128]{1,0:T(8,128)S(1)}, u32[]{:S(2)}, u32[]{:S(2)}) collective-permute-start(f32[80,128]{1,0:T(8,128)S(1)} %get-tuple-element.57.refs_0_), channel_id=1, source_target_pairs={{1,0},{0,1},{3,2},{2,3},{5,4},{4,5},{7,6},{6,7},{9,8},{8,9},{11,10... | collective-permute-start | bytes 122888 | tf_op jit(solution)/shard_map/ppermute | solution.py:441

commit v6 on v5

--- a/solution.py
+++ b/solution.py
@@ -290,26 +290,24 @@
     sums_out[0][part + ROWS :, :] += jnp.concatenate(from_own, axis=1)
 
 
-def step_bits(n_seq_devices, odd, late_first=False):
+def step_bits(n_seq_devices, odd):
     bits = list(range(n_seq_devices.bit_length() - 1))
     if odd:
         for i in range(0, len(bits) - 1, 2):
             bits[i], bits[i + 1] = bits[i + 1], bits[i]
-    if late_first:
-        middle = len(bits) // 2
-        bits = bits[middle:] + bits[:middle]
     return bits
 
 
-def relative_block(mask_of_bits, n_blocks, late_first=False):
+def relative_block(mask_of_bits, n_blocks):
     odd = lax.rem(lax.axis_index("res"), 2)
-    even_mask = mask_of_bits(step_bits(n_blocks, False, late_first))
-    odd_mask = mask_of_bits(step_bits(n_blocks, True, late_first))
+    even_mask = mask_of_bits(step_bits(n_blocks, False))
+    odd_mask = mask_of_bits(step_bits(n_blocks, True))
     return lax.axis_index("seq") ^ (even_mask + odd * (odd_mask - even_mask))
 
 
 def split_blocks(bias_t, state, send):
-    n_blocks = state.shape[0] + send.shape[0]
+    tiles = bias_t.shape[1] // LANES
+    n_blocks = (state.shape[0] + send.shape[0]) // tiles
     keys_each = bias_t.shape[0] // n_blocks
     half = n_blocks // 2
 
@@ -321,52 +319,56 @@
 
         block = relative_block(mask_of_bits, n_blocks)
         values = bias_t[pl.ds(pl.multiple_of(block * keys_each, keys_each), keys_each), :]
-        if slot < half:
-            state[slot] = values
-        else:
-            send[slot - half] = values
-
-
-def bias_step(state, arrived, state_out, send_out):
-    total = state[...] + arrived[...]
-    half = state_out.shape[0]
-    state_out[...] = total[:half]
-    send_out[...] = total[half:]
+        for i in range(tiles):
+            out, at = (state, slot) if slot < half else (send, slot - half)
+            out[at * tiles + i] = values[:, i * LANES : (i + 1) * LANES]
 
 
 def bias_last(state, arrived, bias_out):
-    total = state[0] + arrived[0]
     heads, _, n_rows = bias_out.shape
-    for h in range(heads):
-        bias_out[h] = total[:, h * n_rows : (h + 1) * n_rows]
-
-
-def add_shares(*refs):
-    sums, shared, normed = refs[:-2], refs[-2], refs[-1]
+    each = LANES // n_rows
+    for i in range(state.shape[0]):
+        total = state[i] + arrived[i]
+        for e in range(each):
+            bias_out[i * each + e] = total[:, e * n_rows : (e + 1) * n_rows]
+
+
+def add_shares(bias_send, *refs):
+    sums, send, normed = refs[:-2], refs[-2], refs[-1]
     total = sums[0][...]
     for more in sums[1:]:
         total = total + more[...]
-    rows = shared.shape[0]
-    shared[...] = total[:rows]
+    left = bias_send.shape[0]
+    rows = total.shape[0] - normed.shape[0]
+    send[:left] = bias_send[...]
+    send[left:] = total[:rows].reshape(rows // ROWS, ROWS, LANES)
     normed[...] = total[rows:]
 
 
-def shared_step(part, n_before, shared, arrived, *refs):
-    outs = refs[n_before:]
-    total = shared[:part] + arrived[:part]
-    pieces = shared.shape[0] - part
-    if len(outs) == 2:
-        outs[0][...] = total
-        joined, at = outs[1], 0
-    else:
-        outs[0][:part] = total
-        joined, at = outs[0], part
-    joined[at : at + pieces] = shared[part:]
-    joined[at + pieces :] = arrived[part:]
-
-
-def finish_alignment(own, middle_grad, gains, normed, out):
+def step(part, state, sent, arrived, state_out, send):
+    left = state.shape[0]
+    half = left // 2
+    total = state[...] + arrived[:left]
+    state_out[...] = total[:half]
+    send[:half] = total[half:]
+    send[half : half + part] = sent[left : left + part] + arrived[left : left + part]
+    pieces = sent.shape[0] - left - part
+    send[half + part : half + part + pieces] = sent[left + part :]
+    send[half + part + pieces :] = arrived[left + part :]
+
+
+def last_step(sent, arrived, _, shared, joined):
+    part = shared.shape[0]
+    pieces = joined.shape[0] // 2
+    left = sent.shape[0] - part - pieces
+    shared[...] = sent[left : left + part] + arrived[left : left + part]
+    joined[:pieces] = sent[left + part :]
+    joined[pieces:] = arrived[left + part :]
+
+
+def finish_alignment(own, middle_grad, gains, normed, out, done):
     n_seq = own.shape[0]
+    done[...] = jnp.zeros(done.shape, F32)
     for s in range(n_seq):
         unit, inverse = normalise(own[s].astype(F32))
         grad_normed = normed[:, s * C : (s + 1) * C]
@@ -380,13 +382,13 @@
     me = lax.axis_index("res")
     part = shares.shape[1]
     for away in range(n_res):
-        shares[lax.rem(me + away, n_res)] = parts[away][...]
+        shares[lax.rem(me + away, n_res)] = parts[away][...].reshape(part, LANES)
     n_blocks, _, share, _ = column.shape
     for slot in range(n_blocks):
         block = relative_block(
-            lambda bits: sum(1 << bit for at, bit in enumerate(bits) if slot >> at & 1), n_blocks, True
+            lambda bits: sum(1 << bit for at, bit in enumerate(bits) if slot >> at & 1), n_blocks
         )
-        piece = joined[slot * ROWS : (slot + 1) * ROWS, :]
+        piece = joined[slot]
         column[block, 0] = piece[:share]
         column[block, 1] = piece[share : 2 * share]
     flat = jnp.concatenate([shares[i] for i in range(n_res)], axis=0)
@@ -441,10 +443,10 @@
     return lax.ppermute(values, "res", [((i + away) % count, i) for i in range(count)])
 
 
-def cross(values, at, seq_count, res_count, late_first=False):
+def cross(values, at, seq_count, res_count):
     pairs = []
     for r in range(res_count):
-        bit = 1 << step_bits(seq_count, r % 2, late_first)[at]
+        bit = 1 << step_bits(seq_count, r % 2)[at]
         pairs += [(i * res_count + r, (i ^ bit) * res_count + r) for i in range(seq_count)]
     return lax.ppermute(values, ("seq", "res"), pairs)
 
@@ -503,62 +505,58 @@
     )
     returned = swap_blocks(returned)
     part = -(-5 * C // (2 * ROWS * res_count)) * ROWS
-    wide = H * n_rows
     keys_each = n_keys // seq_count
-    left = seq_count // 2
+    tiles = H * n_rows // LANES
+    left = seq_count // 2 * tiles
     state, send, middle_grad, *sums = call(
         functools.partial(row_backward, res_count),
-        [((left, keys_each, wide), F32)] * 2
+        [((left, keys_each, LANES), F32)] * 2
         + [((n_seq, n_rows, C), F32)]
         + [((part + ROWS + n_rows, LANES), F32)] * res_count,
         returned, exponent, unit, memory, query_gate, mixture, inverse, own_unit, row_project, row_output,
         scratch=[
             pltpu.VMEM((res_count, part + ROWS + n_rows, LANES), F32),
-            pltpu.VMEM((n_keys, wide), F32),
+            pltpu.VMEM((n_keys, H * n_rows), F32),
         ],
         name="row_backward",
     )
     sums = sums[:1] + [shift_residues(sums[away], -away, res_count) for away in away_range]
+    part_tiles = part // ROWS
+    send, normed = call(
+        add_shares,
+        [((left + part_tiles + 1, ROWS, LANES), F32), ((n_rows, LANES), F32)],
+        send, *sums,
+        name="add_shares",
+    )
+    grad_alignment, done = call(
+        finish_alignment,
+        [(alignment.shape, alignment.dtype), ((ROWS, LANES), F32)],
+        alignment, middle_grad, norm_gains, normed,
+        name="finish_alignment",
+    )
     steps = seq_count.bit_length() - 1
-    arrivals = []
-    before = []
     for at in range(steps):
-        arrivals.append(cross(send, at, seq_count, res_count))
+        arrived = cross(send, at, seq_count, res_count)
         if at < steps - 1:
             left //= 2
             state, send = call(
-                bias_step, [((left, keys_each, wide), F32)] * 2, state, arrivals[at], name="bias_step"
+                functools.partial(step, part_tiles),
+                [((left, ROWS, LANES), F32), ((left + part_tiles + (2 << at), ROWS, LANES), F32)],
+                state, send, arrived,
+                name="step",
             )
-            before.append([send] if at == 0 else [])
-    before = [before[0]] + [[arrived] for arrived in arrivals[2:]] + [[]]
-    (bias_grad,) = call(bias_last, [((H, keys_each, n_rows), F32)], state, arrivals[-1], name="bias_last")
-    shared, normed = call(
-        add_shares,
-        [((part + ROWS, LANES), F32), ((n_rows, LANES), F32)],
-        *sums,
-        name="add_shares",
-    )
-    for at in range(steps):
-        arrived_shared = cross(shared, at, seq_count, res_count, True)
-        pieces = ROWS << (at + 1)
-        shapes = [(part + pieces, LANES)] if at < steps - 1 else [(part, LANES), (pieces, LANES)]
-        shared, *joined = call(
-            functools.partial(shared_step, part, len(before[at])),
-            [(shape, F32) for shape in shapes],
-            shared, arrived_shared, *before[at],
-            unread=len(before[at]),
-            name="shared_step",
-        )
-    (grad_alignment,) = call(
-        finish_alignment,
-        [(alignment.shape, alignment.dtype)],
-        alignment, middle_grad, norm_gains, normed,
-        name="finish_alignment",
-    )
+    shared, joined = call(
+        last_step,
+        [((part_tiles, ROWS, LANES), F32), ((seq_count, ROWS, LANES), F32)],
+        send, arrived, done,
+        unread=1,
+        name="last_step",
+    )
+    (bias_grad,) = call(bias_last, [((H, keys_each, n_rows), F32)], state, arrived, name="bias_last")
     grads = call(
         functools.partial(unpack, res_count),
         [((2, C), F32), ((C, 4 * C), F32), ((C, C), F32), ((C, 2 * C + 2 * DH), F32), ((C, C), F32)],
-        *joined, shared, *[shift_residues(shared, away, res_count) for away in away_range],
+        joined, shared, *[shift_residues(shared, away, res_count) for away in away_range],
         norm_gains, row_project, column_project,
         scratch=[
             pltpu.VMEM((res_count, part, LANES), F32),

time: 66 us -> 62.2 us (0.942)
  starting transfers between devices: 7.66 us -> 4.07 us
    ppermute x8 -> x4, starting transfers between devices: 7.07 us -> 3.41 us  [cross(): return lax.ppermute(values, ('seq', 'res'), pairs)]
    ppermute x8 -> x4, waiting for transfers between devices: 18.7 us -> 16.9 us  [cross(): return lax.ppermute(values, ('seq', 'res'), pairs)]
    ppermute x3, waiting for transfers between devices: 0.95 us -> 2.72 us  [shift_residues(): lax.ppermute(values, 'res', [((i + away) % count, i) for i in range(count)])]
    pallas_call x14 -> x11, Pallas kernels: 9.95 us -> 9.95 us  [call(): pl.pallas_call(body, out_shape=[jax.ShapeDtypeStruct(shape, kind) for sha...]
  transfers between devices with their start and end apart: 11 -> 7, of which waited for: 6 -> 7; matrix products, arithmetic and copies ran while one was open for 0% -> 0% of each run, Pallas kernels for 3% -> 3%
where the time goes in v6:
time: 62.2 us; the launch traced here: 61.9 us
  blocking collectives  26.1 us (42%)
  waiting for transfers between devices  19.6 us (32%)
  Pallas kernels  9.95 us (16%)
  starting transfers between devices  4.07 us (7%)
  other arithmetic  1.44 us (2%)
  between operations  0.76 us (1%)
    all_to_all x2, blocking collectives, swap_blocks(): return lax.all_to_all(values, 'seq', 0, 0, tiled=True)  26.1 us
    ppermute x4, waiting for transfers between devices, cross(): return lax.ppermute(values, ('seq', 'res'), pairs)  16.9 us
    pallas_call x11, Pallas kernels, call(): pl.pallas_call(body, out_shape=[jax.ShapeDtypeStruct(shape, kind) for sha...  9.95 us
    ppermute x4, starting transfers between devices, cross(): return lax.ppermute(values, ('seq', 'res'), pairs)  3.41 us
    ppermute x3, waiting for transfers between devices, shift_residues(): lax.ppermute(values, 'res', [((i + away) % count, i) for i in range(count)])  2.72 us
  transfers between devices with their start and end apart: 7, of which 7 were waited for; matrix products, arithmetic and copies ran while one was open for 0% of the time, Pallas kernels for 3%

profile of v6, /device:TPU:0, one launch (start us, length us, event | category | flops | bytes accessed | tf_op | source)
XLA Modules:
  0.0 61.9 jit_solution(17133229112285141265)
XLA Ops:
  0.6 0.7 %convert_element_type.7 = f32[64]{0:T(128)S(1)} convert(s32[64]{0:T(128)} %param.18) | non-fusion elementwise | flops 64 | bytes 512 | tf_op jit(solution)/shard_map/convert_element_type | solution.py:477
  1.3 0.8 %convert_element_type.6 = f32[2,64,64]{2,1,0:T(8,128)S(1)} convert(bf16[2,64,64]{2,1,0:T(8,128)(2,1)} %own.1) | non-fusion elementwise | flops 8192 | bytes 49152 | tf_op jit(solution)/shard_map/convert_element_type | solution.py:479
  2.1 0.5 collective-permute-start
  2.7 0.9 %collective-permute-done.refs_1_ = f32[3,64,64]{2,1,0:T(8,128)S(1)} collective-permute-done((f32[3,64,64]{2,1,0:T(8,128)S(1)}, f32[3,64,64]{2,1,0:T(8,128)S(1)}, u32[]{:S(2)}, u32[]{:S(2)}) %collective-permute-start) | collective-permute-done | bytes 49184 | tf_op jit(solution)/shard_map/ppermute | solution.py:443
  3.6 3.1 %row_forward.1 = (f32[16,3,4,128]{3,2,1,0:T(4,128)S(1)}, f32[2,512,128]{2,1,0:T(8,128)S(1)}, f32[2,128,64]{2,1,0:T(8,128)S(1)}, f32[2,64,64]{2,1,0:T(8,128)S(1)}...) custom-call(s32[2]{0:T(128)S(1)} %copy-done.8, ...), custom_call_target="tpu_custom_call" | custom-call | tf_op jit(solution)/shard_map/row_forward/pallas_call | solution.py:430
  6.8 15.8 %all_to_all.10.arrived = f32[16,3,4,128]{3,2,1,0:T(4,128)S(1)} all-to-all(f32[16,3,4,128]{3,2,1,0:T(4,128)S(1)} %get-tuple-element.37), channel_id=1, replica_groups=mesh['seq'=16,'res'=2] {'seq'}, dimensions={0} | all-to-all | bytes 196608 | tf_op jit(solution)/shard_map/all_to_all | solution.py:455
  22.6 1.7 %column_step.1 = f32[16,3,4,128]{3,2,1,0:T(4,128)S(1)} custom-call(f32[16,3,4,128]{3,2,1,0:T(4,128)S(1)} %all_to_all.10.arrived, f32[2,64]{1,0:T(2,128)S(1)} %copy-done.7, f32[64,144]{1,0:T(8,128)S(1)} %copy-done.2, f32[64,64]{1,0:T(8,128)S(1)} %copy-done.6), custom_call_target="tpu_custom_call" | custom-call | tf_op jit(solution)/shard_map/column_step/pallas_call | solution.py:430
  24.3 10.3 %all_to_all.11.returned = f32[16,3,4,128]{3,2,1,0:T(4,128)S(1)} all-to-all(f32[16,3,4,128]{3,2,1,0:T(4,128)S(1)} %column_step.1), channel_id=1, replica_groups=mesh['seq'=16,'res'=2] {'seq'}, dimensions={0} | all-to-all | bytes 196608 | tf_op jit(solution)/shard_map/all_to_all | solution.py:455
  34.5 2.2 %row_backward.1 = (f32[32,8,128]{2,1,0:T(8,128)S(1)}, f32[32,8,128]{2,1,0:T(8,128)S(1)}, f32[2,64,64]{2,1,0:T(8,128)S(1)}, f32[152,128]{1,0:T(8,128)S(1)}, f32[152,128]{1,0:T(8,128)S(1)}) custom-call(f32[16,3,4,128]{3,2,1,0:T(4,128)S(1)} %all_to_all.11.returned, f32[2,512,128]{2,1,0:T(8,128)S(1)} %get-tuple-element.38.exponent_in, ...), custom_call_target="tpu_custom_call" | custom-call | tf_op jit(solution)/shard_map/row_backward/pallas_call | solution.py:430
  36.7 0.1 collective-permute-start.1
  36.8 1.3 %collective-permute-done.1.refs_1_ = f32[152,128]{1,0:T(8,128)S(1)} collective-permute-done((f32[152,128]{1,0:T(8,128)S(1)}, f32[152,128]{1,0:T(8,128)S(1)}, u32[]{:S(2)}, u32[]{:S(2)}) %collective-permute-start.1) | collective-permute-done | bytes 77856 | tf_op jit(solution)/shard_map/ppermute | solution.py:443
  38.1 1.0 %collective-permute-start.2 = (f32[43,8,128]{2,1,0:T(8,128)S(1)}, f32[43,8,128]{2,1,0:T(8,128)S(1)}, u32[]{:S(2)}, u32[]{:S(2)}) collective-permute-start(f32[43,8,128]{2,1,0:T(8,128)S(1)} %get-tuple-element.52.sent), channel_id=1, source_target_pairs={{0,2},{2,0},{4,6},{6,4},{8,10},{10,8},{12,14},{14,12},{16,18},{18,... | collective-permute-start | bytes 528392 | tf_op jit(solution)/shard_map/ppermute | solution.py:451
  39.1 4.5 %collective-permute-done.2.arrived = f32[43,8,128]{2,1,0:T(8,128)S(1)} collective-permute-done((f32[43,8,128]{2,1,0:T(8,128)S(1)}, f32[43,8,128]{2,1,0:T(8,128)S(1)}, u32[]{:S(2)}, u32[]{:S(2)}) %collective-permute-start.2) | collective-permute-done | bytes 176160 | tf_op jit(solution)/shard_map/ppermute | solution.py:451
  43.6 0.7 %collective-permute-start.3 = (f32[28,8,128]{2,1,0:T(8,128)S(1)}, f32[28,8,128]{2,1,0:T(8,128)S(1)}, u32[]{:S(2)}, u32[]{:S(2)}) collective-permute-start(f32[28,8,128]{2,1,0:T(8,128)S(1)} %get-tuple-element.54.sent), channel_id=1, source_target_pairs={{0,4},{2,6},{4,0},{6,2},{8,12},{10,14},{12,8},{14,10},{16,20},{18,... | collective-permute-start | bytes 344072 | tf_op jit(solution)/shard_map/ppermute | solution.py:451
  44.4 4.1 %collective-permute-done.3.arrived = f32[28,8,128]{2,1,0:T(8,128)S(1)} collective-permute-done((f32[28,8,128]{2,1,0:T(8,128)S(1)}, f32[28,8,128]{2,1,0:T(8,128)S(1)}, u32[]{:S(2)}, u32[]{:S(2)}) %collective-permute-start.3) | collective-permute-done | bytes 114720 | tf_op jit(solution)/shard_map/ppermute | solution.py:451
  48.5 0.8 %collective-permute-start.4 = (f32[22,8,128]{2,1,0:T(8,128)S(1)}, f32[22,8,128]{2,1,0:T(8,128)S(1)}, u32[]{:S(2)}, u32[]{:S(2)}) collective-permute-start(f32[22,8,128]{2,1,0:T(8,128)S(1)} %get-tuple-element.56.sent), channel_id=1, source_target_pairs={{0,8},{2,10},{4,12},{6,14},{8,0},{10,2},{12,4},{14,6},{16,24},{18,... | collective-permute-start | bytes 270344 | tf_op jit(solution)/shard_map/ppermute | solution.py:451
  49.3 3.8 %collective-permute-done.4.arrived = f32[22,8,128]{2,1,0:T(8,128)S(1)} collective-permute-done((f32[22,8,128]{2,1,0:T(8,128)S(1)}, f32[22,8,128]{2,1,0:T(8,128)S(1)}, u32[]{:S(2)}, u32[]{:S(2)}) %collective-permute-start.4) | collective-permute-done | bytes 90144 | tf_op jit(solution)/shard_map/ppermute | solution.py:451
  53.1 0.9 %collective-permute-start.5 = (f32[22,8,128]{2,1,0:T(8,128)S(1)}, f32[22,8,128]{2,1,0:T(8,128)S(1)}, u32[]{:S(2)}, u32[]{:S(2)}) collective-permute-start(f32[22,8,128]{2,1,0:T(8,128)S(1)} %get-tuple-element.58.sent), channel_id=1, source_target_pairs={{0,16},{2,18},{4,20},{6,22},{8,24},{10,26},{12,28},{14,30},{16,0},... | collective-permute-start | bytes 270344 | tf_op jit(solution)/shard_map/ppermute | solution.py:451
  54.0 1.1 %finish_alignment.1 = (bf16[2,64,64]{2,1,0:T(8,128)(2,1)}, f32[8,128]{1,0:T(8,128)S(1)}) custom-call(bf16[2,64,64]{2,1,0:T(8,128)(2,1)S(1)} %copy-done.1, f32[2,64,64]{2,1,0:T(8,128)S(1)} %get-tuple-element.45.middle_grad, f32[2,64]{1,0:T(2,128)S(1)} %copy-done.7, f32[64,128]{1,0:T(8,128)S(1)} %get-tuple-element.49.normed), custom_call_target="tpu_custom_call" | custom-call | tf_op jit(solution)/shard_map/finish_alignment/pallas_call | solution.py:430
  55.1 4.4 %collective-permute-done.5.arrived = f32[22,8,128]{2,1,0:T(8,128)S(1)} collective-permute-done((f32[22,8,128]{2,1,0:T(8,128)S(1)}, f32[22,8,128]{2,1,0:T(8,128)S(1)}, u32[]{:S(2)}, u32[]{:S(2)}) %collective-permute-start.5) | collective-permute-done | bytes 90144 | tf_op jit(solution)/shard_map/ppermute | solution.py:451
  59.6 0.1 collective-permute-start.6
  59.7 0.7 %bias_last.1 = f32[8,8,64]{2,1,0:T(8,128)} custom-call(f32[4,8,128]{2,1,0:T(8,128)S(1)} %get-tuple-element.57.state, f32[22,8,128]{2,1,0:T(8,128)S(1)} %collective-permute-done.5.arrived), custom_call_target="tpu_custom_call" | custom-call | tf_op jit(solution)/shard_map/bias_last/pallas_call | solution.py:430
  60.4 0.5 collective-permute-done.6.refs_1_
  60.9 1.1 %unpack.1 = (f32[2,64]{1,0:T(2,128)}, f32[64,256]{1,0:T(8,128)}, f32[64,64]{1,0:T(8,128)}, f32[64,144]{1,0:T(8,128)}, f32[64,64]{1,0:T(8,128)}) custom-call(f32[16,8,128]{2,1,0:T(8,128)S(1)} %get-tuple-element.60.joined, f32[10,8,128]{2,1,0:T(8,128)S(1)} %get-tuple-element.61.refs_0_, f32[10,8,128]{2,1,0:T(8,128)S(1)} %collective-permute-done.6.refs_1_, ...), custom_call_target="tpu_custom_call" | custom-call | tf_op jit(solution)/shard_map/unpack/pallas_call | solution.py:430
  (25 shorter events, 0.1 us)
Async XLA Ops:
  1.3 2.3 %copy-start.4 = (f32[64,64]{1,0:T(8,128)S(1)}, f32[64,64]{1,0:T(8,128)}, u32[]{:S(2)}) copy-start(f32[64,64]{1,0:T(8,128)} %w_out.3) | copy-start | bytes 49156
  1.3 2.3 %copy-start.5 = (bf16[2,64,64]{2,1,0:T(8,128)(2,1)S(1)}, bf16[2,64,64]{2,1,0:T(8,128)(2,1)}, u32[]{:S(2)}) copy-start(bf16[2,64,64]{2,1,0:T(8,128)(2,1)} %refs_3_.2) | copy-start | bytes 49156
  1.3 2.3 %copy-start.7 = (f32[2,64]{1,0:T(2,128)S(1)}, f32[2,64]{1,0:T(2,128)}, u32[]{:S(2)}) copy-start(f32[2,64]{1,0:T(2,128)} %refs_2_.3) | copy-start | bytes 1540
  2.1 1.5 %copy-start.3 = (bf16[8,64,128]{2,1,0:T(8,128)(2,1)S(1)}, bf16[8,64,128]{2,1,0:T(8,128)(2,1)}, u32[]{:S(2)}) copy-start(bf16[8,64,128]{2,1,0:T(8,128)(2,1)} %refs_4_.2) | copy-start | bytes 393220
  2.1 1.5 %copy-start = (f32[64,256]{1,0:T(8,128)S(1)}, f32[64,256]{1,0:T(8,128)}, u32[]{:S(2)}) copy-start(f32[64,256]{1,0:T(8,128)} %refs_3_.3) | copy-start | bytes 196612
  2.1 1.5 %copy-start.1 = (bf16[2,64,64]{2,1,0:T(8,128)(2,1)S(1)}, bf16[2,64,64]{2,1,0:T(8,128)(2,1)}, u32[]{:S(2)}) copy-start(bf16[2,64,64]{2,1,0:T(8,128)(2,1)} %own.1) | copy-start | bytes 49156
  2.1 1.5 %copy-start.8 = (s32[2]{0:T(128)S(1)}, s32[2]{0:T(128)}, u32[]{:S(2)}) copy-start(s32[2]{0:T(128)} %seq_mask.1) | copy-start | bytes 28
  2.1 1.5 %collective-permute-start = (f32[3,64,64]{2,1,0:T(8,128)S(1)}, f32[3,64,64]{2,1,0:T(8,128)S(1)}, u32[]{:S(2)}, u32[]{:S(2)}) collective-permute-start(f32[3,64,64]{2,1,0:T(8,128)S(1)} %pad_maximum_fusion.refs_0_), channel_id=1, source_target_pairs={{1,0},{0,1},{3,2},{2,3},{5,4},{4,5},{7,6},{6,7},{9,8},{8,9},{11,10... | collective-permute-start | bytes 147464 | tf_op jit(solution)/shard_map/ppermute | solution.py:443
  6.8 15.8 %copy-start.2 = (f32[64,144]{1,0:T(8,128)S(1)}, f32[64,144]{1,0:T(8,128)}, u32[]{:S(2)}) copy-start(f32[64,144]{1,0:T(8,128)} %refs_4_.3) | copy-start | bytes 110596
  6.8 15.8 %copy-start.6 = (f32[64,64]{1,0:T(8,128)S(1)}, f32[64,64]{1,0:T(8,128)}, u32[]{:S(2)}) copy-start(f32[64,64]{1,0:T(8,128)} %w_out.2) | copy-start | bytes 49156
  36.7 1.3 %collective-permute-start.1 = (f32[152,128]{1,0:T(8,128)S(1)}, f32[152,128]{1,0:T(8,128)S(1)}, u32[]{:S(2)}, u32[]{:S(2)}) collective-permute-start(f32[152,128]{1,0:T(8,128)S(1)} %get-tuple-element.48), channel_id=1, source_target_pairs={{1,0},{0,1},{3,2},{2,3},{5,4},{4,5},{7,6},{6,7},{9,8},{8,9},{11,10... | collective-permute-start | bytes 233480 | tf_op jit(solution)/shard_map/ppermute | solution.py:443
  38.1 5.5 %collective-permute-start.2 = (f32[43,8,128]{2,1,0:T(8,128)S(1)}, f32[43,8,128]{2,1,0:T(8,128)S(1)}, u32[]{:S(2)}, u32[]{:S(2)}) collective-permute-start(f32[43,8,128]{2,1,0:T(8,128)S(1)} %get-tuple-element.52.sent), channel_id=1, source_target_pairs={{0,2},{2,0},{4,6},{6,4},{8,10},{10,8},{12,14},{14,12},{16,18},{18,... | collective-permute-start | bytes 528392 | tf_op jit(solution)/shard_map/ppermute | solution.py:451
  43.6 4.9 %collective-permute-start.3 = (f32[28,8,128]{2,1,0:T(8,128)S(1)}, f32[28,8,128]{2,1,0:T(8,128)S(1)}, u32[]{:S(2)}, u32[]{:S(2)}) collective-permute-start(f32[28,8,128]{2,1,0:T(8,128)S(1)} %get-tuple-element.54.sent), channel_id=1, source_target_pairs={{0,4},{2,6},{4,0},{6,2},{8,12},{10,14},{12,8},{14,10},{16,20},{18,... | collective-permute-start | bytes 344072 | tf_op jit(solution)/shard_map/ppermute | solution.py:451
  48.5 4.6 %collective-permute-start.4 = (f32[22,8,128]{2,1,0:T(8,128)S(1)}, f32[22,8,128]{2,1,0:T(8,128)S(1)}, u32[]{:S(2)}, u32[]{:S(2)}) collective-permute-start(f32[22,8,128]{2,1,0:T(8,128)S(1)} %get-tuple-element.56.sent), channel_id=1, source_target_pairs={{0,8},{2,10},{4,12},{6,14},{8,0},{10,2},{12,4},{14,6},{16,24},{18,... | collective-permute-start | bytes 270344 | tf_op jit(solution)/shard_map/ppermute | solution.py:451
  53.1 6.5 %collective-permute-start.5 = (f32[22,8,128]{2,1,0:T(8,128)S(1)}, f32[22,8,128]{2,1,0:T(8,128)S(1)}, u32[]{:S(2)}, u32[]{:S(2)}) collective-permute-start(f32[22,8,128]{2,1,0:T(8,128)S(1)} %get-tuple-element.58.sent), channel_id=1, source_target_pairs={{0,16},{2,18},{4,20},{6,22},{8,24},{10,26},{12,28},{14,30},{16,0},... | collective-permute-start | bytes 270344 | tf_op jit(solution)/shard_map/ppermute | solution.py:451
  59.6 1.3 %collective-permute-start.6 = (f32[10,8,128]{2,1,0:T(8,128)S(1)}, f32[10,8,128]{2,1,0:T(8,128)S(1)}, u32[]{:S(2)}, u32[]{:S(2)}) collective-permute-start(f32[10,8,128]{2,1,0:T(8,128)S(1)} %get-tuple-element.61.refs_0_), channel_id=1, source_target_pairs={{1,0},{0,1},{3,2},{2,3},{5,4},{4,5},{7,6},{6,7},{9,8},{8,9},{11,10... | collective-permute-start | bytes 122888 | tf_op jit(solution)/shard_map/ppermute | solution.py:443

commit v7 on v6

--- a/solution.py
+++ b/solution.py
@@ -56,24 +56,35 @@
 
 
 def head_mask(rows):
-    row = lax.broadcasted_iota(jnp.int32, (H, rows, C), 0)
-    channel = lax.broadcasted_iota(jnp.int32, (H, rows, C), 2)
-    return (row == channel // DH).astype(F32).reshape(H * rows, C)
+    channel = lax.broadcasted_iota(jnp.int32, (C, H * rows), 0)
+    lane = lax.broadcasted_iota(jnp.int32, (C, H * rows), 1)
+    return (lane // rows == channel // DH).astype(F32)
 
 
 def spread_heads(values, mask):
-    return jnp.concatenate([values] * H, axis=0) * mask
+    rows = values.shape[0]
+    turned = jnp.transpose(values)
+    turned = jnp.concatenate([turned] * (LANES // rows), axis=1)
+    return jnp.concatenate([turned] * (H * rows // LANES), axis=1) * mask
 
 
 def join_heads(values, mask):
     masked = values * mask
-    return jnp.sum(masked.reshape(H, -1, masked.shape[1]), axis=0)
+    rows = mask.shape[1] // H
+    total = masked[:, :LANES]
+    for i in range(1, H * rows // LANES):
+        total = total + masked[:, i * LANES : (i + 1) * LANES]
+    joined = total[:, :rows]
+    for i in range(1, LANES // rows):
+        joined = joined + total[:, i * rows : (i + 1) * rows]
+    return jnp.transpose(joined)
 
 
 def row_forward(n_res, seq_mask, *refs):
     sent = refs[:n_res]
     own, cotangent, bias, gains, w_row, w_out = refs[n_res : n_res + 6]
-    payload, exponent_out, unit_out, own_unit_out, memory_out, query_gate_out, mixture_out, inverse_out, gathered = refs[n_res + 6 :]
+    (payload, exponent_out, unit_out, own_unit_out, memory_out, query_gate_out, mixture_out, inverse_out,
+     gathered) = refs[n_res + 6 :]
     n_seq, n_rows, _ = own.shape
     me = lax.axis_index("res")
     for away in range(n_res):
@@ -84,11 +95,10 @@
     gain = gains[0:1, :]
     w_all = w_row[...]
     w_query_gate = jnp.concatenate([w_all[:, :C], w_all[:, 3 * C :]], axis=1)
-    present_keys = jnp.concatenate([gathered[i, n_seq, 0:1, :n_rows] for i in range(n_res)], axis=1)
-    key_bias = MASKED * (present_keys - 1.0)
-    bias_rows = bias[...].reshape(H * n_rows, n_keys).astype(F32)
+    key_bias = MASKED * (gathered[:, n_seq].reshape(n_keys, C)[:, 0:1] - 1.0)
+    bias_t = jnp.transpose(bias[...].reshape(H * n_rows, n_keys).astype(F32))
     mask = head_mask(n_rows)
-    wide_mask = jnp.concatenate([mask, mask], axis=1)
+    wide_mask = jnp.concatenate([mask, mask], axis=0)
     units = jnp.concatenate([gathered[:, s].reshape(n_keys, C) for s in range(n_seq)], axis=0)
     units, _ = normalise(units)
     memories = dot(units * gain, w_all[:, C : 3 * C], precision=EXACT)
@@ -105,10 +115,10 @@
     for s in range(n_seq):
         memory = memories[s * n_keys : (s + 1) * n_keys]
         query = queries[s * n_rows : (s + 1) * n_rows]
-        scores = dot_t(spread_heads(query, mask), memory[:, :C], EXACT) + bias_rows + key_bias
-        exponent = jnp.exp(scores - jnp.max(scores, axis=-1, keepdims=True))
+        scores = dot(memory[:, :C], spread_heads(query, mask), precision=EXACT) + bias_t + key_bias
+        exponent = jnp.exp(scores - jnp.max(scores, axis=0, keepdims=True))
         exponent_out[s] = exponent
-        summed = dot(exponent, jnp.concatenate([memory[:, C:], jnp.ones((n_keys, C), F32)], axis=1))
+        summed = dot_rows(jnp.concatenate([memory[:, C:], jnp.ones((n_keys, C), F32)], axis=1), exponent)
         sums.append(join_heads(summed, wide_mask))
     summed = jnp.concatenate(sums, axis=0)
     inverse = 1.0 / summed[:, C:]
@@ -240,7 +250,7 @@
     grad_gates = grad_gated * mixtures * gates * (1.0 - gates)
     grad_mixtures = grad_gated * gates * inverse_in[...].reshape(n_seq * n_rows, C)
     inners = grad_mixtures * mixtures
-    bias_grad = jnp.zeros((H * n_rows, n_keys), F32)
+    bias_grad = jnp.zeros((n_keys, H * n_rows), F32)
     grad_queries = []
     grad_memories = []
     for s in range(n_seq):
@@ -249,13 +259,13 @@
         exponent = exponent_in[s]
         grad_heads = spread_heads(grad_mixtures[rows], mask)
         query_heads = spread_heads(queries_gates[rows, :C], mask)
-        left = jnp.concatenate([grad_heads, spread_heads(inners[rows], mask)], axis=1)
-        right = jnp.concatenate([memory[:, C:], jnp.full((n_keys, C), -1.0, F32)], axis=1)
-        grad_scores = exponent * dot_t(left, right)
+        right = jnp.concatenate([grad_heads, spread_heads(inners[rows], mask)], axis=0)
+        left = jnp.concatenate([memory[:, C:], jnp.full((n_keys, C), -1.0, F32)], axis=1)
+        grad_scores = exponent * dot(left, right)
         bias_grad = bias_grad + grad_scores
-        grad_queries.append(join_heads(dot(grad_scores, memory[:, :C]), mask) * SCALE)
-        grad_key = dot_rows(grad_scores, query_heads)
-        grad_value = dot_rows(exponent, grad_heads)
+        grad_queries.append(join_heads(dot_rows(memory[:, :C], grad_scores), mask) * SCALE)
+        grad_key = dot_t(grad_scores, query_heads)
+        grad_value = dot_t(exponent, grad_heads)
         grad_memories.append(jnp.concatenate([grad_key, grad_value], axis=1))
     grad_query_gate = jnp.concatenate([jnp.concatenate(grad_queries, axis=0), grad_gates], axis=1)
     grad_memory = jnp.concatenate(grad_memories, axis=0)
@@ -265,7 +275,7 @@
     from_own = dot_t(grad_query_gate, w_query_gate)
     from_memory = [from_memory[s * n_keys : (s + 1) * n_keys] for s in range(n_seq)]
     from_own = [from_own[s * n_rows : (s + 1) * n_rows] for s in range(n_seq)]
-    bias_t[...] = jnp.transpose(bias_grad)
+    bias_t[...] = bias_grad
     split_blocks(bias_t, state, send)
 
     half = C // 2
@@ -474,14 +484,13 @@
     block = n_rows // seq_count
     group = n_seq * block
     away_range = range(1, res_count)
-    present_keys = jnp.pad(residue_mask.astype(F32), (0, C - n_rows))
-    present_keys = jnp.broadcast_to(present_keys[None, None, :], (1, n_rows, C))
+    present_keys = jnp.broadcast_to(residue_mask.astype(F32)[None, :, None], (1, n_rows, C))
     sent = jnp.concatenate([alignment.astype(F32), present_keys], axis=0)
     payload, exponent, unit, own_unit, memory, query_gate, mixture, inverse = call(
         functools.partial(row_forward, res_count),
         [
             ((seq_count, n_seq + 1, block, 2 * C), F32),
-            ((n_seq, H * n_rows, n_keys), F32),
+            ((n_seq, n_keys, H * n_rows), F32),
             ((n_seq, n_keys, C), F32),
             ((n_seq, n_rows, C), F32),
             ((n_seq, n_keys, 2 * C), F32),
@@ -492,7 +501,9 @@
         sequence_mask, sent, *[shift_residues(sent, away, res_count) for away in away_range],
         alignment, cotangent, pair_bias, norm_gains, row_project, row_output,
         smem=1,
-        scratch=[pltpu.VMEM((res_count, n_seq + 1, n_rows, C), F32)],
+        scratch=[
+            pltpu.VMEM((res_count, n_seq + 1, n_rows, C), F32),
+        ],
         name="row_forward",
     )
     arrived = swap_blocks(payload)

time: 62.2 us -> 61.9 us (level)
  no operation moved by 1% of the time
where the time goes in v7:
time: 61.9 us; the launch traced here: 61.6 us
  blocking collectives  26.1 us (42%)
  waiting for transfers between devices  19.6 us (32%)
  Pallas kernels  9.55 us (15%)
  starting transfers between devices  4.07 us (7%)
  other arithmetic  1.44 us (2%)
  between operations  0.75 us (1%)
    all_to_all x2, blocking collectives, swap_blocks(): return lax.all_to_all(values, 'seq', 0, 0, tiled=True)  26.1 us
    ppermute x4, waiting for transfers between devices, cross(): return lax.ppermute(values, ('seq', 'res'), pairs)  16.9 us
    pallas_call x11, Pallas kernels, call(): pl.pallas_call(body, out_shape=[jax.ShapeDtypeStruct(shape, kind) for sha...  9.55 us
    ppermute x4, starting transfers between devices, cross(): return lax.ppermute(values, ('seq', 'res'), pairs)  3.41 us
    ppermute x3, waiting for transfers between devices, shift_residues(): lax.ppermute(values, 'res', [((i + away) % count, i) for i in range(count)])  2.72 us
  transfers between devices with their start and end apart: 7, of which 7 were waited for; matrix products, arithmetic and copies ran while one was open for 0% of the time, Pallas kernels for 3%

profile of v7, /device:TPU:0, one launch (start us, length us, event | category | flops | bytes accessed | tf_op | source)
XLA Modules:
  0.0 61.6 jit_solution(17939525700044869231)
XLA Ops:
  0.6 0.7 %convert_element_type.7 = f32[64]{0:T(128)S(1)} convert(s32[64]{0:T(128)} %param.18) | non-fusion elementwise | flops 64 | bytes 512 | tf_op jit(solution)/shard_map/convert_element_type | solution.py:487
  1.3 0.8 %convert_element_type.6 = f32[2,64,64]{2,1,0:T(8,128)S(1)} convert(bf16[2,64,64]{2,1,0:T(8,128)(2,1)} %own.1) | non-fusion elementwise | flops 8192 | bytes 49152 | tf_op jit(solution)/shard_map/convert_element_type | solution.py:488
  2.2 0.5 collective-permute-start
  2.7 0.9 %collective-permute-done.refs_1_ = f32[3,64,64]{2,1,0:T(8,128)S(1)} collective-permute-done((f32[3,64,64]{2,1,0:T(8,128)S(1)}, f32[3,64,64]{2,1,0:T(8,128)S(1)}, u32[]{:S(2)}, u32[]{:S(2)}) %collective-permute-start) | collective-permute-done | bytes 49184 | tf_op jit(solution)/shard_map/ppermute | solution.py:453
  3.7 2.9 %row_forward.1 = (f32[16,3,4,128]{3,2,1,0:T(4,128)S(1)}, f32[2,128,512]{2,1,0:T(8,128)S(1)}, f32[2,128,64]{2,1,0:T(8,128)S(1)}, f32[2,64,64]{2,1,0:T(8,128)S(1)}...) custom-call(s32[2]{0:T(128)S(1)} %copy-done.8, ...), custom_call_target="tpu_custom_call" | custom-call | tf_op jit(solution)/shard_map/row_forward/pallas_call | solution.py:440
  6.6 15.8 %all_to_all.10.arrived = f32[16,3,4,128]{3,2,1,0:T(4,128)S(1)} all-to-all(f32[16,3,4,128]{3,2,1,0:T(4,128)S(1)} %get-tuple-element.37), channel_id=1, replica_groups=mesh['seq'=16,'res'=2] {'seq'}, dimensions={0} | all-to-all | bytes 196608 | tf_op jit(solution)/shard_map/all_to_all | solution.py:465
  22.4 1.7 %column_step.1 = f32[16,3,4,128]{3,2,1,0:T(4,128)S(1)} custom-call(f32[16,3,4,128]{3,2,1,0:T(4,128)S(1)} %all_to_all.10.arrived, f32[2,64]{1,0:T(2,128)S(1)} %copy-done.7, f32[64,144]{1,0:T(8,128)S(1)} %copy-done.2, f32[64,64]{1,0:T(8,128)S(1)} %copy-done.6), custom_call_target="tpu_custom_call" | custom-call | tf_op jit(solution)/shard_map/column_step/pallas_call | solution.py:440
  24.1 10.3 %all_to_all.11.returned = f32[16,3,4,128]{3,2,1,0:T(4,128)S(1)} all-to-all(f32[16,3,4,128]{3,2,1,0:T(4,128)S(1)} %column_step.1), channel_id=1, replica_groups=mesh['seq'=16,'res'=2] {'seq'}, dimensions={0} | all-to-all | bytes 196608 | tf_op jit(solution)/shard_map/all_to_all | solution.py:465
  34.3 2.0 %row_backward.1 = (f32[32,8,128]{2,1,0:T(8,128)S(1)}, f32[32,8,128]{2,1,0:T(8,128)S(1)}, f32[2,64,64]{2,1,0:T(8,128)S(1)}, f32[152,128]{1,0:T(8,128)S(1)}, f32[152,128]{1,0:T(8,128)S(1)}) custom-call(f32[16,3,4,128]{3,2,1,0:T(4,128)S(1)} %all_to_all.11.returned, f32[2,128,512]{2,1,0:T(8,128)S(1)} %get-tuple-element.38.exponent_in, ...), custom_call_target="tpu_custom_call" | custom-call | tf_op jit(solution)/shard_map/row_backward/pallas_call | solution.py:440
  36.4 0.1 collective-permute-start.1
  36.4 1.3 %collective-permute-done.1.refs_1_ = f32[152,128]{1,0:T(8,128)S(1)} collective-permute-done((f32[152,128]{1,0:T(8,128)S(1)}, f32[152,128]{1,0:T(8,128)S(1)}, u32[]{:S(2)}, u32[]{:S(2)}) %collective-permute-start.1) | collective-permute-done | bytes 77856 | tf_op jit(solution)/shard_map/ppermute | solution.py:453
  37.7 1.0 %collective-permute-start.2 = (f32[43,8,128]{2,1,0:T(8,128)S(1)}, f32[43,8,128]{2,1,0:T(8,128)S(1)}, u32[]{:S(2)}, u32[]{:S(2)}) collective-permute-start(f32[43,8,128]{2,1,0:T(8,128)S(1)} %get-tuple-element.52.sent), channel_id=1, source_target_pairs={{0,2},{2,0},{4,6},{6,4},{8,10},{10,8},{12,14},{14,12},{16,18},{18,... | collective-permute-start | bytes 528392 | tf_op jit(solution)/shard_map/ppermute | solution.py:461
  38.7 4.5 %collective-permute-done.2.arrived = f32[43,8,128]{2,1,0:T(8,128)S(1)} collective-permute-done((f32[43,8,128]{2,1,0:T(8,128)S(1)}, f32[43,8,128]{2,1,0:T(8,128)S(1)}, u32[]{:S(2)}, u32[]{:S(2)}) %collective-permute-start.2) | collective-permute-done | bytes 176160 | tf_op jit(solution)/shard_map/ppermute | solution.py:461
  43.3 0.7 %collective-permute-start.3 = (f32[28,8,128]{2,1,0:T(8,128)S(1)}, f32[28,8,128]{2,1,0:T(8,128)S(1)}, u32[]{:S(2)}, u32[]{:S(2)}) collective-permute-start(f32[28,8,128]{2,1,0:T(8,128)S(1)} %get-tuple-element.54.sent), channel_id=1, source_target_pairs={{0,4},{2,6},{4,0},{6,2},{8,12},{10,14},{12,8},{14,10},{16,20},{18,... | collective-permute-start | bytes 344072 | tf_op jit(solution)/shard_map/ppermute | solution.py:461
  44.0 4.1 %collective-permute-done.3.arrived = f32[28,8,128]{2,1,0:T(8,128)S(1)} collective-permute-done((f32[28,8,128]{2,1,0:T(8,128)S(1)}, f32[28,8,128]{2,1,0:T(8,128)S(1)}, u32[]{:S(2)}, u32[]{:S(2)}) %collective-permute-start.3) | collective-permute-done | bytes 114720 | tf_op jit(solution)/shard_map/ppermute | solution.py:461
  48.1 0.8 %collective-permute-start.4 = (f32[22,8,128]{2,1,0:T(8,128)S(1)}, f32[22,8,128]{2,1,0:T(8,128)S(1)}, u32[]{:S(2)}, u32[]{:S(2)}) collective-permute-start(f32[22,8,128]{2,1,0:T(8,128)S(1)} %get-tuple-element.56.sent), channel_id=1, source_target_pairs={{0,8},{2,10},{4,12},{6,14},{8,0},{10,2},{12,4},{14,6},{16,24},{18,... | collective-permute-start | bytes 270344 | tf_op jit(solution)/shard_map/ppermute | solution.py:461
  48.9 3.8 %collective-permute-done.4.arrived = f32[22,8,128]{2,1,0:T(8,128)S(1)} collective-permute-done((f32[22,8,128]{2,1,0:T(8,128)S(1)}, f32[22,8,128]{2,1,0:T(8,128)S(1)}, u32[]{:S(2)}, u32[]{:S(2)}) %collective-permute-start.4) | collective-permute-done | bytes 90144 | tf_op jit(solution)/shard_map/ppermute | solution.py:461
  52.8 0.9 %collective-permute-start.5 = (f32[22,8,128]{2,1,0:T(8,128)S(1)}, f32[22,8,128]{2,1,0:T(8,128)S(1)}, u32[]{:S(2)}, u32[]{:S(2)}) collective-permute-start(f32[22,8,128]{2,1,0:T(8,128)S(1)} %get-tuple-element.58.sent), channel_id=1, source_target_pairs={{0,16},{2,18},{4,20},{6,22},{8,24},{10,26},{12,28},{14,30},{16,0},... | collective-permute-start | bytes 270344 | tf_op jit(solution)/shard_map/ppermute | solution.py:461
  53.6 1.1 %finish_alignment.1 = (bf16[2,64,64]{2,1,0:T(8,128)(2,1)}, f32[8,128]{1,0:T(8,128)S(1)}) custom-call(bf16[2,64,64]{2,1,0:T(8,128)(2,1)S(1)} %copy-done.1, f32[2,64,64]{2,1,0:T(8,128)S(1)} %get-tuple-element.45.middle_grad, f32[2,64]{1,0:T(2,128)S(1)} %copy-done.7, f32[64,128]{1,0:T(8,128)S(1)} %get-tuple-element.49.normed), custom_call_target="tpu_custom_call" | custom-call | tf_op jit(solution)/shard_map/finish_alignment/pallas_call | solution.py:440
  54.8 4.4 %collective-permute-done.5.arrived = f32[22,8,128]{2,1,0:T(8,128)S(1)} collective-permute-done((f32[22,8,128]{2,1,0:T(8,128)S(1)}, f32[22,8,128]{2,1,0:T(8,128)S(1)}, u32[]{:S(2)}, u32[]{:S(2)}) %collective-permute-start.5) | collective-permute-done | bytes 90144 | tf_op jit(solution)/shard_map/ppermute | solution.py:461
  59.2 0.1 collective-permute-start.6
  59.3 0.7 %bias_last.1 = f32[8,8,64]{2,1,0:T(8,128)} custom-call(f32[4,8,128]{2,1,0:T(8,128)S(1)} %get-tuple-element.57.state, f32[22,8,128]{2,1,0:T(8,128)S(1)} %collective-permute-done.5.arrived), custom_call_target="tpu_custom_call" | custom-call | tf_op jit(solution)/shard_map/bias_last/pallas_call | solution.py:440
  60.0 0.5 collective-permute-done.6.refs_1_
  60.5 1.1 %unpack.1 = (f32[2,64]{1,0:T(2,128)}, f32[64,256]{1,0:T(8,128)}, f32[64,64]{1,0:T(8,128)}, f32[64,144]{1,0:T(8,128)}, f32[64,64]{1,0:T(8,128)}) custom-call(f32[16,8,128]{2,1,0:T(8,128)S(1)} %get-tuple-element.60.joined, f32[10,8,128]{2,1,0:T(8,128)S(1)} %get-tuple-element.61.refs_0_, f32[10,8,128]{2,1,0:T(8,128)S(1)} %collective-permute-done.6.refs_1_, ...), custom_call_target="tpu_custom_call" | custom-call | tf_op jit(solution)/shard_map/unpack/pallas_call | solution.py:440
  (25 shorter events, 0.2 us)
Async XLA Ops:
  1.3 2.3 %copy-start.4 = (f32[64,64]{1,0:T(8,128)S(1)}, f32[64,64]{1,0:T(8,128)}, u32[]{:S(2)}) copy-start(f32[64,64]{1,0:T(8,128)} %w_out.3) | copy-start | bytes 49156
  1.3 2.3 %copy-start.5 = (bf16[2,64,64]{2,1,0:T(8,128)(2,1)S(1)}, bf16[2,64,64]{2,1,0:T(8,128)(2,1)}, u32[]{:S(2)}) copy-start(bf16[2,64,64]{2,1,0:T(8,128)(2,1)} %refs_3_.2) | copy-start | bytes 49156
  1.3 2.3 %copy-start.7 = (f32[2,64]{1,0:T(2,128)S(1)}, f32[2,64]{1,0:T(2,128)}, u32[]{:S(2)}) copy-start(f32[2,64]{1,0:T(2,128)} %refs_2_.3) | copy-start | bytes 1540
  2.1 1.6 %copy-start.3 = (bf16[8,64,128]{2,1,0:T(8,128)(2,1)S(1)}, bf16[8,64,128]{2,1,0:T(8,128)(2,1)}, u32[]{:S(2)}) copy-start(bf16[8,64,128]{2,1,0:T(8,128)(2,1)} %refs_4_.2) | copy-start | bytes 393220
  2.1 1.5 %copy-start = (f32[64,256]{1,0:T(8,128)S(1)}, f32[64,256]{1,0:T(8,128)}, u32[]{:S(2)}) copy-start(f32[64,256]{1,0:T(8,128)} %refs_3_.3) | copy-start | bytes 196612
  2.1 1.5 %copy-start.1 = (bf16[2,64,64]{2,1,0:T(8,128)(2,1)S(1)}, bf16[2,64,64]{2,1,0:T(8,128)(2,1)}, u32[]{:S(2)}) copy-start(bf16[2,64,64]{2,1,0:T(8,128)(2,1)} %own.1) | copy-start | bytes 49156
  2.1 1.5 %copy-start.8 = (s32[2]{0:T(128)S(1)}, s32[2]{0:T(128)}, u32[]{:S(2)}) copy-start(s32[2]{0:T(128)} %seq_mask.1) | copy-start | bytes 28
  2.2 1.5 %collective-permute-start = (f32[3,64,64]{2,1,0:T(8,128)S(1)}, f32[3,64,64]{2,1,0:T(8,128)S(1)}, u32[]{:S(2)}, u32[]{:S(2)}) collective-permute-start(f32[3,64,64]{2,1,0:T(8,128)S(1)} %pad_maximum_fusion.refs_0_), channel_id=1, source_target_pairs={{1,0},{0,1},{3,2},{2,3},{5,4},{4,5},{7,6},{6,7},{9,8},{8,9},{11,10... | collective-permute-start | bytes 147464 | tf_op jit(solution)/shard_map/ppermute | solution.py:453
  6.5 15.8 %copy-start.2 = (f32[64,144]{1,0:T(8,128)S(1)}, f32[64,144]{1,0:T(8,128)}, u32[]{:S(2)}) copy-start(f32[64,144]{1,0:T(8,128)} %refs_4_.3) | copy-start | bytes 110596
  6.6 15.8 %copy-start.6 = (f32[64,64]{1,0:T(8,128)S(1)}, f32[64,64]{1,0:T(8,128)}, u32[]{:S(2)}) copy-start(f32[64,64]{1,0:T(8,128)} %w_out.2) | copy-start | bytes 49156
  36.4 1.3 %collective-permute-start.1 = (f32[152,128]{1,0:T(8,128)S(1)}, f32[152,128]{1,0:T(8,128)S(1)}, u32[]{:S(2)}, u32[]{:S(2)}) collective-permute-start(f32[152,128]{1,0:T(8,128)S(1)} %get-tuple-element.48), channel_id=1, source_target_pairs={{1,0},{0,1},{3,2},{2,3},{5,4},{4,5},{7,6},{6,7},{9,8},{8,9},{11,10... | collective-permute-start | bytes 233480 | tf_op jit(solution)/shard_map/ppermute | solution.py:453
  37.7 5.5 %collective-permute-start.2 = (f32[43,8,128]{2,1,0:T(8,128)S(1)}, f32[43,8,128]{2,1,0:T(8,128)S(1)}, u32[]{:S(2)}, u32[]{:S(2)}) collective-permute-start(f32[43,8,128]{2,1,0:T(8,128)S(1)} %get-tuple-element.52.sent), channel_id=1, source_target_pairs={{0,2},{2,0},{4,6},{6,4},{8,10},{10,8},{12,14},{14,12},{16,18},{18,... | collective-permute-start | bytes 528392 | tf_op jit(solution)/shard_map/ppermute | solution.py:461
  43.3 4.9 %collective-permute-start.3 = (f32[28,8,128]{2,1,0:T(8,128)S(1)}, f32[28,8,128]{2,1,0:T(8,128)S(1)}, u32[]{:S(2)}, u32[]{:S(2)}) collective-permute-start(f32[28,8,128]{2,1,0:T(8,128)S(1)} %get-tuple-element.54.sent), channel_id=1, source_target_pairs={{0,4},{2,6},{4,0},{6,2},{8,12},{10,14},{12,8},{14,10},{16,20},{18,... | collective-permute-start | bytes 344072 | tf_op jit(solution)/shard_map/ppermute | solution.py:461
  48.1 4.6 %collective-permute-start.4 = (f32[22,8,128]{2,1,0:T(8,128)S(1)}, f32[22,8,128]{2,1,0:T(8,128)S(1)}, u32[]{:S(2)}, u32[]{:S(2)}) collective-permute-start(f32[22,8,128]{2,1,0:T(8,128)S(1)} %get-tuple-element.56.sent), channel_id=1, source_target_pairs={{0,8},{2,10},{4,12},{6,14},{8,0},{10,2},{12,4},{14,6},{16,24},{18,... | collective-permute-start | bytes 270344 | tf_op jit(solution)/shard_map/ppermute | solution.py:461
  52.8 6.5 %collective-permute-start.5 = (f32[22,8,128]{2,1,0:T(8,128)S(1)}, f32[22,8,128]{2,1,0:T(8,128)S(1)}, u32[]{:S(2)}, u32[]{:S(2)}) collective-permute-start(f32[22,8,128]{2,1,0:T(8,128)S(1)} %get-tuple-element.58.sent), channel_id=1, source_target_pairs={{0,16},{2,18},{4,20},{6,22},{8,24},{10,26},{12,28},{14,30},{16,0},... | collective-permute-start | bytes 270344 | tf_op jit(solution)/shard_map/ppermute | solution.py:461
  59.2 1.3 %collective-permute-start.6 = (f32[10,8,128]{2,1,0:T(8,128)S(1)}, f32[10,8,128]{2,1,0:T(8,128)S(1)}, u32[]{:S(2)}, u32[]{:S(2)}) collective-permute-start(f32[10,8,128]{2,1,0:T(8,128)S(1)} %get-tuple-element.61.refs_0_), channel_id=1, source_target_pairs={{1,0},{0,1},{3,2},{2,3},{5,4},{4,5},{7,6},{6,7},{9,8},{8,9},{11,10... | collective-permute-start | bytes 122888 | tf_op jit(solution)/shard_map/ppermute | solution.py:453

commit v8 on v7

--- a/solution.py
+++ b/solution.py
@@ -80,42 +80,62 @@
     return jnp.transpose(joined)
 
 
-def row_forward(n_res, seq_mask, *refs):
+def own_half(seq_mask, own, bias, gains, w_row,
+             own_unit_out, query_gate_out, query_heads_out, own_memory_out, bias_out, present_out):
+    n_seq, n_rows, _ = own.shape
+    n_keys = bias.shape[2]
+    w_all = w_row[...]
+    own_units, _ = normalise(own[...].reshape(n_seq * n_rows, C).astype(F32))
+    projected = dot(own_units * gains[0:1, :], w_all, precision=EXACT)
+    queries = projected[:, :C] * SCALE
+    gates = jax.nn.sigmoid(projected[:, 3 * C :])
+    own_unit_out[...] = own_units.reshape(n_seq, n_rows, C)
+    query_gate_out[...] = jnp.concatenate([queries, gates], axis=1).reshape(n_seq, n_rows, 2 * C)
+    own_memory_out[...] = projected[:, C : 3 * C].reshape(n_seq, n_rows, 2 * C)
+    mask = head_mask(n_rows)
+    for s in range(n_seq):
+        query_heads_out[s] = spread_heads(queries[s * n_rows : (s + 1) * n_rows], mask)
+    bias_out[...] = jnp.transpose(bias[...].reshape(H * n_rows, n_keys).astype(F32))
+    lane = lax.broadcasted_iota(jnp.int32, present_out.shape, 1) // (2 * C // n_seq)
+    present = jnp.zeros(present_out.shape, F32)
+    for s in range(n_seq):
+        present = jnp.where(lane == s, seq_mask[s].astype(F32), present)
+    present_out[...] = present
+
+
+def row_forward(n_res, *refs):
     sent = refs[:n_res]
-    own, cotangent, bias, gains, w_row, w_out = refs[n_res : n_res + 6]
-    (payload, exponent_out, unit_out, own_unit_out, memory_out, query_gate_out, mixture_out, inverse_out,
-     gathered) = refs[n_res + 6 :]
+    (own, cotangent, gains, w_row, w_out, own_unit, query_gate, query_heads, own_memory, bias_t, present) = refs[
+        n_res : n_res + 11
+    ]
+    payload, exponent_out, unit_out, memory_out, mixture_out, inverse_out, residue = refs[n_res + 11 :]
     n_seq, n_rows, _ = own.shape
+    n_keys = n_res * n_rows
     me = lax.axis_index("res")
+    w_memory = w_row[:, C : 3 * C]
     for away in range(n_res):
-        gathered[lax.rem(me + away, n_res)] = sent[away][...]
-    n_keys = n_res * n_rows
+        where = lax.rem(me + away, n_res)
+        residue[where] = sent[away][n_seq]
+        if away:
+            units, _ = normalise(sent[away][:n_seq].reshape(n_seq * n_rows, C))
+            memories = dot(units * gains[0:1, :], w_memory, precision=EXACT)
+            units = units.reshape(n_seq, n_rows, C)
+            memories = memories.reshape(n_seq, n_rows, 2 * C)
+        else:
+            units, memories = own_unit[...], own_memory[...]
+        unit_out[where] = units
+        memory_out[where] = memories
     n_blocks = payload.shape[0]
     block = n_rows // n_blocks
-    gain = gains[0:1, :]
-    w_all = w_row[...]
-    w_query_gate = jnp.concatenate([w_all[:, :C], w_all[:, 3 * C :]], axis=1)
-    key_bias = MASKED * (gathered[:, n_seq].reshape(n_keys, C)[:, 0:1] - 1.0)
-    bias_t = jnp.transpose(bias[...].reshape(H * n_rows, n_keys).astype(F32))
+    key_bias = MASKED * (residue[...].reshape(n_keys, C)[:, 0:1] - 1.0)
     mask = head_mask(n_rows)
     wide_mask = jnp.concatenate([mask, mask], axis=0)
-    units = jnp.concatenate([gathered[:, s].reshape(n_keys, C) for s in range(n_seq)], axis=0)
-    units, _ = normalise(units)
-    memories = dot(units * gain, w_all[:, C : 3 * C], precision=EXACT)
     initial = own[...].reshape(n_seq * n_rows, C).astype(F32)
-    own_units, _ = normalise(initial)
-    projected = dot(own_units * gain, w_query_gate, precision=EXACT)
-    queries = projected[:, :C] * SCALE
-    gates = jax.nn.sigmoid(projected[:, C:])
-    unit_out[...] = units.reshape(n_seq, n_keys, C)
-    memory_out[...] = memories.reshape(n_seq, n_keys, 2 * C)
-    own_unit_out[...] = own_units.reshape(n_seq, n_rows, C)
-    query_gate_out[...] = jnp.concatenate([queries, gates], axis=1).reshape(n_seq, n_rows, 2 * C)
+    gates = query_gate[...].reshape(n_seq * n_rows, 2 * C)[:, C:]
     sums = []
     for s in range(n_seq):
-        memory = memories[s * n_keys : (s + 1) * n_keys]
-        query = queries[s * n_rows : (s + 1) * n_rows]
-        scores = dot(memory[:, :C], spread_heads(query, mask), precision=EXACT) + bias_t + key_bias
+        memory = memory_out[:, s].reshape(n_keys, 2 * C)
+        scores = dot(memory[:, :C], query_heads[s], precision=EXACT) + bias_t[...] + key_bias
         exponent = jnp.exp(scores - jnp.max(scores, axis=0, keepdims=True))
         exponent_out[s] = exponent
         summed = dot_rows(jnp.concatenate([memory[:, C:], jnp.ones((n_keys, C), F32)], axis=1), exponent)
@@ -131,12 +151,8 @@
         for b in range(n_blocks):
             row = s * n_rows + b * block
             payload[b, s] = both[row : row + block, :]
-    lane = lax.broadcasted_iota(jnp.int32, (block, 2 * C), 1) // (2 * C // n_seq)
-    present = jnp.zeros((block, 2 * C), F32)
-    for s in range(n_seq):
-        present = jnp.where(lane == s, seq_mask[s].astype(F32), present)
     for b in range(n_blocks):
-        payload[b, n_seq] = present
+        payload[b, n_seq] = present[...]
 
 
 def column_step(arrived, gains, w_col, w_out, returned, gathered, mask_rows, n_seq):
@@ -227,12 +243,12 @@
         returned[src, 2] = second[src * share : (src + 1) * share, :]
 
 
-def row_backward(n_res, returned, exponent_in, unit_in, memory_in, query_gate_in, mixture_in, inverse_in, own_unit_in,
-                 w_row, w_out, state, send, middle_grad, *refs):
-    sums_out, shares, bias_t = refs[:n_res], refs[n_res], refs[n_res + 1]
+def row_backward(n_res, returned, exponent_in, unit_in, memory_in, query_gate_in, query_heads_in, mixture_in, inverse_in,
+                 own_unit_in, w_row, w_out, bias_out, middle_grad, *refs):
+    sums_out, shares = refs[:n_res], refs[n_res]
     me = lax.axis_index("res")
     n_seq, n_rows, _ = middle_grad.shape
-    n_keys = memory_in.shape[1]
+    n_keys = n_res * n_rows
     n_blocks, _, block, _ = returned.shape
     w_all = w_row[...]
     w_memory = w_all[:, C : 3 * C]
@@ -255,29 +271,27 @@
     grad_memories = []
     for s in range(n_seq):
         rows = slice(s * n_rows, (s + 1) * n_rows)
-        memory = memory_in[s]
+        memory = memory_in[:, s].reshape(n_keys, 2 * C)
         exponent = exponent_in[s]
         grad_heads = spread_heads(grad_mixtures[rows], mask)
-        query_heads = spread_heads(queries_gates[rows, :C], mask)
         right = jnp.concatenate([grad_heads, spread_heads(inners[rows], mask)], axis=0)
         left = jnp.concatenate([memory[:, C:], jnp.full((n_keys, C), -1.0, F32)], axis=1)
         grad_scores = exponent * dot(left, right)
         bias_grad = bias_grad + grad_scores
         grad_queries.append(join_heads(dot_rows(memory[:, :C], grad_scores), mask) * SCALE)
-        grad_key = dot_t(grad_scores, query_heads)
+        grad_key = dot_t(grad_scores, query_heads_in[s])
         grad_value = dot_t(exponent, grad_heads)
         grad_memories.append(jnp.concatenate([grad_key, grad_value], axis=1))
     grad_query_gate = jnp.concatenate([jnp.concatenate(grad_queries, axis=0), grad_gates], axis=1)
     grad_memory = jnp.concatenate(grad_memories, axis=0)
     grad_query_gate_weights = dot_rows(own_unit_in[...].reshape(n_seq * n_rows, C), grad_query_gate)
-    grad_memory_weights = dot_rows(unit_in[...].reshape(n_seq * n_keys, C), grad_memory)
+    units = jnp.concatenate([unit_in[:, s].reshape(n_keys, C) for s in range(n_seq)], axis=0)
+    grad_memory_weights = dot_rows(units, grad_memory)
     from_memory = dot_t(grad_memory, w_memory)
     from_own = dot_t(grad_query_gate, w_query_gate)
     from_memory = [from_memory[s * n_keys : (s + 1) * n_keys] for s in range(n_seq)]
     from_own = [from_own[s * n_rows : (s + 1) * n_rows] for s in range(n_seq)]
-    bias_t[...] = bias_grad
-    split_blocks(bias_t, state, send)
-
+    bias_out[...] = bias_grad
     half = C // 2
     weight_grads = jnp.concatenate(
         [grad_query_gate_weights, grad_memory_weights, jnp.concatenate([grad_out[:half], grad_out[half:]], axis=1)],
@@ -486,24 +500,34 @@
     away_range = range(1, res_count)
     present_keys = jnp.broadcast_to(residue_mask.astype(F32)[None, :, None], (1, n_rows, C))
     sent = jnp.concatenate([alignment.astype(F32), present_keys], axis=0)
-    payload, exponent, unit, own_unit, memory, query_gate, mixture, inverse = call(
+    own_unit, query_gate, query_heads, own_memory, bias_t, present = call(
+        own_half,
+        [
+            ((n_seq, n_rows, C), F32),
+            ((n_seq, n_rows, 2 * C), F32),
+            ((n_seq, C, H * n_rows), F32),
+            ((n_seq, n_rows, 2 * C), F32),
+            ((n_keys, H * n_rows), F32),
+            ((block, 2 * C), F32),
+        ],
+        sequence_mask, alignment, pair_bias, norm_gains, row_project,
+        smem=1,
+        name="own_half",
+    )
+    payload, exponent, unit, memory, mixture, inverse = call(
         functools.partial(row_forward, res_count),
         [
             ((seq_count, n_seq + 1, block, 2 * C), F32),
             ((n_seq, n_keys, H * n_rows), F32),
-            ((n_seq, n_keys, C), F32),
-            ((n_seq, n_rows, C), F32),
-            ((n_seq, n_keys, 2 * C), F32),
-            ((n_seq, n_rows, 2 * C), F32),
+            ((res_count, n_seq, n_rows, C), F32),
+            ((res_count, n_seq, n_rows, 2 * C), F32),
             ((n_seq, n_rows, C), F32),
             ((n_seq, n_rows, C), F32),
         ],
-        sequence_mask, sent, *[shift_residues(sent, away, res_count) for away in away_range],
-        alignment, cotangent, pair_bias, norm_gains, row_project, row_output,
-        smem=1,
-        scratch=[
-            pltpu.VMEM((res_count, n_seq + 1, n_rows, C), F32),
-        ],
+        sent, *[shift_residues(sent, away, res_count) for away in away_range],
+        alignment, cotangent, norm_gains, row_project, row_output, own_unit, query_gate, query_heads, own_memory, bias_t,
+        present,
+        scratch=[pltpu.VMEM((res_count, n_rows, C), F32)],
         name="row_forward",
     )
     arrived = swap_blocks(payload)
@@ -519,19 +543,18 @@
     keys_each = n_keys // seq_count
     tiles = H * n_rows // LANES
     left = seq_count // 2 * tiles
-    state, send, middle_grad, *sums = call(
+    bias_grad, middle_grad, *sums = call(
         functools.partial(row_backward, res_count),
-        [((left, keys_each, LANES), F32)] * 2
-        + [((n_seq, n_rows, C), F32)]
+        [((n_keys, H * n_rows), F32), ((n_seq, n_rows, C), F32)]
         + [((part + ROWS + n_rows, LANES), F32)] * res_count,
-        returned, exponent, unit, memory, query_gate, mixture, inverse, own_unit, row_project, row_output,
-        scratch=[
-            pltpu.VMEM((res_count, part + ROWS + n_rows, LANES), F32),
-            pltpu.VMEM((n_keys, H * n_rows), F32),
-        ],
+        returned, exponent, unit, memory, query_gate, query_heads, mixture, inverse, own_unit, row_project, row_output,
+        scratch=[pltpu.VMEM((res_count, part + ROWS + n_rows, LANES), F32)],
         name="row_backward",
     )
     sums = sums[:1] + [shift_residues(sums[away], -away, res_count) for away in away_range]
+    state, send = call(
+        split_blocks, [((left, keys_each, LANES), F32)] * 2, bias_grad, name="split_blocks"
+    )
     part_tiles = part // ROWS
     send, normed = call(
         add_shares,

time: 61.9 us -> 61.8 us (level)
  waiting for transfers between devices: 19.6 us -> 18.6 us
    ppermute x3, waiting for transfers between devices: 2.72 us -> 1.73 us  [shift_residues(): lax.ppermute(values, 'res', [((i + away) % count, i) for i in range(count)])]
    pallas_call x11 -> x13, Pallas kernels: 9.55 us -> 10 us  [call(): pl.pallas_call(body, out_shape=[jax.ShapeDtypeStruct(shape, kind) for sha...]
  transfers between devices with their start and end apart: 7 -> 7, of which waited for: 7 -> 6; matrix products, arithmetic and copies ran while one was open for 0% -> 0% of each run, Pallas kernels for 3% -> 5%
where the time goes in v8:
time: 61.8 us; the launch traced here: 61.5 us
  blocking collectives  26.2 us (42%)
  waiting for transfers between devices  18.6 us (30%)
  Pallas kernels  10 us (16%)
  starting transfers between devices  4.1 us (7%)
  other arithmetic  1.45 us (2%)
  between operations  0.76 us (1%)
    all_to_all x2, blocking collectives, swap_blocks(): return lax.all_to_all(values, 'seq', 0, 0, tiled=True)  26.2 us
    ppermute x4, waiting for transfers between devices, cross(): return lax.ppermute(values, ('seq', 'res'), pairs)  16.9 us
    pallas_call x13, Pallas kernels, call(): pl.pallas_call(body, out_shape=[jax.ShapeDtypeStruct(shape, kind) for sha...  10 us
    ppermute x4, starting transfers between devices, cross(): return lax.ppermute(values, ('seq', 'res'), pairs)  3.44 us
    ppermute x3, waiting for transfers between devices, shift_residues(): lax.ppermute(values, 'res', [((i + away) % count, i) for i in range(count)])  1.73 us
  transfers between devices with their start and end apart: 7, of which 6 were waited for; matrix products, arithmetic and copies ran while one was open for 0% of the time, Pallas kernels for 5%

profile of v8, /device:TPU:0, one launch (start us, length us, event | category | flops | bytes accessed | tf_op | source)
XLA Modules:
  0.0 61.5 jit_solution(13720781262403771884)
XLA Ops:
  0.6 0.7 %convert_element_type.7 = f32[64]{0:T(128)S(1)} convert(s32[64]{0:T(128)} %param.18) | non-fusion elementwise | flops 64 | bytes 512 | tf_op jit(solution)/shard_map/convert_element_type | solution.py:501
  1.3 0.8 %convert_element_type.6 = f32[2,64,64]{2,1,0:T(8,128)S(1)} convert(bf16[2,64,64]{2,1,0:T(8,128)(2,1)} %own.3) | non-fusion elementwise | flops 8192 | bytes 49152 | tf_op jit(solution)/shard_map/convert_element_type | solution.py:502
  2.2 0.5 collective-permute-start
  2.7 0.3 copy-done.4
  3.0 1.2 %own_half.1 = (f32[2,64,64]{2,1,0:T(8,128)S(1)}, f32[2,64,128]{2,1,0:T(8,128)S(1)}, f32[2,64,512]{2,1,0:T(8,128)S(1)}, f32[2,64,128]{2,1,0:T(8,128)S(1)}, f32[128,512]{1,0:T(8,128)S(1)}, /*index=5*/f32[4,128]{1,0:T(4,128)S(1)}) custom-call(s32[2]{0:T(128)S(1)} %copy-done.8, bf16[2,64,64]{2,1,0:T(8,128)(2,1)S(1)} %copy-done.1, ...), custom_call_target="tpu_custom_call" | custom-call | tf_op jit(solution)/shard_map/own_half/pallas_call | solution.py:454
  4.2 2.1 %row_forward.1 = (f32[16,3,4,128]{3,2,1,0:T(4,128)S(1)}, f32[2,128,512]{2,1,0:T(8,128)S(1)}, f32[2,2,64,64]{3,2,1,0:T(8,128)S(1)}, f32[2,2,64,128]{3,2,1,0:T(8,1...) custom-call(f32[3,64,64]{2,1,0:T(8,128)S(1)} %pad_maximum_fusion.refs_0_, ...), custom_call_target="tpu_custom_call" | custom-call | tf_op jit(solution)/shard_map/row_forward/pallas_call | solution.py:454
  6.4 15.9 %all_to_all.10.arrived = f32[16,3,4,128]{3,2,1,0:T(4,128)S(1)} all-to-all(f32[16,3,4,128]{3,2,1,0:T(4,128)S(1)} %get-tuple-element.48), channel_id=1, replica_groups=mesh['seq'=16,'res'=2] {'seq'}, dimensions={0} | all-to-all | bytes 196608 | tf_op jit(solution)/shard_map/all_to_all | solution.py:479
  22.3 1.7 %column_step.1 = f32[16,3,4,128]{3,2,1,0:T(4,128)S(1)} custom-call(f32[16,3,4,128]{3,2,1,0:T(4,128)S(1)} %all_to_all.10.arrived, f32[2,64]{1,0:T(2,128)S(1)} %copy-done.7, f32[64,144]{1,0:T(8,128)S(1)} %copy-done.2, f32[64,64]{1,0:T(8,128)S(1)} %copy-done.6), custom_call_target="tpu_custom_call" | custom-call | tf_op jit(solution)/shard_map/column_step/pallas_call | solution.py:454
  24.0 10.3 %all_to_all.11.returned = f32[16,3,4,128]{3,2,1,0:T(4,128)S(1)} all-to-all(f32[16,3,4,128]{3,2,1,0:T(4,128)S(1)} %column_step.1), channel_id=1, replica_groups=mesh['seq'=16,'res'=2] {'seq'}, dimensions={0} | all-to-all | bytes 196608 | tf_op jit(solution)/shard_map/all_to_all | solution.py:479
  34.2 2.0 %row_backward.1 = (f32[128,512]{1,0:T(8,128)S(1)}, f32[2,64,64]{2,1,0:T(8,128)S(1)}, f32[152,128]{1,0:T(8,128)S(1)}, f32[152,128]{1,0:T(8,128)S(1)}) custom-call(f32[16,3,4,128]{3,2,1,0:T(4,128)S(1)} %all_to_all.11.returned, f32[2,128,512]{2,1,0:T(8,128)S(1)} %get-tuple-element.49.exponent_in, f32[2,2,64,64]{3,2,1,0:T(8,128)S(1)} %get-tuple-element.50.unit_in, ...), custom_call_target="tpu_custom_call" | custom-call | tf_op jit(solution)/shard_map/row_backward/pallas_call | solution.py:454
  36.4 1.2 %collective-permute-done.1.refs_1_ = f32[152,128]{1,0:T(8,128)S(1)} collective-permute-done((f32[152,128]{1,0:T(8,128)S(1)}, f32[152,128]{1,0:T(8,128)S(1)}, u32[]{:S(2)}, u32[]{:S(2)}) %collective-permute-start.1) | collective-permute-done | bytes 77856 | tf_op jit(solution)/shard_map/ppermute | solution.py:467
  37.6 1.0 %collective-permute-start.2 = (f32[43,8,128]{2,1,0:T(8,128)S(1)}, f32[43,8,128]{2,1,0:T(8,128)S(1)}, u32[]{:S(2)}, u32[]{:S(2)}) collective-permute-start(f32[43,8,128]{2,1,0:T(8,128)S(1)} %get-tuple-element.62.sent), channel_id=1, source_target_pairs={{0,2},{2,0},{4,6},{6,4},{8,10},{10,8},{12,14},{14,12},{16,18},{18,... | collective-permute-start | bytes 528392 | tf_op jit(solution)/shard_map/ppermute | solution.py:475
  38.7 4.5 %collective-permute-done.2.arrived = f32[43,8,128]{2,1,0:T(8,128)S(1)} collective-permute-done((f32[43,8,128]{2,1,0:T(8,128)S(1)}, f32[43,8,128]{2,1,0:T(8,128)S(1)}, u32[]{:S(2)}, u32[]{:S(2)}) %collective-permute-start.2) | collective-permute-done | bytes 176160 | tf_op jit(solution)/shard_map/ppermute | solution.py:475
  43.2 0.8 %collective-permute-start.3 = (f32[28,8,128]{2,1,0:T(8,128)S(1)}, f32[28,8,128]{2,1,0:T(8,128)S(1)}, u32[]{:S(2)}, u32[]{:S(2)}) collective-permute-start(f32[28,8,128]{2,1,0:T(8,128)S(1)} %get-tuple-element.64.sent), channel_id=1, source_target_pairs={{0,4},{2,6},{4,0},{6,2},{8,12},{10,14},{12,8},{14,10},{16,20},{18,... | collective-permute-start | bytes 344072 | tf_op jit(solution)/shard_map/ppermute | solution.py:475
  43.9 4.1 %collective-permute-done.3.arrived = f32[28,8,128]{2,1,0:T(8,128)S(1)} collective-permute-done((f32[28,8,128]{2,1,0:T(8,128)S(1)}, f32[28,8,128]{2,1,0:T(8,128)S(1)}, u32[]{:S(2)}, u32[]{:S(2)}) %collective-permute-start.3) | collective-permute-done | bytes 114720 | tf_op jit(solution)/shard_map/ppermute | solution.py:475
  48.1 0.8 %collective-permute-start.4 = (f32[22,8,128]{2,1,0:T(8,128)S(1)}, f32[22,8,128]{2,1,0:T(8,128)S(1)}, u32[]{:S(2)}, u32[]{:S(2)}) collective-permute-start(f32[22,8,128]{2,1,0:T(8,128)S(1)} %get-tuple-element.66.sent), channel_id=1, source_target_pairs={{0,8},{2,10},{4,12},{6,14},{8,0},{10,2},{12,4},{14,6},{16,24},{18,... | collective-permute-start | bytes 270344 | tf_op jit(solution)/shard_map/ppermute | solution.py:475
  48.8 3.8 %collective-permute-done.4.arrived = f32[22,8,128]{2,1,0:T(8,128)S(1)} collective-permute-done((f32[22,8,128]{2,1,0:T(8,128)S(1)}, f32[22,8,128]{2,1,0:T(8,128)S(1)}, u32[]{:S(2)}, u32[]{:S(2)}) %collective-permute-start.4) | collective-permute-done | bytes 90144 | tf_op jit(solution)/shard_map/ppermute | solution.py:475
  52.7 0.9 %collective-permute-start.5 = (f32[22,8,128]{2,1,0:T(8,128)S(1)}, f32[22,8,128]{2,1,0:T(8,128)S(1)}, u32[]{:S(2)}, u32[]{:S(2)}) collective-permute-start(f32[22,8,128]{2,1,0:T(8,128)S(1)} %get-tuple-element.68.sent), channel_id=1, source_target_pairs={{0,16},{2,18},{4,20},{6,22},{8,24},{10,26},{12,28},{14,30},{16,0},... | collective-permute-start | bytes 270344 | tf_op jit(solution)/shard_map/ppermute | solution.py:475
  53.6 1.1 %finish_alignment.1 = (bf16[2,64,64]{2,1,0:T(8,128)(2,1)}, f32[8,128]{1,0:T(8,128)S(1)}) custom-call(bf16[2,64,64]{2,1,0:T(8,128)(2,1)S(1)} %copy-done.1, f32[2,64,64]{2,1,0:T(8,128)S(1)} %get-tuple-element.54.middle_grad, f32[2,64]{1,0:T(2,128)S(1)} %copy-done.7, f32[64,128]{1,0:T(8,128)S(1)} %get-tuple-element.59.normed), custom_call_target="tpu_custom_call" | custom-call | tf_op jit(solution)/shard_map/finish_alignment/pallas_call | solution.py:454
  54.7 4.4 %collective-permute-done.5.arrived = f32[22,8,128]{2,1,0:T(8,128)S(1)} collective-permute-done((f32[22,8,128]{2,1,0:T(8,128)S(1)}, f32[22,8,128]{2,1,0:T(8,128)S(1)}, u32[]{:S(2)}, u32[]{:S(2)}) %collective-permute-start.5) | collective-permute-done | bytes 90144 | tf_op jit(solution)/shard_map/ppermute | solution.py:475
  59.1 0.1 collective-permute-start.6
  59.2 0.7 %bias_last.1 = f32[8,8,64]{2,1,0:T(8,128)} custom-call(f32[4,8,128]{2,1,0:T(8,128)S(1)} %get-tuple-element.67.state, f32[22,8,128]{2,1,0:T(8,128)S(1)} %collective-permute-done.5.arrived), custom_call_target="tpu_custom_call" | custom-call | tf_op jit(solution)/shard_map/bias_last/pallas_call | solution.py:454
  59.9 0.5 collective-permute-done.6.refs_1_
  60.4 1.1 %unpack.1 = (f32[2,64]{1,0:T(2,128)}, f32[64,256]{1,0:T(8,128)}, f32[64,64]{1,0:T(8,128)}, f32[64,144]{1,0:T(8,128)}, f32[64,64]{1,0:T(8,128)}) custom-call(f32[16,8,128]{2,1,0:T(8,128)S(1)} %get-tuple-element.70.joined, f32[10,8,128]{2,1,0:T(8,128)S(1)} %get-tuple-element.71.refs_0_, f32[10,8,128]{2,1,0:T(8,128)S(1)} %collective-permute-done.6.refs_1_, ...), custom_call_target="tpu_custom_call" | custom-call | tf_op jit(solution)/shard_map/unpack/pallas_call | solution.py:454
  (27 shorter events, 0.3 us)
Async XLA Ops:
  1.3 1.4 %copy-start.7 = (f32[2,64]{1,0:T(2,128)S(1)}, f32[2,64]{1,0:T(2,128)}, u32[]{:S(2)}) copy-start(f32[2,64]{1,0:T(2,128)} %refs_2_.3) | copy-start | bytes 1540
  2.1 0.9 %copy-start.4 = (bf16[8,64,128]{2,1,0:T(8,128)(2,1)S(1)}, bf16[8,64,128]{2,1,0:T(8,128)(2,1)}, u32[]{:S(2)}) copy-start(bf16[8,64,128]{2,1,0:T(8,128)(2,1)} %bias.1) | copy-start | bytes 393220
  2.1 0.9 %copy-start = (f32[64,256]{1,0:T(8,128)S(1)}, f32[64,256]{1,0:T(8,128)}, u32[]{:S(2)}) copy-start(f32[64,256]{1,0:T(8,128)} %refs_3_.3) | copy-start | bytes 196612
  2.1 0.9 %copy-start.1 = (bf16[2,64,64]{2,1,0:T(8,128)(2,1)S(1)}, bf16[2,64,64]{2,1,0:T(8,128)(2,1)}, u32[]{:S(2)}) copy-start(bf16[2,64,64]{2,1,0:T(8,128)(2,1)} %own.3) | copy-start | bytes 49156
  2.1 0.9 %copy-start.8 = (s32[2]{0:T(128)S(1)}, s32[2]{0:T(128)}, u32[]{:S(2)}) copy-start(s32[2]{0:T(128)} %seq_mask.1) | copy-start | bytes 28
  2.2 2.0 %collective-permute-start = (f32[3,64,64]{2,1,0:T(8,128)S(1)}, f32[3,64,64]{2,1,0:T(8,128)S(1)}, u32[]{:S(2)}, u32[]{:S(2)}) collective-permute-start(f32[3,64,64]{2,1,0:T(8,128)S(1)} %pad_maximum_fusion.refs_0_), channel_id=1, source_target_pairs={{1,0},{0,1},{3,2},{2,3},{5,4},{4,5},{7,6},{6,7},{9,8},{8,9},{11,10... | collective-permute-start | bytes 147464 | tf_op jit(solution)/shard_map/ppermute | solution.py:467
  3.0 1.2 %copy-start.3 = (f32[64,64]{1,0:T(8,128)S(1)}, f32[64,64]{1,0:T(8,128)}, u32[]{:S(2)}) copy-start(f32[64,64]{1,0:T(8,128)} %w_out.3) | copy-start | bytes 49156
  3.0 1.2 %copy-start.5 = (bf16[2,64,64]{2,1,0:T(8,128)(2,1)S(1)}, bf16[2,64,64]{2,1,0:T(8,128)(2,1)}, u32[]{:S(2)}) copy-start(bf16[2,64,64]{2,1,0:T(8,128)(2,1)} %refs_3_.2) | copy-start | bytes 49156
  6.4 15.9 %copy-start.2 = (f32[64,144]{1,0:T(8,128)S(1)}, f32[64,144]{1,0:T(8,128)}, u32[]{:S(2)}) copy-start(f32[64,144]{1,0:T(8,128)} %refs_4_.3) | copy-start | bytes 110596
  6.4 15.9 %copy-start.6 = (f32[64,64]{1,0:T(8,128)S(1)}, f32[64,64]{1,0:T(8,128)}, u32[]{:S(2)}) copy-start(f32[64,64]{1,0:T(8,128)} %w_out.2) | copy-start | bytes 49156
  36.3 1.3 %collective-permute-start.1 = (f32[152,128]{1,0:T(8,128)S(1)}, f32[152,128]{1,0:T(8,128)S(1)}, u32[]{:S(2)}, u32[]{:S(2)}) collective-permute-start(f32[152,128]{1,0:T(8,128)S(1)} %get-tuple-element.58), channel_id=1, source_target_pairs={{1,0},{0,1},{3,2},{2,3},{5,4},{4,5},{7,6},{6,7},{9,8},{8,9},{11,10... | collective-permute-start | bytes 233480 | tf_op jit(solution)/shard_map/ppermute | solution.py:467
  37.6 5.5 %collective-permute-start.2 = (f32[43,8,128]{2,1,0:T(8,128)S(1)}, f32[43,8,128]{2,1,0:T(8,128)S(1)}, u32[]{:S(2)}, u32[]{:S(2)}) collective-permute-start(f32[43,8,128]{2,1,0:T(8,128)S(1)} %get-tuple-element.62.sent), channel_id=1, source_target_pairs={{0,2},{2,0},{4,6},{6,4},{8,10},{10,8},{12,14},{14,12},{16,18},{18,... | collective-permute-start | bytes 528392 | tf_op jit(solution)/shard_map/ppermute | solution.py:475
  43.2 4.9 %collective-permute-start.3 = (f32[28,8,128]{2,1,0:T(8,128)S(1)}, f32[28,8,128]{2,1,0:T(8,128)S(1)}, u32[]{:S(2)}, u32[]{:S(2)}) collective-permute-start(f32[28,8,128]{2,1,0:T(8,128)S(1)} %get-tuple-element.64.sent), channel_id=1, source_target_pairs={{0,4},{2,6},{4,0},{6,2},{8,12},{10,14},{12,8},{14,10},{16,20},{18,... | collective-permute-start | bytes 344072 | tf_op jit(solution)/shard_map/ppermute | solution.py:475
  48.1 4.6 %collective-permute-start.4 = (f32[22,8,128]{2,1,0:T(8,128)S(1)}, f32[22,8,128]{2,1,0:T(8,128)S(1)}, u32[]{:S(2)}, u32[]{:S(2)}) collective-permute-start(f32[22,8,128]{2,1,0:T(8,128)S(1)} %get-tuple-element.66.sent), channel_id=1, source_target_pairs={{0,8},{2,10},{4,12},{6,14},{8,0},{10,2},{12,4},{14,6},{16,24},{18,... | collective-permute-start | bytes 270344 | tf_op jit(solution)/shard_map/ppermute | solution.py:475
  52.7 6.5 %collective-permute-start.5 = (f32[22,8,128]{2,1,0:T(8,128)S(1)}, f32[22,8,128]{2,1,0:T(8,128)S(1)}, u32[]{:S(2)}, u32[]{:S(2)}) collective-permute-start(f32[22,8,128]{2,1,0:T(8,128)S(1)} %get-tuple-element.68.sent), channel_id=1, source_target_pairs={{0,16},{2,18},{4,20},{6,22},{8,24},{10,26},{12,28},{14,30},{16,0},... | collective-permute-start | bytes 270344 | tf_op jit(solution)/shard_map/ppermute | solution.py:475
  59.1 1.3 %collective-permute-start.6 = (f32[10,8,128]{2,1,0:T(8,128)S(1)}, f32[10,8,128]{2,1,0:T(8,128)S(1)}, u32[]{:S(2)}, u32[]{:S(2)}) collective-permute-start(f32[10,8,128]{2,1,0:T(8,128)S(1)} %get-tuple-element.71.refs_0_), channel_id=1, source_target_pairs={{1,0},{0,1},{3,2},{2,3},{5,4},{4,5},{7,6},{6,7},{9,8},{8,9},{11,10... | collective-permute-start | bytes 122888 | tf_op jit(solution)/shard_map/ppermute | solution.py:467

commit v9 on v8

--- a/solution.py
+++ b/solution.py
@@ -80,10 +80,14 @@
     return jnp.transpose(joined)
 
 
-def own_half(seq_mask, own, bias, gains, w_row,
-             own_unit_out, query_gate_out, query_heads_out, own_memory_out, bias_out, present_out):
+def turn_bias(bias, bias_out):
+    n_keys = bias.shape[2]
+    bias_out[...] = jnp.transpose(bias[...].reshape(-1, n_keys).astype(F32))
+
+
+def own_half(seq_mask, own, gains, w_row,
+             own_unit_out, query_gate_out, query_heads_out, own_memory_out, present_out):
     n_seq, n_rows, _ = own.shape
-    n_keys = bias.shape[2]
     w_all = w_row[...]
     own_units, _ = normalise(own[...].reshape(n_seq * n_rows, C).astype(F32))
     projected = dot(own_units * gains[0:1, :], w_all, precision=EXACT)
@@ -95,7 +99,6 @@
     mask = head_mask(n_rows)
     for s in range(n_seq):
         query_heads_out[s] = spread_heads(queries[s * n_rows : (s + 1) * n_rows], mask)
-    bias_out[...] = jnp.transpose(bias[...].reshape(H * n_rows, n_keys).astype(F32))
     lane = lax.broadcasted_iota(jnp.int32, present_out.shape, 1) // (2 * C // n_seq)
     present = jnp.zeros(present_out.shape, F32)
     for s in range(n_seq):
@@ -108,16 +111,17 @@
     (own, cotangent, gains, w_row, w_out, own_unit, query_gate, query_heads, own_memory, bias_t, present) = refs[
         n_res : n_res + 11
     ]
-    payload, exponent_out, unit_out, memory_out, mixture_out, inverse_out, residue = refs[n_res + 11 :]
+    residues = refs[n_res + 11 : 2 * n_res + 11]
+    payload, exponent_out, unit_out, memory_out, mixture_out, inverse_out, residue = refs[2 * n_res + 11 :]
     n_seq, n_rows, _ = own.shape
     n_keys = n_res * n_rows
     me = lax.axis_index("res")
     w_memory = w_row[:, C : 3 * C]
     for away in range(n_res):
         where = lax.rem(me + away, n_res)
-        residue[where] = sent[away][n_seq]
+        residue[where] = jnp.broadcast_to(residues[away][...].astype(F32), (ROWS, n_rows))
         if away:
-            units, _ = normalise(sent[away][:n_seq].reshape(n_seq * n_rows, C))
+            units, _ = normalise(sent[away][...].reshape(n_seq * n_rows, C))
             memories = dot(units * gains[0:1, :], w_memory, precision=EXACT)
             units = units.reshape(n_seq, n_rows, C)
             memories = memories.reshape(n_seq, n_rows, 2 * C)
@@ -127,7 +131,8 @@
         memory_out[where] = memories
     n_blocks = payload.shape[0]
     block = n_rows // n_blocks
-    key_bias = MASKED * (residue[...].reshape(n_keys, C)[:, 0:1] - 1.0)
+    present_keys = jnp.transpose(jnp.concatenate([residue[i] for i in range(n_res)], axis=1))[:, 0:1]
+    key_bias = MASKED * (present_keys - 1.0)
     mask = head_mask(n_rows)
     wide_mask = jnp.concatenate([mask, mask], axis=0)
     initial = own[...].reshape(n_seq * n_rows, C).astype(F32)
@@ -498,22 +503,23 @@
     block = n_rows // seq_count
     group = n_seq * block
     away_range = range(1, res_count)
-    present_keys = jnp.broadcast_to(residue_mask.astype(F32)[None, :, None], (1, n_rows, C))
-    sent = jnp.concatenate([alignment.astype(F32), present_keys], axis=0)
-    own_unit, query_gate, query_heads, own_memory, bias_t, present = call(
+    residues = [residue_mask] + [shift_residues(residue_mask, away, res_count) for away in away_range]
+    residues = [value.reshape(1, n_rows) for value in residues]
+    sent = lax.optimization_barrier(alignment.astype(F32))
+    own_unit, query_gate, query_heads, own_memory, present = call(
         own_half,
         [
             ((n_seq, n_rows, C), F32),
             ((n_seq, n_rows, 2 * C), F32),
             ((n_seq, C, H * n_rows), F32),
             ((n_seq, n_rows, 2 * C), F32),
-            ((n_keys, H * n_rows), F32),
             ((block, 2 * C), F32),
         ],
-        sequence_mask, alignment, pair_bias, norm_gains, row_project,
+        sequence_mask, alignment, norm_gains, row_project,
         smem=1,
         name="own_half",
     )
+    (bias_t,) = call(turn_bias, [((n_keys, H * n_rows), F32)], pair_bias, name="turn_bias")
     payload, exponent, unit, memory, mixture, inverse = call(
         functools.partial(row_forward, res_count),
         [
@@ -526,8 +532,8 @@
         ],
         sent, *[shift_residues(sent, away, res_count) for away in away_range],
         alignment, cotangent, norm_gains, row_project, row_output, own_unit, query_gate, query_heads, own_memory, bias_t,
-        present,
-        scratch=[pltpu.VMEM((res_count, n_rows, C), F32)],
+        present, *residues,
+        scratch=[pltpu.VMEM((res_count, ROWS, n_rows), F32)],
         name="row_forward",
     )
     arrived = swap_blocks(payload)

time: 61.8 us -> 61.8 us (level)
  other arithmetic: 1.45 us -> 0.78 us
    convert_element_type x2 -> x1, other arithmetic: 1.44 us -> 0.78 us  [local(): sent = lax.optimization_barrier(alignment.astype(F32))]
    pallas_call x13 -> x14, Pallas kernels: 10 us -> 10 us  [call(): pl.pallas_call(body, out_shape=[jax.ShapeDtypeStruct(shape, kind) for sha...]
    ppermute x3 -> x4, waiting for transfers between devices: 1.73 us -> 1.73 us  [shift_residues(): lax.ppermute(values, 'res', [((i + away) % count, i) for i in range(count)])]
  transfers between devices with their start and end apart: 7 -> 8, of which waited for: 6 -> 6; matrix products, arithmetic and copies ran while one was open for 0% -> 0% of each run, Pallas kernels for 5% -> 5%
where the time goes in v9:
time: 61.8 us; the launch traced here: 61.5 us
  blocking collectives  26.1 us (42%)
  waiting for transfers between devices  18.6 us (30%)
  Pallas kernels  10 us (16%)
  starting transfers between devices  4.14 us (7%)
  local copies, waits for them, and re-layouts  0.95 us (2%)
  between operations  0.83 us (1%)
  other arithmetic  0.78 us (1%)
    all_to_all x2, blocking collectives, swap_blocks(): return lax.all_to_all(values, 'seq', 0, 0, tiled=True)  26.1 us
    ppermute x4, waiting for transfers between devices, cross(): return lax.ppermute(values, ('seq', 'res'), pairs)  16.9 us
    pallas_call x14, Pallas kernels, call(): pl.pallas_call(body, out_shape=[jax.ShapeDtypeStruct(shape, kind) for sha...  10 us
    ppermute x4, starting transfers between devices, cross(): return lax.ppermute(values, ('seq', 'res'), pairs)  3.4 us
    ppermute x4, waiting for transfers between devices, shift_residues(): lax.ppermute(values, 'res', [((i + away) % count, i) for i in range(count)])  1.73 us
  transfers between devices with their start and end apart: 8, of which 6 were waited for; matrix products, arithmetic and copies ran while one was open for 0% of the time, Pallas kernels for 5%

profile of v9, /device:TPU:0, one launch (start us, length us, event | category | flops | bytes accessed | tf_op | source)
XLA Modules:
  0.0 61.5 jit_solution(5354814894086760289)
XLA Ops:
  0.7 0.8 %convert_element_type.3.refs_0_ = f32[2,64,64]{2,1,0:T(8,128)S(1)} convert(bf16[2,64,64]{2,1,0:T(8,128)(2,1)} %own.3) | non-fusion elementwise | flops 8192 | bytes 49152 | tf_op jit(solution)/shard_map/convert_element_type | solution.py:508
  1.5 0.5 collective-permute-start
  2.0 0.1 collective-permute-start.1
  2.1 0.9 %copy-done.3 = bf16[8,64,128]{2,1,0:T(8,128)(2,1)S(1)} copy-done((bf16[8,64,128]{2,1,0:T(8,128)(2,1)S(1)}, bf16[8,64,128]{2,1,0:T(8,128)(2,1)}, u32[]{:S(2)}) %copy-start.3) | copy-done | bytes 131096
  3.0 0.1 turn_bias.1.refs_11_
  3.1 1.1 %own_half.1 = (f32[2,64,64]{2,1,0:T(8,128)S(1)}, f32[2,64,128]{2,1,0:T(8,128)S(1)}, f32[2,64,512]{2,1,0:T(8,128)S(1)}, f32[2,64,128]{2,1,0:T(8,128)S(1)}, f32[4,128]{1,0:T(4,128)S(1)}) custom-call(s32[2]{0:T(128)S(1)} %copy-done.8, bf16[2,64,64]{2,1,0:T(8,128)(2,1)S(1)} %copy-done.1, f32[2,64]{1,0:T(2,128)S(1)} %copy-done.7, f32[64,256]{1,0:T(8,128)S(1)} %copy-done), custom_call_target="tpu_custom_call" | custom-call | tf_op jit(solution)/shard_map/own_half/pallas_call | solution.py:459
  4.3 2.1 %row_forward.1 = (f32[16,3,4,128]{3,2,1,0:T(4,128)S(1)}, f32[2,128,512]{2,1,0:T(8,128)S(1)}, f32[2,2,64,64]{3,2,1,0:T(8,128)S(1)}, f32[2,2,64,128]{3,2,1,0:T(8,1...) custom-call(f32[2,64,64]{2,1,0:T(8,128)S(1)} %convert_element_type.3.refs_0_, ...), custom_call_target="tpu_custom_call" | custom-call | tf_op jit(solution)/shard_map/row_forward/pallas_call | solution.py:459
  6.4 15.9 %all_to_all.10.arrived = f32[16,3,4,128]{3,2,1,0:T(4,128)S(1)} all-to-all(f32[16,3,4,128]{3,2,1,0:T(4,128)S(1)} %get-tuple-element.46), channel_id=1, replica_groups=mesh['seq'=16,'res'=2] {'seq'}, dimensions={0} | all-to-all | bytes 196608 | tf_op jit(solution)/shard_map/all_to_all | solution.py:484
  22.3 1.7 %column_step.1 = f32[16,3,4,128]{3,2,1,0:T(4,128)S(1)} custom-call(f32[16,3,4,128]{3,2,1,0:T(4,128)S(1)} %all_to_all.10.arrived, f32[2,64]{1,0:T(2,128)S(1)} %copy-done.7, f32[64,144]{1,0:T(8,128)S(1)} %copy-done.2, f32[64,64]{1,0:T(8,128)S(1)} %copy-done.6), custom_call_target="tpu_custom_call" | custom-call | tf_op jit(solution)/shard_map/column_step/pallas_call | solution.py:459
  24.0 10.3 %all_to_all.11.returned = f32[16,3,4,128]{3,2,1,0:T(4,128)S(1)} all-to-all(f32[16,3,4,128]{3,2,1,0:T(4,128)S(1)} %column_step.1), channel_id=1, replica_groups=mesh['seq'=16,'res'=2] {'seq'}, dimensions={0} | all-to-all | bytes 196608 | tf_op jit(solution)/shard_map/all_to_all | solution.py:484
  34.2 2.0 %row_backward.1 = (f32[128,512]{1,0:T(8,128)S(1)}, f32[2,64,64]{2,1,0:T(8,128)S(1)}, f32[152,128]{1,0:T(8,128)S(1)}, f32[152,128]{1,0:T(8,128)S(1)}) custom-call(f32[16,3,4,128]{3,2,1,0:T(4,128)S(1)} %all_to_all.11.returned, f32[2,128,512]{2,1,0:T(8,128)S(1)} %get-tuple-element.47.exponent_in, f32[2,2,64,64]{3,2,1,0:T(8,128)S(1)} %get-tuple-element.48.unit_in, ...), custom_call_target="tpu_custom_call" | custom-call | tf_op jit(solution)/shard_map/row_backward/pallas_call | solution.py:459
  36.4 1.2 %collective-permute-done.2.refs_1_ = f32[152,128]{1,0:T(8,128)S(1)} collective-permute-done((f32[152,128]{1,0:T(8,128)S(1)}, f32[152,128]{1,0:T(8,128)S(1)}, u32[]{:S(2)}, u32[]{:S(2)}) %collective-permute-start.2) | collective-permute-done | bytes 77856 | tf_op jit(solution)/shard_map/ppermute | solution.py:472
  37.6 1.0 %collective-permute-start.3 = (f32[43,8,128]{2,1,0:T(8,128)S(1)}, f32[43,8,128]{2,1,0:T(8,128)S(1)}, u32[]{:S(2)}, u32[]{:S(2)}) collective-permute-start(f32[43,8,128]{2,1,0:T(8,128)S(1)} %get-tuple-element.60.sent), channel_id=1, source_target_pairs={{0,2},{2,0},{4,6},{6,4},{8,10},{10,8},{12,14},{14,12},{16,18},{18,... | collective-permute-start | bytes 528392 | tf_op jit(solution)/shard_map/ppermute | solution.py:480
  38.6 4.5 %collective-permute-done.3.arrived = f32[43,8,128]{2,1,0:T(8,128)S(1)} collective-permute-done((f32[43,8,128]{2,1,0:T(8,128)S(1)}, f32[43,8,128]{2,1,0:T(8,128)S(1)}, u32[]{:S(2)}, u32[]{:S(2)}) %collective-permute-start.3) | collective-permute-done | bytes 176160 | tf_op jit(solution)/shard_map/ppermute | solution.py:480
  43.2 0.7 %collective-permute-start.4 = (f32[28,8,128]{2,1,0:T(8,128)S(1)}, f32[28,8,128]{2,1,0:T(8,128)S(1)}, u32[]{:S(2)}, u32[]{:S(2)}) collective-permute-start(f32[28,8,128]{2,1,0:T(8,128)S(1)} %get-tuple-element.62.sent), channel_id=1, source_target_pairs={{0,4},{2,6},{4,0},{6,2},{8,12},{10,14},{12,8},{14,10},{16,20},{18,... | collective-permute-start | bytes 344072 | tf_op jit(solution)/shard_map/ppermute | solution.py:480
  43.9 4.1 %collective-permute-done.4.arrived = f32[28,8,128]{2,1,0:T(8,128)S(1)} collective-permute-done((f32[28,8,128]{2,1,0:T(8,128)S(1)}, f32[28,8,128]{2,1,0:T(8,128)S(1)}, u32[]{:S(2)}, u32[]{:S(2)}) %collective-permute-start.4) | collective-permute-done | bytes 114720 | tf_op jit(solution)/shard_map/ppermute | solution.py:480
  48.0 0.8 %collective-permute-start.5 = (f32[22,8,128]{2,1,0:T(8,128)S(1)}, f32[22,8,128]{2,1,0:T(8,128)S(1)}, u32[]{:S(2)}, u32[]{:S(2)}) collective-permute-start(f32[22,8,128]{2,1,0:T(8,128)S(1)} %get-tuple-element.64.sent), channel_id=1, source_target_pairs={{0,8},{2,10},{4,12},{6,14},{8,0},{10,2},{12,4},{14,6},{16,24},{18,... | collective-permute-start | bytes 270344 | tf_op jit(solution)/shard_map/ppermute | solution.py:480
  48.8 3.8 %collective-permute-done.5.arrived = f32[22,8,128]{2,1,0:T(8,128)S(1)} collective-permute-done((f32[22,8,128]{2,1,0:T(8,128)S(1)}, f32[22,8,128]{2,1,0:T(8,128)S(1)}, u32[]{:S(2)}, u32[]{:S(2)}) %collective-permute-start.5) | collective-permute-done | bytes 90144 | tf_op jit(solution)/shard_map/ppermute | solution.py:480
  52.6 0.9 %collective-permute-start.6 = (f32[22,8,128]{2,1,0:T(8,128)S(1)}, f32[22,8,128]{2,1,0:T(8,128)S(1)}, u32[]{:S(2)}, u32[]{:S(2)}) collective-permute-start(f32[22,8,128]{2,1,0:T(8,128)S(1)} %get-tuple-element.66.sent), channel_id=1, source_target_pairs={{0,16},{2,18},{4,20},{6,22},{8,24},{10,26},{12,28},{14,30},{16,0},... | collective-permute-start | bytes 270344 | tf_op jit(solution)/shard_map/ppermute | solution.py:480
  53.5 1.1 %finish_alignment.1 = (bf16[2,64,64]{2,1,0:T(8,128)(2,1)}, f32[8,128]{1,0:T(8,128)S(1)}) custom-call(bf16[2,64,64]{2,1,0:T(8,128)(2,1)S(1)} %copy-done.1, f32[2,64,64]{2,1,0:T(8,128)S(1)} %get-tuple-element.52.middle_grad, f32[2,64]{1,0:T(2,128)S(1)} %copy-done.7, f32[64,128]{1,0:T(8,128)S(1)} %get-tuple-element.57.normed), custom_call_target="tpu_custom_call" | custom-call | tf_op jit(solution)/shard_map/finish_alignment/pallas_call | solution.py:459
  54.7 4.4 %collective-permute-done.6.arrived = f32[22,8,128]{2,1,0:T(8,128)S(1)} collective-permute-done((f32[22,8,128]{2,1,0:T(8,128)S(1)}, f32[22,8,128]{2,1,0:T(8,128)S(1)}, u32[]{:S(2)}, u32[]{:S(2)}) %collective-permute-start.6) | collective-permute-done | bytes 90144 | tf_op jit(solution)/shard_map/ppermute | solution.py:480
  59.2 0.7 %bias_last.1 = f32[8,8,64]{2,1,0:T(8,128)} custom-call(f32[4,8,128]{2,1,0:T(8,128)S(1)} %get-tuple-element.65.state, f32[22,8,128]{2,1,0:T(8,128)S(1)} %collective-permute-done.6.arrived), custom_call_target="tpu_custom_call" | custom-call | tf_op jit(solution)/shard_map/bias_last/pallas_call | solution.py:459
  59.9 0.5 collective-permute-done.7.refs_1_
  60.4 1.1 %unpack.1 = (f32[2,64]{1,0:T(2,128)}, f32[64,256]{1,0:T(8,128)}, f32[64,64]{1,0:T(8,128)}, f32[64,144]{1,0:T(8,128)}, f32[64,64]{1,0:T(8,128)}) custom-call(f32[16,8,128]{2,1,0:T(8,128)S(1)} %get-tuple-element.68.joined, f32[10,8,128]{2,1,0:T(8,128)S(1)} %get-tuple-element.69.refs_0_, f32[10,8,128]{2,1,0:T(8,128)S(1)} %collective-permute-done.7.refs_1_, ...), custom_call_target="tpu_custom_call" | custom-call | tf_op jit(solution)/shard_map/unpack/pallas_call | solution.py:459
  (29 shorter events, 0.3 us)
Async XLA Ops:
  0.6 1.3 %copy-start.9 = (s32[64]{0:T(128)S(1)}, s32[64]{0:T(128)}, u32[]{:S(2)}) copy-start(s32[64]{0:T(128)} %param.18) | copy-start | bytes 772
  0.6 2.4 %copy-start.7 = (f32[2,64]{1,0:T(2,128)S(1)}, f32[2,64]{1,0:T(2,128)}, u32[]{:S(2)}) copy-start(f32[2,64]{1,0:T(2,128)} %refs_2_.3) | copy-start | bytes 1540
  0.7 2.4 %copy-start.8 = (s32[2]{0:T(128)S(1)}, s32[2]{0:T(128)}, u32[]{:S(2)}) copy-start(s32[2]{0:T(128)} %seq_mask.1) | copy-start | bytes 28
  1.4 1.7 %copy-start = (f32[64,256]{1,0:T(8,128)S(1)}, f32[64,256]{1,0:T(8,128)}, u32[]{:S(2)}) copy-start(f32[64,256]{1,0:T(8,128)} %refs_3_.3) | copy-start | bytes 196612
  1.4 1.7 %copy-start.1 = (bf16[2,64,64]{2,1,0:T(8,128)(2,1)S(1)}, bf16[2,64,64]{2,1,0:T(8,128)(2,1)}, u32[]{:S(2)}) copy-start(bf16[2,64,64]{2,1,0:T(8,128)(2,1)} %own.3) | copy-start | bytes 49156
  1.5 2.8 %collective-permute-start = (f32[2,64,64]{2,1,0:T(8,128)S(1)}, f32[2,64,64]{2,1,0:T(8,128)S(1)}, u32[]{:S(2)}, u32[]{:S(2)}) collective-permute-start(f32[2,64,64]{2,1,0:T(8,128)S(1)} %convert_element_type.3.refs_0_), channel_id=1, source_target_pairs={{1,0},{0,1},{3,2},{2,3},{5,4},{4,5},{7,6},{6,7},{9,8},{8,9},{11,10... | collective-permute-start | bytes 98312 | tf_op jit(solution)/shard_map/ppermute | solution.py:472
  2.0 2.3 %collective-permute-start.1 = (s32[64]{0:T(128)S(1)}, s32[64]{0:T(128)S(1)}, u32[]{:S(2)}, u32[]{:S(2)}) collective-permute-start(s32[64]{0:T(128)S(1)} %copy-done.9), channel_id=1, source_target_pairs={{1,0},{0,1},{3,2},{2,3},{5,4},{4,5},{7,6},{6,7},{9,8},{8,9},{11,10... | collective-permute-start | bytes 776 | tf_op jit(solution)/shard_map/ppermute | solution.py:472
  2.1 0.9 %copy-start.3 = (bf16[8,64,128]{2,1,0:T(8,128)(2,1)S(1)}, bf16[8,64,128]{2,1,0:T(8,128)(2,1)}, u32[]{:S(2)}) copy-start(bf16[8,64,128]{2,1,0:T(8,128)(2,1)} %bias.1) | copy-start | bytes 393220
  3.1 1.2 %copy-start.4 = (f32[64,64]{1,0:T(8,128)S(1)}, f32[64,64]{1,0:T(8,128)}, u32[]{:S(2)}) copy-start(f32[64,64]{1,0:T(8,128)} %w_out.3) | copy-start | bytes 49156
  3.1 1.2 %copy-start.5 = (bf16[2,64,64]{2,1,0:T(8,128)(2,1)S(1)}, bf16[2,64,64]{2,1,0:T(8,128)(2,1)}, u32[]{:S(2)}) copy-start(bf16[2,64,64]{2,1,0:T(8,128)(2,1)} %refs_3_.2) | copy-start | bytes 49156
  6.4 15.9 %copy-start.2 = (f32[64,144]{1,0:T(8,128)S(1)}, f32[64,144]{1,0:T(8,128)}, u32[]{:S(2)}) copy-start(f32[64,144]{1,0:T(8,128)} %refs_4_.3) | copy-start | bytes 110596
  6.4 15.9 %copy-start.6 = (f32[64,64]{1,0:T(8,128)S(1)}, f32[64,64]{1,0:T(8,128)}, u32[]{:S(2)}) copy-start(f32[64,64]{1,0:T(8,128)} %w_out.2) | copy-start | bytes 49156
  36.3 1.3 %collective-permute-start.2 = (f32[152,128]{1,0:T(8,128)S(1)}, f32[152,128]{1,0:T(8,128)S(1)}, u32[]{:S(2)}, u32[]{:S(2)}) collective-permute-start(f32[152,128]{1,0:T(8,128)S(1)} %get-tuple-element.56), channel_id=1, source_target_pairs={{1,0},{0,1},{3,2},{2,3},{5,4},{4,5},{7,6},{6,7},{9,8},{8,9},{11,10... | collective-permute-start | bytes 233480 | tf_op jit(solution)/shard_map/ppermute | solution.py:472
  37.6 5.5 %collective-permute-start.3 = (f32[43,8,128]{2,1,0:T(8,128)S(1)}, f32[43,8,128]{2,1,0:T(8,128)S(1)}, u32[]{:S(2)}, u32[]{:S(2)}) collective-permute-start(f32[43,8,128]{2,1,0:T(8,128)S(1)} %get-tuple-element.60.sent), channel_id=1, source_target_pairs={{0,2},{2,0},{4,6},{6,4},{8,10},{10,8},{12,14},{14,12},{16,18},{18,... | collective-permute-start | bytes 528392 | tf_op jit(solution)/shard_map/ppermute | solution.py:480
  43.2 4.9 %collective-permute-start.4 = (f32[28,8,128]{2,1,0:T(8,128)S(1)}, f32[28,8,128]{2,1,0:T(8,128)S(1)}, u32[]{:S(2)}, u32[]{:S(2)}) collective-permute-start(f32[28,8,128]{2,1,0:T(8,128)S(1)} %get-tuple-element.62.sent), channel_id=1, source_target_pairs={{0,4},{2,6},{4,0},{6,2},{8,12},{10,14},{12,8},{14,10},{16,20},{18,... | collective-permute-start | bytes 344072 | tf_op jit(solution)/shard_map/ppermute | solution.py:480
  48.0 4.6 %collective-permute-start.5 = (f32[22,8,128]{2,1,0:T(8,128)S(1)}, f32[22,8,128]{2,1,0:T(8,128)S(1)}, u32[]{:S(2)}, u32[]{:S(2)}) collective-permute-start(f32[22,8,128]{2,1,0:T(8,128)S(1)} %get-tuple-element.64.sent), channel_id=1, source_target_pairs={{0,8},{2,10},{4,12},{6,14},{8,0},{10,2},{12,4},{14,6},{16,24},{18,... | collective-permute-start | bytes 270344 | tf_op jit(solution)/shard_map/ppermute | solution.py:480
  52.6 6.5 %collective-permute-start.6 = (f32[22,8,128]{2,1,0:T(8,128)S(1)}, f32[22,8,128]{2,1,0:T(8,128)S(1)}, u32[]{:S(2)}, u32[]{:S(2)}) collective-permute-start(f32[22,8,128]{2,1,0:T(8,128)S(1)} %get-tuple-element.66.sent), channel_id=1, source_target_pairs={{0,16},{2,18},{4,20},{6,22},{8,24},{10,26},{12,28},{14,30},{16,0},... | collective-permute-start | bytes 270344 | tf_op jit(solution)/shard_map/ppermute | solution.py:480
  59.1 1.3 %collective-permute-start.7 = (f32[10,8,128]{2,1,0:T(8,128)S(1)}, f32[10,8,128]{2,1,0:T(8,128)S(1)}, u32[]{:S(2)}, u32[]{:S(2)}) collective-permute-start(f32[10,8,128]{2,1,0:T(8,128)S(1)} %get-tuple-element.69.refs_0_), channel_id=1, source_target_pairs={{1,0},{0,1},{3,2},{2,3},{5,4},{4,5},{7,6},{6,7},{9,8},{8,9},{11,10... | collective-permute-start | bytes 122888 | tf_op jit(solution)/shard_map/ppermute | solution.py:472

commit v10 on v8

--- a/solution.py
+++ b/solution.py
@@ -80,10 +80,9 @@
     return jnp.transpose(joined)
 
 
-def own_half(seq_mask, own, bias, gains, w_row,
-             own_unit_out, query_gate_out, query_heads_out, own_memory_out, bias_out, present_out):
+def own_half(seq_mask, own, gains, w_row,
+             own_unit_out, query_gate_out, query_heads_out, own_memory_out, present_out):
     n_seq, n_rows, _ = own.shape
-    n_keys = bias.shape[2]
     w_all = w_row[...]
     own_units, _ = normalise(own[...].reshape(n_seq * n_rows, C).astype(F32))
     projected = dot(own_units * gains[0:1, :], w_all, precision=EXACT)
@@ -95,7 +94,6 @@
     mask = head_mask(n_rows)
     for s in range(n_seq):
         query_heads_out[s] = spread_heads(queries[s * n_rows : (s + 1) * n_rows], mask)
-    bias_out[...] = jnp.transpose(bias[...].reshape(H * n_rows, n_keys).astype(F32))
     lane = lax.broadcasted_iota(jnp.int32, present_out.shape, 1) // (2 * C // n_seq)
     present = jnp.zeros(present_out.shape, F32)
     for s in range(n_seq):
@@ -105,7 +103,7 @@
 
 def row_forward(n_res, *refs):
     sent = refs[:n_res]
-    (own, cotangent, gains, w_row, w_out, own_unit, query_gate, query_heads, own_memory, bias_t, present) = refs[
+    (own, cotangent, gains, w_row, w_out, own_unit, query_gate, query_heads, own_memory, bias, present) = refs[
         n_res : n_res + 11
     ]
     payload, exponent_out, unit_out, memory_out, mixture_out, inverse_out, residue = refs[n_res + 11 :]
@@ -127,6 +125,7 @@
         memory_out[where] = memories
     n_blocks = payload.shape[0]
     block = n_rows // n_blocks
+    bias_t = jnp.transpose(bias[...].reshape(H * n_rows, n_keys).astype(F32))
     key_bias = MASKED * (residue[...].reshape(n_keys, C)[:, 0:1] - 1.0)
     mask = head_mask(n_rows)
     wide_mask = jnp.concatenate([mask, mask], axis=0)
@@ -135,7 +134,7 @@
     sums = []
     for s in range(n_seq):
         memory = memory_out[:, s].reshape(n_keys, 2 * C)
-        scores = dot(memory[:, :C], query_heads[s], precision=EXACT) + bias_t[...] + key_bias
+        scores = dot(memory[:, :C], query_heads[s], precision=EXACT) + bias_t + key_bias
         exponent = jnp.exp(scores - jnp.max(scores, axis=0, keepdims=True))
         exponent_out[s] = exponent
         summed = dot_rows(jnp.concatenate([memory[:, C:], jnp.ones((n_keys, C), F32)], axis=1), exponent)
@@ -500,17 +499,16 @@
     away_range = range(1, res_count)
     present_keys = jnp.broadcast_to(residue_mask.astype(F32)[None, :, None], (1, n_rows, C))
     sent = jnp.concatenate([alignment.astype(F32), present_keys], axis=0)
-    own_unit, query_gate, query_heads, own_memory, bias_t, present = call(
+    own_unit, query_gate, query_heads, own_memory, present = call(
         own_half,
         [
             ((n_seq, n_rows, C), F32),
             ((n_seq, n_rows, 2 * C), F32),
             ((n_seq, C, H * n_rows), F32),
             ((n_seq, n_rows, 2 * C), F32),
-            ((n_keys, H * n_rows), F32),
             ((block, 2 * C), F32),
         ],
-        sequence_mask, alignment, pair_bias, norm_gains, row_project,
+        sequence_mask, alignment, norm_gains, row_project,
         smem=1,
         name="own_half",
     )
@@ -525,7 +523,7 @@
             ((n_seq, n_rows, C), F32),
         ],
         sent, *[shift_residues(sent, away, res_count) for away in away_range],
-        alignment, cotangent, norm_gains, row_project, row_output, own_unit, query_gate, query_heads, own_memory, bias_t,
+        alignment, cotangent, norm_gains, row_project, row_output, own_unit, query_gate, query_heads, own_memory, pair_bias,
         present,
         scratch=[pltpu.VMEM((res_count, n_rows, C), F32)],
         name="row_forward",

time: 61.8 us -> 61.8 us (level)
  no operation moved by 1% of the time
where the time goes in v10:
time: 61.8 us; the launch traced here: 61.5 us
  blocking collectives  26.2 us (42%)
  waiting for transfers between devices  18.6 us (30%)
  Pallas kernels  10 us (16%)
  starting transfers between devices  4.08 us (7%)
  other arithmetic  1.43 us (2%)
  between operations  0.78 us (1%)
    all_to_all x2, blocking collectives, swap_blocks(): return lax.all_to_all(values, 'seq', 0, 0, tiled=True)  26.2 us
    ppermute x4, waiting for transfers between devices, cross(): return lax.ppermute(values, ('seq', 'res'), pairs)  16.9 us
    pallas_call x13, Pallas kernels, call(): pl.pallas_call(body, out_shape=[jax.ShapeDtypeStruct(shape, kind) for sha...  10 us
    ppermute x4, starting transfers between devices, cross(): return lax.ppermute(values, ('seq', 'res'), pairs)  3.42 us
    ppermute x3, waiting for transfers between devices, shift_residues(): lax.ppermute(values, 'res', [((i + away) % count, i) for i in range(count)])  1.73 us
  transfers between devices with their start and end apart: 7, of which 6 were waited for; matrix products, arithmetic and copies ran while one was open for 0% of the time, Pallas kernels for 5%

profile of v10, /device:TPU:0, one launch (start us, length us, event | category | flops | bytes accessed | tf_op | source)
XLA Modules:
  0.0 61.5 jit_solution(885530498353495204)
XLA Ops:
  0.6 0.7 %convert_element_type.7 = f32[64]{0:T(128)S(1)} convert(s32[64]{0:T(128)} %param.18) | non-fusion elementwise | flops 64 | bytes 512 | tf_op jit(solution)/shard_map/convert_element_type | solution.py:500
  1.3 0.8 %convert_element_type.6 = f32[2,64,64]{2,1,0:T(8,128)S(1)} convert(bf16[2,64,64]{2,1,0:T(8,128)(2,1)} %own.3) | non-fusion elementwise | flops 8192 | bytes 49152 | tf_op jit(solution)/shard_map/convert_element_type | solution.py:501
  2.1 0.1 broadcast_in_dim.2
  2.2 0.5 collective-permute-start
  2.7 0.2 copy-done
  3.0 1.1 %own_half.1 = (f32[2,64,64]{2,1,0:T(8,128)S(1)}, f32[2,64,128]{2,1,0:T(8,128)S(1)}, f32[2,64,512]{2,1,0:T(8,128)S(1)}, f32[2,64,128]{2,1,0:T(8,128)S(1)}, f32[4,128]{1,0:T(4,128)S(1)}) custom-call(s32[2]{0:T(128)S(1)} %copy-done.8, bf16[2,64,64]{2,1,0:T(8,128)(2,1)S(1)} %copy-done.1, f32[2,64]{1,0:T(2,128)S(1)} %copy-done.7, f32[64,256]{1,0:T(8,128)S(1)} %copy-done), custom_call_target="tpu_custom_call" | custom-call | tf_op jit(solution)/shard_map/own_half/pallas_call | solution.py:453
  4.2 2.2 %row_forward.1 = (f32[16,3,4,128]{3,2,1,0:T(4,128)S(1)}, f32[2,128,512]{2,1,0:T(8,128)S(1)}, f32[2,2,64,64]{3,2,1,0:T(8,128)S(1)}, f32[2,2,64,128]{3,2,1,0:T(8,1...) custom-call(f32[3,64,64]{2,1,0:T(8,128)S(1)} %pad_maximum_fusion.refs_0_, ...), custom_call_target="tpu_custom_call" | custom-call | tf_op jit(solution)/shard_map/row_forward/pallas_call | solution.py:453
  6.3 15.9 %all_to_all.10.arrived = f32[16,3,4,128]{3,2,1,0:T(4,128)S(1)} all-to-all(f32[16,3,4,128]{3,2,1,0:T(4,128)S(1)} %get-tuple-element.46), channel_id=1, replica_groups=mesh['seq'=16,'res'=2] {'seq'}, dimensions={0} | all-to-all | bytes 196608 | tf_op jit(solution)/shard_map/all_to_all | solution.py:478
  22.3 1.7 %column_step.1 = f32[16,3,4,128]{3,2,1,0:T(4,128)S(1)} custom-call(f32[16,3,4,128]{3,2,1,0:T(4,128)S(1)} %all_to_all.10.arrived, f32[2,64]{1,0:T(2,128)S(1)} %copy-done.7, f32[64,144]{1,0:T(8,128)S(1)} %copy-done.2, f32[64,64]{1,0:T(8,128)S(1)} %copy-done.6), custom_call_target="tpu_custom_call" | custom-call | tf_op jit(solution)/shard_map/column_step/pallas_call | solution.py:453
  23.9 10.3 %all_to_all.11.returned = f32[16,3,4,128]{3,2,1,0:T(4,128)S(1)} all-to-all(f32[16,3,4,128]{3,2,1,0:T(4,128)S(1)} %column_step.1), channel_id=1, replica_groups=mesh['seq'=16,'res'=2] {'seq'}, dimensions={0} | all-to-all | bytes 196608 | tf_op jit(solution)/shard_map/all_to_all | solution.py:478
  34.2 2.0 %row_backward.1 = (f32[128,512]{1,0:T(8,128)S(1)}, f32[2,64,64]{2,1,0:T(8,128)S(1)}, f32[152,128]{1,0:T(8,128)S(1)}, f32[152,128]{1,0:T(8,128)S(1)}) custom-call(f32[16,3,4,128]{3,2,1,0:T(4,128)S(1)} %all_to_all.11.returned, f32[2,128,512]{2,1,0:T(8,128)S(1)} %get-tuple-element.47.exponent_in, f32[2,2,64,64]{3,2,1,0:T(8,128)S(1)} %get-tuple-element.48.unit_in, ...), custom_call_target="tpu_custom_call" | custom-call | tf_op jit(solution)/shard_map/row_backward/pallas_call | solution.py:453
  36.3 1.2 %collective-permute-done.1.refs_1_ = f32[152,128]{1,0:T(8,128)S(1)} collective-permute-done((f32[152,128]{1,0:T(8,128)S(1)}, f32[152,128]{1,0:T(8,128)S(1)}, u32[]{:S(2)}, u32[]{:S(2)}) %collective-permute-start.1) | collective-permute-done | bytes 77856 | tf_op jit(solution)/shard_map/ppermute | solution.py:466
  37.6 1.0 %collective-permute-start.2 = (f32[43,8,128]{2,1,0:T(8,128)S(1)}, f32[43,8,128]{2,1,0:T(8,128)S(1)}, u32[]{:S(2)}, u32[]{:S(2)}) collective-permute-start(f32[43,8,128]{2,1,0:T(8,128)S(1)} %get-tuple-element.60.sent), channel_id=1, source_target_pairs={{0,2},{2,0},{4,6},{6,4},{8,10},{10,8},{12,14},{14,12},{16,18},{18,... | collective-permute-start | bytes 528392 | tf_op jit(solution)/shard_map/ppermute | solution.py:474
  38.6 4.5 %collective-permute-done.2.arrived = f32[43,8,128]{2,1,0:T(8,128)S(1)} collective-permute-done((f32[43,8,128]{2,1,0:T(8,128)S(1)}, f32[43,8,128]{2,1,0:T(8,128)S(1)}, u32[]{:S(2)}, u32[]{:S(2)}) %collective-permute-start.2) | collective-permute-done | bytes 176160 | tf_op jit(solution)/shard_map/ppermute | solution.py:474
  43.1 0.7 %collective-permute-start.3 = (f32[28,8,128]{2,1,0:T(8,128)S(1)}, f32[28,8,128]{2,1,0:T(8,128)S(1)}, u32[]{:S(2)}, u32[]{:S(2)}) collective-permute-start(f32[28,8,128]{2,1,0:T(8,128)S(1)} %get-tuple-element.62.sent), channel_id=1, source_target_pairs={{0,4},{2,6},{4,0},{6,2},{8,12},{10,14},{12,8},{14,10},{16,20},{18,... | collective-permute-start | bytes 344072 | tf_op jit(solution)/shard_map/ppermute | solution.py:474
  43.9 4.1 %collective-permute-done.3.arrived = f32[28,8,128]{2,1,0:T(8,128)S(1)} collective-permute-done((f32[28,8,128]{2,1,0:T(8,128)S(1)}, f32[28,8,128]{2,1,0:T(8,128)S(1)}, u32[]{:S(2)}, u32[]{:S(2)}) %collective-permute-start.3) | collective-permute-done | bytes 114720 | tf_op jit(solution)/shard_map/ppermute | solution.py:474
  48.0 0.8 %collective-permute-start.4 = (f32[22,8,128]{2,1,0:T(8,128)S(1)}, f32[22,8,128]{2,1,0:T(8,128)S(1)}, u32[]{:S(2)}, u32[]{:S(2)}) collective-permute-start(f32[22,8,128]{2,1,0:T(8,128)S(1)} %get-tuple-element.64.sent), channel_id=1, source_target_pairs={{0,8},{2,10},{4,12},{6,14},{8,0},{10,2},{12,4},{14,6},{16,24},{18,... | collective-permute-start | bytes 270344 | tf_op jit(solution)/shard_map/ppermute | solution.py:474
  48.8 3.8 %collective-permute-done.4.arrived = f32[22,8,128]{2,1,0:T(8,128)S(1)} collective-permute-done((f32[22,8,128]{2,1,0:T(8,128)S(1)}, f32[22,8,128]{2,1,0:T(8,128)S(1)}, u32[]{:S(2)}, u32[]{:S(2)}) %collective-permute-start.4) | collective-permute-done | bytes 90144 | tf_op jit(solution)/shard_map/ppermute | solution.py:474
  52.6 0.9 %collective-permute-start.5 = (f32[22,8,128]{2,1,0:T(8,128)S(1)}, f32[22,8,128]{2,1,0:T(8,128)S(1)}, u32[]{:S(2)}, u32[]{:S(2)}) collective-permute-start(f32[22,8,128]{2,1,0:T(8,128)S(1)} %get-tuple-element.66.sent), channel_id=1, source_target_pairs={{0,16},{2,18},{4,20},{6,22},{8,24},{10,26},{12,28},{14,30},{16,0},... | collective-permute-start | bytes 270344 | tf_op jit(solution)/shard_map/ppermute | solution.py:474
  53.5 1.1 %finish_alignment.1 = (bf16[2,64,64]{2,1,0:T(8,128)(2,1)}, f32[8,128]{1,0:T(8,128)S(1)}) custom-call(bf16[2,64,64]{2,1,0:T(8,128)(2,1)S(1)} %copy-done.1, f32[2,64,64]{2,1,0:T(8,128)S(1)} %get-tuple-element.52.middle_grad, f32[2,64]{1,0:T(2,128)S(1)} %copy-done.7, f32[64,128]{1,0:T(8,128)S(1)} %get-tuple-element.57.normed), custom_call_target="tpu_custom_call" | custom-call | tf_op jit(solution)/shard_map/finish_alignment/pallas_call | solution.py:453
  54.7 4.4 %collective-permute-done.5.arrived = f32[22,8,128]{2,1,0:T(8,128)S(1)} collective-permute-done((f32[22,8,128]{2,1,0:T(8,128)S(1)}, f32[22,8,128]{2,1,0:T(8,128)S(1)}, u32[]{:S(2)}, u32[]{:S(2)}) %collective-permute-start.5) | collective-permute-done | bytes 90144 | tf_op jit(solution)/shard_map/ppermute | solution.py:474
  59.2 0.7 %bias_last.1 = f32[8,8,64]{2,1,0:T(8,128)} custom-call(f32[4,8,128]{2,1,0:T(8,128)S(1)} %get-tuple-element.65.state, f32[22,8,128]{2,1,0:T(8,128)S(1)} %collective-permute-done.5.arrived), custom_call_target="tpu_custom_call" | custom-call | tf_op jit(solution)/shard_map/bias_last/pallas_call | solution.py:453
  59.9 0.5 collective-permute-done.6.refs_1_
  60.4 1.1 %unpack.1 = (f32[2,64]{1,0:T(2,128)}, f32[64,256]{1,0:T(8,128)}, f32[64,64]{1,0:T(8,128)}, f32[64,144]{1,0:T(8,128)}, f32[64,64]{1,0:T(8,128)}) custom-call(f32[16,8,128]{2,1,0:T(8,128)S(1)} %get-tuple-element.68.joined, f32[10,8,128]{2,1,0:T(8,128)S(1)} %get-tuple-element.69.refs_0_, f32[10,8,128]{2,1,0:T(8,128)S(1)} %collective-permute-done.6.refs_1_, ...), custom_call_target="tpu_custom_call" | custom-call | tf_op jit(solution)/shard_map/unpack/pallas_call | solution.py:453
  (27 shorter events, 0.3 us)
Async XLA Ops:
  2.1 0.7 %copy-start.7 = (f32[2,64]{1,0:T(2,128)S(1)}, f32[2,64]{1,0:T(2,128)}, u32[]{:S(2)}) copy-start(f32[2,64]{1,0:T(2,128)} %refs_2_.3) | copy-start | bytes 1540
  2.1 0.7 %copy-start.8 = (s32[2]{0:T(128)S(1)}, s32[2]{0:T(128)}, u32[]{:S(2)}) copy-start(s32[2]{0:T(128)} %seq_mask.1) | copy-start | bytes 28
  2.1 0.8 %copy-start = (f32[64,256]{1,0:T(8,128)S(1)}, f32[64,256]{1,0:T(8,128)}, u32[]{:S(2)}) copy-start(f32[64,256]{1,0:T(8,128)} %refs_3_.3) | copy-start | bytes 196612
  2.1 0.8 %copy-start.1 = (bf16[2,64,64]{2,1,0:T(8,128)(2,1)S(1)}, bf16[2,64,64]{2,1,0:T(8,128)(2,1)}, u32[]{:S(2)}) copy-start(bf16[2,64,64]{2,1,0:T(8,128)(2,1)} %own.3) | copy-start | bytes 49156
  2.1 2.0 %copy-start.4 = (bf16[8,64,128]{2,1,0:T(8,128)(2,1)S(1)}, bf16[8,64,128]{2,1,0:T(8,128)(2,1)}, u32[]{:S(2)}) copy-start(bf16[8,64,128]{2,1,0:T(8,128)(2,1)} %refs_11_.1) | copy-start | bytes 393220
  2.2 2.0 %copy-start.3 = (f32[64,64]{1,0:T(8,128)S(1)}, f32[64,64]{1,0:T(8,128)}, u32[]{:S(2)}) copy-start(f32[64,64]{1,0:T(8,128)} %w_out.3) | copy-start | bytes 49156
  2.2 2.0 %copy-start.5 = (bf16[2,64,64]{2,1,0:T(8,128)(2,1)S(1)}, bf16[2,64,64]{2,1,0:T(8,128)(2,1)}, u32[]{:S(2)}) copy-start(bf16[2,64,64]{2,1,0:T(8,128)(2,1)} %refs_3_.2) | copy-start | bytes 49156
  2.2 1.9 %collective-permute-start = (f32[3,64,64]{2,1,0:T(8,128)S(1)}, f32[3,64,64]{2,1,0:T(8,128)S(1)}, u32[]{:S(2)}, u32[]{:S(2)}) collective-permute-start(f32[3,64,64]{2,1,0:T(8,128)S(1)} %pad_maximum_fusion.refs_0_), channel_id=1, source_target_pairs={{1,0},{0,1},{3,2},{2,3},{5,4},{4,5},{7,6},{6,7},{9,8},{8,9},{11,10... | collective-permute-start | bytes 147464 | tf_op jit(solution)/shard_map/ppermute | solution.py:466
  6.3 15.9 %copy-start.2 = (f32[64,144]{1,0:T(8,128)S(1)}, f32[64,144]{1,0:T(8,128)}, u32[]{:S(2)}) copy-start(f32[64,144]{1,0:T(8,128)} %refs_4_.3) | copy-start | bytes 110596
  6.3 15.9 %copy-start.6 = (f32[64,64]{1,0:T(8,128)S(1)}, f32[64,64]{1,0:T(8,128)}, u32[]{:S(2)}) copy-start(f32[64,64]{1,0:T(8,128)} %w_out.2) | copy-start | bytes 49156
  36.2 1.3 %collective-permute-start.1 = (f32[152,128]{1,0:T(8,128)S(1)}, f32[152,128]{1,0:T(8,128)S(1)}, u32[]{:S(2)}, u32[]{:S(2)}) collective-permute-start(f32[152,128]{1,0:T(8,128)S(1)} %get-tuple-element.56), channel_id=1, source_target_pairs={{1,0},{0,1},{3,2},{2,3},{5,4},{4,5},{7,6},{6,7},{9,8},{8,9},{11,10... | collective-permute-start | bytes 233480 | tf_op jit(solution)/shard_map/ppermute | solution.py:466
  37.6 5.5 %collective-permute-start.2 = (f32[43,8,128]{2,1,0:T(8,128)S(1)}, f32[43,8,128]{2,1,0:T(8,128)S(1)}, u32[]{:S(2)}, u32[]{:S(2)}) collective-permute-start(f32[43,8,128]{2,1,0:T(8,128)S(1)} %get-tuple-element.60.sent), channel_id=1, source_target_pairs={{0,2},{2,0},{4,6},{6,4},{8,10},{10,8},{12,14},{14,12},{16,18},{18,... | collective-permute-start | bytes 528392 | tf_op jit(solution)/shard_map/ppermute | solution.py:474
  43.1 4.9 %collective-permute-start.3 = (f32[28,8,128]{2,1,0:T(8,128)S(1)}, f32[28,8,128]{2,1,0:T(8,128)S(1)}, u32[]{:S(2)}, u32[]{:S(2)}) collective-permute-start(f32[28,8,128]{2,1,0:T(8,128)S(1)} %get-tuple-element.62.sent), channel_id=1, source_target_pairs={{0,4},{2,6},{4,0},{6,2},{8,12},{10,14},{12,8},{14,10},{16,20},{18,... | collective-permute-start | bytes 344072 | tf_op jit(solution)/shard_map/ppermute | solution.py:474
  48.0 4.6 %collective-permute-start.4 = (f32[22,8,128]{2,1,0:T(8,128)S(1)}, f32[22,8,128]{2,1,0:T(8,128)S(1)}, u32[]{:S(2)}, u32[]{:S(2)}) collective-permute-start(f32[22,8,128]{2,1,0:T(8,128)S(1)} %get-tuple-element.64.sent), channel_id=1, source_target_pairs={{0,8},{2,10},{4,12},{6,14},{8,0},{10,2},{12,4},{14,6},{16,24},{18,... | collective-permute-start | bytes 270344 | tf_op jit(solution)/shard_map/ppermute | solution.py:474
  52.6 6.5 %collective-permute-start.5 = (f32[22,8,128]{2,1,0:T(8,128)S(1)}, f32[22,8,128]{2,1,0:T(8,128)S(1)}, u32[]{:S(2)}, u32[]{:S(2)}) collective-permute-start(f32[22,8,128]{2,1,0:T(8,128)S(1)} %get-tuple-element.66.sent), channel_id=1, source_target_pairs={{0,16},{2,18},{4,20},{6,22},{8,24},{10,26},{12,28},{14,30},{16,0},... | collective-permute-start | bytes 270344 | tf_op jit(solution)/shard_map/ppermute | solution.py:474
  59.1 1.3 %collective-permute-start.6 = (f32[10,8,128]{2,1,0:T(8,128)S(1)}, f32[10,8,128]{2,1,0:T(8,128)S(1)}, u32[]{:S(2)}, u32[]{:S(2)}) collective-permute-start(f32[10,8,128]{2,1,0:T(8,128)S(1)} %get-tuple-element.69.refs_0_), channel_id=1, source_target_pairs={{1,0},{0,1},{3,2},{2,3},{5,4},{4,5},{7,6},{6,7},{9,8},{8,9},{11,10... | collective-permute-start | bytes 122888 | tf_op jit(solution)/shard_map/ppermute | solution.py:466

commit v11 on v10

--- a/solution.py
+++ b/solution.py
@@ -306,7 +306,7 @@
         if rows:
             shares[i, :rows, :] = weight_grads[i * part : i * part + rows, :]
         shares[i, part : part + share, :] = column[0]
-        shares[i, part + share : part + 2 * share, :] = column[1]
+        shares[i, part + ROWS // 2 : part + ROWS // 2 + share, :] = column[1]
         shares[i, part + ROWS :, :] = normed[i * n_rows : (i + 1) * n_rows, :]
     for away in range(n_res):
         sums_out[away][...] = shares[lax.rem(me + away, n_res)]
@@ -364,29 +364,36 @@
     left = bias_send.shape[0]
     rows = total.shape[0] - normed.shape[0]
     send[:left] = bias_send[...]
-    send[left:] = total[:rows].reshape(rows // ROWS, ROWS, LANES)
+    send[left : send.shape[0] - 1] = total[: rows - ROWS].reshape(rows // ROWS - 1, ROWS, LANES)
+    piece = total[rows - ROWS : rows]
+    odd = lax.rem(lax.axis_index("res"), 2)
+    send[send.shape[0] - 1] = jnp.where(odd == 1, pltpu.roll(piece, ROWS // 2, 0), piece)
     normed[...] = total[rows:]
 
 
-def step(part, state, sent, arrived, state_out, send):
+def step(part, first, state, sent, arrived, state_out, send):
     left = state.shape[0]
     half = left // 2
     total = state[...] + arrived[:left]
     state_out[...] = total[:half]
     send[:half] = total[half:]
     send[half : half + part] = sent[left : left + part] + arrived[left : left + part]
-    pieces = sent.shape[0] - left - part
-    send[half + part : half + part + pieces] = sent[left + part :]
-    send[half + part + pieces :] = arrived[left + part :]
-
-
-def last_step(sent, arrived, _, shared, joined):
-    part = shared.shape[0]
-    pieces = joined.shape[0] // 2
+    at = half + part
+    if first:
+        half_rows = ROWS // 2
+        send[at] = jnp.concatenate([sent[left + part][:half_rows], arrived[left + part][:half_rows]], axis=0)
+    else:
+        pieces = sent.shape[0] - left - part
+        send[at : at + pieces] = sent[left + part :]
+        send[at + pieces :] = arrived[left + part :]
+
+
+def last_step(part, sent, arrived, _, shared):
+    pieces = (shared.shape[0] - part) // 2
     left = sent.shape[0] - part - pieces
-    shared[...] = sent[left : left + part] + arrived[left : left + part]
-    joined[:pieces] = sent[left + part :]
-    joined[pieces:] = arrived[left + part :]
+    shared[:part] = sent[left : left + part] + arrived[left : left + part]
+    shared[part : part + pieces] = sent[left + part :]
+    shared[part + pieces :] = arrived[left + part :]
 
 
 def finish_alignment(own, middle_grad, gains, normed, out, done):
@@ -398,23 +405,23 @@
         out[s] = (middle_grad[s] + normalise_back(grad_normed, gains[0:1, :], unit, inverse)).astype(out.dtype)
 
 
-def unpack(n_res, joined, *refs):
+def unpack(n_res, *refs):
     parts = refs[:n_res]
     gains, w_row, w_col, gains_out, row_project_out, row_out_out, col_project_out, col_out_out = refs[n_res : n_res + 8]
     shares, column = refs[n_res + 8 :]
     me = lax.axis_index("res")
-    part = shares.shape[1]
     for away in range(n_res):
-        shares[lax.rem(me + away, n_res)] = parts[away][...].reshape(part, LANES)
+        shares[lax.rem(me + away, n_res)] = parts[away][...]
     n_blocks, _, share, _ = column.shape
-    for slot in range(n_blocks):
-        block = relative_block(
-            lambda bits: sum(1 << bit for at, bit in enumerate(bits) if slot >> at & 1), n_blocks
-        )
-        piece = joined[slot]
-        column[block, 0] = piece[:share]
-        column[block, 1] = piece[share : 2 * share]
-    flat = jnp.concatenate([shares[i] for i in range(n_res)], axis=0)
+    part = shares.shape[1] - n_blocks // 2
+    place = lax.axis_index("seq")
+    for half in range(2):
+        bits = step_bits(n_blocks, half == 1)
+        for slot in range(n_blocks):
+            block = place ^ sum(1 << bit for at, bit in enumerate(bits) if slot >> at & 1)
+            row = slot % 2 * (ROWS // 2)
+            column[block, half] = shares[half, part + slot // 2, row : row + share, :]
+    flat = jnp.concatenate([shares[i, :part].reshape(part * ROWS, LANES) for i in range(n_res)], axis=0)
     query_gate, memory, outs = flat[:C], flat[C : 2 * C], flat[2 * C : 2 * C + C // 2]
     col_query_gate = jnp.concatenate([column[i, 0] for i in range(n_blocks)], axis=0)
     col_rest = jnp.concatenate([column[i, 1] for i in range(n_blocks)], axis=0)
@@ -572,14 +579,14 @@
         if at < steps - 1:
             left //= 2
             state, send = call(
-                functools.partial(step, part_tiles),
-                [((left, ROWS, LANES), F32), ((left + part_tiles + (2 << at), ROWS, LANES), F32)],
+                functools.partial(step, part_tiles, at == 0),
+                [((left, ROWS, LANES), F32), ((left + part_tiles + (1 << at), ROWS, LANES), F32)],
                 state, send, arrived,
                 name="step",
             )
-    shared, joined = call(
-        last_step,
-        [((part_tiles, ROWS, LANES), F32), ((seq_count, ROWS, LANES), F32)],
+    (shared,) = call(
+        functools.partial(last_step, part_tiles),
+        [((part_tiles + seq_count // 2, ROWS, LANES), F32)],
         send, arrived, done,
         unread=1,
         name="last_step",
@@ -588,10 +595,10 @@
     grads = call(
         functools.partial(unpack, res_count),
         [((2, C), F32), ((C, 4 * C), F32), ((C, C), F32), ((C, 2 * C + 2 * DH), F32), ((C, C), F32)],
-        joined, shared, *[shift_residues(shared, away, res_count) for away in away_range],
+        shared, *[shift_residues(shared, away, res_count) for away in away_range],
         norm_gains, row_project, column_project,
         scratch=[
-            pltpu.VMEM((res_count, part, LANES), F32),
+            pltpu.VMEM((res_count, part_tiles + seq_count // 2, ROWS, LANES), F32),
             pltpu.VMEM((seq_count, 2, C // seq_count, LANES), F32),
         ],
         name="unpack",

time: 61.8 us -> 61.3 us (level)
  no operation moved by 1% of the time
where the time goes in v11:
time: 61.3 us; the launch traced here: 61 us
  blocking collectives  26.2 us (43%)
  waiting for transfers between devices  18.1 us (30%)
  Pallas kernels  10 us (16%)
  starting transfers between devices  4.1 us (7%)
  other arithmetic  1.43 us (2%)
  between operations  0.78 us (1%)
    all_to_all x2, blocking collectives, swap_blocks(): return lax.all_to_all(values, 'seq', 0, 0, tiled=True)  26.2 us
    ppermute x4, waiting for transfers between devices, cross(): return lax.ppermute(values, ('seq', 'res'), pairs)  16.4 us
    pallas_call x13, Pallas kernels, call(): pl.pallas_call(body, out_shape=[jax.ShapeDtypeStruct(shape, kind) for sha...  10 us
    ppermute x4, starting transfers between devices, cross(): return lax.ppermute(values, ('seq', 'res'), pairs)  3.44 us
    ppermute x3, waiting for transfers between devices, shift_residues(): lax.ppermute(values, 'res', [((i + away) % count, i) for i in range(count)])  1.78 us
  transfers between devices with their start and end apart: 7, of which 6 were waited for; matrix products, arithmetic and copies ran while one was open for 0% of the time, Pallas kernels for 5%

profile of v11, /device:TPU:0, one launch (start us, length us, event | category | flops | bytes accessed | tf_op | source)
XLA Modules:
  0.0 61.0 jit_solution(15978792978736893749)
XLA Ops:
  0.6 0.7 %convert_element_type.7 = f32[64]{0:T(128)S(1)} convert(s32[64]{0:T(128)} %param.18) | non-fusion elementwise | flops 64 | bytes 512 | tf_op jit(solution)/shard_map/convert_element_type | solution.py:507
  1.3 0.8 %convert_element_type.6 = f32[2,64,64]{2,1,0:T(8,128)S(1)} convert(bf16[2,64,64]{2,1,0:T(8,128)(2,1)} %own.3) | non-fusion elementwise | flops 8192 | bytes 49152 | tf_op jit(solution)/shard_map/convert_element_type | solution.py:508
  2.1 0.1 broadcast_in_dim.2
  2.2 0.5 collective-permute-start
  2.7 0.2 copy-done
  3.0 1.1 %own_half.1 = (f32[2,64,64]{2,1,0:T(8,128)S(1)}, f32[2,64,128]{2,1,0:T(8,128)S(1)}, f32[2,64,512]{2,1,0:T(8,128)S(1)}, f32[2,64,128]{2,1,0:T(8,128)S(1)}, f32[4,128]{1,0:T(4,128)S(1)}) custom-call(s32[2]{0:T(128)S(1)} %copy-done.8, bf16[2,64,64]{2,1,0:T(8,128)(2,1)S(1)} %copy-done.1, f32[2,64]{1,0:T(2,128)S(1)} %copy-done.7, f32[64,256]{1,0:T(8,128)S(1)} %copy-done), custom_call_target="tpu_custom_call" | custom-call | tf_op jit(solution)/shard_map/own_half/pallas_call | solution.py:460
  4.2 2.2 %row_forward.1 = (f32[16,3,4,128]{3,2,1,0:T(4,128)S(1)}, f32[2,128,512]{2,1,0:T(8,128)S(1)}, f32[2,2,64,64]{3,2,1,0:T(8,128)S(1)}, f32[2,2,64,128]{3,2,1,0:T(8,1...) custom-call(f32[3,64,64]{2,1,0:T(8,128)S(1)} %pad_maximum_fusion.refs_0_, ...), custom_call_target="tpu_custom_call" | custom-call | tf_op jit(solution)/shard_map/row_forward/pallas_call | solution.py:460
  6.3 15.9 %all_to_all.10.arrived = f32[16,3,4,128]{3,2,1,0:T(4,128)S(1)} all-to-all(f32[16,3,4,128]{3,2,1,0:T(4,128)S(1)} %get-tuple-element.44), channel_id=1, replica_groups=mesh['seq'=16,'res'=2] {'seq'}, dimensions={0} | all-to-all | bytes 196608 | tf_op jit(solution)/shard_map/all_to_all | solution.py:485
  22.3 1.7 %column_step.1 = f32[16,3,4,128]{3,2,1,0:T(4,128)S(1)} custom-call(f32[16,3,4,128]{3,2,1,0:T(4,128)S(1)} %all_to_all.10.arrived, f32[2,64]{1,0:T(2,128)S(1)} %copy-done.7, f32[64,144]{1,0:T(8,128)S(1)} %copy-done.2, f32[64,64]{1,0:T(8,128)S(1)} %copy-done.6), custom_call_target="tpu_custom_call" | custom-call | tf_op jit(solution)/shard_map/column_step/pallas_call | solution.py:460
  23.9 10.3 %all_to_all.11.returned = f32[16,3,4,128]{3,2,1,0:T(4,128)S(1)} all-to-all(f32[16,3,4,128]{3,2,1,0:T(4,128)S(1)} %column_step.1), channel_id=1, replica_groups=mesh['seq'=16,'res'=2] {'seq'}, dimensions={0} | all-to-all | bytes 196608 | tf_op jit(solution)/shard_map/all_to_all | solution.py:485
  34.2 2.0 %row_backward.1 = (f32[128,512]{1,0:T(8,128)S(1)}, f32[2,64,64]{2,1,0:T(8,128)S(1)}, f32[152,128]{1,0:T(8,128)S(1)}, f32[152,128]{1,0:T(8,128)S(1)}) custom-call(f32[16,3,4,128]{3,2,1,0:T(4,128)S(1)} %all_to_all.11.returned, f32[2,128,512]{2,1,0:T(8,128)S(1)} %get-tuple-element.45.exponent_in, f32[2,2,64,64]{3,2,1,0:T(8,128)S(1)} %get-tuple-element.46.unit_in, ...), custom_call_target="tpu_custom_call" | custom-call | tf_op jit(solution)/shard_map/row_backward/pallas_call | solution.py:460
  36.3 1.2 %collective-permute-done.1.refs_1_ = f32[152,128]{1,0:T(8,128)S(1)} collective-permute-done((f32[152,128]{1,0:T(8,128)S(1)}, f32[152,128]{1,0:T(8,128)S(1)}, u32[]{:S(2)}, u32[]{:S(2)}) %collective-permute-start.1) | collective-permute-done | bytes 77856 | tf_op jit(solution)/shard_map/ppermute | solution.py:473
  37.6 1.0 %collective-permute-start.2 = (f32[43,8,128]{2,1,0:T(8,128)S(1)}, f32[43,8,128]{2,1,0:T(8,128)S(1)}, u32[]{:S(2)}, u32[]{:S(2)}) collective-permute-start(f32[43,8,128]{2,1,0:T(8,128)S(1)} %get-tuple-element.58.sent), channel_id=1, source_target_pairs={{0,2},{2,0},{4,6},{6,4},{8,10},{10,8},{12,14},{14,12},{16,18},{18,... | collective-permute-start | bytes 528392 | tf_op jit(solution)/shard_map/ppermute | solution.py:481
  38.6 4.5 %collective-permute-done.2.arrived = f32[43,8,128]{2,1,0:T(8,128)S(1)} collective-permute-done((f32[43,8,128]{2,1,0:T(8,128)S(1)}, f32[43,8,128]{2,1,0:T(8,128)S(1)}, u32[]{:S(2)}, u32[]{:S(2)}) %collective-permute-start.2) | collective-permute-done | bytes 176160 | tf_op jit(solution)/shard_map/ppermute | solution.py:481
  43.1 0.7 %collective-permute-start.3 = (f32[27,8,128]{2,1,0:T(8,128)S(1)}, f32[27,8,128]{2,1,0:T(8,128)S(1)}, u32[]{:S(2)}, u32[]{:S(2)}) collective-permute-start(f32[27,8,128]{2,1,0:T(8,128)S(1)} %get-tuple-element.60.sent), channel_id=1, source_target_pairs={{0,4},{2,6},{4,0},{6,2},{8,12},{10,14},{12,8},{14,10},{16,20},{18,... | collective-permute-start | bytes 331784 | tf_op jit(solution)/shard_map/ppermute | solution.py:481
  43.9 4.1 %collective-permute-done.3.arrived = f32[27,8,128]{2,1,0:T(8,128)S(1)} collective-permute-done((f32[27,8,128]{2,1,0:T(8,128)S(1)}, f32[27,8,128]{2,1,0:T(8,128)S(1)}, u32[]{:S(2)}, u32[]{:S(2)}) %collective-permute-start.3) | collective-permute-done | bytes 110624 | tf_op jit(solution)/shard_map/ppermute | solution.py:481
  48.0 0.8 %collective-permute-start.4 = (f32[20,8,128]{2,1,0:T(8,128)S(1)}, f32[20,8,128]{2,1,0:T(8,128)S(1)}, u32[]{:S(2)}, u32[]{:S(2)}) collective-permute-start(f32[20,8,128]{2,1,0:T(8,128)S(1)} %get-tuple-element.62.sent), channel_id=1, source_target_pairs={{0,8},{2,10},{4,12},{6,14},{8,0},{10,2},{12,4},{14,6},{16,24},{18,... | collective-permute-start | bytes 245768 | tf_op jit(solution)/shard_map/ppermute | solution.py:481
  48.7 3.7 %collective-permute-done.4.arrived = f32[20,8,128]{2,1,0:T(8,128)S(1)} collective-permute-done((f32[20,8,128]{2,1,0:T(8,128)S(1)}, f32[20,8,128]{2,1,0:T(8,128)S(1)}, u32[]{:S(2)}, u32[]{:S(2)}) %collective-permute-start.4) | collective-permute-done | bytes 81952 | tf_op jit(solution)/shard_map/ppermute | solution.py:481
  52.5 0.9 %collective-permute-start.5 = (f32[18,8,128]{2,1,0:T(8,128)S(1)}, f32[18,8,128]{2,1,0:T(8,128)S(1)}, u32[]{:S(2)}, u32[]{:S(2)}) collective-permute-start(f32[18,8,128]{2,1,0:T(8,128)S(1)} %get-tuple-element.64.sent), channel_id=1, source_target_pairs={{0,16},{2,18},{4,20},{6,22},{8,24},{10,26},{12,28},{14,30},{16,0},... | collective-permute-start | bytes 221192 | tf_op jit(solution)/shard_map/ppermute | solution.py:481
  53.4 1.1 %finish_alignment.1 = (bf16[2,64,64]{2,1,0:T(8,128)(2,1)}, f32[8,128]{1,0:T(8,128)S(1)}) custom-call(bf16[2,64,64]{2,1,0:T(8,128)(2,1)S(1)} %copy-done.1, f32[2,64,64]{2,1,0:T(8,128)S(1)} %get-tuple-element.50.middle_grad, f32[2,64]{1,0:T(2,128)S(1)} %copy-done.7, f32[64,128]{1,0:T(8,128)S(1)} %get-tuple-element.55.normed), custom_call_target="tpu_custom_call" | custom-call | tf_op jit(solution)/shard_map/finish_alignment/pallas_call | solution.py:460
  54.5 4.1 %collective-permute-done.5.arrived = f32[18,8,128]{2,1,0:T(8,128)S(1)} collective-permute-done((f32[18,8,128]{2,1,0:T(8,128)S(1)}, f32[18,8,128]{2,1,0:T(8,128)S(1)}, u32[]{:S(2)}, u32[]{:S(2)}) %collective-permute-start.5) | collective-permute-done | bytes 73760 | tf_op jit(solution)/shard_map/ppermute | solution.py:481
  58.7 0.7 %bias_last.1 = f32[8,8,64]{2,1,0:T(8,128)} custom-call(f32[4,8,128]{2,1,0:T(8,128)S(1)} %get-tuple-element.63.state, f32[18,8,128]{2,1,0:T(8,128)S(1)} %collective-permute-done.5.arrived), custom_call_target="tpu_custom_call" | custom-call | tf_op jit(solution)/shard_map/bias_last/pallas_call | solution.py:460
  59.4 0.6 collective-permute-done.6.refs_1_
  59.9 1.1 %unpack.1 = (f32[2,64]{1,0:T(2,128)}, f32[64,256]{1,0:T(8,128)}, f32[64,64]{1,0:T(8,128)}, f32[64,144]{1,0:T(8,128)}, f32[64,64]{1,0:T(8,128)}) custom-call(f32[18,8,128]{2,1,0:T(8,128)S(1)} %last_step.1.refs_0_, f32[18,8,128]{2,1,0:T(8,128)S(1)} %collective-permute-done.6.refs_1_, f32[2,64]{1,0:T(2,128)S(1)} %copy-done.7, f32[64,256]{1,0:T(8,128)S(1)} %copy-done, ...), custom_call_target="tpu_custom_call" | custom-call | tf_op jit(solution)/shard_map/unpack/pallas_call | solution.py:460
  (27 shorter events, 0.3 us)
Async XLA Ops:
  2.1 0.7 %copy-start.7 = (f32[2,64]{1,0:T(2,128)S(1)}, f32[2,64]{1,0:T(2,128)}, u32[]{:S(2)}) copy-start(f32[2,64]{1,0:T(2,128)} %refs_2_.3) | copy-start | bytes 1540
  2.1 0.7 %copy-start.8 = (s32[2]{0:T(128)S(1)}, s32[2]{0:T(128)}, u32[]{:S(2)}) copy-start(s32[2]{0:T(128)} %seq_mask.1) | copy-start | bytes 28
  2.1 0.8 %copy-start = (f32[64,256]{1,0:T(8,128)S(1)}, f32[64,256]{1,0:T(8,128)}, u32[]{:S(2)}) copy-start(f32[64,256]{1,0:T(8,128)} %refs_3_.3) | copy-start | bytes 196612
  2.1 0.8 %copy-start.1 = (bf16[2,64,64]{2,1,0:T(8,128)(2,1)S(1)}, bf16[2,64,64]{2,1,0:T(8,128)(2,1)}, u32[]{:S(2)}) copy-start(bf16[2,64,64]{2,1,0:T(8,128)(2,1)} %own.3) | copy-start | bytes 49156
  2.1 2.0 %copy-start.4 = (bf16[8,64,128]{2,1,0:T(8,128)(2,1)S(1)}, bf16[8,64,128]{2,1,0:T(8,128)(2,1)}, u32[]{:S(2)}) copy-start(bf16[8,64,128]{2,1,0:T(8,128)(2,1)} %refs_11_.1) | copy-start | bytes 393220
  2.2 2.0 %copy-start.3 = (f32[64,64]{1,0:T(8,128)S(1)}, f32[64,64]{1,0:T(8,128)}, u32[]{:S(2)}) copy-start(f32[64,64]{1,0:T(8,128)} %w_out.3) | copy-start | bytes 49156
  2.2 2.0 %copy-start.5 = (bf16[2,64,64]{2,1,0:T(8,128)(2,1)S(1)}, bf16[2,64,64]{2,1,0:T(8,128)(2,1)}, u32[]{:S(2)}) copy-start(bf16[2,64,64]{2,1,0:T(8,128)(2,1)} %refs_3_.2) | copy-start | bytes 49156
  2.2 1.9 %collective-permute-start = (f32[3,64,64]{2,1,0:T(8,128)S(1)}, f32[3,64,64]{2,1,0:T(8,128)S(1)}, u32[]{:S(2)}, u32[]{:S(2)}) collective-permute-start(f32[3,64,64]{2,1,0:T(8,128)S(1)} %pad_maximum_fusion.refs_0_), channel_id=1, source_target_pairs={{1,0},{0,1},{3,2},{2,3},{5,4},{4,5},{7,6},{6,7},{9,8},{8,9},{11,10... | collective-permute-start | bytes 147464 | tf_op jit(solution)/shard_map/ppermute | solution.py:473
  6.3 15.9 %copy-start.2 = (f32[64,144]{1,0:T(8,128)S(1)}, f32[64,144]{1,0:T(8,128)}, u32[]{:S(2)}) copy-start(f32[64,144]{1,0:T(8,128)} %refs_4_.3) | copy-start | bytes 110596
  6.3 15.9 %copy-start.6 = (f32[64,64]{1,0:T(8,128)S(1)}, f32[64,64]{1,0:T(8,128)}, u32[]{:S(2)}) copy-start(f32[64,64]{1,0:T(8,128)} %w_out.2) | copy-start | bytes 49156
  36.2 1.3 %collective-permute-start.1 = (f32[152,128]{1,0:T(8,128)S(1)}, f32[152,128]{1,0:T(8,128)S(1)}, u32[]{:S(2)}, u32[]{:S(2)}) collective-permute-start(f32[152,128]{1,0:T(8,128)S(1)} %get-tuple-element.54), channel_id=1, source_target_pairs={{1,0},{0,1},{3,2},{2,3},{5,4},{4,5},{7,6},{6,7},{9,8},{8,9},{11,10... | collective-permute-start | bytes 233480 | tf_op jit(solution)/shard_map/ppermute | solution.py:473
  37.6 5.5 %collective-permute-start.2 = (f32[43,8,128]{2,1,0:T(8,128)S(1)}, f32[43,8,128]{2,1,0:T(8,128)S(1)}, u32[]{:S(2)}, u32[]{:S(2)}) collective-permute-start(f32[43,8,128]{2,1,0:T(8,128)S(1)} %get-tuple-element.58.sent), channel_id=1, source_target_pairs={{0,2},{2,0},{4,6},{6,4},{8,10},{10,8},{12,14},{14,12},{16,18},{18,... | collective-permute-start | bytes 528392 | tf_op jit(solution)/shard_map/ppermute | solution.py:481
  43.1 4.8 %collective-permute-start.3 = (f32[27,8,128]{2,1,0:T(8,128)S(1)}, f32[27,8,128]{2,1,0:T(8,128)S(1)}, u32[]{:S(2)}, u32[]{:S(2)}) collective-permute-start(f32[27,8,128]{2,1,0:T(8,128)S(1)} %get-tuple-element.60.sent), channel_id=1, source_target_pairs={{0,4},{2,6},{4,0},{6,2},{8,12},{10,14},{12,8},{14,10},{16,20},{18,... | collective-permute-start | bytes 331784 | tf_op jit(solution)/shard_map/ppermute | solution.py:481
  48.0 4.5 %collective-permute-start.4 = (f32[20,8,128]{2,1,0:T(8,128)S(1)}, f32[20,8,128]{2,1,0:T(8,128)S(1)}, u32[]{:S(2)}, u32[]{:S(2)}) collective-permute-start(f32[20,8,128]{2,1,0:T(8,128)S(1)} %get-tuple-element.62.sent), channel_id=1, source_target_pairs={{0,8},{2,10},{4,12},{6,14},{8,0},{10,2},{12,4},{14,6},{16,24},{18,... | collective-permute-start | bytes 245768 | tf_op jit(solution)/shard_map/ppermute | solution.py:481
  52.5 6.1 %collective-permute-start.5 = (f32[18,8,128]{2,1,0:T(8,128)S(1)}, f32[18,8,128]{2,1,0:T(8,128)S(1)}, u32[]{:S(2)}, u32[]{:S(2)}) collective-permute-start(f32[18,8,128]{2,1,0:T(8,128)S(1)} %get-tuple-element.64.sent), channel_id=1, source_target_pairs={{0,16},{2,18},{4,20},{6,22},{8,24},{10,26},{12,28},{14,30},{16,0},... | collective-permute-start | bytes 221192 | tf_op jit(solution)/shard_map/ppermute | solution.py:481
  58.6 1.3 %collective-permute-start.6 = (f32[18,8,128]{2,1,0:T(8,128)S(1)}, f32[18,8,128]{2,1,0:T(8,128)S(1)}, u32[]{:S(2)}, u32[]{:S(2)}) collective-permute-start(f32[18,8,128]{2,1,0:T(8,128)S(1)} %last_step.1.refs_0_), channel_id=1, source_target_pairs={{1,0},{0,1},{3,2},{2,3},{5,4},{4,5},{7,6},{6,7},{9,8},{8,9},{11,10... | collective-permute-start | bytes 221192 | tf_op jit(solution)/shard_map/ppermute | solution.py:473

commit v12 on v11

--- a/solution.py
+++ b/solution.py
@@ -80,15 +80,20 @@
     return jnp.transpose(joined)
 
 
-def own_half(seq_mask, own, gains, w_row,
-             own_unit_out, query_gate_out, query_heads_out, own_memory_out, present_out):
-    n_seq, n_rows, _ = own.shape
+def own_norm(sent, own_unit_out):
+    n_seq, n_rows, _ = own_unit_out.shape
+    units, _ = normalise(sent[:n_seq].reshape(n_seq * n_rows, C))
+    own_unit_out[...] = units.reshape(n_seq, n_rows, C)
+
+
+def own_half(seq_mask, own_unit, gains, w_row,
+             query_gate_out, query_heads_out, own_memory_out, present_out):
+    n_seq, n_rows, _ = own_unit.shape
     w_all = w_row[...]
-    own_units, _ = normalise(own[...].reshape(n_seq * n_rows, C).astype(F32))
+    own_units = own_unit[...].reshape(n_seq * n_rows, C)
     projected = dot(own_units * gains[0:1, :], w_all, precision=EXACT)
     queries = projected[:, :C] * SCALE
     gates = jax.nn.sigmoid(projected[:, 3 * C :])
-    own_unit_out[...] = own_units.reshape(n_seq, n_rows, C)
     query_gate_out[...] = jnp.concatenate([queries, gates], axis=1).reshape(n_seq, n_rows, 2 * C)
     own_memory_out[...] = projected[:, C : 3 * C].reshape(n_seq, n_rows, 2 * C)
     mask = head_mask(n_rows)
@@ -506,16 +511,16 @@
     away_range = range(1, res_count)
     present_keys = jnp.broadcast_to(residue_mask.astype(F32)[None, :, None], (1, n_rows, C))
     sent = jnp.concatenate([alignment.astype(F32), present_keys], axis=0)
-    own_unit, query_gate, query_heads, own_memory, present = call(
+    (own_unit,) = call(own_norm, [((n_seq, n_rows, C), F32)], sent, name="own_norm")
+    query_gate, query_heads, own_memory, present = call(
         own_half,
         [
-            ((n_seq, n_rows, C), F32),
             ((n_seq, n_rows, 2 * C), F32),
             ((n_seq, C, H * n_rows), F32),
             ((n_seq, n_rows, 2 * C), F32),
             ((block, 2 * C), F32),
         ],
-        sequence_mask, alignment, norm_gains, row_project,
+        sequence_mask, own_unit, norm_gains, row_project,
         smem=1,
         name="own_half",
     )

time: 61.3 us -> 61.2 us (level)
    pallas_call x13 -> x14, Pallas kernels: 10 us -> 10 us  [call(): pl.pallas_call(body, out_shape=[jax.ShapeDtypeStruct(shape, kind) for sha...]
where the time goes in v12:
time: 61.2 us; the launch traced here: 60.9 us
  blocking collectives  26.2 us (43%)
  waiting for transfers between devices  18.2 us (30%)
  Pallas kernels  10 us (16%)
  starting transfers between devices  4.07 us (7%)
  other arithmetic  1.43 us (2%)
  between operations  0.8 us (1%)
    all_to_all x2, blocking collectives, swap_blocks(): return lax.all_to_all(values, 'seq', 0, 0, tiled=True)  26.2 us
    ppermute x4, waiting for transfers between devices, cross(): return lax.ppermute(values, ('seq', 'res'), pairs)  16.4 us
    pallas_call x14, Pallas kernels, call(): pl.pallas_call(body, out_shape=[jax.ShapeDtypeStruct(shape, kind) for sha...  10 us
    ppermute x4, starting transfers between devices, cross(): return lax.ppermute(values, ('seq', 'res'), pairs)  3.41 us
    ppermute x3, waiting for transfers between devices, shift_residues(): lax.ppermute(values, 'res', [((i + away) % count, i) for i in range(count)])  1.78 us
  transfers between devices with their start and end apart: 7, of which 6 were waited for; matrix products, arithmetic and copies ran while one was open for 0% of the time, Pallas kernels for 5%

profile of v12, /device:TPU:0, one launch (start us, length us, event | category | flops | bytes accessed | tf_op | source)
XLA Modules:
  0.0 60.9 jit_solution(2020697965973341047)
XLA Ops:
  0.6 0.7 %convert_element_type.7 = f32[64]{0:T(128)S(1)} convert(s32[64]{0:T(128)} %param.18) | non-fusion elementwise | flops 64 | bytes 512 | tf_op jit(solution)/shard_map/convert_element_type | solution.py:512
  1.3 0.8 %convert_element_type.6 = f32[2,64,64]{2,1,0:T(8,128)S(1)} convert(bf16[2,64,64]{2,1,0:T(8,128)(2,1)} %own.1) | non-fusion elementwise | flops 8192 | bytes 49152 | tf_op jit(solution)/shard_map/convert_element_type | solution.py:513
  2.2 0.5 collective-permute-start
  2.7 0.2 own_norm.1.own_unit.refs_7_.own_unit_in
  2.9 0.1 copy-done
  3.0 1.0 %own_half.1 = (f32[2,64,128]{2,1,0:T(8,128)S(1)}, f32[2,64,512]{2,1,0:T(8,128)S(1)}, f32[2,64,128]{2,1,0:T(8,128)S(1)}, f32[4,128]{1,0:T(4,128)S(1)}) custom-call(s32[2]{0:T(128)S(1)} %copy-done.8, f32[2,64,64]{2,1,0:T(8,128)S(1)} %own_norm.1.own_unit.refs_7_.own_unit_in, f32[2,64]{1,0:T(2,128)S(1)} %copy-done.7, f32[64,256]{1,0:T(8,128)S(1)} %copy-done), custom_call_target="tpu_custom_call" | custom-call | tf_op jit(solution)/shard_map/own_half/pallas_call | solution.py:465
  4.0 2.2 %row_forward.1 = (f32[16,3,4,128]{3,2,1,0:T(4,128)S(1)}, f32[2,128,512]{2,1,0:T(8,128)S(1)}, f32[2,2,64,64]{3,2,1,0:T(8,128)S(1)}, f32[2,2,64,128]{3,2,1,0:T(8,1...) custom-call(f32[3,64,64]{2,1,0:T(8,128)S(1)} %pad_maximum_fusion.sent.refs_0_, ...), custom_call_target="tpu_custom_call" | custom-call | tf_op jit(solution)/shard_map/row_forward/pallas_call | solution.py:465
  6.2 15.9 %all_to_all.10.arrived = f32[16,3,4,128]{3,2,1,0:T(4,128)S(1)} all-to-all(f32[16,3,4,128]{3,2,1,0:T(4,128)S(1)} %get-tuple-element.42), channel_id=1, replica_groups=mesh['seq'=16,'res'=2] {'seq'}, dimensions={0} | all-to-all | bytes 196608 | tf_op jit(solution)/shard_map/all_to_all | solution.py:490
  22.1 1.7 %column_step.1 = f32[16,3,4,128]{3,2,1,0:T(4,128)S(1)} custom-call(f32[16,3,4,128]{3,2,1,0:T(4,128)S(1)} %all_to_all.10.arrived, f32[2,64]{1,0:T(2,128)S(1)} %copy-done.7, f32[64,144]{1,0:T(8,128)S(1)} %copy-done.2, f32[64,64]{1,0:T(8,128)S(1)} %copy-done.6), custom_call_target="tpu_custom_call" | custom-call | tf_op jit(solution)/shard_map/column_step/pallas_call | solution.py:465
  23.8 10.3 %all_to_all.11.returned = f32[16,3,4,128]{3,2,1,0:T(4,128)S(1)} all-to-all(f32[16,3,4,128]{3,2,1,0:T(4,128)S(1)} %column_step.1), channel_id=1, replica_groups=mesh['seq'=16,'res'=2] {'seq'}, dimensions={0} | all-to-all | bytes 196608 | tf_op jit(solution)/shard_map/all_to_all | solution.py:490
  34.1 2.0 %row_backward.1 = (f32[128,512]{1,0:T(8,128)S(1)}, f32[2,64,64]{2,1,0:T(8,128)S(1)}, f32[152,128]{1,0:T(8,128)S(1)}, f32[152,128]{1,0:T(8,128)S(1)}) custom-call(f32[16,3,4,128]{3,2,1,0:T(4,128)S(1)} %all_to_all.11.returned, f32[2,128,512]{2,1,0:T(8,128)S(1)} %get-tuple-element.43.exponent_in, f32[2,2,64,64]{3,2,1,0:T(8,128)S(1)} %get-tuple-element.44.unit_in, ...), custom_call_target="tpu_custom_call" | custom-call | tf_op jit(solution)/shard_map/row_backward/pallas_call | solution.py:465
  36.2 1.2 %collective-permute-done.1.refs_1_ = f32[152,128]{1,0:T(8,128)S(1)} collective-permute-done((f32[152,128]{1,0:T(8,128)S(1)}, f32[152,128]{1,0:T(8,128)S(1)}, u32[]{:S(2)}, u32[]{:S(2)}) %collective-permute-start.1) | collective-permute-done | bytes 77856 | tf_op jit(solution)/shard_map/ppermute | solution.py:478
  37.5 1.0 %collective-permute-start.2 = (f32[43,8,128]{2,1,0:T(8,128)S(1)}, f32[43,8,128]{2,1,0:T(8,128)S(1)}, u32[]{:S(2)}, u32[]{:S(2)}) collective-permute-start(f32[43,8,128]{2,1,0:T(8,128)S(1)} %get-tuple-element.56.sent), channel_id=1, source_target_pairs={{0,2},{2,0},{4,6},{6,4},{8,10},{10,8},{12,14},{14,12},{16,18},{18,... | collective-permute-start | bytes 528392 | tf_op jit(solution)/shard_map/ppermute | solution.py:486
  38.5 4.5 %collective-permute-done.2.arrived = f32[43,8,128]{2,1,0:T(8,128)S(1)} collective-permute-done((f32[43,8,128]{2,1,0:T(8,128)S(1)}, f32[43,8,128]{2,1,0:T(8,128)S(1)}, u32[]{:S(2)}, u32[]{:S(2)}) %collective-permute-start.2) | collective-permute-done | bytes 176160 | tf_op jit(solution)/shard_map/ppermute | solution.py:486
  43.0 0.7 %collective-permute-start.3 = (f32[27,8,128]{2,1,0:T(8,128)S(1)}, f32[27,8,128]{2,1,0:T(8,128)S(1)}, u32[]{:S(2)}, u32[]{:S(2)}) collective-permute-start(f32[27,8,128]{2,1,0:T(8,128)S(1)} %get-tuple-element.58.sent), channel_id=1, source_target_pairs={{0,4},{2,6},{4,0},{6,2},{8,12},{10,14},{12,8},{14,10},{16,20},{18,... | collective-permute-start | bytes 331784 | tf_op jit(solution)/shard_map/ppermute | solution.py:486
  43.7 4.1 %collective-permute-done.3.arrived = f32[27,8,128]{2,1,0:T(8,128)S(1)} collective-permute-done((f32[27,8,128]{2,1,0:T(8,128)S(1)}, f32[27,8,128]{2,1,0:T(8,128)S(1)}, u32[]{:S(2)}, u32[]{:S(2)}) %collective-permute-start.3) | collective-permute-done | bytes 110624 | tf_op jit(solution)/shard_map/ppermute | solution.py:486
  47.8 0.8 %collective-permute-start.4 = (f32[20,8,128]{2,1,0:T(8,128)S(1)}, f32[20,8,128]{2,1,0:T(8,128)S(1)}, u32[]{:S(2)}, u32[]{:S(2)}) collective-permute-start(f32[20,8,128]{2,1,0:T(8,128)S(1)} %get-tuple-element.60.sent), channel_id=1, source_target_pairs={{0,8},{2,10},{4,12},{6,14},{8,0},{10,2},{12,4},{14,6},{16,24},{18,... | collective-permute-start | bytes 245768 | tf_op jit(solution)/shard_map/ppermute | solution.py:486
  48.6 3.7 %collective-permute-done.4.arrived = f32[20,8,128]{2,1,0:T(8,128)S(1)} collective-permute-done((f32[20,8,128]{2,1,0:T(8,128)S(1)}, f32[20,8,128]{2,1,0:T(8,128)S(1)}, u32[]{:S(2)}, u32[]{:S(2)}) %collective-permute-start.4) | collective-permute-done | bytes 81952 | tf_op jit(solution)/shard_map/ppermute | solution.py:486
  52.3 0.9 %collective-permute-start.5 = (f32[18,8,128]{2,1,0:T(8,128)S(1)}, f32[18,8,128]{2,1,0:T(8,128)S(1)}, u32[]{:S(2)}, u32[]{:S(2)}) collective-permute-start(f32[18,8,128]{2,1,0:T(8,128)S(1)} %get-tuple-element.62.sent), channel_id=1, source_target_pairs={{0,16},{2,18},{4,20},{6,22},{8,24},{10,26},{12,28},{14,30},{16,0},... | collective-permute-start | bytes 221192 | tf_op jit(solution)/shard_map/ppermute | solution.py:486
  53.2 1.1 %finish_alignment.1 = (bf16[2,64,64]{2,1,0:T(8,128)(2,1)}, f32[8,128]{1,0:T(8,128)S(1)}) custom-call(bf16[2,64,64]{2,1,0:T(8,128)(2,1)S(1)} %copy-done.1, f32[2,64,64]{2,1,0:T(8,128)S(1)} %get-tuple-element.48.middle_grad, f32[2,64]{1,0:T(2,128)S(1)} %copy-done.7, f32[64,128]{1,0:T(8,128)S(1)} %get-tuple-element.53.normed), custom_call_target="tpu_custom_call" | custom-call | tf_op jit(solution)/shard_map/finish_alignment/pallas_call | solution.py:465
  54.4 4.1 %collective-permute-done.5.arrived = f32[18,8,128]{2,1,0:T(8,128)S(1)} collective-permute-done((f32[18,8,128]{2,1,0:T(8,128)S(1)}, f32[18,8,128]{2,1,0:T(8,128)S(1)}, u32[]{:S(2)}, u32[]{:S(2)}) %collective-permute-start.5) | collective-permute-done | bytes 73760 | tf_op jit(solution)/shard_map/ppermute | solution.py:486
  58.5 0.7 %bias_last.1 = f32[8,8,64]{2,1,0:T(8,128)} custom-call(f32[4,8,128]{2,1,0:T(8,128)S(1)} %get-tuple-element.61.state, f32[18,8,128]{2,1,0:T(8,128)S(1)} %collective-permute-done.5.arrived), custom_call_target="tpu_custom_call" | custom-call | tf_op jit(solution)/shard_map/bias_last/pallas_call | solution.py:465
  59.2 0.6 collective-permute-done.6.refs_1_
  59.8 1.1 %unpack.1 = (f32[2,64]{1,0:T(2,128)}, f32[64,256]{1,0:T(8,128)}, f32[64,64]{1,0:T(8,128)}, f32[64,144]{1,0:T(8,128)}, f32[64,64]{1,0:T(8,128)}) custom-call(f32[18,8,128]{2,1,0:T(8,128)S(1)} %last_step.1.refs_0_, f32[18,8,128]{2,1,0:T(8,128)S(1)} %collective-permute-done.6.refs_1_, f32[2,64]{1,0:T(2,128)S(1)} %copy-done.7, f32[64,256]{1,0:T(8,128)S(1)} %copy-done, ...), custom_call_target="tpu_custom_call" | custom-call | tf_op jit(solution)/shard_map/unpack/pallas_call | solution.py:465
  (28 shorter events, 0.4 us)
Async XLA Ops:
  2.1 0.8 %copy-start.7 = (f32[2,64]{1,0:T(2,128)S(1)}, f32[2,64]{1,0:T(2,128)}, u32[]{:S(2)}) copy-start(f32[2,64]{1,0:T(2,128)} %refs_2_.3) | copy-start | bytes 1540
  2.1 0.8 %copy-start.8 = (s32[2]{0:T(128)S(1)}, s32[2]{0:T(128)}, u32[]{:S(2)}) copy-start(s32[2]{0:T(128)} %seq_mask.1) | copy-start | bytes 28
  2.1 0.9 %copy-start = (f32[64,256]{1,0:T(8,128)S(1)}, f32[64,256]{1,0:T(8,128)}, u32[]{:S(2)}) copy-start(f32[64,256]{1,0:T(8,128)} %refs_3_.3) | copy-start | bytes 196612
  2.2 1.8 %copy-start.4 = (bf16[8,64,128]{2,1,0:T(8,128)(2,1)S(1)}, bf16[8,64,128]{2,1,0:T(8,128)(2,1)}, u32[]{:S(2)}) copy-start(bf16[8,64,128]{2,1,0:T(8,128)(2,1)} %refs_11_.1) | copy-start | bytes 393220
  2.2 1.8 %collective-permute-start = (f32[3,64,64]{2,1,0:T(8,128)S(1)}, f32[3,64,64]{2,1,0:T(8,128)S(1)}, u32[]{:S(2)}, u32[]{:S(2)}) collective-permute-start(f32[3,64,64]{2,1,0:T(8,128)S(1)} %pad_maximum_fusion.sent.refs_0_), channel_id=1, source_target_pairs={{1,0},{0,1},{3,2},{2,3},{5,4},{4,5},{7,6},{6,7},{9,8},{8,9},{11,10... | collective-permute-start | bytes 147464 | tf_op jit(solution)/shard_map/ppermute | solution.py:478
  3.0 1.0 %copy-start.1 = (bf16[2,64,64]{2,1,0:T(8,128)(2,1)S(1)}, bf16[2,64,64]{2,1,0:T(8,128)(2,1)}, u32[]{:S(2)}) copy-start(bf16[2,64,64]{2,1,0:T(8,128)(2,1)} %own.1) | copy-start | bytes 49156
  3.0 1.0 %copy-start.3 = (f32[64,64]{1,0:T(8,128)S(1)}, f32[64,64]{1,0:T(8,128)}, u32[]{:S(2)}) copy-start(f32[64,64]{1,0:T(8,128)} %w_out.3) | copy-start | bytes 49156
  3.0 1.0 %copy-start.5 = (bf16[2,64,64]{2,1,0:T(8,128)(2,1)S(1)}, bf16[2,64,64]{2,1,0:T(8,128)(2,1)}, u32[]{:S(2)}) copy-start(bf16[2,64,64]{2,1,0:T(8,128)(2,1)} %refs_3_.2) | copy-start | bytes 49156
  6.2 15.9 %copy-start.2 = (f32[64,144]{1,0:T(8,128)S(1)}, f32[64,144]{1,0:T(8,128)}, u32[]{:S(2)}) copy-start(f32[64,144]{1,0:T(8,128)} %refs_4_.3) | copy-start | bytes 110596
  6.2 15.9 %copy-start.6 = (f32[64,64]{1,0:T(8,128)S(1)}, f32[64,64]{1,0:T(8,128)}, u32[]{:S(2)}) copy-start(f32[64,64]{1,0:T(8,128)} %w_out.2) | copy-start | bytes 49156
  36.1 1.3 %collective-permute-start.1 = (f32[152,128]{1,0:T(8,128)S(1)}, f32[152,128]{1,0:T(8,128)S(1)}, u32[]{:S(2)}, u32[]{:S(2)}) collective-permute-start(f32[152,128]{1,0:T(8,128)S(1)} %get-tuple-element.52), channel_id=1, source_target_pairs={{1,0},{0,1},{3,2},{2,3},{5,4},{4,5},{7,6},{6,7},{9,8},{8,9},{11,10... | collective-permute-start | bytes 233480 | tf_op jit(solution)/shard_map/ppermute | solution.py:478
  37.5 5.5 %collective-permute-start.2 = (f32[43,8,128]{2,1,0:T(8,128)S(1)}, f32[43,8,128]{2,1,0:T(8,128)S(1)}, u32[]{:S(2)}, u32[]{:S(2)}) collective-permute-start(f32[43,8,128]{2,1,0:T(8,128)S(1)} %get-tuple-element.56.sent), channel_id=1, source_target_pairs={{0,2},{2,0},{4,6},{6,4},{8,10},{10,8},{12,14},{14,12},{16,18},{18,... | collective-permute-start | bytes 528392 | tf_op jit(solution)/shard_map/ppermute | solution.py:486
  43.0 4.8 %collective-permute-start.3 = (f32[27,8,128]{2,1,0:T(8,128)S(1)}, f32[27,8,128]{2,1,0:T(8,128)S(1)}, u32[]{:S(2)}, u32[]{:S(2)}) collective-permute-start(f32[27,8,128]{2,1,0:T(8,128)S(1)} %get-tuple-element.58.sent), channel_id=1, source_target_pairs={{0,4},{2,6},{4,0},{6,2},{8,12},{10,14},{12,8},{14,10},{16,20},{18,... | collective-permute-start | bytes 331784 | tf_op jit(solution)/shard_map/ppermute | solution.py:486
  47.8 4.5 %collective-permute-start.4 = (f32[20,8,128]{2,1,0:T(8,128)S(1)}, f32[20,8,128]{2,1,0:T(8,128)S(1)}, u32[]{:S(2)}, u32[]{:S(2)}) collective-permute-start(f32[20,8,128]{2,1,0:T(8,128)S(1)} %get-tuple-element.60.sent), channel_id=1, source_target_pairs={{0,8},{2,10},{4,12},{6,14},{8,0},{10,2},{12,4},{14,6},{16,24},{18,... | collective-permute-start | bytes 245768 | tf_op jit(solution)/shard_map/ppermute | solution.py:486
  52.3 6.1 %collective-permute-start.5 = (f32[18,8,128]{2,1,0:T(8,128)S(1)}, f32[18,8,128]{2,1,0:T(8,128)S(1)}, u32[]{:S(2)}, u32[]{:S(2)}) collective-permute-start(f32[18,8,128]{2,1,0:T(8,128)S(1)} %get-tuple-element.62.sent), channel_id=1, source_target_pairs={{0,16},{2,18},{4,20},{6,22},{8,24},{10,26},{12,28},{14,30},{16,0},... | collective-permute-start | bytes 221192 | tf_op jit(solution)/shard_map/ppermute | solution.py:486
  58.5 1.3 %collective-permute-start.6 = (f32[18,8,128]{2,1,0:T(8,128)S(1)}, f32[18,8,128]{2,1,0:T(8,128)S(1)}, u32[]{:S(2)}, u32[]{:S(2)}) collective-permute-start(f32[18,8,128]{2,1,0:T(8,128)S(1)} %last_step.1.refs_0_), channel_id=1, source_target_pairs={{1,0},{0,1},{3,2},{2,3},{5,4},{4,5},{7,6},{6,7},{9,8},{8,9},{11,10... | collective-permute-start | bytes 221192 | tf_op jit(solution)/shard_map/ppermute | solution.py:478

commit v13 on v12

--- a/solution.py
+++ b/solution.py
@@ -410,14 +410,15 @@
         out[s] = (middle_grad[s] + normalise_back(grad_normed, gains[0:1, :], unit, inverse)).astype(out.dtype)
 
 
-def unpack(n_res, *refs):
+def unpack(n_res, part_tiles, *refs):
     parts = refs[:n_res]
     gains, w_row, w_col, gains_out, row_project_out, row_out_out, col_project_out, col_out_out = refs[n_res : n_res + 8]
     shares, column = refs[n_res + 8 :]
     me = lax.axis_index("res")
     for away in range(n_res):
         shares[lax.rem(me + away, n_res)] = parts[away][...]
-    n_blocks, _, share, _ = column.shape
+    n_blocks = 2 * parts[0].shape[0] - 2 * part_tiles
+    share = C // n_blocks
     part = shares.shape[1] - n_blocks // 2
     place = lax.axis_index("seq")
     for half in range(2):
@@ -425,11 +426,11 @@
         for slot in range(n_blocks):
             block = place ^ sum(1 << bit for at, bit in enumerate(bits) if slot >> at & 1)
             row = slot % 2 * (ROWS // 2)
-            column[block, half] = shares[half, part + slot // 2, row : row + share, :]
+            column[half, pl.ds(block * share, share), :] = shares[half, part + slot // 2, row : row + share, :]
     flat = jnp.concatenate([shares[i, :part].reshape(part * ROWS, LANES) for i in range(n_res)], axis=0)
     query_gate, memory, outs = flat[:C], flat[C : 2 * C], flat[2 * C : 2 * C + C // 2]
-    col_query_gate = jnp.concatenate([column[i, 0] for i in range(n_blocks)], axis=0)
-    col_rest = jnp.concatenate([column[i, 1] for i in range(n_blocks)], axis=0)
+    col_query_gate = column[0]
+    col_rest = column[1]
     rest = col_rest[:, C : C + 2 * DH]
     gain_row = to_column(gains[0:1, :])
     gain_col = to_column(gains[1:2, :])
@@ -598,13 +599,13 @@
     )
     (bias_grad,) = call(bias_last, [((H, keys_each, n_rows), F32)], state, arrived, name="bias_last")
     grads = call(
-        functools.partial(unpack, res_count),
+        functools.partial(unpack, res_count, part_tiles),
         [((2, C), F32), ((C, 4 * C), F32), ((C, C), F32), ((C, 2 * C + 2 * DH), F32), ((C, C), F32)],
         shared, *[shift_residues(shared, away, res_count) for away in away_range],
         norm_gains, row_project, column_project,
         scratch=[
             pltpu.VMEM((res_count, part_tiles + seq_count // 2, ROWS, LANES), F32),
-            pltpu.VMEM((seq_count, 2, C // seq_count, LANES), F32),
+            pltpu.VMEM((2, C, LANES), F32),
         ],
         name="unpack",
     )

time: 61.2 us -> 61.2 us (level)
  no operation moved by 1% of the time
where the time goes in v13:
time: 61.2 us; the launch traced here: 60.9 us
  blocking collectives  26.2 us (43%)
  waiting for transfers between devices  18.2 us (30%)
  Pallas kernels  10 us (16%)
  starting transfers between devices  4.07 us (7%)
  other arithmetic  1.43 us (2%)
  between operations  0.8 us (1%)
    all_to_all x2, blocking collectives, swap_blocks(): return lax.all_to_all(values, 'seq', 0, 0, tiled=True)  26.2 us
    ppermute x4, waiting for transfers between devices, cross(): return lax.ppermute(values, ('seq', 'res'), pairs)  16.4 us
    pallas_call x14, Pallas kernels, call(): pl.pallas_call(body, out_shape=[jax.ShapeDtypeStruct(shape, kind) for sha...  10 us
    ppermute x4, starting transfers between devices, cross(): return lax.ppermute(values, ('seq', 'res'), pairs)  3.41 us
    ppermute x3, waiting for transfers between devices, shift_residues(): lax.ppermute(values, 'res', [((i + away) % count, i) for i in range(count)])  1.78 us
  transfers between devices with their start and end apart: 7, of which 6 were waited for; matrix products, arithmetic and copies ran while one was open for 0% of the time, Pallas kernels for 5%

profile of v13, /device:TPU:0, one launch (start us, length us, event | category | flops | bytes accessed | tf_op | source)
XLA Modules:
  0.0 60.9 jit_solution(518033965146362807)
XLA Ops:
  0.6 0.7 %convert_element_type.7 = f32[64]{0:T(128)S(1)} convert(s32[64]{0:T(128)} %param.18) | non-fusion elementwise | flops 64 | bytes 512 | tf_op jit(solution)/shard_map/convert_element_type | solution.py:513
  1.3 0.8 %convert_element_type.6 = f32[2,64,64]{2,1,0:T(8,128)S(1)} convert(bf16[2,64,64]{2,1,0:T(8,128)(2,1)} %own.1) | non-fusion elementwise | flops 8192 | bytes 49152 | tf_op jit(solution)/shard_map/convert_element_type | solution.py:514
  2.2 0.5 collective-permute-start
  2.7 0.2 own_norm.1.own_unit.refs_7_.own_unit_in
  2.9 0.1 copy-done
  3.0 1.0 %own_half.1 = (f32[2,64,128]{2,1,0:T(8,128)S(1)}, f32[2,64,512]{2,1,0:T(8,128)S(1)}, f32[2,64,128]{2,1,0:T(8,128)S(1)}, f32[4,128]{1,0:T(4,128)S(1)}) custom-call(s32[2]{0:T(128)S(1)} %copy-done.8, f32[2,64,64]{2,1,0:T(8,128)S(1)} %own_norm.1.own_unit.refs_7_.own_unit_in, f32[2,64]{1,0:T(2,128)S(1)} %copy-done.7, f32[64,256]{1,0:T(8,128)S(1)} %copy-done), custom_call_target="tpu_custom_call" | custom-call | tf_op jit(solution)/shard_map/own_half/pallas_call | solution.py:466
  4.0 2.2 %row_forward.1 = (f32[16,3,4,128]{3,2,1,0:T(4,128)S(1)}, f32[2,128,512]{2,1,0:T(8,128)S(1)}, f32[2,2,64,64]{3,2,1,0:T(8,128)S(1)}, f32[2,2,64,128]{3,2,1,0:T(8,1...) custom-call(f32[3,64,64]{2,1,0:T(8,128)S(1)} %pad_maximum_fusion.sent.refs_0_, ...), custom_call_target="tpu_custom_call" | custom-call | tf_op jit(solution)/shard_map/row_forward/pallas_call | solution.py:466
  6.2 15.9 %all_to_all.10.arrived = f32[16,3,4,128]{3,2,1,0:T(4,128)S(1)} all-to-all(f32[16,3,4,128]{3,2,1,0:T(4,128)S(1)} %get-tuple-element.42), channel_id=1, replica_groups=mesh['seq'=16,'res'=2] {'seq'}, dimensions={0} | all-to-all | bytes 196608 | tf_op jit(solution)/shard_map/all_to_all | solution.py:491
  22.1 1.7 %column_step.1 = f32[16,3,4,128]{3,2,1,0:T(4,128)S(1)} custom-call(f32[16,3,4,128]{3,2,1,0:T(4,128)S(1)} %all_to_all.10.arrived, f32[2,64]{1,0:T(2,128)S(1)} %copy-done.7, f32[64,144]{1,0:T(8,128)S(1)} %copy-done.2, f32[64,64]{1,0:T(8,128)S(1)} %copy-done.6), custom_call_target="tpu_custom_call" | custom-call | tf_op jit(solution)/shard_map/column_step/pallas_call | solution.py:466
  23.8 10.3 %all_to_all.11.returned = f32[16,3,4,128]{3,2,1,0:T(4,128)S(1)} all-to-all(f32[16,3,4,128]{3,2,1,0:T(4,128)S(1)} %column_step.1), channel_id=1, replica_groups=mesh['seq'=16,'res'=2] {'seq'}, dimensions={0} | all-to-all | bytes 196608 | tf_op jit(solution)/shard_map/all_to_all | solution.py:491
  34.1 2.0 %row_backward.1 = (f32[128,512]{1,0:T(8,128)S(1)}, f32[2,64,64]{2,1,0:T(8,128)S(1)}, f32[152,128]{1,0:T(8,128)S(1)}, f32[152,128]{1,0:T(8,128)S(1)}) custom-call(f32[16,3,4,128]{3,2,1,0:T(4,128)S(1)} %all_to_all.11.returned, f32[2,128,512]{2,1,0:T(8,128)S(1)} %get-tuple-element.43.exponent_in, f32[2,2,64,64]{3,2,1,0:T(8,128)S(1)} %get-tuple-element.44.unit_in, ...), custom_call_target="tpu_custom_call" | custom-call | tf_op jit(solution)/shard_map/row_backward/pallas_call | solution.py:466
  36.2 1.2 %collective-permute-done.1.refs_1_ = f32[152,128]{1,0:T(8,128)S(1)} collective-permute-done((f32[152,128]{1,0:T(8,128)S(1)}, f32[152,128]{1,0:T(8,128)S(1)}, u32[]{:S(2)}, u32[]{:S(2)}) %collective-permute-start.1) | collective-permute-done | bytes 77856 | tf_op jit(solution)/shard_map/ppermute | solution.py:479
  37.5 1.0 %collective-permute-start.2 = (f32[43,8,128]{2,1,0:T(8,128)S(1)}, f32[43,8,128]{2,1,0:T(8,128)S(1)}, u32[]{:S(2)}, u32[]{:S(2)}) collective-permute-start(f32[43,8,128]{2,1,0:T(8,128)S(1)} %get-tuple-element.56.sent), channel_id=1, source_target_pairs={{0,2},{2,0},{4,6},{6,4},{8,10},{10,8},{12,14},{14,12},{16,18},{18,... | collective-permute-start | bytes 528392 | tf_op jit(solution)/shard_map/ppermute | solution.py:487
  38.5 4.5 %collective-permute-done.2.arrived = f32[43,8,128]{2,1,0:T(8,128)S(1)} collective-permute-done((f32[43,8,128]{2,1,0:T(8,128)S(1)}, f32[43,8,128]{2,1,0:T(8,128)S(1)}, u32[]{:S(2)}, u32[]{:S(2)}) %collective-permute-start.2) | collective-permute-done | bytes 176160 | tf_op jit(solution)/shard_map/ppermute | solution.py:487
  43.0 0.7 %collective-permute-start.3 = (f32[27,8,128]{2,1,0:T(8,128)S(1)}, f32[27,8,128]{2,1,0:T(8,128)S(1)}, u32[]{:S(2)}, u32[]{:S(2)}) collective-permute-start(f32[27,8,128]{2,1,0:T(8,128)S(1)} %get-tuple-element.58.sent), channel_id=1, source_target_pairs={{0,4},{2,6},{4,0},{6,2},{8,12},{10,14},{12,8},{14,10},{16,20},{18,... | collective-permute-start | bytes 331784 | tf_op jit(solution)/shard_map/ppermute | solution.py:487
  43.7 4.1 %collective-permute-done.3.arrived = f32[27,8,128]{2,1,0:T(8,128)S(1)} collective-permute-done((f32[27,8,128]{2,1,0:T(8,128)S(1)}, f32[27,8,128]{2,1,0:T(8,128)S(1)}, u32[]{:S(2)}, u32[]{:S(2)}) %collective-permute-start.3) | collective-permute-done | bytes 110624 | tf_op jit(solution)/shard_map/ppermute | solution.py:487
  47.8 0.8 %collective-permute-start.4 = (f32[20,8,128]{2,1,0:T(8,128)S(1)}, f32[20,8,128]{2,1,0:T(8,128)S(1)}, u32[]{:S(2)}, u32[]{:S(2)}) collective-permute-start(f32[20,8,128]{2,1,0:T(8,128)S(1)} %get-tuple-element.60.sent), channel_id=1, source_target_pairs={{0,8},{2,10},{4,12},{6,14},{8,0},{10,2},{12,4},{14,6},{16,24},{18,... | collective-permute-start | bytes 245768 | tf_op jit(solution)/shard_map/ppermute | solution.py:487
  48.6 3.7 %collective-permute-done.4.arrived = f32[20,8,128]{2,1,0:T(8,128)S(1)} collective-permute-done((f32[20,8,128]{2,1,0:T(8,128)S(1)}, f32[20,8,128]{2,1,0:T(8,128)S(1)}, u32[]{:S(2)}, u32[]{:S(2)}) %collective-permute-start.4) | collective-permute-done | bytes 81952 | tf_op jit(solution)/shard_map/ppermute | solution.py:487
  52.3 0.9 %collective-permute-start.5 = (f32[18,8,128]{2,1,0:T(8,128)S(1)}, f32[18,8,128]{2,1,0:T(8,128)S(1)}, u32[]{:S(2)}, u32[]{:S(2)}) collective-permute-start(f32[18,8,128]{2,1,0:T(8,128)S(1)} %get-tuple-element.62.sent), channel_id=1, source_target_pairs={{0,16},{2,18},{4,20},{6,22},{8,24},{10,26},{12,28},{14,30},{16,0},... | collective-permute-start | bytes 221192 | tf_op jit(solution)/shard_map/ppermute | solution.py:487
  53.2 1.1 %finish_alignment.1 = (bf16[2,64,64]{2,1,0:T(8,128)(2,1)}, f32[8,128]{1,0:T(8,128)S(1)}) custom-call(bf16[2,64,64]{2,1,0:T(8,128)(2,1)S(1)} %copy-done.1, f32[2,64,64]{2,1,0:T(8,128)S(1)} %get-tuple-element.48.middle_grad, f32[2,64]{1,0:T(2,128)S(1)} %copy-done.7, f32[64,128]{1,0:T(8,128)S(1)} %get-tuple-element.53.normed), custom_call_target="tpu_custom_call" | custom-call | tf_op jit(solution)/shard_map/finish_alignment/pallas_call | solution.py:466
  54.4 4.1 %collective-permute-done.5.arrived = f32[18,8,128]{2,1,0:T(8,128)S(1)} collective-permute-done((f32[18,8,128]{2,1,0:T(8,128)S(1)}, f32[18,8,128]{2,1,0:T(8,128)S(1)}, u32[]{:S(2)}, u32[]{:S(2)}) %collective-permute-start.5) | collective-permute-done | bytes 73760 | tf_op jit(solution)/shard_map/ppermute | solution.py:487
  58.5 0.7 %bias_last.1 = f32[8,8,64]{2,1,0:T(8,128)} custom-call(f32[4,8,128]{2,1,0:T(8,128)S(1)} %get-tuple-element.61.state, f32[18,8,128]{2,1,0:T(8,128)S(1)} %collective-permute-done.5.arrived), custom_call_target="tpu_custom_call" | custom-call | tf_op jit(solution)/shard_map/bias_last/pallas_call | solution.py:466
  59.2 0.6 collective-permute-done.6.refs_1_
  59.8 1.1 %unpack.1 = (f32[2,64]{1,0:T(2,128)}, f32[64,256]{1,0:T(8,128)}, f32[64,64]{1,0:T(8,128)}, f32[64,144]{1,0:T(8,128)}, f32[64,64]{1,0:T(8,128)}) custom-call(f32[18,8,128]{2,1,0:T(8,128)S(1)} %last_step.1.refs_0_, f32[18,8,128]{2,1,0:T(8,128)S(1)} %collective-permute-done.6.refs_1_, f32[2,64]{1,0:T(2,128)S(1)} %copy-done.7, f32[64,256]{1,0:T(8,128)S(1)} %copy-done, ...), custom_call_target="tpu_custom_call" | custom-call | tf_op jit(solution)/shard_map/unpack/pallas_call | solution.py:466
  (28 shorter events, 0.4 us)
Async XLA Ops:
  2.1 0.8 %copy-start.7 = (f32[2,64]{1,0:T(2,128)S(1)}, f32[2,64]{1,0:T(2,128)}, u32[]{:S(2)}) copy-start(f32[2,64]{1,0:T(2,128)} %refs_2_.3) | copy-start | bytes 1540
  2.1 0.8 %copy-start.8 = (s32[2]{0:T(128)S(1)}, s32[2]{0:T(128)}, u32[]{:S(2)}) copy-start(s32[2]{0:T(128)} %seq_mask.1) | copy-start | bytes 28
  2.1 0.9 %copy-start = (f32[64,256]{1,0:T(8,128)S(1)}, f32[64,256]{1,0:T(8,128)}, u32[]{:S(2)}) copy-start(f32[64,256]{1,0:T(8,128)} %refs_3_.3) | copy-start | bytes 196612
  2.2 1.8 %copy-start.4 = (bf16[8,64,128]{2,1,0:T(8,128)(2,1)S(1)}, bf16[8,64,128]{2,1,0:T(8,128)(2,1)}, u32[]{:S(2)}) copy-start(bf16[8,64,128]{2,1,0:T(8,128)(2,1)} %refs_11_.1) | copy-start | bytes 393220
  2.2 1.8 %collective-permute-start = (f32[3,64,64]{2,1,0:T(8,128)S(1)}, f32[3,64,64]{2,1,0:T(8,128)S(1)}, u32[]{:S(2)}, u32[]{:S(2)}) collective-permute-start(f32[3,64,64]{2,1,0:T(8,128)S(1)} %pad_maximum_fusion.sent.refs_0_), channel_id=1, source_target_pairs={{1,0},{0,1},{3,2},{2,3},{5,4},{4,5},{7,6},{6,7},{9,8},{8,9},{11,10... | collective-permute-start | bytes 147464 | tf_op jit(solution)/shard_map/ppermute | solution.py:479
  3.0 1.0 %copy-start.1 = (bf16[2,64,64]{2,1,0:T(8,128)(2,1)S(1)}, bf16[2,64,64]{2,1,0:T(8,128)(2,1)}, u32[]{:S(2)}) copy-start(bf16[2,64,64]{2,1,0:T(8,128)(2,1)} %own.1) | copy-start | bytes 49156
  3.0 1.0 %copy-start.3 = (f32[64,64]{1,0:T(8,128)S(1)}, f32[64,64]{1,0:T(8,128)}, u32[]{:S(2)}) copy-start(f32[64,64]{1,0:T(8,128)} %w_out.3) | copy-start | bytes 49156
  3.0 1.0 %copy-start.5 = (bf16[2,64,64]{2,1,0:T(8,128)(2,1)S(1)}, bf16[2,64,64]{2,1,0:T(8,128)(2,1)}, u32[]{:S(2)}) copy-start(bf16[2,64,64]{2,1,0:T(8,128)(2,1)} %refs_3_.2) | copy-start | bytes 49156
  6.2 15.9 %copy-start.2 = (f32[64,144]{1,0:T(8,128)S(1)}, f32[64,144]{1,0:T(8,128)}, u32[]{:S(2)}) copy-start(f32[64,144]{1,0:T(8,128)} %refs_4_.3) | copy-start | bytes 110596
  6.2 15.9 %copy-start.6 = (f32[64,64]{1,0:T(8,128)S(1)}, f32[64,64]{1,0:T(8,128)}, u32[]{:S(2)}) copy-start(f32[64,64]{1,0:T(8,128)} %w_out.2) | copy-start | bytes 49156
  36.1 1.3 %collective-permute-start.1 = (f32[152,128]{1,0:T(8,128)S(1)}, f32[152,128]{1,0:T(8,128)S(1)}, u32[]{:S(2)}, u32[]{:S(2)}) collective-permute-start(f32[152,128]{1,0:T(8,128)S(1)} %get-tuple-element.52), channel_id=1, source_target_pairs={{1,0},{0,1},{3,2},{2,3},{5,4},{4,5},{7,6},{6,7},{9,8},{8,9},{11,10... | collective-permute-start | bytes 233480 | tf_op jit(solution)/shard_map/ppermute | solution.py:479
  37.5 5.5 %collective-permute-start.2 = (f32[43,8,128]{2,1,0:T(8,128)S(1)}, f32[43,8,128]{2,1,0:T(8,128)S(1)}, u32[]{:S(2)}, u32[]{:S(2)}) collective-permute-start(f32[43,8,128]{2,1,0:T(8,128)S(1)} %get-tuple-element.56.sent), channel_id=1, source_target_pairs={{0,2},{2,0},{4,6},{6,4},{8,10},{10,8},{12,14},{14,12},{16,18},{18,... | collective-permute-start | bytes 528392 | tf_op jit(solution)/shard_map/ppermute | solution.py:487
  43.0 4.8 %collective-permute-start.3 = (f32[27,8,128]{2,1,0:T(8,128)S(1)}, f32[27,8,128]{2,1,0:T(8,128)S(1)}, u32[]{:S(2)}, u32[]{:S(2)}) collective-permute-start(f32[27,8,128]{2,1,0:T(8,128)S(1)} %get-tuple-element.58.sent), channel_id=1, source_target_pairs={{0,4},{2,6},{4,0},{6,2},{8,12},{10,14},{12,8},{14,10},{16,20},{18,... | collective-permute-start | bytes 331784 | tf_op jit(solution)/shard_map/ppermute | solution.py:487
  47.8 4.5 %collective-permute-start.4 = (f32[20,8,128]{2,1,0:T(8,128)S(1)}, f32[20,8,128]{2,1,0:T(8,128)S(1)}, u32[]{:S(2)}, u32[]{:S(2)}) collective-permute-start(f32[20,8,128]{2,1,0:T(8,128)S(1)} %get-tuple-element.60.sent), channel_id=1, source_target_pairs={{0,8},{2,10},{4,12},{6,14},{8,0},{10,2},{12,4},{14,6},{16,24},{18,... | collective-permute-start | bytes 245768 | tf_op jit(solution)/shard_map/ppermute | solution.py:487
  52.3 6.1 %collective-permute-start.5 = (f32[18,8,128]{2,1,0:T(8,128)S(1)}, f32[18,8,128]{2,1,0:T(8,128)S(1)}, u32[]{:S(2)}, u32[]{:S(2)}) collective-permute-start(f32[18,8,128]{2,1,0:T(8,128)S(1)} %get-tuple-element.62.sent), channel_id=1, source_target_pairs={{0,16},{2,18},{4,20},{6,22},{8,24},{10,26},{12,28},{14,30},{16,0},... | collective-permute-start | bytes 221192 | tf_op jit(solution)/shard_map/ppermute | solution.py:487
  58.5 1.3 %collective-permute-start.6 = (f32[18,8,128]{2,1,0:T(8,128)S(1)}, f32[18,8,128]{2,1,0:T(8,128)S(1)}, u32[]{:S(2)}, u32[]{:S(2)}) collective-permute-start(f32[18,8,128]{2,1,0:T(8,128)S(1)} %last_step.1.refs_0_), channel_id=1, source_target_pairs={{1,0},{0,1},{3,2},{2,3},{5,4},{4,5},{7,6},{6,7},{9,8},{8,9},{11,10... | collective-permute-start | bytes 221192 | tf_op jit(solution)/shard_map/ppermute | solution.py:479
